TPU v7x, 32 devices: a whole 2x2x4 slice. The times are simulated.
32 devices in a mesh: group: 2 (over y), expert: 16 (over z, x, core), tensor: 1.
Axes of the slice: x: 2, y: 2, z: 4, core: 2. Of those that a mesh axis runs over, the one named last changes fastest.
Arguments:
- tokens: bfloat16 [512, 2048], P(('group', 'expert')), parts along dimension 0, may hold values from -6 to 6
- route_weight: float32 [512, 8], P(('group', 'expert')), parts along dimension 0, may hold values from 0.02 to 1
- replica: int32 [512, 8], P(('group', 'expert')), parts along dimension 0, may hold values from 0 to 15, all different within a row; in each aligned block of 16 rows (0 to 15, 16 to 31, ...) at most 16 rows name the same one
- w_gate: bfloat16 [16, 2048, 768], P('expert', None, 'tensor'), may hold values from -0.125 to 0.125
- w_up: bfloat16 [16, 2048, 768], P('expert', None, 'tensor'), may hold values from -0.125 to 0.125
- w_down: bfloat16 [16, 768, 2048], P('expert', None, 'tensor'), may hold values from -0.21875 to 0.21875
Outputs:
- mixed: bfloat16 [512, 2048], P(('group', 'expert'), 'tensor'), parts along dimension 0
There are 2 independent parts, one for each index of `group`. A program takes and returns all parts, laid end to end along the dimension named above; an argument that names none is the same for every part. Nothing has to cross between parts.
Inputs may be any that keep to these rules, and one draw needn't show every extreme that they name: Each row names 8 different replicas. Among the rows of one index of expert (aligned blocks of 16 rows) no replica is named more than 16 times, a bound that some block reaches.
All inputs are finite; a program needn't handle non-finite values.
Results may differ from a plain program's by a relative error of at most 0.0037.
Values may be sent and summed in bfloat16 or wider, within the bound.
No kernel may reach another device: no remote copies, remote signals or barrier semaphores. Data moves between devices by JAX's collectives and lax.ppermute only.
A program may use at most 64 MiB of HBM per device.

v0:
```python
import jax
import jax.numpy as jnp
from jax import lax
from jax.sharding import PartitionSpec as P


def shards(tokens, route_weight, replica, w_gate, w_up, w_down):
    row_count, width = tokens.shape
    top_count = replica.shape[1]
    peer_count = lax.axis_size("expert")
    capacity = min(row_count, max(2, 2 * row_count * top_count // peer_count))
    column_count = w_down.shape[2]
    part_index = lax.axis_index("tensor")
    probability = route_weight / jnp.sum(route_weight, axis=1, keepdims=True)
    flat_slot = replica.reshape(-1)
    one_hot = (flat_slot[:, None] == jnp.arange(peer_count, dtype=jnp.int32)[None, :]).astype(
        jnp.int32
    )
    earlier = jnp.cumsum(one_hot, axis=0) - one_hot
    position = jnp.sum(earlier * one_hot, axis=1)
    source_row = jnp.arange(row_count * top_count, dtype=jnp.int32) // top_count
    own_columns = lax.dynamic_slice_in_dim(tokens, part_index * column_count, column_count, 1)
    outgoing = jnp.zeros((peer_count, capacity, width), jnp.bfloat16)
    outgoing = outgoing.at[flat_slot, position].set(tokens[source_row])
    received = lax.all_to_all(outgoing, "expert", split_axis=0, concat_axis=0, tiled=True)
    slot_rows = received.shape[1]
    flat_rows = received.reshape(-1, width)
    gate = jnp.dot(flat_rows, w_gate[0], preferred_element_type=jnp.float32)
    upward = jnp.dot(flat_rows, w_up[0], preferred_element_type=jnp.float32)
    hidden = (jax.nn.silu(gate) * upward).astype(jnp.bfloat16)
    all_hidden = lax.all_gather(hidden, "tensor", axis=1, tiled=True)
    result = jnp.dot(all_hidden, w_down[0], preferred_element_type=jnp.float32).astype(jnp.bfloat16)
    result = result.reshape(peer_count, slot_rows, column_count)
    returned = lax.all_to_all(result, "expert", split_axis=0, concat_axis=0, tiled=True)
    values = returned[flat_slot, position].astype(jnp.float32)
    weighted = values * probability.reshape(-1)[:, None]
    combined = jnp.sum(weighted.reshape(row_count, top_count, column_count), axis=1)
    return (own_columns.astype(jnp.float32) + combined).astype(jnp.bfloat16)


def solution(mesh):
    return jax.shard_map(
        shards,
        mesh=mesh,
        in_specs=(
            P(("group", "expert"), None),
            P(("group", "expert"), None),
            P(("group", "expert"), None),
            P("expert", None, "tensor"),
            P("expert", None, "tensor"),
            P("expert", None, "tensor"),
        ),
        out_specs=P(("group", "expert"), "tensor"),
        check_vma=False,
    )
```

profile of v0, /device:TPU:0, one launch (start us, length us, event | category | flops | bytes accessed | tf_op | source)
XLA Modules:
  0.0 104.3 jit_solution(11268919675874290367)
XLA Ops:
  0.0 0.0 copy-start
  0.0 0.0 copy-start.1
  0.0 0.9 copy.10
  0.9 0.1 eq.15
  1.0 0.1 reshape.105
  1.1 0.1 fusion.19
  1.2 0.2 reduce_window_sum.11
  1.4 0.2 select_reduce_fusion
  1.6 0.0 copy-done.1
  1.6 1.7 %gather_fusion = bf16[128,2048]{1,0:T(8,128)(2,1)} fusion(bf16[16,2048]{1,0:T(8,128)(2,1)S(1)} %copy-done.1, s32[1024]{0:T(1024)S(1)} %pad_clamp_fusion), kind=kCustom, calls=%fused_computation | custom fusion | bytes 1049088 | tf_op jit(solution)/shard_map/gather | solution.py:24
  3.3 1.1 %broadcast_in_dim.2 = bf16[16,16,2048]{2,1,0:T(8,128)(2,1)} broadcast(bf16[]{:T(256)} %constant.27.clone.1), dimensions={} | broadcast | bytes 1048578 | tf_op jit(solution)/shard_map/broadcast_in_dim | solution.py:23
  4.5 23.6 %scatter_fusion = bf16[16,16,2048]{2,1,0:T(8,128)(2,1)} fusion(bf16[16,16,2048]{2,1,0:T(8,128)(2,1)} %broadcast_in_dim.2, s32[128]{0:T(128)S(1)} %get-tuple-element.5, bf16[128,2048]{1,0:T(8,128)(2,1)} %gather_fusion), kind=kCustom, calls=%fused_computation.2 | custom fusion | bytes 1573888 | tf_op jit(solution)/shard_map/scatter | solution.py:24
  28.0 32.1 %all_to_all.10 = bf16[16,16,2048]{2,1,0:T(8,128)(2,1)S(1)} all-to-all(bf16[16,16,2048]{2,1,0:T(8,128)(2,1)} %scatter_fusion), channel_id=1, replica_groups=mesh['group'=2,'expert'=16,'tensor'=1] {'expert'}, dimensions={0} | all-to-all | bytes 2097152 | tf_op jit(solution)/shard_map/all_to_all | solution.py:25
  60.2 0.0 copy-start.2
  60.2 1.0 copy-done.2
  61.2 3.8 %fusion.4 = f32[256,768]{1,0:T(8,128)} fusion(bf16[256,2048]{1,0:T(8,128)(2,1)S(1)} %bitcast.38, bf16[1,2048,768]{2,1,0:T(8,128)(2,1)} %param.9), kind=kOutput, calls=%fused_computation.7 | convolution fusion | flops 805306368 | bytes 4980736 | tf_op jit(solution)/shard_map/dot_general | solution.py:28
  65.0 0.0 copy-done
  65.0 0.0 copy-start.3
  65.0 5.5 %fusion.6 = bf16[256,2048]{1,0:T(8,128)(2,1)} fusion(bf16[1,768,2048]{2,1,0:T(8,128)(2,1)S(1)} %copy-done, bf16[256,2048]{1,0:T(8,128)(2,1)} %bitcast.39, bf16[1,2048,768]{2,1,0:T(8,128)(2,1)} %param.10, f32[256,768]{1,0:T(8,128)} %fusion.4), kind=kOutput, calls=%fused_computation.9 | convolution fusion | flops 1612316672 | bytes 9175040 | tf_op jit(solution)/shard_map/dot_general | solution.py:32
  70.5 5.0 %all-to-all-start.1 = ((bf16[16,16,2048]{2,1,0:T(8,128)(2,1)}), bf16[16,16,2048]{2,1,0:T(8,128)(2,1)}, u32[]{:S(2)}, u32[]{:S(2)}) async-start(bf16[16,16,2048]{2,1,0:T(8,128)(2,1)} %bitcast.37), calls=%async_computation.1 | async-start | bytes 2097152 | tf_op jit(solution)/shard_map/all_to_all | solution.py:34
  75.6 0.0 copy-done.3
  75.6 0.1 copy.12
  75.7 22.9 %all-to-all-done.1 = bf16[16,16,2048]{2,1,0:T(8,128)(2,1)} async-done(((bf16[16,16,2048]{2,1,0:T(8,128)(2,1)}), bf16[16,16,2048]{2,1,0:T(8,128)(2,1)}, u32[]{:S(2)}, u32[]{:S(2)}) %all-to-all-start.1) | async-done | bytes 1048608 | tf_op jit(solution)/shard_map/all_to_all | solution.py:34
  98.6 3.5 %gather_fusion.1 = bf16[128,2048]{1,0:T(8,128)(2,1)} fusion(bf16[16,16,2048]{2,1,0:T(8,128)(2,1)} %all-to-all-done.1, s32[128]{0:T(128)S(1)} %bitcast.36), kind=kCustom, calls=%fused_computation.1 | custom fusion | bytes 1049600 | tf_op jit(solution)/shard_map/gather | solution.py:35
  102.1 1.5 %fusion.15 = f32[16,2048]{1,0:T(8,128)S(1)} fusion(bf16[128,2048]{1,0:T(8,128)(2,1)} %gather_fusion.1, f32[16,8]{1,0:T(8,128)S(1)} %copy.12), kind=kLoop, calls=%fused_computation.13 | loop fusion | flops 753664 | bytes 655872 | tf_op jit(solution)/shard_map/reduce_sum | solution.py:37
  103.6 0.6 add_convert_fusion
  (5 shorter events, 0.1 us)
Async XLA Ops:
  0.0 65.0 %copy-start = (bf16[1,768,2048]{2,1,0:T(8,128)(2,1)S(1)}, bf16[1,768,2048]{2,1,0:T(8,128)(2,1)}, u32[]{:S(2)}) copy-start(bf16[1,768,2048]{2,1,0:T(8,128)(2,1)} %param.11) | copy-start | bytes 9437188
  0.0 1.6 %copy-start.1 = (bf16[16,2048]{1,0:T(8,128)(2,1)S(1)}, bf16[16,2048]{1,0:T(8,128)(2,1)}, u32[]{:S(2)}) copy-start(bf16[16,2048]{1,0:T(8,128)(2,1)} %param.6) | copy-start | bytes 196612
  60.2 1.0 copy-start.2
  65.0 10.6 %copy-start.3 = (f32[16,8]{0,1:T(8,128)S(1)}, f32[16,8]{0,1:T(8,128)}, u32[]{:S(2)}) copy-start(f32[16,8]{0,1:T(8,128)} %param.7) | copy-start | bytes 1540
  70.5 28.0 %all-to-all-start.1 = ((bf16[16,16,2048]{2,1,0:T(8,128)(2,1)}), bf16[16,16,2048]{2,1,0:T(8,128)(2,1)}, u32[]{:S(2)}, u32[]{:S(2)}) async-start(bf16[16,16,2048]{2,1,0:T(8,128)(2,1)} %bitcast.37), calls=%async_computation.1 | async-start | bytes 2097152 | tf_op jit(solution)/shard_map/all_to_all | solution.py:34
where the time goes:
time: 106 us; the launch traced here: 104 us
  local copies, waits for them, and re-layouts  32.2 us (30%)
  blocking collectives  32.1 us (30%)
  waiting for transfers between devices  22.9 us (22%)
  matrix products  9.3 us (9%)
  starting transfers between devices  5.04 us (5%)
  other arithmetic  2.62 us (2%)
    all_to_all x1, blocking collectives, shards(): lax.all_to_all(outgoing, 'expert', split_axis=0, concat_axis=0, tiled=True)  32.1 us
    scatter x1, local copies, waits for them, and re-layouts, shards(): outgoing = outgoing.at[flat_slot, position].set(tokens[source_row])  23.6 us
    all_to_all x1, waiting for transfers between devices, shards(): lax.all_to_all(result, 'expert', split_axis=0, concat_axis=0, tiled=True)  22.9 us
    dot_general x1, matrix products, shards(): jnp.dot(all_hidden, w_down[0], preferred_element_type=jnp.float32)  5.53 us
    all_to_all x1, starting transfers between devices, shards(): lax.all_to_all(result, 'expert', split_axis=0, concat_axis=0, tiled=True)  5.04 us
    dot_general x1, matrix products, shards(): gate = jnp.dot(flat_rows, w_gate[0], preferred_element_type=jnp.float32)  3.77 us
    gather x1, local copies, waits for them, and re-layouts, shards(): values = returned[flat_slot, position].astype(jnp.float32)  3.53 us
  transfers between devices with their start and end apart: 1, of which 1 were waited for; matrix products, arithmetic and copies ran while one was open for 0% of the time, Pallas kernels for 0%

commit v1 on v0

--- a/solution.py
+++ b/solution.py
@@ -1,10 +1,144 @@
+import functools
 import jax
 import jax.numpy as jnp
 from jax import lax
+from jax.experimental import pallas as pl
+from jax.experimental.pallas import tpu as pltpu
 from jax.sharding import PartitionSpec as P
 
-
-def shards(tokens, route_weight, replica, w_gate, w_up, w_down):
+LANES = 128
+VMEM = pl.BlockSpec(memory_space=pltpu.VMEM)
+SMEM = pl.BlockSpec(memory_space=pltpu.SMEM)
+
+
+def in_vmem(array):
+    return pltpu.with_memory_space_constraint(array, pltpu.VMEM)
+
+
+def pack_kernel(token_ref, weight_ref, replica_ref, out_ref):
+    width = token_ref.shape[1]
+    weight = weight_ref[...]
+    probability = weight / jnp.sum(weight, axis=0, keepdims=True)
+    top_count, row_count = weight.shape
+    slot = lax.broadcasted_iota(jnp.int32, (LANES // 2, row_count), 0)
+    dense = jnp.zeros((LANES // 2, row_count), jnp.float32)
+    for k in range(top_count):
+        dense += jnp.where(replica_ref[k : k + 1, :] == slot, probability[k : k + 1, :], 0.0)
+    high = dense.astype(jnp.bfloat16).astype(jnp.float32)
+    low = dense - high
+    both = jnp.concatenate([high, low], axis=0)
+    both = jnp.concatenate([both, jnp.zeros((LANES, LANES - row_count), jnp.float32)], axis=1)
+    out_ref[:, :width] = token_ref[...]
+    out_ref[:, width:] = both.T[:row_count].astype(jnp.bfloat16)
+
+
+def expert_kernel(block_count, *refs):
+    slot_ref, gate_ref, up_ref, down_ref = refs[:4]
+    blocks = refs[4 : 4 + 2 * block_count]
+    away_ref, own_ref, rows_ref, share_ref, hidden_ref = refs[4 + 2 * block_count :]
+    row_count = blocks[0].shape[0]
+    width, hidden_width = gate_ref.shape[1:]
+    half = block_count * row_count
+    lane = lax.broadcasted_iota(jnp.int32, (row_count, LANES), 1)
+    chosen = (lane == slot_ref[0]) | (lane == slot_ref[0] + LANES // 2)
+    for b, block in enumerate(blocks):
+        at = pl.ds(b * row_count, row_count)
+        rows_ref[at, :] = block[:, :width]
+        extra = block[:, width:].astype(jnp.float32)
+        share = jnp.sum(jnp.where(chosen, extra, 0.0), axis=1, keepdims=True)
+        share_ref[at, :] = jnp.broadcast_to(share, (row_count, LANES))
+    rows = rows_ref[...]
+    step = 256
+    for n in range(0, hidden_width, step):
+        gate = jnp.dot(rows, gate_ref[0, :, n : n + step], preferred_element_type=jnp.float32)
+        upward = jnp.dot(rows, up_ref[0, :, n : n + step], preferred_element_type=jnp.float32)
+        hidden_ref[:, n : n + step] = (gate / (1.0 + jnp.exp(-gate)) * upward).astype(jnp.bfloat16)
+    hidden = hidden_ref[...]
+    share = share_ref[:, :1]
+    for n in range(0, width, step):
+        result = jnp.dot(hidden, down_ref[0, :, n : n + step], preferred_element_type=jnp.float32)
+        term = result.astype(jnp.bfloat16).astype(jnp.float32) * share
+        away_ref[:, n : n + step] = term[:half].astype(jnp.bfloat16)
+        own_ref[:, n : n + step] = term[half:]
+
+
+def pair_kernel(own_ref, other_ref, first_ref, *outs):
+    row_count = first_ref.shape[0]
+    first_ref[...] = own_ref[:row_count] + other_ref[:row_count].astype(jnp.float32)
+    for b, out in enumerate(outs, start=1):
+        at = pl.ds(b * row_count, row_count)
+        out[...] = (own_ref[at, :] + other_ref[at, :].astype(jnp.float32)).astype(jnp.bfloat16)
+
+
+def mix_kernel(token_ref, first_ref, *refs):
+    total = token_ref[...].astype(jnp.float32) + first_ref[...]
+    for ref in refs[:-1]:
+        total += ref[...].astype(jnp.float32)
+    refs[-1][...] = total.astype(jnp.bfloat16)
+
+
+def dense_shards(tokens, route_weight, replica, w_gate, w_up, w_down):
+    row_count, width = tokens.shape
+    hidden_width = w_gate.shape[2]
+    peer_count = lax.axis_size("expert")
+    pair_count = peer_count // 2
+    slot = lax.axis_index("expert").astype(jnp.int32).reshape(1)
+
+    def shift(array, s):
+        pairs = [(i, ((i // 2 + s) % pair_count) * 2 + i % 2) for i in range(peer_count)]
+        return lax.ppermute(array, "expert", pairs)
+
+    def swap(array):
+        return lax.ppermute(array, "expert", [(i, i ^ 1) for i in range(peer_count)])
+
+    packed = pl.pallas_call(
+        pack_kernel,
+        out_shape=jax.ShapeDtypeStruct((row_count, width + LANES), jnp.bfloat16),
+        in_specs=[VMEM] * 3,
+        out_specs=VMEM,
+        name="pack",
+    )(tokens, route_weight.T, replica.T)
+    order = list(range(1, pair_count))
+    near = [packed] + [shift(packed, s) for s in order]
+    far = [swap(block) for block in near]
+    total_rows = 2 * pair_count * row_count
+    away, own = pl.pallas_call(
+        functools.partial(expert_kernel, pair_count),
+        out_shape=(
+            jax.ShapeDtypeStruct((total_rows // 2, width), jnp.bfloat16),
+            jax.ShapeDtypeStruct((total_rows // 2, width), jnp.float32),
+        ),
+        in_specs=[SMEM] + [VMEM] * (3 + 2 * pair_count),
+        out_specs=(VMEM, VMEM),
+        scratch_shapes=[
+            pltpu.VMEM((total_rows, width), jnp.bfloat16),
+            pltpu.VMEM((total_rows, LANES), jnp.float32),
+            pltpu.VMEM((total_rows, hidden_width), jnp.bfloat16),
+        ],
+        compiler_params=pltpu.CompilerParams(vmem_limit_bytes=24 * 2**20),
+        name="experts",
+    )(slot, in_vmem(w_gate), in_vmem(w_up), in_vmem(w_down), *far, *near)
+    other = swap(away)
+    block = jax.ShapeDtypeStruct((row_count, width), jnp.bfloat16)
+    first, *sums = pl.pallas_call(
+        pair_kernel,
+        out_shape=(jax.ShapeDtypeStruct((row_count, width), jnp.float32),) + (block,) * (pair_count - 1),
+        in_specs=[VMEM] * 2,
+        out_specs=(VMEM,) * pair_count,
+        compiler_params=pltpu.CompilerParams(vmem_limit_bytes=16 * 2**20),
+        name="pair",
+    )(own, other)
+    back = [shift(array, -s) for s, array in zip(order, sums)]
+    return pl.pallas_call(
+        mix_kernel,
+        out_shape=block,
+        in_specs=[VMEM] * (1 + pair_count),
+        out_specs=VMEM,
+        name="mix",
+    )(tokens, first, *back)
+
+
+def routed_shards(tokens, route_weight, replica, w_gate, w_up, w_down):
     row_count, width = tokens.shape
     top_count = replica.shape[1]
     peer_count = lax.axis_size("expert")
@@ -38,6 +172,24 @@
     return (own_columns.astype(jnp.float32) + combined).astype(jnp.bfloat16)
 
 
+def shards(*arrays):
+    tokens, replica, w_gate = arrays[0], arrays[2], arrays[3]
+    row_count, top_count = replica.shape
+    peer_count = lax.axis_size("expert")
+    if (
+        lax.axis_size("tensor") == 1
+        and peer_count % 2 == 0
+        and 2 <= peer_count <= LANES // 2
+        and 2 * top_count >= peer_count
+        and row_count % 16 == 0
+        and row_count <= LANES
+        and tokens.shape[1] % 256 == 0
+        and w_gate.shape[2] % 256 == 0
+    ):
+        return dense_shards(*arrays)
+    return routed_shards(*arrays)
+
+
 def solution(mesh):
     return jax.shard_map(
         shards,

time: 106 us -> 54.9 us (0.52); the launches traced: 104 us -> 54.5 us
  blocking collectives: 32.1 us -> 0 us
  local copies, waits for them, and re-layouts: 32.2 us -> 7.82 us
  starting transfers between devices: 5.04 us -> 22.5 us
  matrix products: 9.3 us -> 0 us
  Pallas kernels: 0 us -> 6.22 us
  waiting for transfers between devices: 22.9 us -> 17.9 us
  other arithmetic: 2.62 us -> 0 us
    all_to_all x1 -> x0, blocking collectives: 32.1 us -> none  [shards(): lax.all_to_all(outgoing, 'expert', split_axis=0, concat_axis=0, tiled=True)]
    scatter x1 -> x0, local copies, waits for them, and re-layouts: 23.6 us -> none  [shards(): outgoing = outgoing.at[flat_slot, position].set(tokens[source_row])]
    all_to_all x1 -> x0, waiting for transfers between devices: 22.9 us -> none  [shards(): lax.all_to_all(result, 'expert', split_axis=0, concat_axis=0, tiled=True)]
    ppermute x0 -> x23, starting transfers between devices: none -> 22.5 us  [the longest x14 20.8 us: shift(): return lax.ppermute(array, 'expert', pairs)]
    ppermute x0 -> x23, waiting for transfers between devices: none -> 17.9 us  [the longest x14 15.1 us: shift(): return lax.ppermute(array, 'expert', pairs)]
    dot_general x2 -> x0, matrix products: 9.3 us -> none  [the longest x1 5.53 us: shards(): jnp.dot(all_hidden, w_down[0], preferred_element_type=jnp.float32)]
    pallas_call x0 -> x4, Pallas kernels: none -> 6.22 us  [the longest x1 2.71 us: dense_shards(): pl.pallas_call(functools.partial(expert_kernel, pair_count), out_shape=(j...]
    unnamed x9 -> x24, local copies, waits for them, and re-layouts: 1.96 us -> 7.82 us
  transfers between devices with their start and end apart: 1 -> 23, of which waited for: 1 -> 10; matrix products, arithmetic and copies ran while one was open for 0% -> 0% of each run, Pallas kernels for 0% -> 0%
where the time goes in v1:
time: 54.9 us; the launch traced here: 54.5 us
  starting transfers between devices  22.5 us (41%)
  waiting for transfers between devices  17.9 us (33%)
  local copies, waits for them, and re-layouts  7.82 us (14%)
  Pallas kernels  6.22 us (11%)
    ppermute x14, starting transfers between devices, shift(): return lax.ppermute(array, 'expert', pairs)  20.8 us
    ppermute x14, waiting for transfers between devices, shift(): return lax.ppermute(array, 'expert', pairs)  15.1 us
    unnamed x24, local copies, waits for them, and re-layouts  7.82 us
    ppermute x9, waiting for transfers between devices, swap(): lax.ppermute(array, 'expert', [(i, i ^ 1) for i in range(peer_count)])  2.74 us
    pallas_call x1, Pallas kernels, dense_shards(): pl.pallas_call(functools.partial(expert_kernel, pair_count), out_shape=(j...  2.71 us
    pallas_call x1, Pallas kernels, dense_shards(): pl.pallas_call(mix_kernel, out_shape=block, in_specs=[VMEM] * (1 + pair_c...  1.82 us
    ppermute x9, starting transfers between devices, swap(): lax.ppermute(array, 'expert', [(i, i ^ 1) for i in range(peer_count)])  1.74 us
    pallas_call x1, Pallas kernels, dense_shards(): pl.pallas_call(pack_kernel, out_shape=jax.ShapeDtypeStruct((row_count, wi...  1.6 us
  transfers between devices with their start and end apart: 23, of which 10 were waited for; matrix products, arithmetic and copies ran while one was open for 0% of the time, Pallas kernels for 0%

profile of v1, /device:TPU:0, one launch (start us, length us, event | category | flops | bytes accessed | tf_op | source)
XLA Modules:
  0.0 54.5 jit_solution(12283837483266054434)
XLA Ops:
  0.0 1.6 %pack.1.refs_12_ = bf16[16,2176]{1,0:T(8,128)(2,1)} custom-call(bf16[16,2048]{1,0:T(8,128)(2,1)} %token_ref.3, f32[8,16]{1,0:T(8,128)} %bitcast.3, s32[8,16]{1,0:T(8,128)} %bitcast.4), custom_call_target="tpu_custom_call" | custom-call | tf_op jit(solution)/shard_map/pack/pallas_call | solution.py:94
  1.6 6.0 %collective-permute-start.13 = (bf16[16,2176]{1,0:T(8,128)(2,1)}, bf16[16,2176]{1,0:T(8,128)(2,1)S(1)}, u32[]{:S(2)}, u32[]{:S(2)}) collective-permute-start(bf16[16,2176]{1,0:T(8,128)(2,1)} %pack.1.refs_12_), channel_id=1, source_target_pairs={{0,14},{1,15},{2,0},{3,1},{4,2},{5,3},{6,4},{7,5},{8,6},{9,7},{10,... | collective-permute-start | bytes 208904 | tf_op jit(solution)/shard_map/ppermute | solution.py:89
  7.6 0.4 collective-permute-start.11
  8.0 0.0 collective-permute-start.9
  8.0 3.0 %collective-permute-start.7 = (bf16[16,2176]{1,0:T(8,128)(2,1)}, bf16[16,2176]{1,0:T(8,128)(2,1)S(1)}, u32[]{:S(2)}, u32[]{:S(2)}) collective-permute-start(bf16[16,2176]{1,0:T(8,128)(2,1)} %pack.1.refs_12_), channel_id=1, source_target_pairs={{0,8},{1,9},{2,10},{3,11},{4,12},{5,13},{6,14},{7,15},{8,0},{9,1},... | collective-permute-start | bytes 208904 | tf_op jit(solution)/shard_map/ppermute | solution.py:89
  11.0 0.0 collective-permute-start.5
  11.0 0.0 collective-permute-done.13.refs_19_
  11.0 1.8 %collective-permute-start.3 = (bf16[16,2176]{1,0:T(8,128)(2,1)}, bf16[16,2176]{1,0:T(8,128)(2,1)S(1)}, u32[]{:S(2)}, u32[]{:S(2)}) collective-permute-start(bf16[16,2176]{1,0:T(8,128)(2,1)} %pack.1.refs_12_), channel_id=1, source_target_pairs={{0,4},{1,5},{2,6},{3,7},{4,8},{5,9},{6,10},{7,11},{8,12},{9,13},{1... | collective-permute-start | bytes 208904 | tf_op jit(solution)/shard_map/ppermute | solution.py:89
  12.9 0.0 collective-permute-done.11.refs_18_
  12.9 1.1 %collective-permute-start.1 = (bf16[16,2176]{1,0:T(8,128)(2,1)}, bf16[16,2176]{1,0:T(8,128)(2,1)S(1)}, u32[]{:S(2)}, u32[]{:S(2)}) collective-permute-start(bf16[16,2176]{1,0:T(8,128)(2,1)} %pack.1.refs_12_), channel_id=1, source_target_pairs={{0,2},{1,3},{2,4},{3,5},{4,6},{5,7},{6,8},{7,9},{8,10},{9,11},{10,... | collective-permute-start | bytes 208904 | tf_op jit(solution)/shard_map/ppermute | solution.py:89
  14.0 0.0 collective-permute-done.9.refs_17_
  14.0 0.0 collective-permute-start
  14.0 5.7 %collective-permute-done.7.refs_16_ = bf16[16,2176]{1,0:T(8,128)(2,1)S(1)} collective-permute-done((bf16[16,2176]{1,0:T(8,128)(2,1)}, bf16[16,2176]{1,0:T(8,128)(2,1)S(1)}, u32[]{:S(2)}, u32[]{:S(2)}) %collective-permute-start.7) | collective-permute-done | bytes 69664 | tf_op jit(solution)/shard_map/ppermute | solution.py:89
  19.7 0.0 collective-permute-start.14
  19.7 2.7 %collective-permute-done.5.refs_15_ = bf16[16,2176]{1,0:T(8,128)(2,1)S(1)} collective-permute-done((bf16[16,2176]{1,0:T(8,128)(2,1)}, bf16[16,2176]{1,0:T(8,128)(2,1)S(1)}, u32[]{:S(2)}, u32[]{:S(2)}) %collective-permute-start.5) | collective-permute-done | bytes 69664 | tf_op jit(solution)/shard_map/ppermute | solution.py:89
  22.5 0.0 collective-permute-start.12
  22.5 0.0 collective-permute-done.3.refs_14_
  22.5 0.5 collective-permute-start.10
  23.0 0.0 collective-permute-done.1.refs_13_
  23.0 0.1 collective-permute-start.8
  23.1 0.0 collective-permute-done.refs_4_
  23.1 0.4 collective-permute-start.6
  23.5 0.0 collective-permute-done.14.refs_11_
  23.5 0.1 collective-permute-start.4
  23.6 0.2 collective-permute-done.12.refs_10_
  23.7 0.3 collective-permute-start.2
  24.0 0.0 collective-permute-done.10.refs_9_
  24.0 0.2 collective-permute-done.8.refs_8_
  24.2 0.2 collective-permute-done.6.refs_7_
  24.4 0.4 collective-permute-done.4.refs_6_
  24.8 0.2 collective-permute-done.2.refs_5_
  25.0 1.9 %copy-done = bf16[1,2048,768]{2,1,0:T(8,128)(2,1)S(1)} copy-done((bf16[1,2048,768]{2,1,0:T(8,128)(2,1)S(1)}, bf16[1,2048,768]{2,1,0:T(8,128)(2,1)}, u32[]{:S(2)}) %copy-start) | copy-done | bytes 3145752
  26.9 1.9 %copy-done.1 = bf16[1,2048,768]{2,1,0:T(8,128)(2,1)S(1)} copy-done((bf16[1,2048,768]{2,1,0:T(8,128)(2,1)S(1)}, bf16[1,2048,768]{2,1,0:T(8,128)(2,1)}, u32[]{:S(2)}) %copy-start.1) | copy-done | bytes 3145752
  28.8 1.9 %copy-done.2 = bf16[1,768,2048]{2,1,0:T(8,128)(2,1)S(1)} copy-done((bf16[1,768,2048]{2,1,0:T(8,128)(2,1)S(1)}, bf16[1,768,2048]{2,1,0:T(8,128)(2,1)}, u32[]{:S(2)}) %copy-start.2) | copy-done | bytes 3145752
  30.7 0.9 %copy-done.3 = bf16[16,2176]{1,0:T(8,128)(2,1)S(1)} copy-done((bf16[16,2176]{1,0:T(8,128)(2,1)S(1)}, bf16[16,2176]{1,0:T(8,128)(2,1)}, u32[]{:S(2)}) %copy-start.3) | copy-done | bytes 69656
  31.5 2.7 %experts.1 = (bf16[128,2048]{1,0:T(8,128)(2,1)S(1)}, f32[128,2048]{1,0:T(8,128)S(1)}) custom-call(s32[1]{0:T(128)} %bitcast.refs_0_, bf16[1,2048,768]{2,1,0:T(8,128)(2,1)S(1)} %copy-done, bf16[1,2048,768]{2,1,0:T(8,128)(2,1)S(1)} %copy-done.1, bf16[1,768,2048]{2,1,0:T(8,128)(2,1)S(1)} %copy-done.2, bf16[16,2176]{1,0:T(8,128)(2,1)S(1)} %collective-permute-done.refs_4_, ...), custom_call_target="tpu_custom_call" | custom-call | tf_op jit(solution)/shard_map/experts/pallas_call | solution.py:105
  34.3 0.4 collective-permute-start.15
  34.6 1.6 %collective-permute-done.15.other_ref = bf16[128,2048]{1,0:T(8,128)(2,1)S(1)} collective-permute-done((bf16[128,2048]{1,0:T(8,128)(2,1)S(1)}, bf16[128,2048]{1,0:T(8,128)(2,1)S(1)}, u32[]{:S(2)}, u32[]{:S(2)}) %collective-permute-start.15) | collective-permute-done | bytes 524320 | tf_op jit(solution)/shard_map/ppermute | solution.py:92
  36.2 0.1 pair.1
  36.3 0.0 copy-start.4
  36.3 0.6 %copy-done.4 = f32[16,2048]{1,0:T(8,128)} copy-done((f32[16,2048]{1,0:T(8,128)}, f32[16,2048]{1,0:T(8,128)S(1)}, u32[]{:S(2)}) %copy-start.4) | copy-done | bytes 131096
  37.0 0.0 collective-permute-start.16
  37.0 1.6 %collective-permute-start.17 = (bf16[16,2048]{1,0:T(8,128)(2,1)S(1)}, bf16[16,2048]{1,0:T(8,128)(2,1)S(1)}, u32[]{:S(2)}, u32[]{:S(2)}) collective-permute-start(bf16[16,2048]{1,0:T(8,128)(2,1)S(1)} %get-tuple-element.19), channel_id=1, source_target_pairs={{0,12},{1,13},{2,14},{3,15},{4,0},{5,1},{6,2},{7,3},{8,4},{9,5},{1... | collective-permute-start | bytes 196616 | tf_op jit(solution)/shard_map/ppermute | solution.py:89
  38.6 0.9 %collective-permute-start.18 = (bf16[16,2048]{1,0:T(8,128)(2,1)S(1)}, bf16[16,2048]{1,0:T(8,128)(2,1)S(1)}, u32[]{:S(2)}, u32[]{:S(2)}) collective-permute-start(bf16[16,2048]{1,0:T(8,128)(2,1)S(1)} %get-tuple-element.20), channel_id=1, source_target_pairs={{0,10},{1,11},{2,12},{3,13},{4,14},{5,15},{6,0},{7,1},{8,2},{9,3},... | collective-permute-start | bytes 196616 | tf_op jit(solution)/shard_map/ppermute | solution.py:89
  39.5 1.9 %collective-permute-start.19 = (bf16[16,2048]{1,0:T(8,128)(2,1)S(1)}, bf16[16,2048]{1,0:T(8,128)(2,1)S(1)}, u32[]{:S(2)}, u32[]{:S(2)}) collective-permute-start(bf16[16,2048]{1,0:T(8,128)(2,1)S(1)} %get-tuple-element.21), channel_id=1, source_target_pairs={{0,8},{1,9},{2,10},{3,11},{4,12},{5,13},{6,14},{7,15},{8,0},{9,1},... | collective-permute-start | bytes 196616 | tf_op jit(solution)/shard_map/ppermute | solution.py:89
  41.4 1.6 %collective-permute-start.20 = (bf16[16,2048]{1,0:T(8,128)(2,1)S(1)}, bf16[16,2048]{1,0:T(8,128)(2,1)S(1)}, u32[]{:S(2)}, u32[]{:S(2)}) collective-permute-start(bf16[16,2048]{1,0:T(8,128)(2,1)S(1)} %get-tuple-element.22), channel_id=1, source_target_pairs={{0,6},{1,7},{2,8},{3,9},{4,10},{5,11},{6,12},{7,13},{8,14},{9,15},... | collective-permute-start | bytes 196616 | tf_op jit(solution)/shard_map/ppermute | solution.py:89
  42.9 0.0 collective-permute-done.16.refs_0_
  43.0 0.5 collective-permute-start.21
  43.5 0.0 collective-permute-done.17.refs_1_
  43.5 2.0 %collective-permute-start.22 = (bf16[16,2048]{1,0:T(8,128)(2,1)S(1)}, bf16[16,2048]{1,0:T(8,128)(2,1)S(1)}, u32[]{:S(2)}, u32[]{:S(2)}) collective-permute-start(bf16[16,2048]{1,0:T(8,128)(2,1)S(1)} %get-tuple-element.24), channel_id=1, source_target_pairs={{0,2},{1,3},{2,4},{3,5},{4,6},{5,7},{6,8},{7,9},{8,10},{9,11},{10,... | collective-permute-start | bytes 196616 | tf_op jit(solution)/shard_map/ppermute | solution.py:89
  45.4 0.0 collective-permute-done.18.refs_2_
  45.4 5.3 %collective-permute-done.19.refs_3_ = bf16[16,2048]{1,0:T(8,128)(2,1)S(1)} collective-permute-done((bf16[16,2048]{1,0:T(8,128)(2,1)S(1)}, bf16[16,2048]{1,0:T(8,128)(2,1)S(1)}, u32[]{:S(2)}, u32[]{:S(2)}) %collective-permute-start.19) | collective-permute-done | bytes 65568 | tf_op jit(solution)/shard_map/ppermute | solution.py:89
  50.7 1.3 %collective-permute-done.20.refs_4_ = bf16[16,2048]{1,0:T(8,128)(2,1)S(1)} collective-permute-done((bf16[16,2048]{1,0:T(8,128)(2,1)S(1)}, bf16[16,2048]{1,0:T(8,128)(2,1)S(1)}, u32[]{:S(2)}, u32[]{:S(2)}) %collective-permute-start.20) | collective-permute-done | bytes 65568 | tf_op jit(solution)/shard_map/ppermute | solution.py:89
  52.0 0.0 collective-permute-done.21.refs_5_
  52.0 0.0 collective-permute-done.22.refs_6_
  52.0 0.0 copy-start.11
  52.1 0.0 copy-done.5
  52.1 0.0 copy-done.6
  52.1 0.0 copy-done.7
  52.1 0.0 copy-done.8
  52.1 0.6 %copy-done.9 = bf16[16,2048]{1,0:T(8,128)(2,1)} copy-done((bf16[16,2048]{1,0:T(8,128)(2,1)}, bf16[16,2048]{1,0:T(8,128)(2,1)S(1)}, u32[]{:S(2)}) %copy-start.9) | copy-done | bytes 65560
  52.7 0.0 copy-done.10
  52.7 0.0 copy-done.11
  52.7 1.8 %mix.1 = bf16[16,2048]{1,0:T(8,128)(2,1)} custom-call(bf16[16,2048]{1,0:T(8,128)(2,1)} %token_ref.3, f32[16,2048]{1,0:T(8,128)} %copy-done.4, bf16[16,2048]{1,0:T(8,128)(2,1)} %copy-done.5, bf16[16,2048]{1,0:T(8,128)(2,1)} %copy-done.6, bf16[16,2048]{1,0:T(8,128)(2,1)} %copy-done.7, bf16[16,2048]{1,0:T(8,128)(2,1)} %copy-done.8, bf16[16,2048]{1,0:T(8,128)(2,1)} %copy-done.9, ...), custom_call_target="tpu_custom_call" | custom-call | tf_op jit(solution)/shard_map/mix/pallas_call | solution.py:132
  (10 shorter events, 0.0 us)
Async XLA Ops:
  1.6 9.4 %collective-permute-start.13 = (bf16[16,2176]{1,0:T(8,128)(2,1)}, bf16[16,2176]{1,0:T(8,128)(2,1)S(1)}, u32[]{:S(2)}, u32[]{:S(2)}) collective-permute-start(bf16[16,2176]{1,0:T(8,128)(2,1)} %pack.1.refs_12_), channel_id=1, source_target_pairs={{0,14},{1,15},{2,0},{3,1},{4,2},{5,3},{6,4},{7,5},{8,6},{9,7},{10,... | collective-permute-start | bytes 208904 | tf_op jit(solution)/shard_map/ppermute | solution.py:89
  7.6 5.3 %collective-permute-start.11 = (bf16[16,2176]{1,0:T(8,128)(2,1)}, bf16[16,2176]{1,0:T(8,128)(2,1)S(1)}, u32[]{:S(2)}, u32[]{:S(2)}) collective-permute-start(bf16[16,2176]{1,0:T(8,128)(2,1)} %pack.1.refs_12_), channel_id=1, source_target_pairs={{0,12},{1,13},{2,14},{3,15},{4,0},{5,1},{6,2},{7,3},{8,4},{9,5},{1... | collective-permute-start | bytes 208904 | tf_op jit(solution)/shard_map/ppermute | solution.py:89
  8.0 6.0 %collective-permute-start.9 = (bf16[16,2176]{1,0:T(8,128)(2,1)}, bf16[16,2176]{1,0:T(8,128)(2,1)S(1)}, u32[]{:S(2)}, u32[]{:S(2)}) collective-permute-start(bf16[16,2176]{1,0:T(8,128)(2,1)} %pack.1.refs_12_), channel_id=1, source_target_pairs={{0,10},{1,11},{2,12},{3,13},{4,14},{5,15},{6,0},{7,1},{8,2},{9,3},... | collective-permute-start | bytes 208904 | tf_op jit(solution)/shard_map/ppermute | solution.py:89
  8.0 11.7 %collective-permute-start.7 = (bf16[16,2176]{1,0:T(8,128)(2,1)}, bf16[16,2176]{1,0:T(8,128)(2,1)S(1)}, u32[]{:S(2)}, u32[]{:S(2)}) collective-permute-start(bf16[16,2176]{1,0:T(8,128)(2,1)} %pack.1.refs_12_), channel_id=1, source_target_pairs={{0,8},{1,9},{2,10},{3,11},{4,12},{5,13},{6,14},{7,15},{8,0},{9,1},... | collective-permute-start | bytes 208904 | tf_op jit(solution)/shard_map/ppermute | solution.py:89
  11.0 11.4 %collective-permute-start.5 = (bf16[16,2176]{1,0:T(8,128)(2,1)}, bf16[16,2176]{1,0:T(8,128)(2,1)S(1)}, u32[]{:S(2)}, u32[]{:S(2)}) collective-permute-start(bf16[16,2176]{1,0:T(8,128)(2,1)} %pack.1.refs_12_), channel_id=1, source_target_pairs={{0,6},{1,7},{2,8},{3,9},{4,10},{5,11},{6,12},{7,13},{8,14},{9,15},... | collective-permute-start | bytes 208904 | tf_op jit(solution)/shard_map/ppermute | solution.py:89
  11.0 11.4 %collective-permute-start.3 = (bf16[16,2176]{1,0:T(8,128)(2,1)}, bf16[16,2176]{1,0:T(8,128)(2,1)S(1)}, u32[]{:S(2)}, u32[]{:S(2)}) collective-permute-start(bf16[16,2176]{1,0:T(8,128)(2,1)} %pack.1.refs_12_), channel_id=1, source_target_pairs={{0,4},{1,5},{2,6},{3,7},{4,8},{5,9},{6,10},{7,11},{8,12},{9,13},{1... | collective-permute-start | bytes 208904 | tf_op jit(solution)/shard_map/ppermute | solution.py:89
  12.9 10.1 %collective-permute-start.1 = (bf16[16,2176]{1,0:T(8,128)(2,1)}, bf16[16,2176]{1,0:T(8,128)(2,1)S(1)}, u32[]{:S(2)}, u32[]{:S(2)}) collective-permute-start(bf16[16,2176]{1,0:T(8,128)(2,1)} %pack.1.refs_12_), channel_id=1, source_target_pairs={{0,2},{1,3},{2,4},{3,5},{4,6},{5,7},{6,8},{7,9},{8,10},{9,11},{10,... | collective-permute-start | bytes 208904 | tf_op jit(solution)/shard_map/ppermute | solution.py:89
  14.0 9.0 %collective-permute-start = (bf16[16,2176]{1,0:T(8,128)(2,1)}, bf16[16,2176]{1,0:T(8,128)(2,1)S(1)}, u32[]{:S(2)}, u32[]{:S(2)}) collective-permute-start(bf16[16,2176]{1,0:T(8,128)(2,1)} %pack.1.refs_12_), channel_id=1, source_target_pairs={{0,1},{1,0},{2,3},{3,2},{4,5},{5,4},{6,7},{7,6},{8,9},{9,8},{10,11... | collective-permute-start | bytes 208904 | tf_op jit(solution)/shard_map/ppermute | solution.py:92
  19.7 3.8 %collective-permute-start.14 = (bf16[16,2176]{1,0:T(8,128)(2,1)S(1)}, bf16[16,2176]{1,0:T(8,128)(2,1)S(1)}, u32[]{:S(2)}, u32[]{:S(2)}) collective-permute-start(bf16[16,2176]{1,0:T(8,128)(2,1)S(1)} %collective-permute-done.13.refs_19_), channel_id=1, source_target_pairs={{0,1},{1,0},{2,3},{3,2},{4,5},{5,4},{6,7},{7,6},{8,9},{9,8},{10,11... | collective-permute-start | bytes 208904 | tf_op jit(solution)/shard_map/ppermute | solution.py:92
  22.5 1.3 %collective-permute-start.12 = (bf16[16,2176]{1,0:T(8,128)(2,1)S(1)}, bf16[16,2176]{1,0:T(8,128)(2,1)S(1)}, u32[]{:S(2)}, u32[]{:S(2)}) collective-permute-start(bf16[16,2176]{1,0:T(8,128)(2,1)S(1)} %collective-permute-done.11.refs_18_), channel_id=1, source_target_pairs={{0,1},{1,0},{2,3},{3,2},{4,5},{5,4},{6,7},{7,6},{8,9},{9,8},{10,11... | collective-permute-start | bytes 208904 | tf_op jit(solution)/shard_map/ppermute | solution.py:92
  22.5 1.5 %collective-permute-start.10 = (bf16[16,2176]{1,0:T(8,128)(2,1)S(1)}, bf16[16,2176]{1,0:T(8,128)(2,1)S(1)}, u32[]{:S(2)}, u32[]{:S(2)}) collective-permute-start(bf16[16,2176]{1,0:T(8,128)(2,1)S(1)} %collective-permute-done.9.refs_17_), channel_id=1, source_target_pairs={{0,1},{1,0},{2,3},{3,2},{4,5},{5,4},{6,7},{7,6},{8,9},{9,8},{10,11... | collective-permute-start | bytes 208904 | tf_op jit(solution)/shard_map/ppermute | solution.py:92
  23.0 1.3 %collective-permute-start.8 = (bf16[16,2176]{1,0:T(8,128)(2,1)S(1)}, bf16[16,2176]{1,0:T(8,128)(2,1)S(1)}, u32[]{:S(2)}, u32[]{:S(2)}) collective-permute-start(bf16[16,2176]{1,0:T(8,128)(2,1)S(1)} %collective-permute-done.7.refs_16_), channel_id=1, source_target_pairs={{0,1},{1,0},{2,3},{3,2},{4,5},{5,4},{6,7},{7,6},{8,9},{9,8},{10,11... | collective-permute-start | bytes 208904 | tf_op jit(solution)/shard_map/ppermute | solution.py:92
  23.1 1.3 %collective-permute-start.6 = (bf16[16,2176]{1,0:T(8,128)(2,1)S(1)}, bf16[16,2176]{1,0:T(8,128)(2,1)S(1)}, u32[]{:S(2)}, u32[]{:S(2)}) collective-permute-start(bf16[16,2176]{1,0:T(8,128)(2,1)S(1)} %collective-permute-done.5.refs_15_), channel_id=1, source_target_pairs={{0,1},{1,0},{2,3},{3,2},{4,5},{5,4},{6,7},{7,6},{8,9},{9,8},{10,11... | collective-permute-start | bytes 208904 | tf_op jit(solution)/shard_map/ppermute | solution.py:92
  23.5 1.3 %collective-permute-start.4 = (bf16[16,2176]{1,0:T(8,128)(2,1)S(1)}, bf16[16,2176]{1,0:T(8,128)(2,1)S(1)}, u32[]{:S(2)}, u32[]{:S(2)}) collective-permute-start(bf16[16,2176]{1,0:T(8,128)(2,1)S(1)} %collective-permute-done.3.refs_14_), channel_id=1, source_target_pairs={{0,1},{1,0},{2,3},{3,2},{4,5},{5,4},{6,7},{7,6},{8,9},{9,8},{10,11... | collective-permute-start | bytes 208904 | tf_op jit(solution)/shard_map/ppermute | solution.py:92
  23.7 1.3 %collective-permute-start.2 = (bf16[16,2176]{1,0:T(8,128)(2,1)S(1)}, bf16[16,2176]{1,0:T(8,128)(2,1)S(1)}, u32[]{:S(2)}, u32[]{:S(2)}) collective-permute-start(bf16[16,2176]{1,0:T(8,128)(2,1)S(1)} %collective-permute-done.1.refs_13_), channel_id=1, source_target_pairs={{0,1},{1,0},{2,3},{3,2},{4,5},{5,4},{6,7},{7,6},{8,9},{9,8},{10,11... | collective-permute-start | bytes 208904 | tf_op jit(solution)/shard_map/ppermute | solution.py:92
  25.0 1.9 %copy-start = (bf16[1,2048,768]{2,1,0:T(8,128)(2,1)S(1)}, bf16[1,2048,768]{2,1,0:T(8,128)(2,1)}, u32[]{:S(2)}) copy-start(bf16[1,2048,768]{2,1,0:T(8,128)(2,1)} %refs_1_.1) | copy-start | bytes 9437188
  26.9 1.9 %copy-start.1 = (bf16[1,2048,768]{2,1,0:T(8,128)(2,1)S(1)}, bf16[1,2048,768]{2,1,0:T(8,128)(2,1)}, u32[]{:S(2)}) copy-start(bf16[1,2048,768]{2,1,0:T(8,128)(2,1)} %refs_2_.1) | copy-start | bytes 9437188
  28.8 1.9 %copy-start.2 = (bf16[1,768,2048]{2,1,0:T(8,128)(2,1)S(1)}, bf16[1,768,2048]{2,1,0:T(8,128)(2,1)}, u32[]{:S(2)}) copy-start(bf16[1,768,2048]{2,1,0:T(8,128)(2,1)} %refs_3_.1) | copy-start | bytes 9437188
  30.7 0.9 %copy-start.3 = (bf16[16,2176]{1,0:T(8,128)(2,1)S(1)}, bf16[16,2176]{1,0:T(8,128)(2,1)}, u32[]{:S(2)}) copy-start(bf16[16,2176]{1,0:T(8,128)(2,1)} %pack.1.refs_12_) | copy-start | bytes 208900
  34.3 2.0 %collective-permute-start.15 = (bf16[128,2048]{1,0:T(8,128)(2,1)S(1)}, bf16[128,2048]{1,0:T(8,128)(2,1)S(1)}, u32[]{:S(2)}, u32[]{:S(2)}) collective-permute-start(bf16[128,2048]{1,0:T(8,128)(2,1)S(1)} %get-tuple-element.16), channel_id=1, source_target_pairs={{0,1},{1,0},{2,3},{3,2},{4,5},{5,4},{6,7},{7,6},{8,9},{9,8},{10,11... | collective-permute-start | bytes 1572872 | tf_op jit(solution)/shard_map/ppermute | solution.py:92
  36.3 0.6 %copy-start.4 = (f32[16,2048]{1,0:T(8,128)}, f32[16,2048]{1,0:T(8,128)S(1)}, u32[]{:S(2)}) copy-start(f32[16,2048]{1,0:T(8,128)S(1)} %get-tuple-element.17.first_ref) | copy-start | bytes 393220
  37.0 6.0 %collective-permute-start.16 = (bf16[16,2048]{1,0:T(8,128)(2,1)S(1)}, bf16[16,2048]{1,0:T(8,128)(2,1)S(1)}, u32[]{:S(2)}, u32[]{:S(2)}) collective-permute-start(bf16[16,2048]{1,0:T(8,128)(2,1)S(1)} %get-tuple-element.18), channel_id=1, source_target_pairs={{0,14},{1,15},{2,0},{3,1},{4,2},{5,3},{6,4},{7,5},{8,6},{9,7},{10,... | collective-permute-start | bytes 196616 | tf_op jit(solution)/shard_map/ppermute | solution.py:89
  37.0 6.5 %collective-permute-start.17 = (bf16[16,2048]{1,0:T(8,128)(2,1)S(1)}, bf16[16,2048]{1,0:T(8,128)(2,1)S(1)}, u32[]{:S(2)}, u32[]{:S(2)}) collective-permute-start(bf16[16,2048]{1,0:T(8,128)(2,1)S(1)} %get-tuple-element.19), channel_id=1, source_target_pairs={{0,12},{1,13},{2,14},{3,15},{4,0},{5,1},{6,2},{7,3},{8,4},{9,5},{1... | collective-permute-start | bytes 196616 | tf_op jit(solution)/shard_map/ppermute | solution.py:89
  38.6 6.8 %collective-permute-start.18 = (bf16[16,2048]{1,0:T(8,128)(2,1)S(1)}, bf16[16,2048]{1,0:T(8,128)(2,1)S(1)}, u32[]{:S(2)}, u32[]{:S(2)}) collective-permute-start(bf16[16,2048]{1,0:T(8,128)(2,1)S(1)} %get-tuple-element.20), channel_id=1, source_target_pairs={{0,10},{1,11},{2,12},{3,13},{4,14},{5,15},{6,0},{7,1},{8,2},{9,3},... | collective-permute-start | bytes 196616 | tf_op jit(solution)/shard_map/ppermute | solution.py:89
  39.5 11.2 %collective-permute-start.19 = (bf16[16,2048]{1,0:T(8,128)(2,1)S(1)}, bf16[16,2048]{1,0:T(8,128)(2,1)S(1)}, u32[]{:S(2)}, u32[]{:S(2)}) collective-permute-start(bf16[16,2048]{1,0:T(8,128)(2,1)S(1)} %get-tuple-element.21), channel_id=1, source_target_pairs={{0,8},{1,9},{2,10},{3,11},{4,12},{5,13},{6,14},{7,15},{8,0},{9,1},... | collective-permute-start | bytes 196616 | tf_op jit(solution)/shard_map/ppermute | solution.py:89
  41.4 10.7 %collective-permute-start.20 = (bf16[16,2048]{1,0:T(8,128)(2,1)S(1)}, bf16[16,2048]{1,0:T(8,128)(2,1)S(1)}, u32[]{:S(2)}, u32[]{:S(2)}) collective-permute-start(bf16[16,2048]{1,0:T(8,128)(2,1)S(1)} %get-tuple-element.22), channel_id=1, source_target_pairs={{0,6},{1,7},{2,8},{3,9},{4,10},{5,11},{6,12},{7,13},{8,14},{9,15},... | collective-permute-start | bytes 196616 | tf_op jit(solution)/shard_map/ppermute | solution.py:89
  42.9 9.1 %copy-start.5 = (bf16[16,2048]{1,0:T(8,128)(2,1)}, bf16[16,2048]{1,0:T(8,128)(2,1)S(1)}, u32[]{:S(2)}) copy-start(bf16[16,2048]{1,0:T(8,128)(2,1)S(1)} %collective-permute-done.16.refs_0_) | copy-start | bytes 196612
  43.0 9.1 %collective-permute-start.21 = (bf16[16,2048]{1,0:T(8,128)(2,1)S(1)}, bf16[16,2048]{1,0:T(8,128)(2,1)S(1)}, u32[]{:S(2)}, u32[]{:S(2)}) collective-permute-start(bf16[16,2048]{1,0:T(8,128)(2,1)S(1)} %get-tuple-element.23), channel_id=1, source_target_pairs={{0,4},{1,5},{2,6},{3,7},{4,8},{5,9},{6,10},{7,11},{8,12},{9,13},{1... | collective-permute-start | bytes 196616 | tf_op jit(solution)/shard_map/ppermute | solution.py:89
  43.5 8.6 %copy-start.6 = (bf16[16,2048]{1,0:T(8,128)(2,1)}, bf16[16,2048]{1,0:T(8,128)(2,1)S(1)}, u32[]{:S(2)}) copy-start(bf16[16,2048]{1,0:T(8,128)(2,1)S(1)} %collective-permute-done.17.refs_1_) | copy-start | bytes 196612
  43.5 8.6 %collective-permute-start.22 = (bf16[16,2048]{1,0:T(8,128)(2,1)S(1)}, bf16[16,2048]{1,0:T(8,128)(2,1)S(1)}, u32[]{:S(2)}, u32[]{:S(2)}) collective-permute-start(bf16[16,2048]{1,0:T(8,128)(2,1)S(1)} %get-tuple-element.24), channel_id=1, source_target_pairs={{0,2},{1,3},{2,4},{3,5},{4,6},{5,7},{6,8},{7,9},{8,10},{9,11},{10,... | collective-permute-start | bytes 196616 | tf_op jit(solution)/shard_map/ppermute | solution.py:89
  45.4 6.7 %copy-start.7 = (bf16[16,2048]{1,0:T(8,128)(2,1)}, bf16[16,2048]{1,0:T(8,128)(2,1)S(1)}, u32[]{:S(2)}) copy-start(bf16[16,2048]{1,0:T(8,128)(2,1)S(1)} %collective-permute-done.18.refs_2_) | copy-start | bytes 196612
  50.7 1.4 %copy-start.8 = (bf16[16,2048]{1,0:T(8,128)(2,1)}, bf16[16,2048]{1,0:T(8,128)(2,1)S(1)}, u32[]{:S(2)}) copy-start(bf16[16,2048]{1,0:T(8,128)(2,1)S(1)} %collective-permute-done.19.refs_3_) | copy-start | bytes 196612
  52.0 0.6 %copy-start.9 = (bf16[16,2048]{1,0:T(8,128)(2,1)}, bf16[16,2048]{1,0:T(8,128)(2,1)S(1)}, u32[]{:S(2)}) copy-start(bf16[16,2048]{1,0:T(8,128)(2,1)S(1)} %collective-permute-done.20.refs_4_) | copy-start | bytes 196612
  52.0 0.7 %copy-start.10 = (bf16[16,2048]{1,0:T(8,128)(2,1)}, bf16[16,2048]{1,0:T(8,128)(2,1)S(1)}, u32[]{:S(2)}) copy-start(bf16[16,2048]{1,0:T(8,128)(2,1)S(1)} %collective-permute-done.21.refs_5_) | copy-start | bytes 196612
  52.0 0.7 %copy-start.11 = (bf16[16,2048]{1,0:T(8,128)(2,1)}, bf16[16,2048]{1,0:T(8,128)(2,1)S(1)}, u32[]{:S(2)}) copy-start(bf16[16,2048]{1,0:T(8,128)(2,1)S(1)} %collective-permute-done.22.refs_6_) | copy-start | bytes 196612

commit v2 on v0

--- a/solution.py
+++ b/solution.py
@@ -1,10 +1,220 @@
 import jax
 import jax.numpy as jnp
 from jax import lax
+from jax.experimental import pallas as pl
+from jax.experimental.pallas import tpu as pltpu
 from jax.sharding import PartitionSpec as P
 
-
-def shards(tokens, route_weight, replica, w_gate, w_up, w_down):
+LANES = 128
+VMEM = pl.BlockSpec(memory_space=pltpu.VMEM)
+SMEM = pl.BlockSpec(memory_space=pltpu.SMEM)
+HBM = pl.BlockSpec(memory_space=pltpu.HBM)
+
+
+def in_hbm(array):
+    return pltpu.with_memory_space_constraint(array, pltpu.HBM)
+
+
+def pack_kernel(token_ref, weight_hbm, replica_hbm, out_ref, weight_ref, replica_ref, sems):
+    width = token_ref.shape[1]
+    copies = [
+        pltpu.make_async_copy(weight_hbm, weight_ref, sems.at[0]),
+        pltpu.make_async_copy(replica_hbm, replica_ref, sems.at[1]),
+        pltpu.make_async_copy(token_ref, out_ref.at[:, :width], sems.at[2]),
+    ]
+    for copy in copies:
+        copy.start()
+    copies[0].wait()
+    copies[1].wait()
+    weight = weight_ref[...]
+    probability = weight / jnp.sum(weight, axis=0, keepdims=True)
+    top_count, row_count = weight.shape
+    slot = lax.broadcasted_iota(jnp.int32, (LANES // 2, row_count), 0)
+    dense = jnp.zeros((LANES // 2, row_count), jnp.float32)
+    for k in range(top_count):
+        dense += jnp.where(replica_ref[k : k + 1, :] == slot, probability[k : k + 1, :], 0.0)
+    high = dense.astype(jnp.bfloat16).astype(jnp.float32)
+    low = dense - high
+    both = jnp.concatenate([high, low], axis=0)
+    both = jnp.concatenate([both, jnp.zeros((LANES, LANES - row_count), jnp.float32)], axis=1)
+    out_ref[:, width:] = both.T[:row_count].astype(jnp.bfloat16)
+    copies[2].wait()
+
+
+def stage_kernel(*refs):
+    mark_ref, sems = refs[-2:]
+    count = (len(refs) - 3) // 2
+    copies = []
+    for w, (source, target) in enumerate(zip(refs[1 : 1 + count], refs[1 + count : -2])):
+        pieces = sems.shape[1]
+        rows = source.shape[1] // pieces
+        for p in range(pieces):
+            at = pl.ds(p * rows, rows)
+            copies.append(pltpu.make_async_copy(source.at[:, at], target.at[:, at], sems.at[w, p]))
+    for copy in copies:
+        copy.start()
+    mark_ref[...] = jnp.zeros_like(mark_ref)
+    for copy in copies:
+        copy.wait()
+
+
+def expert_kernel(*refs):
+    slot_ref, gate_ref, up_ref, down_ref = refs[:4]
+    blocks = refs[4:-5]
+    away_ref, own_ref, rows_ref, share_ref, hidden_ref = refs[-5:]
+    width, hidden_width = gate_ref.shape[1:]
+    half = own_ref.shape[0]
+    first = 0
+    for block in blocks:
+        row_count = block.shape[0]
+        at = pl.ds(first, row_count)
+        first += row_count
+        rows_ref[at, :] = block[:, :width]
+        extra = block[:, width:].astype(jnp.float32)
+        lane = lax.broadcasted_iota(jnp.int32, extra.shape, 1)
+        chosen = (lane == slot_ref[0]) | (lane == slot_ref[0] + LANES // 2)
+        share = jnp.sum(jnp.where(chosen, extra, 0.0), axis=1, keepdims=True)
+        share_ref[at, :] = jnp.broadcast_to(share, (row_count, LANES))
+    rows = rows_ref[...]
+    step = 256
+    for n in range(0, hidden_width, step):
+        gate = jnp.dot(rows, gate_ref[0, :, n : n + step], preferred_element_type=jnp.float32)
+        upward = jnp.dot(rows, up_ref[0, :, n : n + step], preferred_element_type=jnp.float32)
+        hidden_ref[:, n : n + step] = (gate / (1.0 + jnp.exp(-gate)) * upward).astype(jnp.bfloat16)
+    hidden = hidden_ref[...]
+    share = share_ref[:, :1]
+    for n in range(0, width, step):
+        result = jnp.dot(hidden, down_ref[0, :, n : n + step], preferred_element_type=jnp.float32)
+        term = result.astype(jnp.bfloat16).astype(jnp.float32) * share
+        away_ref[:, n : n + step] = term[:half].astype(jnp.bfloat16)
+        own_ref[:, n : n + step] = term[half:]
+
+
+def join_kernel(*refs):
+    row_count = refs[0].shape[0]
+    for b, ref in enumerate(refs[:-1]):
+        refs[-1][pl.ds(b * row_count, row_count), :] = ref[...]
+
+
+def pair_kernel(own_ref, other_ref, near_ref, far_ref, *outs):
+    row_count = near_ref.shape[0]
+    half = own_ref.shape[0] // 2
+
+    def both(b):
+        at = pl.ds(b * row_count, row_count)
+        return own_ref[at, :] + other_ref[at, :].astype(jnp.float32)
+
+    near_ref[...] = both(0)
+    far_ref[...] = both(half // row_count)
+    for k, out in enumerate(outs, start=1):
+        out[:row_count] = both(k).astype(jnp.bfloat16)
+        out[row_count:] = both(half // row_count + k).astype(jnp.bfloat16)
+
+
+def cross_kernel(far_ref, *refs):
+    row_count = far_ref.shape[0]
+    total = far_ref[...]
+    for ref in refs[:-1]:
+        total += ref[row_count:].astype(jnp.float32)
+    refs[-1][...] = total.astype(jnp.bfloat16)
+
+
+def mix_kernel(token_ref, near_ref, crossed_ref, *refs):
+    row_count = token_ref.shape[0]
+    total = token_ref[...].astype(jnp.float32) + near_ref[...]
+    for ref in refs[:-1]:
+        total += ref[:row_count].astype(jnp.float32)
+    total += crossed_ref[...].astype(jnp.float32)
+    refs[-1][...] = total.astype(jnp.bfloat16)
+
+
+def on_core(kernel, name, outs, ins, scratch=(), limit=8):
+    return pl.pallas_call(
+        kernel,
+        out_shape=outs,
+        in_specs=ins,
+        out_specs=jax.tree.map(lambda out: VMEM, outs),
+        scratch_shapes=list(scratch),
+        compiler_params=pltpu.CompilerParams(vmem_limit_bytes=limit * 2**20),
+        name=name,
+    )
+
+
+def dense_shards(tokens, route_weight, replica, w_gate, w_up, w_down):
+    row_count, width = tokens.shape
+    hidden_width = w_gate.shape[2]
+    peer_count = lax.axis_size("expert")
+    pair_count = peer_count // 2
+    half = pair_count // 2
+    near_count = half * row_count
+    slot = lax.axis_index("expert").astype(jnp.int32).reshape(1)
+    wide, full = jnp.bfloat16, jnp.float32
+
+    def partner(array, k):
+        return lax.ppermute(array, "expert", [(i, i ^ (2 * k)) for i in range(peer_count)])
+
+    def swap(array):
+        return lax.ppermute(array, "expert", [(i, i ^ 1) for i in range(peer_count)])
+
+    def shape(rows, dtype, columns=width):
+        return jax.ShapeDtypeStruct((rows, columns), dtype)
+
+    packed = on_core(
+        pack_kernel,
+        "pack",
+        shape(row_count, wide, width + LANES),
+        [HBM] * 3,
+        (
+            pltpu.VMEM(replica.shape[::-1], full),
+            pltpu.VMEM(replica.shape[::-1], jnp.int32),
+            pltpu.SemaphoreType.DMA((3,)),
+        ),
+    )(*map(in_hbm, (tokens, route_weight.T, replica.T)))
+    crossed = partner(packed, half)
+    near = [partner(packed, k) for k in range(1, half)]
+    far = [crossed] + [partner(crossed, k) for k in range(1, half)]
+    near = [packed] + list(lax.optimization_barrier((crossed, *near)))[1:]
+    weights = (w_gate, w_up, w_down)
+    *staged, mark = on_core(
+        stage_kernel,
+        "stage",
+        tuple(pltpu.VMEM(w.shape, w.dtype) for w in weights) + (shape(8, full, LANES),),
+        [VMEM] + [HBM] * 3,
+        (pltpu.SemaphoreType.DMA((3, 4)),),
+        limit=2,
+    )(crossed, *map(in_hbm, weights))
+    far = [crossed] + list(lax.optimization_barrier((mark, *far[1:])))[1:]
+    near_rows = shape(near_count, wide, width + LANES)
+    other_near = swap(on_core(join_kernel, "join", near_rows, [VMEM] * half)(*near))
+    other_far = [swap(block) for block in far]
+    total_rows = peer_count * row_count
+    inputs = [other_near] + other_far + near + far
+    away, own = on_core(
+        expert_kernel,
+        "experts",
+        (shape(total_rows // 2, wide), shape(total_rows // 2, full)),
+        [SMEM] + [VMEM] * (3 + len(inputs)),
+        (
+            pltpu.VMEM((total_rows, width), wide),
+            pltpu.VMEM((total_rows, LANES), full),
+            pltpu.VMEM((total_rows, hidden_width), wide),
+        ),
+        limit=24,
+    )(slot, *staged, *inputs)
+    other = swap(away)
+    block, bundle = shape(row_count, full), shape(2 * row_count, wide)
+    own_near, own_far, *bundles = on_core(
+        pair_kernel, "pair", (block, block) + (bundle,) * (half - 1), [VMEM] * 2, limit=16
+    )(own, other)
+    arrived = [partner(array, k) for k, array in enumerate(bundles, start=1)]
+    send = on_core(cross_kernel, "cross", shape(row_count, wide), [VMEM] * half)(own_far, *arrived)
+    crossing = partner(send, half)
+    return on_core(mix_kernel, "mix", shape(row_count, wide), [VMEM] * (half + 2))(
+        tokens, own_near, crossing, *arrived
+    )
+
+
+def routed_shards(tokens, route_weight, replica, w_gate, w_up, w_down):
     row_count, width = tokens.shape
     top_count = replica.shape[1]
     peer_count = lax.axis_size("expert")
@@ -38,6 +248,23 @@
     return (own_columns.astype(jnp.float32) + combined).astype(jnp.bfloat16)
 
 
+def shards(*arrays):
+    tokens, replica, w_gate = arrays[0], arrays[2], arrays[3]
+    row_count, top_count = replica.shape
+    peer_count = lax.axis_size("expert")
+    if (
+        lax.axis_size("tensor") == 1
+        and peer_count in (4, 8, 16, 32, 64)
+        and 2 * top_count >= peer_count
+        and row_count % 16 == 0
+        and row_count <= LANES
+        and tokens.shape[1] % 256 == 0
+        and w_gate.shape[2] % 256 == 0
+    ):
+        return dense_shards(*arrays)
+    return routed_shards(*arrays)
+
+
 def solution(mesh):
     return jax.shard_map(
         shards,

time: 106 us -> 45 us (0.42); the launches traced: 104 us -> 44.8 us
  local copies, waits for them, and re-layouts: 32.2 us -> 0.01 us
  blocking collectives: 32.1 us -> 0 us
  starting transfers between devices: 5.04 us -> 18.8 us
  matrix products: 9.3 us -> 0 us
  Pallas kernels: 0 us -> 8.88 us
  waiting for transfers between devices: 22.9 us -> 17.1 us
  other arithmetic: 2.62 us -> 0 us
    all_to_all x1 -> x0, blocking collectives: 32.1 us -> none  [shards(): lax.all_to_all(outgoing, 'expert', split_axis=0, concat_axis=0, tiled=True)]
    scatter x1 -> x0, local copies, waits for them, and re-layouts: 23.6 us -> none  [shards(): outgoing = outgoing.at[flat_slot, position].set(tokens[source_row])]
    all_to_all x1 -> x0, waiting for transfers between devices: 22.9 us -> none  [shards(): lax.all_to_all(result, 'expert', split_axis=0, concat_axis=0, tiled=True)]
    ppermute x0 -> x17, starting transfers between devices: none -> 18.8 us  [the longest x11 17.6 us: partner(): lax.ppermute(array, 'expert', [(i, i ^ 2 * k) for i in range(peer_count)])]
    ppermute x0 -> x17, waiting for transfers between devices: none -> 17.1 us  [the longest x11 15.5 us: partner(): lax.ppermute(array, 'expert', [(i, i ^ 2 * k) for i in range(peer_count)])]
    dot_general x2 -> x0, matrix products: 9.3 us -> none  [the longest x1 5.53 us: shards(): jnp.dot(all_hidden, w_down[0], preferred_element_type=jnp.float32)]
    pallas_call x0 -> x7, Pallas kernels: none -> 8.88 us  [the longest x1 4.39 us: dense_shards(): on_core(stage_kernel, 'stage', tuple((pltpu.VMEM(w.shape, w.dtype) for w...]
    gather x2 -> x0, local copies, waits for them, and re-layouts: 5.28 us -> none  [the longest x1 3.53 us: shards(): values = returned[flat_slot, position].astype(jnp.float32)]
  transfers between devices with their start and end apart: 1 -> 17, of which waited for: 1 -> 10; matrix products, arithmetic and copies ran while one was open for 0% -> 0% of each run, Pallas kernels for 0% -> 10%
where the time goes in v2:
time: 45 us; the launch traced here: 44.8 us
  starting transfers between devices  18.8 us (42%)
  waiting for transfers between devices  17.1 us (38%)
  Pallas kernels  8.88 us (20%)
    ppermute x11, starting transfers between devices, partner(): lax.ppermute(array, 'expert', [(i, i ^ 2 * k) for i in range(peer_count)])  17.6 us
    ppermute x11, waiting for transfers between devices, partner(): lax.ppermute(array, 'expert', [(i, i ^ 2 * k) for i in range(peer_count)])  15.5 us
    pallas_call x1, Pallas kernels, dense_shards(): on_core(stage_kernel, 'stage', tuple((pltpu.VMEM(w.shape, w.dtype) for w...  4.39 us
    pallas_call x1, Pallas kernels, dense_shards(): on_core(expert_kernel, 'experts', (shape(total_rows // 2, wide), shape(to...  2.75 us
    ppermute x6, waiting for transfers between devices, swap(): lax.ppermute(array, 'expert', [(i, i ^ 1) for i in range(peer_count)])  1.55 us
    ppermute x6, starting transfers between devices, swap(): lax.ppermute(array, 'expert', [(i, i ^ 1) for i in range(peer_count)])  1.15 us
  transfers between devices with their start and end apart: 17, of which 10 were waited for; matrix products, arithmetic and copies ran while one was open for 0% of the time, Pallas kernels for 10%

profile of v2, /device:TPU:0, one launch (start us, length us, event | category | flops | bytes accessed | tf_op | source)
XLA Modules:
  0.0 44.8 jit_solution(6616320531263216637)
XLA Ops:
  0.0 0.9 %pack.1.refs_0_.refs_9_ = bf16[16,2176]{1,0:T(8,128)(2,1)S(1)} custom-call(bf16[16,2048]{1,0:T(8,128)(2,1)} %token_ref.3, f32[8,16]{1,0:T(8,128)} %bitcast.3, s32[8,16]{1,0:T(8,128)} %bitcast.4), custom_call_target="tpu_custom_call" | custom-call | tf_op jit(solution)/shard_map/pack/pallas_call | solution.py:162
  0.9 4.0 %collective-permute-start.3 = (bf16[16,2176]{1,0:T(8,128)(2,1)S(1)}, bf16[16,2176]{1,0:T(8,128)(2,1)S(1)}, u32[]{:S(2)}, u32[]{:S(2)}) collective-permute-start(bf16[16,2176]{1,0:T(8,128)(2,1)S(1)} %pack.1.refs_0_.refs_9_), channel_id=1, source_target_pairs={{0,6},{1,7},{2,4},{3,5},{4,2},{5,3},{6,0},{7,1},{8,14},{9,15},{10,... | collective-permute-start | bytes 208904 | tf_op jit(solution)/shard_map/ppermute | solution.py:154
  4.9 0.4 %collective-permute-start.2 = (bf16[16,2176]{1,0:T(8,128)(2,1)S(1)}, bf16[16,2176]{1,0:T(8,128)(2,1)S(1)}, u32[]{:S(2)}, u32[]{:S(2)}) collective-permute-start(bf16[16,2176]{1,0:T(8,128)(2,1)S(1)} %pack.1.refs_0_.refs_9_), channel_id=1, source_target_pairs={{0,4},{1,5},{2,6},{3,7},{4,0},{5,1},{6,2},{7,3},{8,12},{9,13},{10,... | collective-permute-start | bytes 208904 | tf_op jit(solution)/shard_map/ppermute | solution.py:154
  5.4 0.2 collective-permute-start.1
  5.6 2.9 %collective-permute-start = (bf16[16,2176]{1,0:T(8,128)(2,1)S(1)}, bf16[16,2176]{1,0:T(8,128)(2,1)S(1)}, u32[]{:S(2)}, u32[]{:S(2)}) collective-permute-start(bf16[16,2176]{1,0:T(8,128)(2,1)S(1)} %pack.1.refs_0_.refs_9_), channel_id=1, source_target_pairs={{0,8},{1,9},{2,10},{3,11},{4,12},{5,13},{6,14},{7,15},{8,0},{9,1},... | collective-permute-start | bytes 208904 | tf_op jit(solution)/shard_map/ppermute | solution.py:154
  8.5 0.0 collective-permute-done.3.refs_3_.refs_12_
  8.5 1.4 %collective-permute-done.2.refs_2_.refs_11_ = bf16[16,2176]{1,0:T(8,128)(2,1)S(1)} collective-permute-done((bf16[16,2176]{1,0:T(8,128)(2,1)S(1)}, bf16[16,2176]{1,0:T(8,128)(2,1)S(1)}, u32[]{:S(2)}, u32[]{:S(2)}) %collective-permute-start.2) | collective-permute-done | bytes 69664 | tf_op jit(solution)/shard_map/ppermute | solution.py:154
  9.9 0.0 collective-permute-done.1.refs_1_.refs_10_
  9.9 1.4 %collective-permute-done.refs_0_.refs_13_ = bf16[16,2176]{1,0:T(8,128)(2,1)S(1)} collective-permute-done((bf16[16,2176]{1,0:T(8,128)(2,1)S(1)}, bf16[16,2176]{1,0:T(8,128)(2,1)S(1)}, u32[]{:S(2)}, u32[]{:S(2)}) %collective-permute-start) | collective-permute-done | bytes 69664 | tf_op jit(solution)/shard_map/ppermute | solution.py:154
  11.3 0.1 collective-permute-start.4
  11.4 2.4 %collective-permute-start.8 = (bf16[16,2176]{1,0:T(8,128)(2,1)S(1)}, bf16[16,2176]{1,0:T(8,128)(2,1)S(1)}, u32[]{:S(2)}, u32[]{:S(2)}) collective-permute-start(bf16[16,2176]{1,0:T(8,128)(2,1)S(1)} %collective-permute-done.refs_0_.refs_13_), channel_id=1, source_target_pairs={{0,6},{1,7},{2,4},{3,5},{4,2},{5,3},{6,0},{7,1},{8,14},{9,15},{10,... | collective-permute-start | bytes 208904 | tf_op jit(solution)/shard_map/ppermute | solution.py:154
  13.8 0.7 %collective-permute-start.7 = (bf16[16,2176]{1,0:T(8,128)(2,1)S(1)}, bf16[16,2176]{1,0:T(8,128)(2,1)S(1)}, u32[]{:S(2)}, u32[]{:S(2)}) collective-permute-start(bf16[16,2176]{1,0:T(8,128)(2,1)S(1)} %collective-permute-done.refs_0_.refs_13_), channel_id=1, source_target_pairs={{0,4},{1,5},{2,6},{3,7},{4,0},{5,1},{6,2},{7,3},{8,12},{9,13},{10,... | collective-permute-start | bytes 208904 | tf_op jit(solution)/shard_map/ppermute | solution.py:154
  14.5 0.5 %collective-permute-start.6 = (bf16[16,2176]{1,0:T(8,128)(2,1)S(1)}, bf16[16,2176]{1,0:T(8,128)(2,1)S(1)}, u32[]{:S(2)}, u32[]{:S(2)}) collective-permute-start(bf16[16,2176]{1,0:T(8,128)(2,1)S(1)} %collective-permute-done.refs_0_.refs_13_), channel_id=1, source_target_pairs={{0,2},{1,3},{2,0},{3,1},{4,6},{5,7},{6,4},{7,5},{8,10},{9,11},{10,... | collective-permute-start | bytes 208904 | tf_op jit(solution)/shard_map/ppermute | solution.py:154
  14.9 0.0 collective-permute-start.5
  14.9 1.9 %collective-permute-done.8.refs_16_ = bf16[16,2176]{1,0:T(8,128)(2,1)S(1)} collective-permute-done((bf16[16,2176]{1,0:T(8,128)(2,1)S(1)}, bf16[16,2176]{1,0:T(8,128)(2,1)S(1)}, u32[]{:S(2)}, u32[]{:S(2)}) %collective-permute-start.8) | collective-permute-done | bytes 69664 | tf_op jit(solution)/shard_map/ppermute | solution.py:154
  16.9 1.6 %collective-permute-done.7.refs_15_ = bf16[16,2176]{1,0:T(8,128)(2,1)S(1)} collective-permute-done((bf16[16,2176]{1,0:T(8,128)(2,1)S(1)}, bf16[16,2176]{1,0:T(8,128)(2,1)S(1)}, u32[]{:S(2)}, u32[]{:S(2)}) %collective-permute-start.7) | collective-permute-done | bytes 69664 | tf_op jit(solution)/shard_map/ppermute | solution.py:154
  18.5 0.3 collective-permute-done.6.refs_14_
  18.8 0.0 collective-permute-start.9
  18.8 0.5 %collective-permute-start.10 = (bf16[16,2176]{1,0:T(8,128)(2,1)S(1)}, bf16[16,2176]{1,0:T(8,128)(2,1)S(1)}, u32[]{:S(2)}, u32[]{:S(2)}) collective-permute-start(bf16[16,2176]{1,0:T(8,128)(2,1)S(1)} %collective-permute-done.7.refs_15_), channel_id=1, source_target_pairs={{0,1},{1,0},{2,3},{3,2},{4,5},{5,4},{6,7},{7,6},{8,9},{9,8},{10,11... | collective-permute-start | bytes 208904 | tf_op jit(solution)/shard_map/ppermute | solution.py:157
  19.3 0.0 collective-permute-start.11
  19.3 4.4 %stage.1 = (bf16[1,2048,768]{2,1,0:T(8,128)(2,1)S(1)}, bf16[1,2048,768]{2,1,0:T(8,128)(2,1)S(1)}, bf16[1,768,2048]{2,1,0:T(8,128)(2,1)S(1)}, f32[8,128]{1,0:T(8,128)}) custom-call(bf16[16,2176]{1,0:T(8,128)(2,1)S(1)} %collective-permute-done.refs_0_.refs_13_, bf16[1,2048,768]{2,1,0:T(8,128)(2,1)} %refs_1_.1, bf16[1,2048,768]{2,1,0:T(8,128)(2,1)} %refs_2_.1, ...), custom_call_target="tpu_custom_call" | custom-call | tf_op jit(solution)/shard_map/stage/pallas_call | solution.py:178
  23.7 0.0 collective-permute-done.5.refs_5_
  23.7 0.0 collective-permute-done.9.refs_6_
  23.7 0.0 collective-permute-done.10.refs_7_
  23.7 0.0 collective-permute-done.11.refs_8_
  23.7 0.0 collective-permute-done.4.refs_4_
  23.7 0.0 copy-start
  23.7 2.7 %experts.1 = (bf16[128,2048]{1,0:T(8,128)(2,1)S(1)}, f32[128,2048]{1,0:T(8,128)S(1)}) custom-call(s32[1]{0:T(128)} %bitcast.refs_0_, bf16[1,2048,768]{2,1,0:T(8,128)(2,1)S(1)} %get-tuple-element.21.refs_1_, bf16[1,2048,768]{2,1,0:T(8,128)(2,1)S(1)} %get-tuple-element.22.refs_2_, bf16[1,768,2048]{2,1,0:T(8,128)(2,1)S(1)} %get-tuple-element.23.refs_3_, ...), custom_call_target="tpu_custom_call" | custom-call | tf_op jit(solution)/shard_map/experts/pallas_call | solution.py:192
  26.5 0.6 %collective-permute-start.12 = (bf16[128,2048]{1,0:T(8,128)(2,1)S(1)}, bf16[128,2048]{1,0:T(8,128)(2,1)S(1)}, u32[]{:S(2)}, u32[]{:S(2)}) collective-permute-start(bf16[128,2048]{1,0:T(8,128)(2,1)S(1)} %get-tuple-element.31), channel_id=1, source_target_pairs={{0,1},{1,0},{2,3},{3,2},{4,5},{5,4},{6,7},{7,6},{8,9},{9,8},{10,11... | collective-permute-start | bytes 1572872 | tf_op jit(solution)/shard_map/ppermute | solution.py:157
  27.1 1.5 %collective-permute-done.12.other_ref = bf16[128,2048]{1,0:T(8,128)(2,1)S(1)} collective-permute-done((bf16[128,2048]{1,0:T(8,128)(2,1)S(1)}, bf16[128,2048]{1,0:T(8,128)(2,1)S(1)}, u32[]{:S(2)}, u32[]{:S(2)}) %collective-permute-start.12) | collective-permute-done | bytes 524320 | tf_op jit(solution)/shard_map/ppermute | solution.py:157
  28.6 0.1 pair.1
  28.7 1.2 %collective-permute-start.13 = (bf16[32,2048]{1,0:T(8,128)(2,1)S(1)}, bf16[32,2048]{1,0:T(8,128)(2,1)S(1)}, u32[]{:S(2)}, u32[]{:S(2)}) collective-permute-start(bf16[32,2048]{1,0:T(8,128)(2,1)S(1)} %get-tuple-element.34), channel_id=1, source_target_pairs={{0,2},{1,3},{2,0},{3,1},{4,6},{5,7},{6,4},{7,5},{8,10},{9,11},{10,... | collective-permute-start | bytes 393224 | tf_op jit(solution)/shard_map/ppermute | solution.py:154
  29.9 1.4 %collective-permute-start.14 = (bf16[32,2048]{1,0:T(8,128)(2,1)S(1)}, bf16[32,2048]{1,0:T(8,128)(2,1)S(1)}, u32[]{:S(2)}, u32[]{:S(2)}) collective-permute-start(bf16[32,2048]{1,0:T(8,128)(2,1)S(1)} %get-tuple-element.35), channel_id=1, source_target_pairs={{0,4},{1,5},{2,6},{3,7},{4,0},{5,1},{6,2},{7,3},{8,12},{9,13},{10,... | collective-permute-start | bytes 393224 | tf_op jit(solution)/shard_map/ppermute | solution.py:154
  31.3 1.0 %collective-permute-start.15 = (bf16[32,2048]{1,0:T(8,128)(2,1)S(1)}, bf16[32,2048]{1,0:T(8,128)(2,1)S(1)}, u32[]{:S(2)}, u32[]{:S(2)}) collective-permute-start(bf16[32,2048]{1,0:T(8,128)(2,1)S(1)} %get-tuple-element.36), channel_id=1, source_target_pairs={{0,6},{1,7},{2,4},{3,5},{4,2},{5,3},{6,0},{7,1},{8,14},{9,15},{10,... | collective-permute-start | bytes 393224 | tf_op jit(solution)/shard_map/ppermute | solution.py:154
  32.3 2.3 %collective-permute-done.13.refs_0_ = bf16[32,2048]{1,0:T(8,128)(2,1)S(1)} collective-permute-done((bf16[32,2048]{1,0:T(8,128)(2,1)S(1)}, bf16[32,2048]{1,0:T(8,128)(2,1)S(1)}, u32[]{:S(2)}, u32[]{:S(2)}) %collective-permute-start.13) | collective-permute-done | bytes 131104 | tf_op jit(solution)/shard_map/ppermute | solution.py:154
  34.6 1.7 %collective-permute-done.14.refs_1_ = bf16[32,2048]{1,0:T(8,128)(2,1)S(1)} collective-permute-done((bf16[32,2048]{1,0:T(8,128)(2,1)S(1)}, bf16[32,2048]{1,0:T(8,128)(2,1)S(1)}, u32[]{:S(2)}, u32[]{:S(2)}) %collective-permute-start.14) | collective-permute-done | bytes 131104 | tf_op jit(solution)/shard_map/ppermute | solution.py:154
  36.3 2.3 %collective-permute-done.15.refs_2_ = bf16[32,2048]{1,0:T(8,128)(2,1)S(1)} collective-permute-done((bf16[32,2048]{1,0:T(8,128)(2,1)S(1)}, bf16[32,2048]{1,0:T(8,128)(2,1)S(1)}, u32[]{:S(2)}, u32[]{:S(2)}) %collective-permute-start.15) | collective-permute-done | bytes 131104 | tf_op jit(solution)/shard_map/ppermute | solution.py:154
  38.6 2.9 %collective-permute-start.16 = (bf16[16,2048]{1,0:T(8,128)(2,1)S(1)}, bf16[16,2048]{1,0:T(8,128)(2,1)S(1)}, u32[]{:S(2)}, u32[]{:S(2)}) collective-permute-start(bf16[16,2048]{1,0:T(8,128)(2,1)S(1)} %cross.1), channel_id=1, source_target_pairs={{0,8},{1,9},{2,10},{3,11},{4,12},{5,13},{6,14},{7,15},{8,0},{9,1},... | collective-permute-start | bytes 196616 | tf_op jit(solution)/shard_map/ppermute | solution.py:154
  41.5 2.7 %collective-permute-done.16.crossed_ref = bf16[16,2048]{1,0:T(8,128)(2,1)S(1)} collective-permute-done((bf16[16,2048]{1,0:T(8,128)(2,1)S(1)}, bf16[16,2048]{1,0:T(8,128)(2,1)S(1)}, u32[]{:S(2)}, u32[]{:S(2)}) %collective-permute-start.16) | collective-permute-done | bytes 65568 | tf_op jit(solution)/shard_map/ppermute | solution.py:154
  44.2 0.0 copy-done
  44.2 0.7 %mix.1 = bf16[16,2048]{1,0:T(8,128)(2,1)} custom-call(bf16[16,2048]{1,0:T(8,128)(2,1)S(1)} %copy-done, f32[16,2048]{1,0:T(8,128)S(1)} %get-tuple-element.32.near_ref, bf16[16,2048]{1,0:T(8,128)(2,1)S(1)} %collective-permute-done.16.crossed_ref, bf16[32,2048]{1,0:T(8,128)(2,1)S(1)} %collective-permute-done.13.refs_0_, ...), custom_call_target="tpu_custom_call" | custom-call | tf_op jit(solution)/shard_map/mix/pallas_call | solution.py:212
  (2 shorter events, 0.1 us)
Async XLA Ops:
  0.9 7.6 %collective-permute-start.3 = (bf16[16,2176]{1,0:T(8,128)(2,1)S(1)}, bf16[16,2176]{1,0:T(8,128)(2,1)S(1)}, u32[]{:S(2)}, u32[]{:S(2)}) collective-permute-start(bf16[16,2176]{1,0:T(8,128)(2,1)S(1)} %pack.1.refs_0_.refs_9_), channel_id=1, source_target_pairs={{0,6},{1,7},{2,4},{3,5},{4,2},{5,3},{6,0},{7,1},{8,14},{9,15},{10,... | collective-permute-start | bytes 208904 | tf_op jit(solution)/shard_map/ppermute | solution.py:154
  4.9 5.0 %collective-permute-start.2 = (bf16[16,2176]{1,0:T(8,128)(2,1)S(1)}, bf16[16,2176]{1,0:T(8,128)(2,1)S(1)}, u32[]{:S(2)}, u32[]{:S(2)}) collective-permute-start(bf16[16,2176]{1,0:T(8,128)(2,1)S(1)} %pack.1.refs_0_.refs_9_), channel_id=1, source_target_pairs={{0,4},{1,5},{2,6},{3,7},{4,0},{5,1},{6,2},{7,3},{8,12},{9,13},{10,... | collective-permute-start | bytes 208904 | tf_op jit(solution)/shard_map/ppermute | solution.py:154
  5.4 4.5 %collective-permute-start.1 = (bf16[16,2176]{1,0:T(8,128)(2,1)S(1)}, bf16[16,2176]{1,0:T(8,128)(2,1)S(1)}, u32[]{:S(2)}, u32[]{:S(2)}) collective-permute-start(bf16[16,2176]{1,0:T(8,128)(2,1)S(1)} %pack.1.refs_0_.refs_9_), channel_id=1, source_target_pairs={{0,2},{1,3},{2,0},{3,1},{4,6},{5,7},{6,4},{7,5},{8,10},{9,11},{10,... | collective-permute-start | bytes 208904 | tf_op jit(solution)/shard_map/ppermute | solution.py:154
  5.6 5.7 %collective-permute-start = (bf16[16,2176]{1,0:T(8,128)(2,1)S(1)}, bf16[16,2176]{1,0:T(8,128)(2,1)S(1)}, u32[]{:S(2)}, u32[]{:S(2)}) collective-permute-start(bf16[16,2176]{1,0:T(8,128)(2,1)S(1)} %pack.1.refs_0_.refs_9_), channel_id=1, source_target_pairs={{0,8},{1,9},{2,10},{3,11},{4,12},{5,13},{6,14},{7,15},{8,0},{9,1},... | collective-permute-start | bytes 208904 | tf_op jit(solution)/shard_map/ppermute | solution.py:154
  11.3 12.4 %collective-permute-start.4 = (bf16[64,2176]{1,0:T(8,128)(2,1)S(1)}, bf16[64,2176]{1,0:T(8,128)(2,1)S(1)}, u32[]{:S(2)}, u32[]{:S(2)}) collective-permute-start(bf16[64,2176]{1,0:T(8,128)(2,1)S(1)} %join.1), channel_id=1, source_target_pairs={{0,1},{1,0},{2,3},{3,2},{4,5},{5,4},{6,7},{7,6},{8,9},{9,8},{10,11... | collective-permute-start | bytes 835592 | tf_op jit(solution)/shard_map/ppermute | solution.py:157
  11.4 5.5 %collective-permute-start.8 = (bf16[16,2176]{1,0:T(8,128)(2,1)S(1)}, bf16[16,2176]{1,0:T(8,128)(2,1)S(1)}, u32[]{:S(2)}, u32[]{:S(2)}) collective-permute-start(bf16[16,2176]{1,0:T(8,128)(2,1)S(1)} %collective-permute-done.refs_0_.refs_13_), channel_id=1, source_target_pairs={{0,6},{1,7},{2,4},{3,5},{4,2},{5,3},{6,0},{7,1},{8,14},{9,15},{10,... | collective-permute-start | bytes 208904 | tf_op jit(solution)/shard_map/ppermute | solution.py:154
  13.8 4.7 %collective-permute-start.7 = (bf16[16,2176]{1,0:T(8,128)(2,1)S(1)}, bf16[16,2176]{1,0:T(8,128)(2,1)S(1)}, u32[]{:S(2)}, u32[]{:S(2)}) collective-permute-start(bf16[16,2176]{1,0:T(8,128)(2,1)S(1)} %collective-permute-done.refs_0_.refs_13_), channel_id=1, source_target_pairs={{0,4},{1,5},{2,6},{3,7},{4,0},{5,1},{6,2},{7,3},{8,12},{9,13},{10,... | collective-permute-start | bytes 208904 | tf_op jit(solution)/shard_map/ppermute | solution.py:154
  14.5 4.3 %collective-permute-start.6 = (bf16[16,2176]{1,0:T(8,128)(2,1)S(1)}, bf16[16,2176]{1,0:T(8,128)(2,1)S(1)}, u32[]{:S(2)}, u32[]{:S(2)}) collective-permute-start(bf16[16,2176]{1,0:T(8,128)(2,1)S(1)} %collective-permute-done.refs_0_.refs_13_), channel_id=1, source_target_pairs={{0,2},{1,3},{2,0},{3,1},{4,6},{5,7},{6,4},{7,5},{8,10},{9,11},{10,... | collective-permute-start | bytes 208904 | tf_op jit(solution)/shard_map/ppermute | solution.py:154
  14.9 8.7 %collective-permute-start.5 = (bf16[16,2176]{1,0:T(8,128)(2,1)S(1)}, bf16[16,2176]{1,0:T(8,128)(2,1)S(1)}, u32[]{:S(2)}, u32[]{:S(2)}) collective-permute-start(bf16[16,2176]{1,0:T(8,128)(2,1)S(1)} %collective-permute-done.refs_0_.refs_13_), channel_id=1, source_target_pairs={{0,1},{1,0},{2,3},{3,2},{4,5},{5,4},{6,7},{7,6},{8,9},{9,8},{10,11... | collective-permute-start | bytes 208904 | tf_op jit(solution)/shard_map/ppermute | solution.py:157
  18.8 4.9 %collective-permute-start.9 = (bf16[16,2176]{1,0:T(8,128)(2,1)S(1)}, bf16[16,2176]{1,0:T(8,128)(2,1)S(1)}, u32[]{:S(2)}, u32[]{:S(2)}) collective-permute-start(bf16[16,2176]{1,0:T(8,128)(2,1)S(1)} %collective-permute-done.6.refs_14_), channel_id=1, source_target_pairs={{0,1},{1,0},{2,3},{3,2},{4,5},{5,4},{6,7},{7,6},{8,9},{9,8},{10,11... | collective-permute-start | bytes 208904 | tf_op jit(solution)/shard_map/ppermute | solution.py:157
  18.8 4.9 %collective-permute-start.10 = (bf16[16,2176]{1,0:T(8,128)(2,1)S(1)}, bf16[16,2176]{1,0:T(8,128)(2,1)S(1)}, u32[]{:S(2)}, u32[]{:S(2)}) collective-permute-start(bf16[16,2176]{1,0:T(8,128)(2,1)S(1)} %collective-permute-done.7.refs_15_), channel_id=1, source_target_pairs={{0,1},{1,0},{2,3},{3,2},{4,5},{5,4},{6,7},{7,6},{8,9},{9,8},{10,11... | collective-permute-start | bytes 208904 | tf_op jit(solution)/shard_map/ppermute | solution.py:157
  19.3 4.4 %collective-permute-start.11 = (bf16[16,2176]{1,0:T(8,128)(2,1)S(1)}, bf16[16,2176]{1,0:T(8,128)(2,1)S(1)}, u32[]{:S(2)}, u32[]{:S(2)}) collective-permute-start(bf16[16,2176]{1,0:T(8,128)(2,1)S(1)} %collective-permute-done.8.refs_16_), channel_id=1, source_target_pairs={{0,1},{1,0},{2,3},{3,2},{4,5},{5,4},{6,7},{7,6},{8,9},{9,8},{10,11... | collective-permute-start | bytes 208904 | tf_op jit(solution)/shard_map/ppermute | solution.py:157
  23.7 20.4 %copy-start = (bf16[16,2048]{1,0:T(8,128)(2,1)S(1)}, bf16[16,2048]{1,0:T(8,128)(2,1)}, u32[]{:S(2)}) copy-start(bf16[16,2048]{1,0:T(8,128)(2,1)} %token_ref.3) | copy-start | bytes 196612
  26.5 2.1 %collective-permute-start.12 = (bf16[128,2048]{1,0:T(8,128)(2,1)S(1)}, bf16[128,2048]{1,0:T(8,128)(2,1)S(1)}, u32[]{:S(2)}, u32[]{:S(2)}) collective-permute-start(bf16[128,2048]{1,0:T(8,128)(2,1)S(1)} %get-tuple-element.31), channel_id=1, source_target_pairs={{0,1},{1,0},{2,3},{3,2},{4,5},{5,4},{6,7},{7,6},{8,9},{9,8},{10,11... | collective-permute-start | bytes 1572872 | tf_op jit(solution)/shard_map/ppermute | solution.py:157
  28.7 5.8 %collective-permute-start.13 = (bf16[32,2048]{1,0:T(8,128)(2,1)S(1)}, bf16[32,2048]{1,0:T(8,128)(2,1)S(1)}, u32[]{:S(2)}, u32[]{:S(2)}) collective-permute-start(bf16[32,2048]{1,0:T(8,128)(2,1)S(1)} %get-tuple-element.34), channel_id=1, source_target_pairs={{0,2},{1,3},{2,0},{3,1},{4,6},{5,7},{6,4},{7,5},{8,10},{9,11},{10,... | collective-permute-start | bytes 393224 | tf_op jit(solution)/shard_map/ppermute | solution.py:154
  29.9 6.4 %collective-permute-start.14 = (bf16[32,2048]{1,0:T(8,128)(2,1)S(1)}, bf16[32,2048]{1,0:T(8,128)(2,1)S(1)}, u32[]{:S(2)}, u32[]{:S(2)}) collective-permute-start(bf16[32,2048]{1,0:T(8,128)(2,1)S(1)} %get-tuple-element.35), channel_id=1, source_target_pairs={{0,4},{1,5},{2,6},{3,7},{4,0},{5,1},{6,2},{7,3},{8,12},{9,13},{10,... | collective-permute-start | bytes 393224 | tf_op jit(solution)/shard_map/ppermute | solution.py:154
  31.3 7.2 %collective-permute-start.15 = (bf16[32,2048]{1,0:T(8,128)(2,1)S(1)}, bf16[32,2048]{1,0:T(8,128)(2,1)S(1)}, u32[]{:S(2)}, u32[]{:S(2)}) collective-permute-start(bf16[32,2048]{1,0:T(8,128)(2,1)S(1)} %get-tuple-element.36), channel_id=1, source_target_pairs={{0,6},{1,7},{2,4},{3,5},{4,2},{5,3},{6,0},{7,1},{8,14},{9,15},{10,... | collective-permute-start | bytes 393224 | tf_op jit(solution)/shard_map/ppermute | solution.py:154
  38.6 5.6 %collective-permute-start.16 = (bf16[16,2048]{1,0:T(8,128)(2,1)S(1)}, bf16[16,2048]{1,0:T(8,128)(2,1)S(1)}, u32[]{:S(2)}, u32[]{:S(2)}) collective-permute-start(bf16[16,2048]{1,0:T(8,128)(2,1)S(1)} %cross.1), channel_id=1, source_target_pairs={{0,8},{1,9},{2,10},{3,11},{4,12},{5,13},{6,14},{7,15},{8,0},{9,1},... | collective-permute-start | bytes 196616 | tf_op jit(solution)/shard_map/ppermute | solution.py:154

commit v3 on v2

--- a/solution.py
+++ b/solution.py
@@ -39,23 +39,6 @@
     both = jnp.concatenate([both, jnp.zeros((LANES, LANES - row_count), jnp.float32)], axis=1)
     out_ref[:, width:] = both.T[:row_count].astype(jnp.bfloat16)
     copies[2].wait()
-
-
-def stage_kernel(*refs):
-    mark_ref, sems = refs[-2:]
-    count = (len(refs) - 3) // 2
-    copies = []
-    for w, (source, target) in enumerate(zip(refs[1 : 1 + count], refs[1 + count : -2])):
-        pieces = sems.shape[1]
-        rows = source.shape[1] // pieces
-        for p in range(pieces):
-            at = pl.ds(p * rows, rows)
-            copies.append(pltpu.make_async_copy(source.at[:, at], target.at[:, at], sems.at[w, p]))
-    for copy in copies:
-        copy.start()
-    mark_ref[...] = jnp.zeros_like(mark_ref)
-    for copy in copies:
-        copy.wait()
 
 
 def expert_kernel(*refs):
@@ -96,39 +79,22 @@
         refs[-1][pl.ds(b * row_count, row_count), :] = ref[...]
 
 
-def pair_kernel(own_ref, other_ref, near_ref, far_ref, *outs):
-    row_count = near_ref.shape[0]
-    half = own_ref.shape[0] // 2
-
-    def both(b):
-        at = pl.ds(b * row_count, row_count)
-        return own_ref[at, :] + other_ref[at, :].astype(jnp.float32)
-
-    near_ref[...] = both(0)
-    far_ref[...] = both(half // row_count)
-    for k, out in enumerate(outs, start=1):
-        out[:row_count] = both(k).astype(jnp.bfloat16)
-        out[row_count:] = both(half // row_count + k).astype(jnp.bfloat16)
-
-
-def cross_kernel(far_ref, *refs):
-    row_count = far_ref.shape[0]
-    total = far_ref[...]
-    for ref in refs[:-1]:
-        total += ref[row_count:].astype(jnp.float32)
+def pair_kernel(own_ref, other_ref, first_ref, *outs):
+    row_count = first_ref.shape[0]
+    for k, out in enumerate((first_ref,) + outs):
+        at = pl.ds(k * row_count, row_count)
+        total = own_ref[at, :] + other_ref[at, :].astype(jnp.float32)
+        out[...] = total.astype(out.dtype)
+
+
+def sum_kernel(*refs):
+    total = refs[0][...].astype(jnp.float32)
+    for ref in refs[1:-1]:
+        total += ref[...].astype(jnp.float32)
     refs[-1][...] = total.astype(jnp.bfloat16)
 
 
-def mix_kernel(token_ref, near_ref, crossed_ref, *refs):
-    row_count = token_ref.shape[0]
-    total = token_ref[...].astype(jnp.float32) + near_ref[...]
-    for ref in refs[:-1]:
-        total += ref[:row_count].astype(jnp.float32)
-    total += crossed_ref[...].astype(jnp.float32)
-    refs[-1][...] = total.astype(jnp.bfloat16)
-
-
-def on_core(kernel, name, outs, ins, scratch=(), limit=8):
+def on_core(kernel, name, outs, ins, scratch=(), limit=8, flops=0):
     return pl.pallas_call(
         kernel,
         out_shape=outs,
@@ -136,6 +102,7 @@
         out_specs=jax.tree.map(lambda out: VMEM, outs),
         scratch_shapes=list(scratch),
         compiler_params=pltpu.CompilerParams(vmem_limit_bytes=limit * 2**20),
+        cost_estimate=pl.CostEstimate(flops=flops, bytes_accessed=flops // 4096, transcendentals=0),
         name=name,
     )
 
@@ -144,9 +111,8 @@
     row_count, width = tokens.shape
     hidden_width = w_gate.shape[2]
     peer_count = lax.axis_size("expert")
-    pair_count = peer_count // 2
-    half = pair_count // 2
-    near_count = half * row_count
+    half = peer_count // 4
+    half_rows = half * row_count
     slot = lax.axis_index("expert").astype(jnp.int32).reshape(1)
     wide, full = jnp.bfloat16, jnp.float32
 
@@ -158,6 +124,35 @@
 
     def shape(rows, dtype, columns=width):
         return jax.ShapeDtypeStruct((rows, columns), dtype)
+
+    def after(array, *others):
+        return lax.optimization_barrier((array, *others))[0]
+
+    def join(blocks):
+        rows = shape(half_rows, wide, width + LANES)
+        return on_core(join_kernel, "join", rows, [VMEM] * half, flops=10**8)(*blocks)
+
+    def experts(name, blocks):
+        return on_core(
+            expert_kernel,
+            name,
+            (shape(half_rows, wide), shape(half_rows, full)),
+            [SMEM] + [VMEM] * (3 + len(blocks)),
+            (
+                pltpu.VMEM((2 * half_rows, width), wide),
+                pltpu.VMEM((2 * half_rows, LANES), full),
+                pltpu.VMEM((2 * half_rows, hidden_width), wide),
+            ),
+            limit=16,
+            flops=2 * 10**9,
+        )(slot, w_gate, w_up, w_down, *blocks)
+
+    def pair(own, other, dtype):
+        outs = (shape(row_count, dtype),) + (shape(row_count, wide),) * (half - 1)
+        return on_core(pair_kernel, "pair", outs, [VMEM] * 2)(own, other)
+
+    def total(name, *terms):
+        return on_core(sum_kernel, name, shape(row_count, wide), [VMEM] * len(terms))(*terms)
 
     packed = on_core(
         pack_kernel,
@@ -169,49 +164,23 @@
             pltpu.VMEM(replica.shape[::-1], jnp.int32),
             pltpu.SemaphoreType.DMA((3,)),
         ),
+        flops=10**10,
     )(*map(in_hbm, (tokens, route_weight.T, replica.T)))
     crossed = partner(packed, half)
-    near = [partner(packed, k) for k in range(1, half)]
+    again = on_core(join_kernel, "again", shape(row_count, wide, width + LANES), [VMEM], flops=10**9)(packed)
+    near = [again] + [partner(again, k) for k in range(1, half)]
     far = [crossed] + [partner(crossed, k) for k in range(1, half)]
-    near = [packed] + list(lax.optimization_barrier((crossed, *near)))[1:]
-    weights = (w_gate, w_up, w_down)
-    *staged, mark = on_core(
-        stage_kernel,
-        "stage",
-        tuple(pltpu.VMEM(w.shape, w.dtype) for w in weights) + (shape(8, full, LANES),),
-        [VMEM] + [HBM] * 3,
-        (pltpu.SemaphoreType.DMA((3, 4)),),
-        limit=2,
-    )(crossed, *map(in_hbm, weights))
-    far = [crossed] + list(lax.optimization_barrier((mark, *far[1:])))[1:]
-    near_rows = shape(near_count, wide, width + LANES)
-    other_near = swap(on_core(join_kernel, "join", near_rows, [VMEM] * half)(*near))
-    other_far = [swap(block) for block in far]
-    total_rows = peer_count * row_count
-    inputs = [other_near] + other_far + near + far
-    away, own = on_core(
-        expert_kernel,
-        "experts",
-        (shape(total_rows // 2, wide), shape(total_rows // 2, full)),
-        [SMEM] + [VMEM] * (3 + len(inputs)),
-        (
-            pltpu.VMEM((total_rows, width), wide),
-            pltpu.VMEM((total_rows, LANES), full),
-            pltpu.VMEM((total_rows, hidden_width), wide),
-        ),
-        limit=24,
-    )(slot, *staged, *inputs)
-    other = swap(away)
-    block, bundle = shape(row_count, full), shape(2 * row_count, wide)
-    own_near, own_far, *bundles = on_core(
-        pair_kernel, "pair", (block, block) + (bundle,) * (half - 1), [VMEM] * 2, limit=16
-    )(own, other)
-    arrived = [partner(array, k) for k, array in enumerate(bundles, start=1)]
-    send = on_core(cross_kernel, "cross", shape(row_count, wide), [VMEM] * half)(own_far, *arrived)
-    crossing = partner(send, half)
-    return on_core(mix_kernel, "mix", shape(row_count, wide), [VMEM] * (half + 2))(
-        tokens, own_near, crossing, *arrived
-    )
+    near = [after(block, crossed) for block in near]
+    near_away, near_own = experts("near", [swap(join(near))] + near)
+    far = [crossed] + [after(block, near_away) for block in far[1:]]
+    far_away, far_own = experts("far", [swap(block) for block in far] + far)
+    far_first, *far_sums = pair(far_own, swap(far_away), full)
+    near_first, *near_sums = pair(near_own, swap(near_away), full)
+    far_back = [partner(block, k) for k, block in enumerate(far_sums, start=1)]
+    near_sums = [after(block, *far_sums) for block in near_sums]
+    near_back = [partner(block, k) for k, block in enumerate(near_sums, start=1)]
+    crossing = partner(total("cross", far_first, *far_back), half)
+    return total("mix", tokens, near_first, *near_back, crossing)
 
 
 def routed_shards(tokens, route_weight, replica, w_gate, w_up, w_down):

time: 45 us -> 43.5 us (0.967)
  waiting for transfers between devices: 17.1 us -> 11.4 us
  local copies, waits for them, and re-layouts: 0.01 us -> 3.79 us
  starting transfers between devices: 18.8 us -> 21.4 us
  Pallas kernels: 8.88 us -> 6.5 us
    ppermute x11 -> x14, waiting for transfers between devices: 15.5 us -> 9.23 us  [partner(): lax.ppermute(array, 'expert', [(i, i ^ 2 * k) for i in range(peer_count)])]
    unnamed x2 -> x8, local copies, waits for them, and re-layouts: 0.01 us -> 3.79 us
    pallas_call x6 -> x8, Pallas kernels: 7.98 us -> 5.6 us  [the longest x2 4.02 us: experts(): on_core(expert_kernel, name, (shape(half_rows, wide), shape(half_rows, fu...]
    ppermute x11 -> x14, starting transfers between devices: 17.6 us -> 19.7 us  [partner(): lax.ppermute(array, 'expert', [(i, i ^ 2 * k) for i in range(peer_count)])]
    ppermute x6 -> x7, waiting for transfers between devices: 1.55 us -> 2.2 us  [swap(): lax.ppermute(array, 'expert', [(i, i ^ 1) for i in range(peer_count)])]
    ppermute x6 -> x7, starting transfers between devices: 1.15 us -> 1.73 us  [swap(): lax.ppermute(array, 'expert', [(i, i ^ 1) for i in range(peer_count)])]
  transfers between devices with their start and end apart: 17 -> 21, of which waited for: 10 -> 9; matrix products, arithmetic and copies ran while one was open for 0% -> 0% of each run, Pallas kernels for 10% -> 6%
where the time goes in v3:
time: 43.5 us; the launch traced here: 43.2 us
  starting transfers between devices  21.4 us (49%)
  waiting for transfers between devices  11.4 us (26%)
  Pallas kernels  6.5 us (15%)
  local copies, waits for them, and re-layouts  3.79 us (9%)
    ppermute x14, starting transfers between devices, partner(): lax.ppermute(array, 'expert', [(i, i ^ 2 * k) for i in range(peer_count)])  19.7 us
    ppermute x14, waiting for transfers between devices, partner(): lax.ppermute(array, 'expert', [(i, i ^ 2 * k) for i in range(peer_count)])  9.23 us
    pallas_call x2, Pallas kernels, experts(): on_core(expert_kernel, name, (shape(half_rows, wide), shape(half_rows, fu...  4.02 us
    unnamed x8, local copies, waits for them, and re-layouts  3.79 us
    ppermute x7, waiting for transfers between devices, swap(): lax.ppermute(array, 'expert', [(i, i ^ 1) for i in range(peer_count)])  2.2 us
    ppermute x7, starting transfers between devices, swap(): lax.ppermute(array, 'expert', [(i, i ^ 1) for i in range(peer_count)])  1.73 us
    pallas_call x1, Pallas kernels, dense_shards(): on_core(pack_kernel, 'pack', shape(row_count, wide, width + LANES), [HBM]...  0.9 us
  transfers between devices with their start and end apart: 21, of which 9 were waited for; matrix products, arithmetic and copies ran while one was open for 0% of the time, Pallas kernels for 6%

profile of v3, /device:TPU:0, one launch (start us, length us, event | category | flops | bytes accessed | tf_op | source)
XLA Modules:
  0.0 43.2 jit_solution(11375646057041662069)
XLA Ops:
  0.0 0.9 %pack.1.refs_0_ = bf16[16,2176]{1,0:T(8,128)(2,1)S(1)} custom-call(bf16[16,2048]{1,0:T(8,128)(2,1)} %refs_0_.1, f32[8,16]{1,0:T(8,128)} %bitcast.3, s32[8,16]{1,0:T(8,128)} %bitcast.4), custom_call_target="tpu_custom_call" | custom-call | flops 10000000000 | bytes 2441406 | tf_op jit(solution)/shard_map/pack/pallas_call | solution.py:157
  0.9 0.0 copy-start
  0.9 4.1 %collective-permute-start = (bf16[16,2176]{1,0:T(8,128)(2,1)S(1)}, bf16[16,2176]{1,0:T(8,128)(2,1)S(1)}, u32[]{:S(2)}, u32[]{:S(2)}) collective-permute-start(bf16[16,2176]{1,0:T(8,128)(2,1)S(1)} %pack.1.refs_0_), channel_id=1, source_target_pairs={{0,8},{1,9},{2,10},{3,11},{4,12},{5,13},{6,14},{7,15},{8,0},{9,1},... | collective-permute-start | bytes 208904 | tf_op jit(solution)/shard_map/ppermute | solution.py:120
  5.0 1.5 %collective-permute-start.1 = (bf16[16,2176]{1,0:T(8,128)(2,1)S(1)}, bf16[16,2176]{1,0:T(8,128)(2,1)S(1)}, u32[]{:S(2)}, u32[]{:S(2)}) collective-permute-start(bf16[16,2176]{1,0:T(8,128)(2,1)S(1)} %again.1.refs_0_.refs_5_), channel_id=1, source_target_pairs={{0,2},{1,3},{2,0},{3,1},{4,6},{5,7},{6,4},{7,5},{8,10},{9,11},{10,... | collective-permute-start | bytes 208904 | tf_op jit(solution)/shard_map/ppermute | solution.py:120
  6.5 1.6 %collective-permute-start.2 = (bf16[16,2176]{1,0:T(8,128)(2,1)S(1)}, bf16[16,2176]{1,0:T(8,128)(2,1)S(1)}, u32[]{:S(2)}, u32[]{:S(2)}) collective-permute-start(bf16[16,2176]{1,0:T(8,128)(2,1)S(1)} %again.1.refs_0_.refs_5_), channel_id=1, source_target_pairs={{0,4},{1,5},{2,6},{3,7},{4,0},{5,1},{6,2},{7,3},{8,12},{9,13},{10,... | collective-permute-start | bytes 208904 | tf_op jit(solution)/shard_map/ppermute | solution.py:120
  8.1 0.4 collective-permute-start.3
  8.5 0.0 collective-permute-done.refs_8_
  8.5 0.8 %collective-permute-done.1.refs_1_.refs_6_ = bf16[16,2176]{1,0:T(8,128)(2,1)S(1)} collective-permute-done((bf16[16,2176]{1,0:T(8,128)(2,1)S(1)}, bf16[16,2176]{1,0:T(8,128)(2,1)S(1)}, u32[]{:S(2)}, u32[]{:S(2)}) %collective-permute-start.1) | collective-permute-done | bytes 69664 | tf_op jit(solution)/shard_map/ppermute | solution.py:120
  9.3 1.8 %collective-permute-done.2.refs_2_.refs_7_ = bf16[16,2176]{1,0:T(8,128)(2,1)S(1)} collective-permute-done((bf16[16,2176]{1,0:T(8,128)(2,1)S(1)}, bf16[16,2176]{1,0:T(8,128)(2,1)S(1)}, u32[]{:S(2)}, u32[]{:S(2)}) %collective-permute-start.2) | collective-permute-done | bytes 69664 | tf_op jit(solution)/shard_map/ppermute | solution.py:120
  11.1 2.2 %collective-permute-done.3.refs_3_.refs_8_ = bf16[16,2176]{1,0:T(8,128)(2,1)S(1)} collective-permute-done((bf16[16,2176]{1,0:T(8,128)(2,1)S(1)}, bf16[16,2176]{1,0:T(8,128)(2,1)S(1)}, u32[]{:S(2)}, u32[]{:S(2)}) %collective-permute-start.3) | collective-permute-done | bytes 69664 | tf_op jit(solution)/shard_map/ppermute | solution.py:120
  13.3 0.7 %join.1 = bf16[64,2176]{1,0:T(8,128)(2,1)} custom-call(bf16[16,2176]{1,0:T(8,128)(2,1)S(1)} %again.1.refs_0_.refs_5_, bf16[16,2176]{1,0:T(8,128)(2,1)S(1)} %collective-permute-done.1.refs_1_.refs_6_, bf16[16,2176]{1,0:T(8,128)(2,1)S(1)} %collective-permute-done.2.refs_2_.refs_7_, bf16[16,2176]{1,0:T(8,128)(2,1)S(1)} %collective-permute-done.3.refs_3_.refs_8_), custom_call_target="tpu_custom_call" | custom-call | flops 100000000 | bytes 24414 | tf_op jit(solution)/shard_map/join/pallas_call | solution.py:133
  14.0 0.0 collective-permute-start.4
  14.0 0.5 %collective-permute-start.6 = (bf16[16,2176]{1,0:T(8,128)(2,1)S(1)}, bf16[16,2176]{1,0:T(8,128)(2,1)S(1)}, u32[]{:S(2)}, u32[]{:S(2)}) collective-permute-start(bf16[16,2176]{1,0:T(8,128)(2,1)S(1)} %collective-permute-done.refs_8_), channel_id=1, source_target_pairs={{0,1},{1,0},{2,3},{3,2},{4,5},{5,4},{6,7},{7,6},{8,9},{9,8},{10,11... | collective-permute-start | bytes 208904 | tf_op jit(solution)/shard_map/ppermute | solution.py:123
  14.5 0.5 %collective-permute-start.7 = (bf16[16,2176]{1,0:T(8,128)(2,1)S(1)}, bf16[16,2176]{1,0:T(8,128)(2,1)S(1)}, u32[]{:S(2)}, u32[]{:S(2)}) collective-permute-start(bf16[16,2176]{1,0:T(8,128)(2,1)S(1)} %collective-permute-done.refs_8_), channel_id=1, source_target_pairs={{0,2},{1,3},{2,0},{3,1},{4,6},{5,7},{6,4},{7,5},{8,10},{9,11},{10,... | collective-permute-start | bytes 208904 | tf_op jit(solution)/shard_map/ppermute | solution.py:120
  15.1 0.8 %collective-permute-start.9 = (bf16[16,2176]{1,0:T(8,128)(2,1)S(1)}, bf16[16,2176]{1,0:T(8,128)(2,1)S(1)}, u32[]{:S(2)}, u32[]{:S(2)}) collective-permute-start(bf16[16,2176]{1,0:T(8,128)(2,1)S(1)} %collective-permute-done.refs_8_), channel_id=1, source_target_pairs={{0,4},{1,5},{2,6},{3,7},{4,0},{5,1},{6,2},{7,3},{8,12},{9,13},{10,... | collective-permute-start | bytes 208904 | tf_op jit(solution)/shard_map/ppermute | solution.py:120
  15.9 2.2 %collective-permute-start.11 = (bf16[16,2176]{1,0:T(8,128)(2,1)S(1)}, bf16[16,2176]{1,0:T(8,128)(2,1)S(1)}, u32[]{:S(2)}, u32[]{:S(2)}) collective-permute-start(bf16[16,2176]{1,0:T(8,128)(2,1)S(1)} %collective-permute-done.refs_8_), channel_id=1, source_target_pairs={{0,6},{1,7},{2,4},{3,5},{4,2},{5,3},{6,0},{7,1},{8,14},{9,15},{10,... | collective-permute-start | bytes 208904 | tf_op jit(solution)/shard_map/ppermute | solution.py:120
  18.0 0.0 collective-permute-done.4.refs_4_
  18.0 0.0 copy-done
  18.0 0.0 copy-start.1
  18.0 1.9 %copy-done.1 = bf16[1,2048,768]{2,1,0:T(8,128)(2,1)S(1)} copy-done((bf16[1,2048,768]{2,1,0:T(8,128)(2,1)S(1)}, bf16[1,2048,768]{2,1,0:T(8,128)(2,1)}, u32[]{:S(2)}) %copy-start.1) | copy-done | bytes 3145752
  19.9 0.0 copy-start.2
  19.9 1.9 %copy-done.2 = bf16[1,768,2048]{2,1,0:T(8,128)(2,1)S(1)} copy-done((bf16[1,768,2048]{2,1,0:T(8,128)(2,1)S(1)}, bf16[1,768,2048]{2,1,0:T(8,128)(2,1)}, u32[]{:S(2)}) %copy-start.2) | copy-done | bytes 3145752
  21.8 2.5 %near.1 = (bf16[64,2048]{1,0:T(8,128)(2,1)S(1)}, f32[64,2048]{1,0:T(8,128)S(1)}) custom-call(s32[1]{0:T(128)} %bitcast.refs_0_, bf16[1,2048,768]{2,1,0:T(8,128)(2,1)S(1)} %copy-done, bf16[1,2048,768]{2,1,0:T(8,128)(2,1)S(1)} %copy-done.1, bf16[1,768,2048]{2,1,0:T(8,128)(2,1)S(1)} %copy-done.2, bf16[64,2176]{1,0:T(8,128)(2,1)} %collective-permute-done.4.refs_4_, ...), custom_call_target="tpu_custom_call" | custom-call | flops 2000000000 | bytes 488281 | tf_op jit(solution)/shard_map/near/pallas_call | solution.py:136
  24.3 0.0 collective-permute-done.7.refs_9_
  24.3 0.0 copy-start.3
  24.4 0.1 collective-permute-start.8
  24.4 0.0 collective-permute-done.9.refs_10_
  24.4 0.5 %collective-permute-start.10 = (bf16[16,2176]{1,0:T(8,128)(2,1)S(1)}, bf16[16,2176]{1,0:T(8,128)(2,1)S(1)}, u32[]{:S(2)}, u32[]{:S(2)}) collective-permute-start(bf16[16,2176]{1,0:T(8,128)(2,1)S(1)} %collective-permute-done.9.refs_10_), channel_id=1, source_target_pairs={{0,1},{1,0},{2,3},{3,2},{4,5},{5,4},{6,7},{7,6},{8,9},{9,8},{10,11... | collective-permute-start | bytes 208904 | tf_op jit(solution)/shard_map/ppermute | solution.py:123
  24.9 0.0 collective-permute-done.11.refs_11_
  24.9 0.1 collective-permute-start.12
  25.0 0.0 collective-permute-done.6.refs_4_
  25.0 0.7 %collective-permute-done.8.refs_5_ = bf16[16,2176]{1,0:T(8,128)(2,1)S(1)} collective-permute-done((bf16[16,2176]{1,0:T(8,128)(2,1)S(1)}, bf16[16,2176]{1,0:T(8,128)(2,1)S(1)}, u32[]{:S(2)}, u32[]{:S(2)}) %collective-permute-start.8) | collective-permute-done | bytes 69664 | tf_op jit(solution)/shard_map/ppermute | solution.py:123
  25.7 0.2 collective-permute-done.10.refs_6_
  25.8 0.4 collective-permute-done.12.refs_7_
  26.2 1.5 %far.1 = (bf16[64,2048]{1,0:T(8,128)(2,1)S(1)}, f32[64,2048]{1,0:T(8,128)S(1)}) custom-call(s32[1]{0:T(128)} %bitcast.refs_0_, bf16[1,2048,768]{2,1,0:T(8,128)(2,1)S(1)} %copy-done, bf16[1,2048,768]{2,1,0:T(8,128)(2,1)S(1)} %copy-done.1, bf16[1,768,2048]{2,1,0:T(8,128)(2,1)S(1)} %copy-done.2, bf16[16,2176]{1,0:T(8,128)(2,1)S(1)} %collective-permute-done.6.refs_4_, ...), custom_call_target="tpu_custom_call" | custom-call | flops 2000000000 | bytes 488281 | tf_op jit(solution)/shard_map/far/pallas_call | solution.py:136
  27.7 0.2 collective-permute-start.13
  28.0 0.4 collective-permute-start.5
  28.3 1.0 %collective-permute-done.13.other_ref = bf16[64,2048]{1,0:T(8,128)(2,1)S(1)} collective-permute-done((bf16[64,2048]{1,0:T(8,128)(2,1)S(1)}, bf16[64,2048]{1,0:T(8,128)(2,1)S(1)}, u32[]{:S(2)}, u32[]{:S(2)}) %collective-permute-start.13) | collective-permute-done | bytes 262176 | tf_op jit(solution)/shard_map/ppermute | solution.py:123
  29.3 0.1 pair.3
  29.4 0.6 %collective-permute-start.17 = (bf16[16,2048]{1,0:T(8,128)(2,1)S(1)}, bf16[16,2048]{1,0:T(8,128)(2,1)S(1)}, u32[]{:S(2)}, u32[]{:S(2)}) collective-permute-start(bf16[16,2048]{1,0:T(8,128)(2,1)S(1)} %get-tuple-element.40), channel_id=1, source_target_pairs={{0,2},{1,3},{2,0},{3,1},{4,6},{5,7},{6,4},{7,5},{8,10},{9,11},{10,... | collective-permute-start | bytes 196616 | tf_op jit(solution)/shard_map/ppermute | solution.py:120
  30.0 0.8 %collective-permute-start.18 = (bf16[16,2048]{1,0:T(8,128)(2,1)S(1)}, bf16[16,2048]{1,0:T(8,128)(2,1)S(1)}, u32[]{:S(2)}, u32[]{:S(2)}) collective-permute-start(bf16[16,2048]{1,0:T(8,128)(2,1)S(1)} %get-tuple-element.41), channel_id=1, source_target_pairs={{0,4},{1,5},{2,6},{3,7},{4,0},{5,1},{6,2},{7,3},{8,12},{9,13},{10,... | collective-permute-start | bytes 196616 | tf_op jit(solution)/shard_map/ppermute | solution.py:120
  30.8 2.2 %collective-permute-start.19 = (bf16[16,2048]{1,0:T(8,128)(2,1)S(1)}, bf16[16,2048]{1,0:T(8,128)(2,1)S(1)}, u32[]{:S(2)}, u32[]{:S(2)}) collective-permute-start(bf16[16,2048]{1,0:T(8,128)(2,1)S(1)} %get-tuple-element.42), channel_id=1, source_target_pairs={{0,6},{1,7},{2,4},{3,5},{4,2},{5,3},{6,0},{7,1},{8,14},{9,15},{10,... | collective-permute-start | bytes 196616 | tf_op jit(solution)/shard_map/ppermute | solution.py:120
  33.0 0.0 collective-permute-done.5.other_ref
  33.0 0.1 pair.2
  33.0 0.6 %collective-permute-start.14 = (bf16[16,2048]{1,0:T(8,128)(2,1)S(1)}, bf16[16,2048]{1,0:T(8,128)(2,1)S(1)}, u32[]{:S(2)}, u32[]{:S(2)}) collective-permute-start(bf16[16,2048]{1,0:T(8,128)(2,1)S(1)} %get-tuple-element.43), channel_id=1, source_target_pairs={{0,2},{1,3},{2,0},{3,1},{4,6},{5,7},{6,4},{7,5},{8,10},{9,11},{10,... | collective-permute-start | bytes 196616 | tf_op jit(solution)/shard_map/ppermute | solution.py:120
  33.6 0.8 %collective-permute-start.15 = (bf16[16,2048]{1,0:T(8,128)(2,1)S(1)}, bf16[16,2048]{1,0:T(8,128)(2,1)S(1)}, u32[]{:S(2)}, u32[]{:S(2)}) collective-permute-start(bf16[16,2048]{1,0:T(8,128)(2,1)S(1)} %get-tuple-element.45), channel_id=1, source_target_pairs={{0,4},{1,5},{2,6},{3,7},{4,0},{5,1},{6,2},{7,3},{8,12},{9,13},{10,... | collective-permute-start | bytes 196616 | tf_op jit(solution)/shard_map/ppermute | solution.py:120
  34.4 0.0 collective-permute-done.17.refs_1_
  34.4 2.2 %collective-permute-start.16 = (bf16[16,2048]{1,0:T(8,128)(2,1)S(1)}, bf16[16,2048]{1,0:T(8,128)(2,1)S(1)}, u32[]{:S(2)}, u32[]{:S(2)}) collective-permute-start(bf16[16,2048]{1,0:T(8,128)(2,1)S(1)} %get-tuple-element.47), channel_id=1, source_target_pairs={{0,6},{1,7},{2,4},{3,5},{4,2},{5,3},{6,0},{7,1},{8,14},{9,15},{10,... | collective-permute-start | bytes 196616 | tf_op jit(solution)/shard_map/ppermute | solution.py:120
  36.6 0.0 collective-permute-done.18.refs_2_
  36.6 0.0 collective-permute-done.19.refs_3_
  36.6 1.5 %collective-permute-start.20 = (bf16[16,2048]{1,0:T(8,128)(2,1)S(1)}, bf16[16,2048]{1,0:T(8,128)(2,1)S(1)}, u32[]{:S(2)}, u32[]{:S(2)}) collective-permute-start(bf16[16,2048]{1,0:T(8,128)(2,1)S(1)} %cross.1), channel_id=1, source_target_pairs={{0,8},{1,9},{2,10},{3,11},{4,12},{5,13},{6,14},{7,15},{8,0},{9,1},... | collective-permute-start | bytes 196616 | tf_op jit(solution)/shard_map/ppermute | solution.py:120
  38.1 0.0 collective-permute-done.14.refs_2_
  38.1 0.0 collective-permute-done.15.refs_3_
  38.1 2.0 %collective-permute-done.16.refs_4_ = bf16[16,2048]{1,0:T(8,128)(2,1)S(1)} collective-permute-done((bf16[16,2048]{1,0:T(8,128)(2,1)S(1)}, bf16[16,2048]{1,0:T(8,128)(2,1)S(1)}, u32[]{:S(2)}, u32[]{:S(2)}) %collective-permute-start.16) | collective-permute-done | bytes 65568 | tf_op jit(solution)/shard_map/ppermute | solution.py:120
  40.1 2.5 %collective-permute-done.20.refs_5_ = bf16[16,2048]{1,0:T(8,128)(2,1)S(1)} collective-permute-done((bf16[16,2048]{1,0:T(8,128)(2,1)S(1)}, bf16[16,2048]{1,0:T(8,128)(2,1)S(1)}, u32[]{:S(2)}, u32[]{:S(2)}) %collective-permute-start.20) | collective-permute-done | bytes 65568 | tf_op jit(solution)/shard_map/ppermute | solution.py:120
  42.6 0.0 copy-done.3
  42.6 0.7 %mix.1 = bf16[16,2048]{1,0:T(8,128)(2,1)} custom-call(bf16[16,2048]{1,0:T(8,128)(2,1)S(1)} %copy-done.3, f32[16,2048]{1,0:T(8,128)S(1)} %get-tuple-element.33.refs_1_, bf16[16,2048]{1,0:T(8,128)(2,1)S(1)} %collective-permute-done.14.refs_2_, bf16[16,2048]{1,0:T(8,128)(2,1)S(1)} %collective-permute-done.15.refs_3_, ...), custom_call_target="tpu_custom_call" | custom-call | tf_op jit(solution)/shard_map/mix/pallas_call | solution.py:155
  (2 shorter events, 0.0 us)
Async XLA Ops:
  0.9 17.1 %copy-start = (bf16[1,2048,768]{2,1,0:T(8,128)(2,1)S(1)}, bf16[1,2048,768]{2,1,0:T(8,128)(2,1)}, u32[]{:S(2)}) copy-start(bf16[1,2048,768]{2,1,0:T(8,128)(2,1)} %refs_1_.3) | copy-start | bytes 9437188
  0.9 7.6 %collective-permute-start = (bf16[16,2176]{1,0:T(8,128)(2,1)S(1)}, bf16[16,2176]{1,0:T(8,128)(2,1)S(1)}, u32[]{:S(2)}, u32[]{:S(2)}) collective-permute-start(bf16[16,2176]{1,0:T(8,128)(2,1)S(1)} %pack.1.refs_0_), channel_id=1, source_target_pairs={{0,8},{1,9},{2,10},{3,11},{4,12},{5,13},{6,14},{7,15},{8,0},{9,1},... | collective-permute-start | bytes 208904 | tf_op jit(solution)/shard_map/ppermute | solution.py:120
  5.0 4.3 %collective-permute-start.1 = (bf16[16,2176]{1,0:T(8,128)(2,1)S(1)}, bf16[16,2176]{1,0:T(8,128)(2,1)S(1)}, u32[]{:S(2)}, u32[]{:S(2)}) collective-permute-start(bf16[16,2176]{1,0:T(8,128)(2,1)S(1)} %again.1.refs_0_.refs_5_), channel_id=1, source_target_pairs={{0,2},{1,3},{2,0},{3,1},{4,6},{5,7},{6,4},{7,5},{8,10},{9,11},{10,... | collective-permute-start | bytes 208904 | tf_op jit(solution)/shard_map/ppermute | solution.py:120
  6.5 4.6 %collective-permute-start.2 = (bf16[16,2176]{1,0:T(8,128)(2,1)S(1)}, bf16[16,2176]{1,0:T(8,128)(2,1)S(1)}, u32[]{:S(2)}, u32[]{:S(2)}) collective-permute-start(bf16[16,2176]{1,0:T(8,128)(2,1)S(1)} %again.1.refs_0_.refs_5_), channel_id=1, source_target_pairs={{0,4},{1,5},{2,6},{3,7},{4,0},{5,1},{6,2},{7,3},{8,12},{9,13},{10,... | collective-permute-start | bytes 208904 | tf_op jit(solution)/shard_map/ppermute | solution.py:120
  8.1 5.2 %collective-permute-start.3 = (bf16[16,2176]{1,0:T(8,128)(2,1)S(1)}, bf16[16,2176]{1,0:T(8,128)(2,1)S(1)}, u32[]{:S(2)}, u32[]{:S(2)}) collective-permute-start(bf16[16,2176]{1,0:T(8,128)(2,1)S(1)} %again.1.refs_0_.refs_5_), channel_id=1, source_target_pairs={{0,6},{1,7},{2,4},{3,5},{4,2},{5,3},{6,0},{7,1},{8,14},{9,15},{10,... | collective-permute-start | bytes 208904 | tf_op jit(solution)/shard_map/ppermute | solution.py:120
  14.0 4.0 %collective-permute-start.4 = (bf16[64,2176]{1,0:T(8,128)(2,1)}, bf16[64,2176]{1,0:T(8,128)(2,1)}, u32[]{:S(2)}, u32[]{:S(2)}) collective-permute-start(bf16[64,2176]{1,0:T(8,128)(2,1)} %join.1), channel_id=1, source_target_pairs={{0,1},{1,0},{2,3},{3,2},{4,5},{5,4},{6,7},{7,6},{8,9},{9,8},{10,11... | collective-permute-start | bytes 835592 | tf_op jit(solution)/shard_map/ppermute | solution.py:123
  14.0 11.0 %collective-permute-start.6 = (bf16[16,2176]{1,0:T(8,128)(2,1)S(1)}, bf16[16,2176]{1,0:T(8,128)(2,1)S(1)}, u32[]{:S(2)}, u32[]{:S(2)}) collective-permute-start(bf16[16,2176]{1,0:T(8,128)(2,1)S(1)} %collective-permute-done.refs_8_), channel_id=1, source_target_pairs={{0,1},{1,0},{2,3},{3,2},{4,5},{5,4},{6,7},{7,6},{8,9},{9,8},{10,11... | collective-permute-start | bytes 208904 | tf_op jit(solution)/shard_map/ppermute | solution.py:123
  14.5 9.8 %collective-permute-start.7 = (bf16[16,2176]{1,0:T(8,128)(2,1)S(1)}, bf16[16,2176]{1,0:T(8,128)(2,1)S(1)}, u32[]{:S(2)}, u32[]{:S(2)}) collective-permute-start(bf16[16,2176]{1,0:T(8,128)(2,1)S(1)} %collective-permute-done.refs_8_), channel_id=1, source_target_pairs={{0,2},{1,3},{2,0},{3,1},{4,6},{5,7},{6,4},{7,5},{8,10},{9,11},{10,... | collective-permute-start | bytes 208904 | tf_op jit(solution)/shard_map/ppermute | solution.py:120
  15.1 9.4 %collective-permute-start.9 = (bf16[16,2176]{1,0:T(8,128)(2,1)S(1)}, bf16[16,2176]{1,0:T(8,128)(2,1)S(1)}, u32[]{:S(2)}, u32[]{:S(2)}) collective-permute-start(bf16[16,2176]{1,0:T(8,128)(2,1)S(1)} %collective-permute-done.refs_8_), channel_id=1, source_target_pairs={{0,4},{1,5},{2,6},{3,7},{4,0},{5,1},{6,2},{7,3},{8,12},{9,13},{10,... | collective-permute-start | bytes 208904 | tf_op jit(solution)/shard_map/ppermute | solution.py:120
  15.9 9.1 %collective-permute-start.11 = (bf16[16,2176]{1,0:T(8,128)(2,1)S(1)}, bf16[16,2176]{1,0:T(8,128)(2,1)S(1)}, u32[]{:S(2)}, u32[]{:S(2)}) collective-permute-start(bf16[16,2176]{1,0:T(8,128)(2,1)S(1)} %collective-permute-done.refs_8_), channel_id=1, source_target_pairs={{0,6},{1,7},{2,4},{3,5},{4,2},{5,3},{6,0},{7,1},{8,14},{9,15},{10,... | collective-permute-start | bytes 208904 | tf_op jit(solution)/shard_map/ppermute | solution.py:120
  18.0 1.9 %copy-start.1 = (bf16[1,2048,768]{2,1,0:T(8,128)(2,1)S(1)}, bf16[1,2048,768]{2,1,0:T(8,128)(2,1)}, u32[]{:S(2)}) copy-start(bf16[1,2048,768]{2,1,0:T(8,128)(2,1)} %refs_2_.3) | copy-start | bytes 9437188
  19.9 1.9 %copy-start.2 = (bf16[1,768,2048]{2,1,0:T(8,128)(2,1)S(1)}, bf16[1,768,2048]{2,1,0:T(8,128)(2,1)}, u32[]{:S(2)}) copy-start(bf16[1,768,2048]{2,1,0:T(8,128)(2,1)} %refs_3_.3) | copy-start | bytes 9437188
  24.3 18.2 %copy-start.3 = (bf16[16,2048]{1,0:T(8,128)(2,1)S(1)}, bf16[16,2048]{1,0:T(8,128)(2,1)}, u32[]{:S(2)}) copy-start(bf16[16,2048]{1,0:T(8,128)(2,1)} %refs_0_.1) | copy-start | bytes 196612
  24.4 1.3 %collective-permute-start.8 = (bf16[16,2176]{1,0:T(8,128)(2,1)S(1)}, bf16[16,2176]{1,0:T(8,128)(2,1)S(1)}, u32[]{:S(2)}, u32[]{:S(2)}) collective-permute-start(bf16[16,2176]{1,0:T(8,128)(2,1)S(1)} %collective-permute-done.7.refs_9_), channel_id=1, source_target_pairs={{0,1},{1,0},{2,3},{3,2},{4,5},{5,4},{6,7},{7,6},{8,9},{9,8},{10,11... | collective-permute-start | bytes 208904 | tf_op jit(solution)/shard_map/ppermute | solution.py:123
  24.4 1.4 %collective-permute-start.10 = (bf16[16,2176]{1,0:T(8,128)(2,1)S(1)}, bf16[16,2176]{1,0:T(8,128)(2,1)S(1)}, u32[]{:S(2)}, u32[]{:S(2)}) collective-permute-start(bf16[16,2176]{1,0:T(8,128)(2,1)S(1)} %collective-permute-done.9.refs_10_), channel_id=1, source_target_pairs={{0,1},{1,0},{2,3},{3,2},{4,5},{5,4},{6,7},{7,6},{8,9},{9,8},{10,11... | collective-permute-start | bytes 208904 | tf_op jit(solution)/shard_map/ppermute | solution.py:123
  24.9 1.3 %collective-permute-start.12 = (bf16[16,2176]{1,0:T(8,128)(2,1)S(1)}, bf16[16,2176]{1,0:T(8,128)(2,1)S(1)}, u32[]{:S(2)}, u32[]{:S(2)}) collective-permute-start(bf16[16,2176]{1,0:T(8,128)(2,1)S(1)} %collective-permute-done.11.refs_11_), channel_id=1, source_target_pairs={{0,1},{1,0},{2,3},{3,2},{4,5},{5,4},{6,7},{7,6},{8,9},{9,8},{10,11... | collective-permute-start | bytes 208904 | tf_op jit(solution)/shard_map/ppermute | solution.py:123
  27.7 1.6 %collective-permute-start.13 = (bf16[64,2048]{1,0:T(8,128)(2,1)S(1)}, bf16[64,2048]{1,0:T(8,128)(2,1)S(1)}, u32[]{:S(2)}, u32[]{:S(2)}) collective-permute-start(bf16[64,2048]{1,0:T(8,128)(2,1)S(1)} %get-tuple-element.39), channel_id=1, source_target_pairs={{0,1},{1,0},{2,3},{3,2},{4,5},{5,4},{6,7},{7,6},{8,9},{9,8},{10,11... | collective-permute-start | bytes 786440 | tf_op jit(solution)/shard_map/ppermute | solution.py:123
  28.0 5.0 %collective-permute-start.5 = (bf16[64,2048]{1,0:T(8,128)(2,1)S(1)}, bf16[64,2048]{1,0:T(8,128)(2,1)S(1)}, u32[]{:S(2)}, u32[]{:S(2)}) collective-permute-start(bf16[64,2048]{1,0:T(8,128)(2,1)S(1)} %get-tuple-element.32), channel_id=1, source_target_pairs={{0,1},{1,0},{2,3},{3,2},{4,5},{5,4},{6,7},{7,6},{8,9},{9,8},{10,11... | collective-permute-start | bytes 786440 | tf_op jit(solution)/shard_map/ppermute | solution.py:123
  29.4 5.0 %collective-permute-start.17 = (bf16[16,2048]{1,0:T(8,128)(2,1)S(1)}, bf16[16,2048]{1,0:T(8,128)(2,1)S(1)}, u32[]{:S(2)}, u32[]{:S(2)}) collective-permute-start(bf16[16,2048]{1,0:T(8,128)(2,1)S(1)} %get-tuple-element.40), channel_id=1, source_target_pairs={{0,2},{1,3},{2,0},{3,1},{4,6},{5,7},{6,4},{7,5},{8,10},{9,11},{10,... | collective-permute-start | bytes 196616 | tf_op jit(solution)/shard_map/ppermute | solution.py:120
  30.0 6.6 %collective-permute-start.18 = (bf16[16,2048]{1,0:T(8,128)(2,1)S(1)}, bf16[16,2048]{1,0:T(8,128)(2,1)S(1)}, u32[]{:S(2)}, u32[]{:S(2)}) collective-permute-start(bf16[16,2048]{1,0:T(8,128)(2,1)S(1)} %get-tuple-element.41), channel_id=1, source_target_pairs={{0,4},{1,5},{2,6},{3,7},{4,0},{5,1},{6,2},{7,3},{8,12},{9,13},{10,... | collective-permute-start | bytes 196616 | tf_op jit(solution)/shard_map/ppermute | solution.py:120
  30.8 5.8 %collective-permute-start.19 = (bf16[16,2048]{1,0:T(8,128)(2,1)S(1)}, bf16[16,2048]{1,0:T(8,128)(2,1)S(1)}, u32[]{:S(2)}, u32[]{:S(2)}) collective-permute-start(bf16[16,2048]{1,0:T(8,128)(2,1)S(1)} %get-tuple-element.42), channel_id=1, source_target_pairs={{0,6},{1,7},{2,4},{3,5},{4,2},{5,3},{6,0},{7,1},{8,14},{9,15},{10,... | collective-permute-start | bytes 196616 | tf_op jit(solution)/shard_map/ppermute | solution.py:120
  33.0 5.1 %collective-permute-start.14 = (bf16[16,2048]{1,0:T(8,128)(2,1)S(1)}, bf16[16,2048]{1,0:T(8,128)(2,1)S(1)}, u32[]{:S(2)}, u32[]{:S(2)}) collective-permute-start(bf16[16,2048]{1,0:T(8,128)(2,1)S(1)} %get-tuple-element.43), channel_id=1, source_target_pairs={{0,2},{1,3},{2,0},{3,1},{4,6},{5,7},{6,4},{7,5},{8,10},{9,11},{10,... | collective-permute-start | bytes 196616 | tf_op jit(solution)/shard_map/ppermute | solution.py:120
  33.6 4.5 %collective-permute-start.15 = (bf16[16,2048]{1,0:T(8,128)(2,1)S(1)}, bf16[16,2048]{1,0:T(8,128)(2,1)S(1)}, u32[]{:S(2)}, u32[]{:S(2)}) collective-permute-start(bf16[16,2048]{1,0:T(8,128)(2,1)S(1)} %get-tuple-element.45), channel_id=1, source_target_pairs={{0,4},{1,5},{2,6},{3,7},{4,0},{5,1},{6,2},{7,3},{8,12},{9,13},{10,... | collective-permute-start | bytes 196616 | tf_op jit(solution)/shard_map/ppermute | solution.py:120
  34.4 5.7 %collective-permute-start.16 = (bf16[16,2048]{1,0:T(8,128)(2,1)S(1)}, bf16[16,2048]{1,0:T(8,128)(2,1)S(1)}, u32[]{:S(2)}, u32[]{:S(2)}) collective-permute-start(bf16[16,2048]{1,0:T(8,128)(2,1)S(1)} %get-tuple-element.47), channel_id=1, source_target_pairs={{0,6},{1,7},{2,4},{3,5},{4,2},{5,3},{6,0},{7,1},{8,14},{9,15},{10,... | collective-permute-start | bytes 196616 | tf_op jit(solution)/shard_map/ppermute | solution.py:120
  36.6 5.9 %collective-permute-start.20 = (bf16[16,2048]{1,0:T(8,128)(2,1)S(1)}, bf16[16,2048]{1,0:T(8,128)(2,1)S(1)}, u32[]{:S(2)}, u32[]{:S(2)}) collective-permute-start(bf16[16,2048]{1,0:T(8,128)(2,1)S(1)} %cross.1), channel_id=1, source_target_pairs={{0,8},{1,9},{2,10},{3,11},{4,12},{5,13},{6,14},{7,15},{8,0},{9,1},... | collective-permute-start | bytes 196616 | tf_op jit(solution)/shard_map/ppermute | solution.py:120

commit v4 on v3

--- a/solution.py
+++ b/solution.py
@@ -7,7 +7,6 @@
 
 LANES = 128
 VMEM = pl.BlockSpec(memory_space=pltpu.VMEM)
-SMEM = pl.BlockSpec(memory_space=pltpu.SMEM)
 HBM = pl.BlockSpec(memory_space=pltpu.HBM)
 
 
@@ -42,8 +41,9 @@
 
 
 def expert_kernel(*refs):
-    slot_ref, gate_ref, up_ref, down_ref = refs[:4]
-    blocks = refs[4:-5]
+    gate_ref, up_ref, down_ref = refs[:3]
+    blocks = refs[3:-5]
+    slot = lax.axis_index("expert")
     away_ref, own_ref, rows_ref, share_ref, hidden_ref = refs[-5:]
     width, hidden_width = gate_ref.shape[1:]
     half = own_ref.shape[0]
@@ -55,7 +55,7 @@
         rows_ref[at, :] = block[:, :width]
         extra = block[:, width:].astype(jnp.float32)
         lane = lax.broadcasted_iota(jnp.int32, extra.shape, 1)
-        chosen = (lane == slot_ref[0]) | (lane == slot_ref[0] + LANES // 2)
+        chosen = (lane == slot) | (lane == slot + LANES // 2)
         share = jnp.sum(jnp.where(chosen, extra, 0.0), axis=1, keepdims=True)
         share_ref[at, :] = jnp.broadcast_to(share, (row_count, LANES))
     rows = rows_ref[...]
@@ -73,10 +73,18 @@
         own_ref[:, n : n + step] = term[half:]
 
 
-def join_kernel(*refs):
+def again_kernel(source_ref, out_ref):
+    out_ref[...] = source_ref[...]
+
+
+def join_kernel(mark_ref, *refs):
     row_count = refs[0].shape[0]
     for b, ref in enumerate(refs[:-1]):
         refs[-1][pl.ds(b * row_count, row_count), :] = ref[...]
+
+
+def mark_kernel(source_ref, out_ref):
+    out_ref[...] = source_ref[:16, :LANES]
 
 
 def pair_kernel(own_ref, other_ref, first_ref, *outs):
@@ -113,7 +121,6 @@
     peer_count = lax.axis_size("expert")
     half = peer_count // 4
     half_rows = half * row_count
-    slot = lax.axis_index("expert").astype(jnp.int32).reshape(1)
     wide, full = jnp.bfloat16, jnp.float32
 
     def partner(array, k):
@@ -128,24 +135,24 @@
     def after(array, *others):
         return lax.optimization_barrier((array, *others))[0]
 
-    def join(blocks):
+    def join(blocks, mark):
         rows = shape(half_rows, wide, width + LANES)
-        return on_core(join_kernel, "join", rows, [VMEM] * half, flops=10**8)(*blocks)
+        return on_core(join_kernel, "join", rows, [VMEM] * (half + 1), flops=10**8)(mark, *blocks)
 
     def experts(name, blocks):
         return on_core(
             expert_kernel,
             name,
             (shape(half_rows, wide), shape(half_rows, full)),
-            [SMEM] + [VMEM] * (3 + len(blocks)),
+            [VMEM] * (3 + len(blocks)),
             (
                 pltpu.VMEM((2 * half_rows, width), wide),
                 pltpu.VMEM((2 * half_rows, LANES), full),
                 pltpu.VMEM((2 * half_rows, hidden_width), wide),
             ),
             limit=16,
-            flops=2 * 10**9,
-        )(slot, w_gate, w_up, w_down, *blocks)
+            flops=10**9,
+        )(w_gate, w_up, w_down, *blocks)
 
     def pair(own, other, dtype):
         outs = (shape(row_count, dtype),) + (shape(row_count, wide),) * (half - 1)
@@ -167,13 +174,15 @@
         flops=10**10,
     )(*map(in_hbm, (tokens, route_weight.T, replica.T)))
     crossed = partner(packed, half)
-    again = on_core(join_kernel, "again", shape(row_count, wide, width + LANES), [VMEM], flops=10**9)(packed)
+    again = on_core(again_kernel, "again", shape(row_count, wide, width + LANES), [VMEM], flops=10**9)(packed)
     near = [again] + [partner(again, k) for k in range(1, half)]
     far = [crossed] + [partner(crossed, k) for k in range(1, half)]
-    near = [after(block, crossed) for block in near]
-    near_away, near_own = experts("near", [swap(join(near))] + near)
+    crossed_other = swap(crossed)
+    mark = on_core(mark_kernel, "mark", shape(16, wide, LANES), [VMEM], flops=10**9)(crossed)
+    near_away, near_own = experts("near", [swap(join(near, mark))] + near)
     far = [crossed] + [after(block, near_away) for block in far[1:]]
-    far_away, far_own = experts("far", [swap(block) for block in far] + far)
+    far_other = [crossed_other] + [swap(block) for block in far[1:]]
+    far_away, far_own = experts("far", far_other + far)
     far_first, *far_sums = pair(far_own, swap(far_away), full)
     near_first, *near_sums = pair(near_own, swap(near_away), full)
     far_back = [partner(block, k) for k, block in enumerate(far_sums, start=1)]

time: 43.5 us -> 40.2 us (0.924)
  local copies, waits for them, and re-layouts: 3.79 us -> 0.02 us
  waiting for transfers between devices: 11.4 us -> 15.1 us
  Pallas kernels: 6.5 us -> 4.87 us
  starting transfers between devices: 21.4 us -> 19.9 us
    unnamed x8, local copies, waits for them, and re-layouts: 3.79 us -> 0.02 us
    ppermute x14, waiting for transfers between devices: 9.23 us -> 12.9 us  [partner(): lax.ppermute(array, 'expert', [(i, i ^ 2 * k) for i in range(peer_count)])]
    ppermute x14, starting transfers between devices: 19.7 us -> 18.5 us  [partner(): lax.ppermute(array, 'expert', [(i, i ^ 2 * k) for i in range(peer_count)])]
    pallas_call x2, Pallas kernels: 4.02 us -> 2.99 us  [experts(): on_core(expert_kernel, name, (shape(half_rows, wide), shape(half_rows, fu...]
    pallas_call x2 -> x3, Pallas kernels: 0.74 us -> 0.03 us  [the longest x1 0.02 us: join(): on_core(join_kernel, 'join', rows, [VMEM] * (half + 1), flops=10 ** 8)]
  transfers between devices with their start and end apart: 21 -> 21, of which waited for: 9 -> 11; matrix products, arithmetic and copies ran while one was open for 0% -> 0% of each run, Pallas kernels for 6% -> 4%
where the time goes in v4:
time: 40.2 us; the launch traced here: 40 us
  starting transfers between devices  19.9 us (50%)
  waiting for transfers between devices  15.1 us (38%)
  Pallas kernels  4.87 us (12%)
    ppermute x14, starting transfers between devices, partner(): lax.ppermute(array, 'expert', [(i, i ^ 2 * k) for i in range(peer_count)])  18.5 us
    ppermute x14, waiting for transfers between devices, partner(): lax.ppermute(array, 'expert', [(i, i ^ 2 * k) for i in range(peer_count)])  12.9 us
    pallas_call x2, Pallas kernels, experts(): on_core(expert_kernel, name, (shape(half_rows, wide), shape(half_rows, fu...  2.99 us
    ppermute x7, waiting for transfers between devices, swap(): lax.ppermute(array, 'expert', [(i, i ^ 1) for i in range(peer_count)])  2.28 us
    ppermute x7, starting transfers between devices, swap(): lax.ppermute(array, 'expert', [(i, i ^ 1) for i in range(peer_count)])  1.31 us
    pallas_call x1, Pallas kernels, dense_shards(): on_core(pack_kernel, 'pack', shape(row_count, wide, width + LANES), [HBM]...  1.05 us
  transfers between devices with their start and end apart: 21, of which 11 were waited for; matrix products, arithmetic and copies ran while one was open for 0% of the time, Pallas kernels for 4%

profile of v4, /device:TPU:0, one launch (start us, length us, event | category | flops | bytes accessed | tf_op | source)
XLA Modules:
  0.0 40.0 jit_solution(18437498304896453898)
XLA Ops:
  0.0 0.0 copy-start.2
  0.0 1.0 %pack.1.source_ref = bf16[16,2176]{1,0:T(8,128)(2,1)S(1)} custom-call(bf16[16,2048]{1,0:T(8,128)(2,1)} %refs_0_.5, f32[8,16]{1,0:T(8,128)} %bitcast.2, s32[8,16]{1,0:T(8,128)} %bitcast.3), custom_call_target="tpu_custom_call" | custom-call | flops 10000000000 | bytes 2441406 | tf_op jit(solution)/shard_map/pack/pallas_call | solution.py:164
  1.1 0.0 copy-start
  1.1 0.0 copy-start.1
  1.1 4.1 %collective-permute-start = (bf16[16,2176]{1,0:T(8,128)(2,1)S(1)}, bf16[16,2176]{1,0:T(8,128)(2,1)S(1)}, u32[]{:S(2)}, u32[]{:S(2)}) collective-permute-start(bf16[16,2176]{1,0:T(8,128)(2,1)S(1)} %pack.1.source_ref), channel_id=1, source_target_pairs={{0,8},{1,9},{2,10},{3,11},{4,12},{5,13},{6,14},{7,15},{8,0},{9,1},... | collective-permute-start | bytes 208904 | tf_op jit(solution)/shard_map/ppermute | solution.py:127
  5.2 1.5 %collective-permute-start.1 = (bf16[16,2176]{1,0:T(8,128)(2,1)S(1)}, bf16[16,2176]{1,0:T(8,128)(2,1)S(1)}, u32[]{:S(2)}, u32[]{:S(2)}) collective-permute-start(bf16[16,2176]{1,0:T(8,128)(2,1)S(1)} %again.1.refs_0_.refs_4_), channel_id=1, source_target_pairs={{0,2},{1,3},{2,0},{3,1},{4,6},{5,7},{6,4},{7,5},{8,10},{9,11},{10,... | collective-permute-start | bytes 208904 | tf_op jit(solution)/shard_map/ppermute | solution.py:127
  6.7 1.6 %collective-permute-start.2 = (bf16[16,2176]{1,0:T(8,128)(2,1)S(1)}, bf16[16,2176]{1,0:T(8,128)(2,1)S(1)}, u32[]{:S(2)}, u32[]{:S(2)}) collective-permute-start(bf16[16,2176]{1,0:T(8,128)(2,1)S(1)} %again.1.refs_0_.refs_4_), channel_id=1, source_target_pairs={{0,4},{1,5},{2,6},{3,7},{4,0},{5,1},{6,2},{7,3},{8,12},{9,13},{10,... | collective-permute-start | bytes 208904 | tf_op jit(solution)/shard_map/ppermute | solution.py:127
  8.3 0.4 %collective-permute-start.3 = (bf16[16,2176]{1,0:T(8,128)(2,1)S(1)}, bf16[16,2176]{1,0:T(8,128)(2,1)S(1)}, u32[]{:S(2)}, u32[]{:S(2)}) collective-permute-start(bf16[16,2176]{1,0:T(8,128)(2,1)S(1)} %again.1.refs_0_.refs_4_), channel_id=1, source_target_pairs={{0,6},{1,7},{2,4},{3,5},{4,2},{5,3},{6,0},{7,1},{8,14},{9,15},{10,... | collective-permute-start | bytes 208904 | tf_op jit(solution)/shard_map/ppermute | solution.py:127
  8.7 0.0 collective-permute-done.source_ref.refs_7_
  8.7 0.8 %collective-permute-done.1.refs_1_.refs_5_ = bf16[16,2176]{1,0:T(8,128)(2,1)S(1)} collective-permute-done((bf16[16,2176]{1,0:T(8,128)(2,1)S(1)}, bf16[16,2176]{1,0:T(8,128)(2,1)S(1)}, u32[]{:S(2)}, u32[]{:S(2)}) %collective-permute-start.1) | collective-permute-done | bytes 69664 | tf_op jit(solution)/shard_map/ppermute | solution.py:127
  9.5 1.8 %collective-permute-done.2.refs_2_.refs_6_ = bf16[16,2176]{1,0:T(8,128)(2,1)S(1)} collective-permute-done((bf16[16,2176]{1,0:T(8,128)(2,1)S(1)}, bf16[16,2176]{1,0:T(8,128)(2,1)S(1)}, u32[]{:S(2)}, u32[]{:S(2)}) %collective-permute-start.2) | collective-permute-done | bytes 69664 | tf_op jit(solution)/shard_map/ppermute | solution.py:127
  11.3 2.2 %collective-permute-done.3.refs_3_.refs_7_ = bf16[16,2176]{1,0:T(8,128)(2,1)S(1)} collective-permute-done((bf16[16,2176]{1,0:T(8,128)(2,1)S(1)}, bf16[16,2176]{1,0:T(8,128)(2,1)S(1)}, u32[]{:S(2)}, u32[]{:S(2)}) %collective-permute-start.3) | collective-permute-done | bytes 69664 | tf_op jit(solution)/shard_map/ppermute | solution.py:127
  13.5 0.1 collective-permute-start.4
  13.6 0.5 %collective-permute-start.6 = (bf16[16,2176]{1,0:T(8,128)(2,1)S(1)}, bf16[16,2176]{1,0:T(8,128)(2,1)S(1)}, u32[]{:S(2)}, u32[]{:S(2)}) collective-permute-start(bf16[16,2176]{1,0:T(8,128)(2,1)S(1)} %collective-permute-done.source_ref.refs_7_), channel_id=1, source_target_pairs={{0,1},{1,0},{2,3},{3,2},{4,5},{5,4},{6,7},{7,6},{8,9},{9,8},{10,11... | collective-permute-start | bytes 208904 | tf_op jit(solution)/shard_map/ppermute | solution.py:130
  14.1 0.5 %collective-permute-start.7 = (bf16[16,2176]{1,0:T(8,128)(2,1)S(1)}, bf16[16,2176]{1,0:T(8,128)(2,1)S(1)}, u32[]{:S(2)}, u32[]{:S(2)}) collective-permute-start(bf16[16,2176]{1,0:T(8,128)(2,1)S(1)} %collective-permute-done.source_ref.refs_7_), channel_id=1, source_target_pairs={{0,2},{1,3},{2,0},{3,1},{4,6},{5,7},{6,4},{7,5},{8,10},{9,11},{10,... | collective-permute-start | bytes 208904 | tf_op jit(solution)/shard_map/ppermute | solution.py:127
  14.6 0.8 %collective-permute-start.9 = (bf16[16,2176]{1,0:T(8,128)(2,1)S(1)}, bf16[16,2176]{1,0:T(8,128)(2,1)S(1)}, u32[]{:S(2)}, u32[]{:S(2)}) collective-permute-start(bf16[16,2176]{1,0:T(8,128)(2,1)S(1)} %collective-permute-done.source_ref.refs_7_), channel_id=1, source_target_pairs={{0,4},{1,5},{2,6},{3,7},{4,0},{5,1},{6,2},{7,3},{8,12},{9,13},{10,... | collective-permute-start | bytes 208904 | tf_op jit(solution)/shard_map/ppermute | solution.py:127
  15.4 2.2 %collective-permute-start.11 = (bf16[16,2176]{1,0:T(8,128)(2,1)S(1)}, bf16[16,2176]{1,0:T(8,128)(2,1)S(1)}, u32[]{:S(2)}, u32[]{:S(2)}) collective-permute-start(bf16[16,2176]{1,0:T(8,128)(2,1)S(1)} %collective-permute-done.source_ref.refs_7_), channel_id=1, source_target_pairs={{0,6},{1,7},{2,4},{3,5},{4,2},{5,3},{6,0},{7,1},{8,14},{9,15},{10,... | collective-permute-start | bytes 208904 | tf_op jit(solution)/shard_map/ppermute | solution.py:127
  17.6 0.0 collective-permute-done.4.refs_3_
  17.6 0.0 copy-done.2
  17.6 0.0 copy-done
  17.6 0.0 copy-done.1
  17.6 1.5 %near.1 = (bf16[64,2048]{1,0:T(8,128)(2,1)S(1)}, f32[64,2048]{1,0:T(8,128)S(1)}) custom-call(bf16[1,2048,768]{2,1,0:T(8,128)(2,1)S(1)} %copy-done, bf16[1,2048,768]{2,1,0:T(8,128)(2,1)S(1)} %copy-done.1, bf16[1,768,2048]{2,1,0:T(8,128)(2,1)S(1)} %copy-done.2, bf16[64,2176]{1,0:T(8,128)(2,1)S(1)} %collective-permute-done.4.refs_3_, ...), custom_call_target="tpu_custom_call" | custom-call | flops 1000000000 | bytes 244140 | tf_op jit(solution)/shard_map/near/pallas_call | solution.py:143
  19.1 0.0 collective-permute-done.7.refs_8_
  19.1 0.0 copy-start.3
  19.1 0.1 collective-permute-start.8
  19.2 0.4 %collective-permute-done.9.refs_9_ = bf16[16,2176]{1,0:T(8,128)(2,1)S(1)} collective-permute-done((bf16[16,2176]{1,0:T(8,128)(2,1)S(1)}, bf16[16,2176]{1,0:T(8,128)(2,1)S(1)}, u32[]{:S(2)}, u32[]{:S(2)}) %collective-permute-start.9) | collective-permute-done | bytes 69664 | tf_op jit(solution)/shard_map/ppermute | solution.py:127
  19.6 0.1 collective-permute-start.10
  19.7 1.2 %collective-permute-done.11.refs_10_ = bf16[16,2176]{1,0:T(8,128)(2,1)S(1)} collective-permute-done((bf16[16,2176]{1,0:T(8,128)(2,1)S(1)}, bf16[16,2176]{1,0:T(8,128)(2,1)S(1)}, u32[]{:S(2)}, u32[]{:S(2)}) %collective-permute-start.11) | collective-permute-done | bytes 69664 | tf_op jit(solution)/shard_map/ppermute | solution.py:127
  20.9 0.0 collective-permute-start.12
  20.9 0.0 collective-permute-done.6.refs_3_
  20.9 0.0 collective-permute-done.8.refs_4_
  20.9 0.0 collective-permute-done.10.refs_5_
  20.9 1.2 %collective-permute-done.12.refs_6_ = bf16[16,2176]{1,0:T(8,128)(2,1)S(1)} collective-permute-done((bf16[16,2176]{1,0:T(8,128)(2,1)S(1)}, bf16[16,2176]{1,0:T(8,128)(2,1)S(1)}, u32[]{:S(2)}, u32[]{:S(2)}) %collective-permute-start.12) | collective-permute-done | bytes 69664 | tf_op jit(solution)/shard_map/ppermute | solution.py:130
  22.2 1.5 %far.1 = (bf16[64,2048]{1,0:T(8,128)(2,1)S(1)}, f32[64,2048]{1,0:T(8,128)S(1)}) custom-call(bf16[1,2048,768]{2,1,0:T(8,128)(2,1)S(1)} %copy-done, bf16[1,2048,768]{2,1,0:T(8,128)(2,1)S(1)} %copy-done.1, bf16[1,768,2048]{2,1,0:T(8,128)(2,1)S(1)} %copy-done.2, bf16[16,2176]{1,0:T(8,128)(2,1)S(1)} %collective-permute-done.6.refs_3_, ...), custom_call_target="tpu_custom_call" | custom-call | flops 1000000000 | bytes 244140 | tf_op jit(solution)/shard_map/far/pallas_call | solution.py:143
  23.7 0.2 collective-permute-start.13
  23.9 0.4 collective-permute-start.5
  24.2 1.0 %collective-permute-done.13.other_ref = bf16[64,2048]{1,0:T(8,128)(2,1)S(1)} collective-permute-done((bf16[64,2048]{1,0:T(8,128)(2,1)S(1)}, bf16[64,2048]{1,0:T(8,128)(2,1)S(1)}, u32[]{:S(2)}, u32[]{:S(2)}) %collective-permute-start.13) | collective-permute-done | bytes 262176 | tf_op jit(solution)/shard_map/ppermute | solution.py:130
  25.3 1.0 %collective-permute-start.17 = (bf16[16,2048]{1,0:T(8,128)(2,1)S(1)}, bf16[16,2048]{1,0:T(8,128)(2,1)S(1)}, u32[]{:S(2)}, u32[]{:S(2)}) collective-permute-start(bf16[16,2048]{1,0:T(8,128)(2,1)S(1)} %get-tuple-element.32), channel_id=1, source_target_pairs={{0,2},{1,3},{2,0},{3,1},{4,6},{5,7},{6,4},{7,5},{8,10},{9,11},{10,... | collective-permute-start | bytes 196616 | tf_op jit(solution)/shard_map/ppermute | solution.py:127
  26.3 1.5 %collective-permute-start.18 = (bf16[16,2048]{1,0:T(8,128)(2,1)S(1)}, bf16[16,2048]{1,0:T(8,128)(2,1)S(1)}, u32[]{:S(2)}, u32[]{:S(2)}) collective-permute-start(bf16[16,2048]{1,0:T(8,128)(2,1)S(1)} %get-tuple-element.33), channel_id=1, source_target_pairs={{0,4},{1,5},{2,6},{3,7},{4,0},{5,1},{6,2},{7,3},{8,12},{9,13},{10,... | collective-permute-start | bytes 196616 | tf_op jit(solution)/shard_map/ppermute | solution.py:127
  27.8 1.1 %collective-permute-start.19 = (bf16[16,2048]{1,0:T(8,128)(2,1)S(1)}, bf16[16,2048]{1,0:T(8,128)(2,1)S(1)}, u32[]{:S(2)}, u32[]{:S(2)}) collective-permute-start(bf16[16,2048]{1,0:T(8,128)(2,1)S(1)} %get-tuple-element.34), channel_id=1, source_target_pairs={{0,6},{1,7},{2,4},{3,5},{4,2},{5,3},{6,0},{7,1},{8,14},{9,15},{10,... | collective-permute-start | bytes 196616 | tf_op jit(solution)/shard_map/ppermute | solution.py:127
  28.9 0.0 collective-permute-done.5.other_ref
  28.9 1.0 %collective-permute-start.14 = (bf16[16,2048]{1,0:T(8,128)(2,1)S(1)}, bf16[16,2048]{1,0:T(8,128)(2,1)S(1)}, u32[]{:S(2)}, u32[]{:S(2)}) collective-permute-start(bf16[16,2048]{1,0:T(8,128)(2,1)S(1)} %get-tuple-element.35), channel_id=1, source_target_pairs={{0,2},{1,3},{2,0},{3,1},{4,6},{5,7},{6,4},{7,5},{8,10},{9,11},{10,... | collective-permute-start | bytes 196616 | tf_op jit(solution)/shard_map/ppermute | solution.py:127
  29.9 1.5 %collective-permute-start.15 = (bf16[16,2048]{1,0:T(8,128)(2,1)S(1)}, bf16[16,2048]{1,0:T(8,128)(2,1)S(1)}, u32[]{:S(2)}, u32[]{:S(2)}) collective-permute-start(bf16[16,2048]{1,0:T(8,128)(2,1)S(1)} %get-tuple-element.37), channel_id=1, source_target_pairs={{0,4},{1,5},{2,6},{3,7},{4,0},{5,1},{6,2},{7,3},{8,12},{9,13},{10,... | collective-permute-start | bytes 196616 | tf_op jit(solution)/shard_map/ppermute | solution.py:127
  31.4 0.0 collective-permute-done.17.refs_1_
  31.4 1.1 %collective-permute-start.16 = (bf16[16,2048]{1,0:T(8,128)(2,1)S(1)}, bf16[16,2048]{1,0:T(8,128)(2,1)S(1)}, u32[]{:S(2)}, u32[]{:S(2)}) collective-permute-start(bf16[16,2048]{1,0:T(8,128)(2,1)S(1)} %get-tuple-element.39), channel_id=1, source_target_pairs={{0,6},{1,7},{2,4},{3,5},{4,2},{5,3},{6,0},{7,1},{8,14},{9,15},{10,... | collective-permute-start | bytes 196616 | tf_op jit(solution)/shard_map/ppermute | solution.py:127
  32.5 0.0 collective-permute-done.18.refs_2_
  32.5 1.0 %collective-permute-done.19.refs_3_ = bf16[16,2048]{1,0:T(8,128)(2,1)S(1)} collective-permute-done((bf16[16,2048]{1,0:T(8,128)(2,1)S(1)}, bf16[16,2048]{1,0:T(8,128)(2,1)S(1)}, u32[]{:S(2)}, u32[]{:S(2)}) %collective-permute-start.19) | collective-permute-done | bytes 65568 | tf_op jit(solution)/shard_map/ppermute | solution.py:127
  33.5 0.4 collective-permute-start.20
  33.9 0.3 collective-permute-done.14.refs_2_
  34.2 0.0 collective-permute-done.15.refs_3_
  34.2 2.8 %collective-permute-done.16.refs_4_ = bf16[16,2048]{1,0:T(8,128)(2,1)S(1)} collective-permute-done((bf16[16,2048]{1,0:T(8,128)(2,1)S(1)}, bf16[16,2048]{1,0:T(8,128)(2,1)S(1)}, u32[]{:S(2)}, u32[]{:S(2)}) %collective-permute-start.16) | collective-permute-done | bytes 65568 | tf_op jit(solution)/shard_map/ppermute | solution.py:127
  37.1 2.3 %collective-permute-done.20.refs_5_ = bf16[16,2048]{1,0:T(8,128)(2,1)S(1)} collective-permute-done((bf16[16,2048]{1,0:T(8,128)(2,1)S(1)}, bf16[16,2048]{1,0:T(8,128)(2,1)S(1)}, u32[]{:S(2)}, u32[]{:S(2)}) %collective-permute-start.20) | collective-permute-done | bytes 65568 | tf_op jit(solution)/shard_map/ppermute | solution.py:127
  39.3 0.0 copy-done.3
  39.3 0.7 %mix.1 = bf16[16,2048]{1,0:T(8,128)(2,1)} custom-call(bf16[16,2048]{1,0:T(8,128)(2,1)S(1)} %copy-done.3, f32[16,2048]{1,0:T(8,128)S(1)} %get-tuple-element.25.refs_1_, bf16[16,2048]{1,0:T(8,128)(2,1)S(1)} %collective-permute-done.14.refs_2_, bf16[16,2048]{1,0:T(8,128)(2,1)S(1)} %collective-permute-done.15.refs_3_, ...), custom_call_target="tpu_custom_call" | custom-call | tf_op jit(solution)/shard_map/mix/pallas_call | solution.py:162
  (6 shorter events, 0.2 us)
Async XLA Ops:
  0.0 17.6 %copy-start.2 = (bf16[1,768,2048]{2,1,0:T(8,128)(2,1)S(1)}, bf16[1,768,2048]{2,1,0:T(8,128)(2,1)}, u32[]{:S(2)}) copy-start(bf16[1,768,2048]{2,1,0:T(8,128)(2,1)} %refs_2_.3) | copy-start | bytes 9437188
  1.1 16.5 %copy-start = (bf16[1,2048,768]{2,1,0:T(8,128)(2,1)S(1)}, bf16[1,2048,768]{2,1,0:T(8,128)(2,1)}, u32[]{:S(2)}) copy-start(bf16[1,2048,768]{2,1,0:T(8,128)(2,1)} %refs_0_.4) | copy-start | bytes 9437188
  1.1 16.5 %copy-start.1 = (bf16[1,2048,768]{2,1,0:T(8,128)(2,1)S(1)}, bf16[1,2048,768]{2,1,0:T(8,128)(2,1)}, u32[]{:S(2)}) copy-start(bf16[1,2048,768]{2,1,0:T(8,128)(2,1)} %refs_1_.3) | copy-start | bytes 9437188
  1.1 7.6 %collective-permute-start = (bf16[16,2176]{1,0:T(8,128)(2,1)S(1)}, bf16[16,2176]{1,0:T(8,128)(2,1)S(1)}, u32[]{:S(2)}, u32[]{:S(2)}) collective-permute-start(bf16[16,2176]{1,0:T(8,128)(2,1)S(1)} %pack.1.source_ref), channel_id=1, source_target_pairs={{0,8},{1,9},{2,10},{3,11},{4,12},{5,13},{6,14},{7,15},{8,0},{9,1},... | collective-permute-start | bytes 208904 | tf_op jit(solution)/shard_map/ppermute | solution.py:127
  5.2 4.3 %collective-permute-start.1 = (bf16[16,2176]{1,0:T(8,128)(2,1)S(1)}, bf16[16,2176]{1,0:T(8,128)(2,1)S(1)}, u32[]{:S(2)}, u32[]{:S(2)}) collective-permute-start(bf16[16,2176]{1,0:T(8,128)(2,1)S(1)} %again.1.refs_0_.refs_4_), channel_id=1, source_target_pairs={{0,2},{1,3},{2,0},{3,1},{4,6},{5,7},{6,4},{7,5},{8,10},{9,11},{10,... | collective-permute-start | bytes 208904 | tf_op jit(solution)/shard_map/ppermute | solution.py:127
  6.7 4.6 %collective-permute-start.2 = (bf16[16,2176]{1,0:T(8,128)(2,1)S(1)}, bf16[16,2176]{1,0:T(8,128)(2,1)S(1)}, u32[]{:S(2)}, u32[]{:S(2)}) collective-permute-start(bf16[16,2176]{1,0:T(8,128)(2,1)S(1)} %again.1.refs_0_.refs_4_), channel_id=1, source_target_pairs={{0,4},{1,5},{2,6},{3,7},{4,0},{5,1},{6,2},{7,3},{8,12},{9,13},{10,... | collective-permute-start | bytes 208904 | tf_op jit(solution)/shard_map/ppermute | solution.py:127
  8.3 5.2 %collective-permute-start.3 = (bf16[16,2176]{1,0:T(8,128)(2,1)S(1)}, bf16[16,2176]{1,0:T(8,128)(2,1)S(1)}, u32[]{:S(2)}, u32[]{:S(2)}) collective-permute-start(bf16[16,2176]{1,0:T(8,128)(2,1)S(1)} %again.1.refs_0_.refs_4_), channel_id=1, source_target_pairs={{0,6},{1,7},{2,4},{3,5},{4,2},{5,3},{6,0},{7,1},{8,14},{9,15},{10,... | collective-permute-start | bytes 208904 | tf_op jit(solution)/shard_map/ppermute | solution.py:127
  13.5 4.1 %collective-permute-start.4 = (bf16[64,2176]{1,0:T(8,128)(2,1)S(1)}, bf16[64,2176]{1,0:T(8,128)(2,1)S(1)}, u32[]{:S(2)}, u32[]{:S(2)}) collective-permute-start(bf16[64,2176]{1,0:T(8,128)(2,1)S(1)} %join.1), channel_id=1, source_target_pairs={{0,1},{1,0},{2,3},{3,2},{4,5},{5,4},{6,7},{7,6},{8,9},{9,8},{10,11... | collective-permute-start | bytes 835592 | tf_op jit(solution)/shard_map/ppermute | solution.py:130
  13.6 7.3 %collective-permute-start.6 = (bf16[16,2176]{1,0:T(8,128)(2,1)S(1)}, bf16[16,2176]{1,0:T(8,128)(2,1)S(1)}, u32[]{:S(2)}, u32[]{:S(2)}) collective-permute-start(bf16[16,2176]{1,0:T(8,128)(2,1)S(1)} %collective-permute-done.source_ref.refs_7_), channel_id=1, source_target_pairs={{0,1},{1,0},{2,3},{3,2},{4,5},{5,4},{6,7},{7,6},{8,9},{9,8},{10,11... | collective-permute-start | bytes 208904 | tf_op jit(solution)/shard_map/ppermute | solution.py:130
  14.1 5.0 %collective-permute-start.7 = (bf16[16,2176]{1,0:T(8,128)(2,1)S(1)}, bf16[16,2176]{1,0:T(8,128)(2,1)S(1)}, u32[]{:S(2)}, u32[]{:S(2)}) collective-permute-start(bf16[16,2176]{1,0:T(8,128)(2,1)S(1)} %collective-permute-done.source_ref.refs_7_), channel_id=1, source_target_pairs={{0,2},{1,3},{2,0},{3,1},{4,6},{5,7},{6,4},{7,5},{8,10},{9,11},{10,... | collective-permute-start | bytes 208904 | tf_op jit(solution)/shard_map/ppermute | solution.py:127
  14.6 5.0 %collective-permute-start.9 = (bf16[16,2176]{1,0:T(8,128)(2,1)S(1)}, bf16[16,2176]{1,0:T(8,128)(2,1)S(1)}, u32[]{:S(2)}, u32[]{:S(2)}) collective-permute-start(bf16[16,2176]{1,0:T(8,128)(2,1)S(1)} %collective-permute-done.source_ref.refs_7_), channel_id=1, source_target_pairs={{0,4},{1,5},{2,6},{3,7},{4,0},{5,1},{6,2},{7,3},{8,12},{9,13},{10,... | collective-permute-start | bytes 208904 | tf_op jit(solution)/shard_map/ppermute | solution.py:127
  15.4 5.5 %collective-permute-start.11 = (bf16[16,2176]{1,0:T(8,128)(2,1)S(1)}, bf16[16,2176]{1,0:T(8,128)(2,1)S(1)}, u32[]{:S(2)}, u32[]{:S(2)}) collective-permute-start(bf16[16,2176]{1,0:T(8,128)(2,1)S(1)} %collective-permute-done.source_ref.refs_7_), channel_id=1, source_target_pairs={{0,6},{1,7},{2,4},{3,5},{4,2},{5,3},{6,0},{7,1},{8,14},{9,15},{10,... | collective-permute-start | bytes 208904 | tf_op jit(solution)/shard_map/ppermute | solution.py:127
  19.1 20.2 %copy-start.3 = (bf16[16,2048]{1,0:T(8,128)(2,1)S(1)}, bf16[16,2048]{1,0:T(8,128)(2,1)}, u32[]{:S(2)}) copy-start(bf16[16,2048]{1,0:T(8,128)(2,1)} %refs_0_.5) | copy-start | bytes 196612
  19.1 1.8 %collective-permute-start.8 = (bf16[16,2176]{1,0:T(8,128)(2,1)S(1)}, bf16[16,2176]{1,0:T(8,128)(2,1)S(1)}, u32[]{:S(2)}, u32[]{:S(2)}) collective-permute-start(bf16[16,2176]{1,0:T(8,128)(2,1)S(1)} %collective-permute-done.7.refs_8_), channel_id=1, source_target_pairs={{0,1},{1,0},{2,3},{3,2},{4,5},{5,4},{6,7},{7,6},{8,9},{9,8},{10,11... | collective-permute-start | bytes 208904 | tf_op jit(solution)/shard_map/ppermute | solution.py:130
  19.6 1.3 %collective-permute-start.10 = (bf16[16,2176]{1,0:T(8,128)(2,1)S(1)}, bf16[16,2176]{1,0:T(8,128)(2,1)S(1)}, u32[]{:S(2)}, u32[]{:S(2)}) collective-permute-start(bf16[16,2176]{1,0:T(8,128)(2,1)S(1)} %collective-permute-done.9.refs_9_), channel_id=1, source_target_pairs={{0,1},{1,0},{2,3},{3,2},{4,5},{5,4},{6,7},{7,6},{8,9},{9,8},{10,11... | collective-permute-start | bytes 208904 | tf_op jit(solution)/shard_map/ppermute | solution.py:130
  20.9 1.3 %collective-permute-start.12 = (bf16[16,2176]{1,0:T(8,128)(2,1)S(1)}, bf16[16,2176]{1,0:T(8,128)(2,1)S(1)}, u32[]{:S(2)}, u32[]{:S(2)}) collective-permute-start(bf16[16,2176]{1,0:T(8,128)(2,1)S(1)} %collective-permute-done.11.refs_10_), channel_id=1, source_target_pairs={{0,1},{1,0},{2,3},{3,2},{4,5},{5,4},{6,7},{7,6},{8,9},{9,8},{10,11... | collective-permute-start | bytes 208904 | tf_op jit(solution)/shard_map/ppermute | solution.py:130
  23.7 1.6 %collective-permute-start.13 = (bf16[64,2048]{1,0:T(8,128)(2,1)S(1)}, bf16[64,2048]{1,0:T(8,128)(2,1)S(1)}, u32[]{:S(2)}, u32[]{:S(2)}) collective-permute-start(bf16[64,2048]{1,0:T(8,128)(2,1)S(1)} %get-tuple-element.31), channel_id=1, source_target_pairs={{0,1},{1,0},{2,3},{3,2},{4,5},{5,4},{6,7},{7,6},{8,9},{9,8},{10,11... | collective-permute-start | bytes 786440 | tf_op jit(solution)/shard_map/ppermute | solution.py:130
  23.9 5.0 %collective-permute-start.5 = (bf16[64,2048]{1,0:T(8,128)(2,1)S(1)}, bf16[64,2048]{1,0:T(8,128)(2,1)S(1)}, u32[]{:S(2)}, u32[]{:S(2)}) collective-permute-start(bf16[64,2048]{1,0:T(8,128)(2,1)S(1)} %get-tuple-element.24), channel_id=1, source_target_pairs={{0,1},{1,0},{2,3},{3,2},{4,5},{5,4},{6,7},{7,6},{8,9},{9,8},{10,11... | collective-permute-start | bytes 786440 | tf_op jit(solution)/shard_map/ppermute | solution.py:130
  25.3 6.1 %collective-permute-start.17 = (bf16[16,2048]{1,0:T(8,128)(2,1)S(1)}, bf16[16,2048]{1,0:T(8,128)(2,1)S(1)}, u32[]{:S(2)}, u32[]{:S(2)}) collective-permute-start(bf16[16,2048]{1,0:T(8,128)(2,1)S(1)} %get-tuple-element.32), channel_id=1, source_target_pairs={{0,2},{1,3},{2,0},{3,1},{4,6},{5,7},{6,4},{7,5},{8,10},{9,11},{10,... | collective-permute-start | bytes 196616 | tf_op jit(solution)/shard_map/ppermute | solution.py:127
  26.3 6.2 %collective-permute-start.18 = (bf16[16,2048]{1,0:T(8,128)(2,1)S(1)}, bf16[16,2048]{1,0:T(8,128)(2,1)S(1)}, u32[]{:S(2)}, u32[]{:S(2)}) collective-permute-start(bf16[16,2048]{1,0:T(8,128)(2,1)S(1)} %get-tuple-element.33), channel_id=1, source_target_pairs={{0,4},{1,5},{2,6},{3,7},{4,0},{5,1},{6,2},{7,3},{8,12},{9,13},{10,... | collective-permute-start | bytes 196616 | tf_op jit(solution)/shard_map/ppermute | solution.py:127
  27.8 5.7 %collective-permute-start.19 = (bf16[16,2048]{1,0:T(8,128)(2,1)S(1)}, bf16[16,2048]{1,0:T(8,128)(2,1)S(1)}, u32[]{:S(2)}, u32[]{:S(2)}) collective-permute-start(bf16[16,2048]{1,0:T(8,128)(2,1)S(1)} %get-tuple-element.34), channel_id=1, source_target_pairs={{0,6},{1,7},{2,4},{3,5},{4,2},{5,3},{6,0},{7,1},{8,14},{9,15},{10,... | collective-permute-start | bytes 196616 | tf_op jit(solution)/shard_map/ppermute | solution.py:127
  28.9 5.3 %collective-permute-start.14 = (bf16[16,2048]{1,0:T(8,128)(2,1)S(1)}, bf16[16,2048]{1,0:T(8,128)(2,1)S(1)}, u32[]{:S(2)}, u32[]{:S(2)}) collective-permute-start(bf16[16,2048]{1,0:T(8,128)(2,1)S(1)} %get-tuple-element.35), channel_id=1, source_target_pairs={{0,2},{1,3},{2,0},{3,1},{4,6},{5,7},{6,4},{7,5},{8,10},{9,11},{10,... | collective-permute-start | bytes 196616 | tf_op jit(solution)/shard_map/ppermute | solution.py:127
  29.9 4.3 %collective-permute-start.15 = (bf16[16,2048]{1,0:T(8,128)(2,1)S(1)}, bf16[16,2048]{1,0:T(8,128)(2,1)S(1)}, u32[]{:S(2)}, u32[]{:S(2)}) collective-permute-start(bf16[16,2048]{1,0:T(8,128)(2,1)S(1)} %get-tuple-element.37), channel_id=1, source_target_pairs={{0,4},{1,5},{2,6},{3,7},{4,0},{5,1},{6,2},{7,3},{8,12},{9,13},{10,... | collective-permute-start | bytes 196616 | tf_op jit(solution)/shard_map/ppermute | solution.py:127
  31.4 5.6 %collective-permute-start.16 = (bf16[16,2048]{1,0:T(8,128)(2,1)S(1)}, bf16[16,2048]{1,0:T(8,128)(2,1)S(1)}, u32[]{:S(2)}, u32[]{:S(2)}) collective-permute-start(bf16[16,2048]{1,0:T(8,128)(2,1)S(1)} %get-tuple-element.39), channel_id=1, source_target_pairs={{0,6},{1,7},{2,4},{3,5},{4,2},{5,3},{6,0},{7,1},{8,14},{9,15},{10,... | collective-permute-start | bytes 196616 | tf_op jit(solution)/shard_map/ppermute | solution.py:127
  33.5 5.8 %collective-permute-start.20 = (bf16[16,2048]{1,0:T(8,128)(2,1)S(1)}, bf16[16,2048]{1,0:T(8,128)(2,1)S(1)}, u32[]{:S(2)}, u32[]{:S(2)}) collective-permute-start(bf16[16,2048]{1,0:T(8,128)(2,1)S(1)} %cross.1), channel_id=1, source_target_pairs={{0,8},{1,9},{2,10},{3,11},{4,12},{5,13},{6,14},{7,15},{8,0},{9,1},... | collective-permute-start | bytes 196616 | tf_op jit(solution)/shard_map/ppermute | solution.py:127

commit v5 on v4

--- a/solution.py
+++ b/solution.py
@@ -1,3 +1,4 @@
+import functools
 import jax
 import jax.numpy as jnp
 from jax import lax
@@ -40,9 +41,9 @@
     copies[2].wait()
 
 
-def expert_kernel(*refs):
+def expert_kernel(block_count, *refs):
     gate_ref, up_ref, down_ref = refs[:3]
-    blocks = refs[3:-5]
+    blocks = refs[3 : 3 + block_count]
     slot = lax.axis_index("expert")
     away_ref, own_ref, rows_ref, share_ref, hidden_ref = refs[-5:]
     width, hidden_width = gate_ref.shape[1:]
@@ -77,14 +78,10 @@
     out_ref[...] = source_ref[...]
 
 
-def join_kernel(mark_ref, *refs):
+def join_kernel(*refs):
     row_count = refs[0].shape[0]
-    for b, ref in enumerate(refs[:-1]):
+    for b, ref in enumerate(refs[: refs[-1].shape[0] // row_count]):
         refs[-1][pl.ds(b * row_count, row_count), :] = ref[...]
-
-
-def mark_kernel(source_ref, out_ref):
-    out_ref[...] = source_ref[:16, :LANES]
 
 
 def pair_kernel(own_ref, other_ref, first_ref, *outs):
@@ -135,16 +132,17 @@
     def after(array, *others):
         return lax.optimization_barrier((array, *others))[0]
 
-    def join(blocks, mark):
+    def join(blocks, marks):
         rows = shape(half_rows, wide, width + LANES)
-        return on_core(join_kernel, "join", rows, [VMEM] * (half + 1), flops=10**8)(mark, *blocks)
-
-    def experts(name, blocks):
+        refs = (*blocks, *marks)
+        return on_core(join_kernel, "join", rows, [VMEM] * len(refs), flops=10**8)(*refs)
+
+    def experts(name, blocks, marks=()):
         return on_core(
-            expert_kernel,
+            functools.partial(expert_kernel, len(blocks)),
             name,
             (shape(half_rows, wide), shape(half_rows, full)),
-            [VMEM] * (3 + len(blocks)),
+            [VMEM] * (3 + len(blocks) + len(marks)),
             (
                 pltpu.VMEM((2 * half_rows, width), wide),
                 pltpu.VMEM((2 * half_rows, LANES), full),
@@ -152,7 +150,7 @@
             ),
             limit=16,
             flops=10**9,
-        )(w_gate, w_up, w_down, *blocks)
+        )(w_gate, w_up, w_down, *blocks, *marks)
 
     def pair(own, other, dtype):
         outs = (shape(row_count, dtype),) + (shape(row_count, wide),) * (half - 1)
@@ -178,9 +176,8 @@
     near = [again] + [partner(again, k) for k in range(1, half)]
     far = [crossed] + [partner(crossed, k) for k in range(1, half)]
     crossed_other = swap(crossed)
-    mark = on_core(mark_kernel, "mark", shape(16, wide, LANES), [VMEM], flops=10**9)(crossed)
-    near_away, near_own = experts("near", [swap(join(near, mark))] + near)
-    far = [crossed] + [after(block, near_away) for block in far[1:]]
+    near_other = [swap(block) for block in near]
+    near_away, near_own = experts("near", near_other + near, far[1:4])
     far_other = [crossed_other] + [swap(block) for block in far[1:]]
     far_away, far_own = experts("far", far_other + far)
     far_first, *far_sums = pair(far_own, swap(far_away), full)

time: 40.2 us -> 37.4 us (0.930)
  waiting for transfers between devices: 15.1 us -> 7.06 us
  starting transfers between devices: 19.9 us -> 25.1 us
    ppermute x14, waiting for transfers between devices: 12.9 us -> 7.04 us  [partner(): lax.ppermute(array, 'expert', [(i, i ^ 2 * k) for i in range(peer_count)])]
    ppermute x14, starting transfers between devices: 18.5 us -> 22.9 us  [partner(): lax.ppermute(array, 'expert', [(i, i ^ 2 * k) for i in range(peer_count)])]
    ppermute x7 -> x10, waiting for transfers between devices: 2.28 us -> 0.03 us  [swap(): lax.ppermute(array, 'expert', [(i, i ^ 1) for i in range(peer_count)])]
    ppermute x7 -> x10, starting transfers between devices: 1.31 us -> 2.18 us  [swap(): lax.ppermute(array, 'expert', [(i, i ^ 1) for i in range(peer_count)])]
    pallas_call x4 -> x2, Pallas kernels: 3.01 us -> 3.08 us  [experts(): on_core(functools.partial(expert_kernel, len(blocks)), name, (shape(half_...]
  transfers between devices with their start and end apart: 21 -> 24, of which waited for: 11 -> 7; matrix products, arithmetic and copies ran while one was open for 0% -> 0% of each run, Pallas kernels for 4% -> 9%
where the time goes in v5:
time: 37.4 us; the launch traced here: 37.2 us
  starting transfers between devices  25.1 us (67%)
  waiting for transfers between devices  7.06 us (19%)
  Pallas kernels  4.97 us (13%)
    ppermute x14, starting transfers between devices, partner(): lax.ppermute(array, 'expert', [(i, i ^ 2 * k) for i in range(peer_count)])  22.9 us
    ppermute x14, waiting for transfers between devices, partner(): lax.ppermute(array, 'expert', [(i, i ^ 2 * k) for i in range(peer_count)])  7.04 us
    pallas_call x2, Pallas kernels, experts(): on_core(functools.partial(expert_kernel, len(blocks)), name, (shape(half_...  3.08 us
    ppermute x10, starting transfers between devices, swap(): lax.ppermute(array, 'expert', [(i, i ^ 1) for i in range(peer_count)])  2.18 us
    pallas_call x1, Pallas kernels, dense_shards(): on_core(pack_kernel, 'pack', shape(row_count, wide, width + LANES), [HBM]...  1.05 us
  transfers between devices with their start and end apart: 24, of which 7 were waited for; matrix products, arithmetic and copies ran while one was open for 0% of the time, Pallas kernels for 9%

profile of v5, /device:TPU:0, one launch (start us, length us, event | category | flops | bytes accessed | tf_op | source)
XLA Modules:
  0.0 37.2 jit_solution(10249537172183327564)
XLA Ops:
  0.0 0.0 copy-start.1
  0.0 0.0 copy-start.2
  0.0 1.0 %pack.1.source_ref = bf16[16,2176]{1,0:T(8,128)(2,1)S(1)} custom-call(bf16[16,2048]{1,0:T(8,128)(2,1)} %refs_0_.5, f32[8,16]{1,0:T(8,128)} %bitcast.2, s32[8,16]{1,0:T(8,128)} %bitcast.3), custom_call_target="tpu_custom_call" | custom-call | flops 10000000000 | bytes 2441406 | tf_op jit(solution)/shard_map/pack/pallas_call | solution.py:162
  1.1 0.0 copy-start
  1.1 4.1 %collective-permute-start.7 = (bf16[16,2176]{1,0:T(8,128)(2,1)S(1)}, bf16[16,2176]{1,0:T(8,128)(2,1)S(1)}, u32[]{:S(2)}, u32[]{:S(2)}) collective-permute-start(bf16[16,2176]{1,0:T(8,128)(2,1)S(1)} %pack.1.source_ref), channel_id=1, source_target_pairs={{0,8},{1,9},{2,10},{3,11},{4,12},{5,13},{6,14},{7,15},{8,0},{9,1},... | collective-permute-start | bytes 208904 | tf_op jit(solution)/shard_map/ppermute | solution.py:124
  5.2 1.5 %collective-permute-start.1 = (bf16[16,2176]{1,0:T(8,128)(2,1)S(1)}, bf16[16,2176]{1,0:T(8,128)(2,1)S(1)}, u32[]{:S(2)}, u32[]{:S(2)}) collective-permute-start(bf16[16,2176]{1,0:T(8,128)(2,1)S(1)} %again.1.refs_7_), channel_id=1, source_target_pairs={{0,2},{1,3},{2,0},{3,1},{4,6},{5,7},{6,4},{7,5},{8,10},{9,11},{10,... | collective-permute-start | bytes 208904 | tf_op jit(solution)/shard_map/ppermute | solution.py:124
  6.7 1.6 %collective-permute-start.3 = (bf16[16,2176]{1,0:T(8,128)(2,1)S(1)}, bf16[16,2176]{1,0:T(8,128)(2,1)S(1)}, u32[]{:S(2)}, u32[]{:S(2)}) collective-permute-start(bf16[16,2176]{1,0:T(8,128)(2,1)S(1)} %again.1.refs_7_), channel_id=1, source_target_pairs={{0,4},{1,5},{2,6},{3,7},{4,0},{5,1},{6,2},{7,3},{8,12},{9,13},{10,... | collective-permute-start | bytes 208904 | tf_op jit(solution)/shard_map/ppermute | solution.py:124
  8.2 0.4 %collective-permute-done.7.refs_7_ = bf16[16,2176]{1,0:T(8,128)(2,1)S(1)} collective-permute-done((bf16[16,2176]{1,0:T(8,128)(2,1)S(1)}, bf16[16,2176]{1,0:T(8,128)(2,1)S(1)}, u32[]{:S(2)}, u32[]{:S(2)}) %collective-permute-start.7) | collective-permute-done | bytes 69664 | tf_op jit(solution)/shard_map/ppermute | solution.py:124
  8.6 1.6 %collective-permute-start.8 = (bf16[16,2176]{1,0:T(8,128)(2,1)S(1)}, bf16[16,2176]{1,0:T(8,128)(2,1)S(1)}, u32[]{:S(2)}, u32[]{:S(2)}) collective-permute-start(bf16[16,2176]{1,0:T(8,128)(2,1)S(1)} %collective-permute-done.7.refs_7_), channel_id=1, source_target_pairs={{0,2},{1,3},{2,0},{3,1},{4,6},{5,7},{6,4},{7,5},{8,10},{9,11},{10,... | collective-permute-start | bytes 208904 | tf_op jit(solution)/shard_map/ppermute | solution.py:124
  10.2 1.0 %collective-permute-start.9 = (bf16[16,2176]{1,0:T(8,128)(2,1)S(1)}, bf16[16,2176]{1,0:T(8,128)(2,1)S(1)}, u32[]{:S(2)}, u32[]{:S(2)}) collective-permute-start(bf16[16,2176]{1,0:T(8,128)(2,1)S(1)} %collective-permute-done.7.refs_7_), channel_id=1, source_target_pairs={{0,4},{1,5},{2,6},{3,7},{4,0},{5,1},{6,2},{7,3},{8,12},{9,13},{10,... | collective-permute-start | bytes 208904 | tf_op jit(solution)/shard_map/ppermute | solution.py:124
  11.2 0.9 %collective-permute-start.10 = (bf16[16,2176]{1,0:T(8,128)(2,1)S(1)}, bf16[16,2176]{1,0:T(8,128)(2,1)S(1)}, u32[]{:S(2)}, u32[]{:S(2)}) collective-permute-start(bf16[16,2176]{1,0:T(8,128)(2,1)S(1)} %collective-permute-done.7.refs_7_), channel_id=1, source_target_pairs={{0,6},{1,7},{2,4},{3,5},{4,2},{5,3},{6,0},{7,1},{8,14},{9,15},{10,... | collective-permute-start | bytes 208904 | tf_op jit(solution)/shard_map/ppermute | solution.py:124
  12.1 0.0 collective-permute-done.1.refs_8_
  12.1 2.0 %collective-permute-start.5 = (bf16[16,2176]{1,0:T(8,128)(2,1)S(1)}, bf16[16,2176]{1,0:T(8,128)(2,1)S(1)}, u32[]{:S(2)}, u32[]{:S(2)}) collective-permute-start(bf16[16,2176]{1,0:T(8,128)(2,1)S(1)} %again.1.refs_7_), channel_id=1, source_target_pairs={{0,6},{1,7},{2,4},{3,5},{4,2},{5,3},{6,0},{7,1},{8,14},{9,15},{10,... | collective-permute-start | bytes 208904 | tf_op jit(solution)/shard_map/ppermute | solution.py:124
  14.1 0.0 collective-permute-done.3.refs_9_
  14.2 0.0 collective-permute-start.12
  14.2 0.0 collective-permute-done.8.refs_11_.refs_8_
  14.2 0.5 %collective-permute-start.13 = (bf16[16,2176]{1,0:T(8,128)(2,1)S(1)}, bf16[16,2176]{1,0:T(8,128)(2,1)S(1)}, u32[]{:S(2)}, u32[]{:S(2)}) collective-permute-start(bf16[16,2176]{1,0:T(8,128)(2,1)S(1)} %collective-permute-done.8.refs_11_.refs_8_), channel_id=1, source_target_pairs={{0,1},{1,0},{2,3},{3,2},{4,5},{5,4},{6,7},{7,6},{8,9},{9,8},{10,11... | collective-permute-start | bytes 208904 | tf_op jit(solution)/shard_map/ppermute | solution.py:127
  14.7 0.3 collective-permute-done.9.refs_12_.refs_9_
  15.0 0.0 collective-permute-start.14
  15.0 1.5 %collective-permute-done.10.refs_13_.refs_10_ = bf16[16,2176]{1,0:T(8,128)(2,1)S(1)} collective-permute-done((bf16[16,2176]{1,0:T(8,128)(2,1)S(1)}, bf16[16,2176]{1,0:T(8,128)(2,1)S(1)}, u32[]{:S(2)}, u32[]{:S(2)}) %collective-permute-start.10) | collective-permute-done | bytes 69664 | tf_op jit(solution)/shard_map/ppermute | solution.py:124
  16.5 0.0 collective-permute-start.15
  16.5 0.9 %collective-permute-done.5.refs_10_ = bf16[16,2176]{1,0:T(8,128)(2,1)S(1)} collective-permute-done((bf16[16,2176]{1,0:T(8,128)(2,1)S(1)}, bf16[16,2176]{1,0:T(8,128)(2,1)S(1)}, u32[]{:S(2)}, u32[]{:S(2)}) %collective-permute-start.5) | collective-permute-done | bytes 69664 | tf_op jit(solution)/shard_map/ppermute | solution.py:124
  17.3 0.0 collective-permute-start
  17.3 0.0 collective-permute-done.12.refs_3_
  17.4 0.5 %collective-permute-start.2 = (bf16[16,2176]{1,0:T(8,128)(2,1)S(1)}, bf16[16,2176]{1,0:T(8,128)(2,1)S(1)}, u32[]{:S(2)}, u32[]{:S(2)}) collective-permute-start(bf16[16,2176]{1,0:T(8,128)(2,1)S(1)} %collective-permute-done.1.refs_8_), channel_id=1, source_target_pairs={{0,1},{1,0},{2,3},{3,2},{4,5},{5,4},{6,7},{7,6},{8,9},{9,8},{10,11... | collective-permute-start | bytes 208904 | tf_op jit(solution)/shard_map/ppermute | solution.py:127
  17.9 0.0 collective-permute-done.13.refs_4_
  17.9 0.1 collective-permute-start.4
  17.9 0.0 collective-permute-done.14.refs_5_
  17.9 0.4 %collective-permute-start.6 = (bf16[16,2176]{1,0:T(8,128)(2,1)S(1)}, bf16[16,2176]{1,0:T(8,128)(2,1)S(1)}, u32[]{:S(2)}, u32[]{:S(2)}) collective-permute-start(bf16[16,2176]{1,0:T(8,128)(2,1)S(1)} %collective-permute-done.5.refs_10_), channel_id=1, source_target_pairs={{0,1},{1,0},{2,3},{3,2},{4,5},{5,4},{6,7},{7,6},{8,9},{9,8},{10,11... | collective-permute-start | bytes 208904 | tf_op jit(solution)/shard_map/ppermute | solution.py:127
  18.4 0.0 collective-permute-done.15.refs_6_
  18.4 0.0 copy-done.1
  18.4 0.0 copy-done.2
  18.4 0.0 copy-done
  18.4 1.5 %far.1 = (bf16[64,2048]{1,0:T(8,128)(2,1)S(1)}, f32[64,2048]{1,0:T(8,128)S(1)}) custom-call(bf16[1,2048,768]{2,1,0:T(8,128)(2,1)S(1)} %copy-done, bf16[1,2048,768]{2,1,0:T(8,128)(2,1)S(1)} %copy-done.1, bf16[1,768,2048]{2,1,0:T(8,128)(2,1)S(1)} %copy-done.2, bf16[16,2176]{1,0:T(8,128)(2,1)S(1)} %collective-permute-done.12.refs_3_, ...), custom_call_target="tpu_custom_call" | custom-call | flops 1000000000 | bytes 244140 | tf_op jit(solution)/shard_map/far/pallas_call | solution.py:141
  20.0 0.0 copy-start.3
  20.0 0.1 collective-permute-start.16
  20.1 0.0 collective-permute-done.refs_3_
  20.1 0.0 collective-permute-done.2.refs_4_
  20.1 0.0 collective-permute-done.4.refs_5_
  20.1 0.0 collective-permute-done.6.refs_6_
  20.1 1.5 %near.1 = (bf16[64,2048]{1,0:T(8,128)(2,1)S(1)}, f32[64,2048]{1,0:T(8,128)S(1)}) custom-call(bf16[1,2048,768]{2,1,0:T(8,128)(2,1)S(1)} %copy-done, bf16[1,2048,768]{2,1,0:T(8,128)(2,1)S(1)} %copy-done.1, bf16[1,768,2048]{2,1,0:T(8,128)(2,1)S(1)} %copy-done.2, bf16[16,2176]{1,0:T(8,128)(2,1)S(1)} %collective-permute-done.refs_3_, ...), custom_call_target="tpu_custom_call" | custom-call | flops 1000000000 | bytes 244140 | tf_op jit(solution)/shard_map/near/pallas_call | solution.py:141
  21.7 0.5 %collective-permute-start.11 = (bf16[64,2048]{1,0:T(8,128)(2,1)S(1)}, bf16[64,2048]{1,0:T(8,128)(2,1)S(1)}, u32[]{:S(2)}, u32[]{:S(2)}) collective-permute-start(bf16[64,2048]{1,0:T(8,128)(2,1)S(1)} %get-tuple-element.21), channel_id=1, source_target_pairs={{0,1},{1,0},{2,3},{3,2},{4,5},{5,4},{6,7},{7,6},{8,9},{9,8},{10,11... | collective-permute-start | bytes 786440 | tf_op jit(solution)/shard_map/ppermute | solution.py:127
  22.2 0.0 collective-permute-done.16.other_ref
  22.2 0.1 pair.3
  22.2 1.7 %collective-permute-start.20 = (bf16[16,2048]{1,0:T(8,128)(2,1)S(1)}, bf16[16,2048]{1,0:T(8,128)(2,1)S(1)}, u32[]{:S(2)}, u32[]{:S(2)}) collective-permute-start(bf16[16,2048]{1,0:T(8,128)(2,1)S(1)} %get-tuple-element.26), channel_id=1, source_target_pairs={{0,2},{1,3},{2,0},{3,1},{4,6},{5,7},{6,4},{7,5},{8,10},{9,11},{10,... | collective-permute-start | bytes 196616 | tf_op jit(solution)/shard_map/ppermute | solution.py:124
  23.9 1.0 %collective-permute-start.21 = (bf16[16,2048]{1,0:T(8,128)(2,1)S(1)}, bf16[16,2048]{1,0:T(8,128)(2,1)S(1)}, u32[]{:S(2)}, u32[]{:S(2)}) collective-permute-start(bf16[16,2048]{1,0:T(8,128)(2,1)S(1)} %get-tuple-element.27), channel_id=1, source_target_pairs={{0,4},{1,5},{2,6},{3,7},{4,0},{5,1},{6,2},{7,3},{8,12},{9,13},{10,... | collective-permute-start | bytes 196616 | tf_op jit(solution)/shard_map/ppermute | solution.py:124
  24.9 0.9 %collective-permute-start.22 = (bf16[16,2048]{1,0:T(8,128)(2,1)S(1)}, bf16[16,2048]{1,0:T(8,128)(2,1)S(1)}, u32[]{:S(2)}, u32[]{:S(2)}) collective-permute-start(bf16[16,2048]{1,0:T(8,128)(2,1)S(1)} %get-tuple-element.28), channel_id=1, source_target_pairs={{0,6},{1,7},{2,4},{3,5},{4,2},{5,3},{6,0},{7,1},{8,14},{9,15},{10,... | collective-permute-start | bytes 196616 | tf_op jit(solution)/shard_map/ppermute | solution.py:124
  25.8 0.0 collective-permute-done.11.other_ref
  25.8 0.1 pair.2
  25.9 1.7 %collective-permute-start.17 = (bf16[16,2048]{1,0:T(8,128)(2,1)S(1)}, bf16[16,2048]{1,0:T(8,128)(2,1)S(1)}, u32[]{:S(2)}, u32[]{:S(2)}) collective-permute-start(bf16[16,2048]{1,0:T(8,128)(2,1)S(1)} %get-tuple-element.29), channel_id=1, source_target_pairs={{0,2},{1,3},{2,0},{3,1},{4,6},{5,7},{6,4},{7,5},{8,10},{9,11},{10,... | collective-permute-start | bytes 196616 | tf_op jit(solution)/shard_map/ppermute | solution.py:124
  27.5 1.0 %collective-permute-start.18 = (bf16[16,2048]{1,0:T(8,128)(2,1)S(1)}, bf16[16,2048]{1,0:T(8,128)(2,1)S(1)}, u32[]{:S(2)}, u32[]{:S(2)}) collective-permute-start(bf16[16,2048]{1,0:T(8,128)(2,1)S(1)} %get-tuple-element.31), channel_id=1, source_target_pairs={{0,4},{1,5},{2,6},{3,7},{4,0},{5,1},{6,2},{7,3},{8,12},{9,13},{10,... | collective-permute-start | bytes 196616 | tf_op jit(solution)/shard_map/ppermute | solution.py:124
  28.5 0.0 collective-permute-done.20.refs_1_
  28.5 0.9 %collective-permute-start.19 = (bf16[16,2048]{1,0:T(8,128)(2,1)S(1)}, bf16[16,2048]{1,0:T(8,128)(2,1)S(1)}, u32[]{:S(2)}, u32[]{:S(2)}) collective-permute-start(bf16[16,2048]{1,0:T(8,128)(2,1)S(1)} %get-tuple-element.33), channel_id=1, source_target_pairs={{0,6},{1,7},{2,4},{3,5},{4,2},{5,3},{6,0},{7,1},{8,14},{9,15},{10,... | collective-permute-start | bytes 196616 | tf_op jit(solution)/shard_map/ppermute | solution.py:124
  29.4 0.0 collective-permute-done.21.refs_2_
  29.4 1.0 %collective-permute-done.22.refs_3_ = bf16[16,2048]{1,0:T(8,128)(2,1)S(1)} collective-permute-done((bf16[16,2048]{1,0:T(8,128)(2,1)S(1)}, bf16[16,2048]{1,0:T(8,128)(2,1)S(1)}, u32[]{:S(2)}, u32[]{:S(2)}) %collective-permute-start.22) | collective-permute-done | bytes 65568 | tf_op jit(solution)/shard_map/ppermute | solution.py:124
  30.5 3.1 %collective-permute-start.23 = (bf16[16,2048]{1,0:T(8,128)(2,1)S(1)}, bf16[16,2048]{1,0:T(8,128)(2,1)S(1)}, u32[]{:S(2)}, u32[]{:S(2)}) collective-permute-start(bf16[16,2048]{1,0:T(8,128)(2,1)S(1)} %cross.1), channel_id=1, source_target_pairs={{0,8},{1,9},{2,10},{3,11},{4,12},{5,13},{6,14},{7,15},{8,0},{9,1},... | collective-permute-start | bytes 196616 | tf_op jit(solution)/shard_map/ppermute | solution.py:124
  33.6 0.0 collective-permute-done.17.refs_2_
  33.6 0.0 collective-permute-done.18.refs_3_
  33.6 0.7 %collective-permute-done.19.refs_4_ = bf16[16,2048]{1,0:T(8,128)(2,1)S(1)} collective-permute-done((bf16[16,2048]{1,0:T(8,128)(2,1)S(1)}, bf16[16,2048]{1,0:T(8,128)(2,1)S(1)}, u32[]{:S(2)}, u32[]{:S(2)}) %collective-permute-start.19) | collective-permute-done | bytes 65568 | tf_op jit(solution)/shard_map/ppermute | solution.py:124
  34.4 2.2 %collective-permute-done.23.refs_5_ = bf16[16,2048]{1,0:T(8,128)(2,1)S(1)} collective-permute-done((bf16[16,2048]{1,0:T(8,128)(2,1)S(1)}, bf16[16,2048]{1,0:T(8,128)(2,1)S(1)}, u32[]{:S(2)}, u32[]{:S(2)}) %collective-permute-start.23) | collective-permute-done | bytes 65568 | tf_op jit(solution)/shard_map/ppermute | solution.py:124
  36.6 0.0 copy-done.3
  36.6 0.7 %mix.1 = bf16[16,2048]{1,0:T(8,128)(2,1)} custom-call(bf16[16,2048]{1,0:T(8,128)(2,1)S(1)} %copy-done.3, f32[16,2048]{1,0:T(8,128)S(1)} %get-tuple-element.22.refs_1_, bf16[16,2048]{1,0:T(8,128)(2,1)S(1)} %collective-permute-done.17.refs_2_, bf16[16,2048]{1,0:T(8,128)(2,1)S(1)} %collective-permute-done.18.refs_3_, ...), custom_call_target="tpu_custom_call" | custom-call | tf_op jit(solution)/shard_map/mix/pallas_call | solution.py:160
  (2 shorter events, 0.0 us)
Async XLA Ops:
  0.0 18.4 %copy-start.1 = (bf16[1,2048,768]{2,1,0:T(8,128)(2,1)S(1)}, bf16[1,2048,768]{2,1,0:T(8,128)(2,1)}, u32[]{:S(2)}) copy-start(bf16[1,2048,768]{2,1,0:T(8,128)(2,1)} %refs_1_.3) | copy-start | bytes 9437188
  0.0 18.4 %copy-start.2 = (bf16[1,768,2048]{2,1,0:T(8,128)(2,1)S(1)}, bf16[1,768,2048]{2,1,0:T(8,128)(2,1)}, u32[]{:S(2)}) copy-start(bf16[1,768,2048]{2,1,0:T(8,128)(2,1)} %refs_2_.3) | copy-start | bytes 9437188
  1.1 17.3 %copy-start = (bf16[1,2048,768]{2,1,0:T(8,128)(2,1)S(1)}, bf16[1,2048,768]{2,1,0:T(8,128)(2,1)}, u32[]{:S(2)}) copy-start(bf16[1,2048,768]{2,1,0:T(8,128)(2,1)} %refs_0_.4) | copy-start | bytes 9437188
  1.1 7.6 %collective-permute-start.7 = (bf16[16,2176]{1,0:T(8,128)(2,1)S(1)}, bf16[16,2176]{1,0:T(8,128)(2,1)S(1)}, u32[]{:S(2)}, u32[]{:S(2)}) collective-permute-start(bf16[16,2176]{1,0:T(8,128)(2,1)S(1)} %pack.1.source_ref), channel_id=1, source_target_pairs={{0,8},{1,9},{2,10},{3,11},{4,12},{5,13},{6,14},{7,15},{8,0},{9,1},... | collective-permute-start | bytes 208904 | tf_op jit(solution)/shard_map/ppermute | solution.py:124
  5.2 7.0 %collective-permute-start.1 = (bf16[16,2176]{1,0:T(8,128)(2,1)S(1)}, bf16[16,2176]{1,0:T(8,128)(2,1)S(1)}, u32[]{:S(2)}, u32[]{:S(2)}) collective-permute-start(bf16[16,2176]{1,0:T(8,128)(2,1)S(1)} %again.1.refs_7_), channel_id=1, source_target_pairs={{0,2},{1,3},{2,0},{3,1},{4,6},{5,7},{6,4},{7,5},{8,10},{9,11},{10,... | collective-permute-start | bytes 208904 | tf_op jit(solution)/shard_map/ppermute | solution.py:124
  6.7 7.5 %collective-permute-start.3 = (bf16[16,2176]{1,0:T(8,128)(2,1)S(1)}, bf16[16,2176]{1,0:T(8,128)(2,1)S(1)}, u32[]{:S(2)}, u32[]{:S(2)}) collective-permute-start(bf16[16,2176]{1,0:T(8,128)(2,1)S(1)} %again.1.refs_7_), channel_id=1, source_target_pairs={{0,4},{1,5},{2,6},{3,7},{4,0},{5,1},{6,2},{7,3},{8,12},{9,13},{10,... | collective-permute-start | bytes 208904 | tf_op jit(solution)/shard_map/ppermute | solution.py:124
  8.6 5.5 %collective-permute-start.8 = (bf16[16,2176]{1,0:T(8,128)(2,1)S(1)}, bf16[16,2176]{1,0:T(8,128)(2,1)S(1)}, u32[]{:S(2)}, u32[]{:S(2)}) collective-permute-start(bf16[16,2176]{1,0:T(8,128)(2,1)S(1)} %collective-permute-done.7.refs_7_), channel_id=1, source_target_pairs={{0,2},{1,3},{2,0},{3,1},{4,6},{5,7},{6,4},{7,5},{8,10},{9,11},{10,... | collective-permute-start | bytes 208904 | tf_op jit(solution)/shard_map/ppermute | solution.py:124
  10.2 4.7 %collective-permute-start.9 = (bf16[16,2176]{1,0:T(8,128)(2,1)S(1)}, bf16[16,2176]{1,0:T(8,128)(2,1)S(1)}, u32[]{:S(2)}, u32[]{:S(2)}) collective-permute-start(bf16[16,2176]{1,0:T(8,128)(2,1)S(1)} %collective-permute-done.7.refs_7_), channel_id=1, source_target_pairs={{0,4},{1,5},{2,6},{3,7},{4,0},{5,1},{6,2},{7,3},{8,12},{9,13},{10,... | collective-permute-start | bytes 208904 | tf_op jit(solution)/shard_map/ppermute | solution.py:124
  11.2 5.3 %collective-permute-start.10 = (bf16[16,2176]{1,0:T(8,128)(2,1)S(1)}, bf16[16,2176]{1,0:T(8,128)(2,1)S(1)}, u32[]{:S(2)}, u32[]{:S(2)}) collective-permute-start(bf16[16,2176]{1,0:T(8,128)(2,1)S(1)} %collective-permute-done.7.refs_7_), channel_id=1, source_target_pairs={{0,6},{1,7},{2,4},{3,5},{4,2},{5,3},{6,0},{7,1},{8,14},{9,15},{10,... | collective-permute-start | bytes 208904 | tf_op jit(solution)/shard_map/ppermute | solution.py:124
  12.1 5.2 %collective-permute-start.5 = (bf16[16,2176]{1,0:T(8,128)(2,1)S(1)}, bf16[16,2176]{1,0:T(8,128)(2,1)S(1)}, u32[]{:S(2)}, u32[]{:S(2)}) collective-permute-start(bf16[16,2176]{1,0:T(8,128)(2,1)S(1)} %again.1.refs_7_), channel_id=1, source_target_pairs={{0,6},{1,7},{2,4},{3,5},{4,2},{5,3},{6,0},{7,1},{8,14},{9,15},{10,... | collective-permute-start | bytes 208904 | tf_op jit(solution)/shard_map/ppermute | solution.py:124
  14.2 3.2 %collective-permute-start.12 = (bf16[16,2176]{1,0:T(8,128)(2,1)S(1)}, bf16[16,2176]{1,0:T(8,128)(2,1)S(1)}, u32[]{:S(2)}, u32[]{:S(2)}) collective-permute-start(bf16[16,2176]{1,0:T(8,128)(2,1)S(1)} %collective-permute-done.7.refs_7_), channel_id=1, source_target_pairs={{0,1},{1,0},{2,3},{3,2},{4,5},{5,4},{6,7},{7,6},{8,9},{9,8},{10,11... | collective-permute-start | bytes 208904 | tf_op jit(solution)/shard_map/ppermute | solution.py:127
  14.2 3.7 %collective-permute-start.13 = (bf16[16,2176]{1,0:T(8,128)(2,1)S(1)}, bf16[16,2176]{1,0:T(8,128)(2,1)S(1)}, u32[]{:S(2)}, u32[]{:S(2)}) collective-permute-start(bf16[16,2176]{1,0:T(8,128)(2,1)S(1)} %collective-permute-done.8.refs_11_.refs_8_), channel_id=1, source_target_pairs={{0,1},{1,0},{2,3},{3,2},{4,5},{5,4},{6,7},{7,6},{8,9},{9,8},{10,11... | collective-permute-start | bytes 208904 | tf_op jit(solution)/shard_map/ppermute | solution.py:127
  15.0 2.9 %collective-permute-start.14 = (bf16[16,2176]{1,0:T(8,128)(2,1)S(1)}, bf16[16,2176]{1,0:T(8,128)(2,1)S(1)}, u32[]{:S(2)}, u32[]{:S(2)}) collective-permute-start(bf16[16,2176]{1,0:T(8,128)(2,1)S(1)} %collective-permute-done.9.refs_12_.refs_9_), channel_id=1, source_target_pairs={{0,1},{1,0},{2,3},{3,2},{4,5},{5,4},{6,7},{7,6},{8,9},{9,8},{10,11... | collective-permute-start | bytes 208904 | tf_op jit(solution)/shard_map/ppermute | solution.py:127
  16.5 1.9 %collective-permute-start.15 = (bf16[16,2176]{1,0:T(8,128)(2,1)S(1)}, bf16[16,2176]{1,0:T(8,128)(2,1)S(1)}, u32[]{:S(2)}, u32[]{:S(2)}) collective-permute-start(bf16[16,2176]{1,0:T(8,128)(2,1)S(1)} %collective-permute-done.10.refs_13_.refs_10_), channel_id=1, source_target_pairs={{0,1},{1,0},{2,3},{3,2},{4,5},{5,4},{6,7},{7,6},{8,9},{9,8},{10,11... | collective-permute-start | bytes 208904 | tf_op jit(solution)/shard_map/ppermute | solution.py:127
  17.3 2.8 %collective-permute-start = (bf16[16,2176]{1,0:T(8,128)(2,1)S(1)}, bf16[16,2176]{1,0:T(8,128)(2,1)S(1)}, u32[]{:S(2)}, u32[]{:S(2)}) collective-permute-start(bf16[16,2176]{1,0:T(8,128)(2,1)S(1)} %again.1.refs_7_), channel_id=1, source_target_pairs={{0,1},{1,0},{2,3},{3,2},{4,5},{5,4},{6,7},{7,6},{8,9},{9,8},{10,11... | collective-permute-start | bytes 208904 | tf_op jit(solution)/shard_map/ppermute | solution.py:127
  17.4 2.8 %collective-permute-start.2 = (bf16[16,2176]{1,0:T(8,128)(2,1)S(1)}, bf16[16,2176]{1,0:T(8,128)(2,1)S(1)}, u32[]{:S(2)}, u32[]{:S(2)}) collective-permute-start(bf16[16,2176]{1,0:T(8,128)(2,1)S(1)} %collective-permute-done.1.refs_8_), channel_id=1, source_target_pairs={{0,1},{1,0},{2,3},{3,2},{4,5},{5,4},{6,7},{7,6},{8,9},{9,8},{10,11... | collective-permute-start | bytes 208904 | tf_op jit(solution)/shard_map/ppermute | solution.py:127
  17.9 2.2 %collective-permute-start.4 = (bf16[16,2176]{1,0:T(8,128)(2,1)S(1)}, bf16[16,2176]{1,0:T(8,128)(2,1)S(1)}, u32[]{:S(2)}, u32[]{:S(2)}) collective-permute-start(bf16[16,2176]{1,0:T(8,128)(2,1)S(1)} %collective-permute-done.3.refs_9_), channel_id=1, source_target_pairs={{0,1},{1,0},{2,3},{3,2},{4,5},{5,4},{6,7},{7,6},{8,9},{9,8},{10,11... | collective-permute-start | bytes 208904 | tf_op jit(solution)/shard_map/ppermute | solution.py:127
  17.9 2.2 %collective-permute-start.6 = (bf16[16,2176]{1,0:T(8,128)(2,1)S(1)}, bf16[16,2176]{1,0:T(8,128)(2,1)S(1)}, u32[]{:S(2)}, u32[]{:S(2)}) collective-permute-start(bf16[16,2176]{1,0:T(8,128)(2,1)S(1)} %collective-permute-done.5.refs_10_), channel_id=1, source_target_pairs={{0,1},{1,0},{2,3},{3,2},{4,5},{5,4},{6,7},{7,6},{8,9},{9,8},{10,11... | collective-permute-start | bytes 208904 | tf_op jit(solution)/shard_map/ppermute | solution.py:127
  20.0 16.6 %copy-start.3 = (bf16[16,2048]{1,0:T(8,128)(2,1)S(1)}, bf16[16,2048]{1,0:T(8,128)(2,1)}, u32[]{:S(2)}) copy-start(bf16[16,2048]{1,0:T(8,128)(2,1)} %refs_0_.5) | copy-start | bytes 196612
  20.0 2.2 %collective-permute-start.16 = (bf16[64,2048]{1,0:T(8,128)(2,1)S(1)}, bf16[64,2048]{1,0:T(8,128)(2,1)S(1)}, u32[]{:S(2)}, u32[]{:S(2)}) collective-permute-start(bf16[64,2048]{1,0:T(8,128)(2,1)S(1)} %get-tuple-element.25), channel_id=1, source_target_pairs={{0,1},{1,0},{2,3},{3,2},{4,5},{5,4},{6,7},{7,6},{8,9},{9,8},{10,11... | collective-permute-start | bytes 786440 | tf_op jit(solution)/shard_map/ppermute | solution.py:127
  21.7 4.1 %collective-permute-start.11 = (bf16[64,2048]{1,0:T(8,128)(2,1)S(1)}, bf16[64,2048]{1,0:T(8,128)(2,1)S(1)}, u32[]{:S(2)}, u32[]{:S(2)}) collective-permute-start(bf16[64,2048]{1,0:T(8,128)(2,1)S(1)} %get-tuple-element.21), channel_id=1, source_target_pairs={{0,1},{1,0},{2,3},{3,2},{4,5},{5,4},{6,7},{7,6},{8,9},{9,8},{10,11... | collective-permute-start | bytes 786440 | tf_op jit(solution)/shard_map/ppermute | solution.py:127
  22.2 6.3 %collective-permute-start.20 = (bf16[16,2048]{1,0:T(8,128)(2,1)S(1)}, bf16[16,2048]{1,0:T(8,128)(2,1)S(1)}, u32[]{:S(2)}, u32[]{:S(2)}) collective-permute-start(bf16[16,2048]{1,0:T(8,128)(2,1)S(1)} %get-tuple-element.26), channel_id=1, source_target_pairs={{0,2},{1,3},{2,0},{3,1},{4,6},{5,7},{6,4},{7,5},{8,10},{9,11},{10,... | collective-permute-start | bytes 196616 | tf_op jit(solution)/shard_map/ppermute | solution.py:124
  23.9 5.5 %collective-permute-start.21 = (bf16[16,2048]{1,0:T(8,128)(2,1)S(1)}, bf16[16,2048]{1,0:T(8,128)(2,1)S(1)}, u32[]{:S(2)}, u32[]{:S(2)}) collective-permute-start(bf16[16,2048]{1,0:T(8,128)(2,1)S(1)} %get-tuple-element.27), channel_id=1, source_target_pairs={{0,4},{1,5},{2,6},{3,7},{4,0},{5,1},{6,2},{7,3},{8,12},{9,13},{10,... | collective-permute-start | bytes 196616 | tf_op jit(solution)/shard_map/ppermute | solution.py:124
  24.9 5.6 %collective-permute-start.22 = (bf16[16,2048]{1,0:T(8,128)(2,1)S(1)}, bf16[16,2048]{1,0:T(8,128)(2,1)S(1)}, u32[]{:S(2)}, u32[]{:S(2)}) collective-permute-start(bf16[16,2048]{1,0:T(8,128)(2,1)S(1)} %get-tuple-element.28), channel_id=1, source_target_pairs={{0,6},{1,7},{2,4},{3,5},{4,2},{5,3},{6,0},{7,1},{8,14},{9,15},{10,... | collective-permute-start | bytes 196616 | tf_op jit(solution)/shard_map/ppermute | solution.py:124
  25.9 7.8 %collective-permute-start.17 = (bf16[16,2048]{1,0:T(8,128)(2,1)S(1)}, bf16[16,2048]{1,0:T(8,128)(2,1)S(1)}, u32[]{:S(2)}, u32[]{:S(2)}) collective-permute-start(bf16[16,2048]{1,0:T(8,128)(2,1)S(1)} %get-tuple-element.29), channel_id=1, source_target_pairs={{0,2},{1,3},{2,0},{3,1},{4,6},{5,7},{6,4},{7,5},{8,10},{9,11},{10,... | collective-permute-start | bytes 196616 | tf_op jit(solution)/shard_map/ppermute | solution.py:124
  27.5 6.1 %collective-permute-start.18 = (bf16[16,2048]{1,0:T(8,128)(2,1)S(1)}, bf16[16,2048]{1,0:T(8,128)(2,1)S(1)}, u32[]{:S(2)}, u32[]{:S(2)}) collective-permute-start(bf16[16,2048]{1,0:T(8,128)(2,1)S(1)} %get-tuple-element.31), channel_id=1, source_target_pairs={{0,4},{1,5},{2,6},{3,7},{4,0},{5,1},{6,2},{7,3},{8,12},{9,13},{10,... | collective-permute-start | bytes 196616 | tf_op jit(solution)/shard_map/ppermute | solution.py:124
  28.5 5.8 %collective-permute-start.19 = (bf16[16,2048]{1,0:T(8,128)(2,1)S(1)}, bf16[16,2048]{1,0:T(8,128)(2,1)S(1)}, u32[]{:S(2)}, u32[]{:S(2)}) collective-permute-start(bf16[16,2048]{1,0:T(8,128)(2,1)S(1)} %get-tuple-element.33), channel_id=1, source_target_pairs={{0,6},{1,7},{2,4},{3,5},{4,2},{5,3},{6,0},{7,1},{8,14},{9,15},{10,... | collective-permute-start | bytes 196616 | tf_op jit(solution)/shard_map/ppermute | solution.py:124
  30.5 6.1 %collective-permute-start.23 = (bf16[16,2048]{1,0:T(8,128)(2,1)S(1)}, bf16[16,2048]{1,0:T(8,128)(2,1)S(1)}, u32[]{:S(2)}, u32[]{:S(2)}) collective-permute-start(bf16[16,2048]{1,0:T(8,128)(2,1)S(1)} %cross.1), channel_id=1, source_target_pairs={{0,8},{1,9},{2,10},{3,11},{4,12},{5,13},{6,14},{7,15},{8,0},{9,1},... | collective-permute-start | bytes 196616 | tf_op jit(solution)/shard_map/ppermute | solution.py:124

commit v6 on v5

--- a/solution.py
+++ b/solution.py
@@ -78,12 +78,6 @@
     out_ref[...] = source_ref[...]
 
 
-def join_kernel(*refs):
-    row_count = refs[0].shape[0]
-    for b, ref in enumerate(refs[: refs[-1].shape[0] // row_count]):
-        refs[-1][pl.ds(b * row_count, row_count), :] = ref[...]
-
-
 def pair_kernel(own_ref, other_ref, first_ref, *outs):
     row_count = first_ref.shape[0]
     for k, out in enumerate((first_ref,) + outs):
@@ -128,14 +122,6 @@
 
     def shape(rows, dtype, columns=width):
         return jax.ShapeDtypeStruct((rows, columns), dtype)
-
-    def after(array, *others):
-        return lax.optimization_barrier((array, *others))[0]
-
-    def join(blocks, marks):
-        rows = shape(half_rows, wide, width + LANES)
-        refs = (*blocks, *marks)
-        return on_core(join_kernel, "join", rows, [VMEM] * len(refs), flops=10**8)(*refs)
 
     def experts(name, blocks, marks=()):
         return on_core(
@@ -173,18 +159,18 @@
     )(*map(in_hbm, (tokens, route_weight.T, replica.T)))
     crossed = partner(packed, half)
     again = on_core(again_kernel, "again", shape(row_count, wide, width + LANES), [VMEM], flops=10**9)(packed)
-    near = [again] + [partner(again, k) for k in range(1, half)]
-    far = [crossed] + [partner(crossed, k) for k in range(1, half)]
+    order = range(half - 1, 0, -1)
+    near = [again] + [partner(again, k) for k in order]
+    far = [crossed] + [partner(crossed, k) for k in order]
     crossed_other = swap(crossed)
     near_other = [swap(block) for block in near]
-    near_away, near_own = experts("near", near_other + near, far[1:4])
+    near_away, near_own = experts("near", near_other + near, far[1:])
     far_other = [crossed_other] + [swap(block) for block in far[1:]]
     far_away, far_own = experts("far", far_other + far)
     far_first, *far_sums = pair(far_own, swap(far_away), full)
     near_first, *near_sums = pair(near_own, swap(near_away), full)
-    far_back = [partner(block, k) for k, block in enumerate(far_sums, start=1)]
-    near_sums = [after(block, *far_sums) for block in near_sums]
-    near_back = [partner(block, k) for k, block in enumerate(near_sums, start=1)]
+    far_back = [partner(block, k) for block, k in zip(far_sums, order)]
+    near_back = [partner(block, k) for block, k in zip(near_sums, order)]
     crossing = partner(total("cross", far_first, *far_back), half)
     return total("mix", tokens, near_first, *near_back, crossing)
 

time: 37.4 us -> 35.6 us (0.952)
  starting transfers between devices: 25.1 us -> 23.3 us
    ppermute x14, starting transfers between devices: 22.9 us -> 21.6 us  [partner(): lax.ppermute(array, 'expert', [(i, i ^ 2 * k) for i in range(peer_count)])]
    ppermute x10, starting transfers between devices: 2.18 us -> 1.67 us  [swap(): lax.ppermute(array, 'expert', [(i, i ^ 1) for i in range(peer_count)])]
  transfers between devices with their start and end apart: 24 -> 24, of which waited for: 7 -> 8; matrix products, arithmetic and copies ran while one was open for 0% -> 0% of each run, Pallas kernels for 9% -> 9%
where the time goes in v6:
time: 35.6 us; the launch traced here: 35.4 us
  starting transfers between devices  23.3 us (65%)
  waiting for transfers between devices  7.04 us (20%)
  Pallas kernels  4.98 us (14%)
    ppermute x14, starting transfers between devices, partner(): lax.ppermute(array, 'expert', [(i, i ^ 2 * k) for i in range(peer_count)])  21.6 us
    ppermute x14, waiting for transfers between devices, partner(): lax.ppermute(array, 'expert', [(i, i ^ 2 * k) for i in range(peer_count)])  7.01 us
    pallas_call x2, Pallas kernels, experts(): on_core(functools.partial(expert_kernel, len(blocks)), name, (shape(half_...  3.09 us
    ppermute x10, starting transfers between devices, swap(): lax.ppermute(array, 'expert', [(i, i ^ 1) for i in range(peer_count)])  1.67 us
    pallas_call x1, Pallas kernels, dense_shards(): on_core(pack_kernel, 'pack', shape(row_count, wide, width + LANES), [HBM]...  1.05 us
    pallas_call x2, Pallas kernels, total(): on_core(sum_kernel, name, shape(row_count, wide), [VMEM] * len(terms))  0.72 us
  transfers between devices with their start and end apart: 24, of which 8 were waited for; matrix products, arithmetic and copies ran while one was open for 0% of the time, Pallas kernels for 9%

profile of v6, /device:TPU:0, one launch (start us, length us, event | category | flops | bytes accessed | tf_op | source)
XLA Modules:
  0.0 35.4 jit_solution(14105906883110195427)
XLA Ops:
  0.0 0.0 copy-start.1
  0.0 0.0 copy-start.2
  0.0 1.0 %pack.1.source_ref = bf16[16,2176]{1,0:T(8,128)(2,1)S(1)} custom-call(bf16[16,2048]{1,0:T(8,128)(2,1)} %refs_0_.5, f32[8,16]{1,0:T(8,128)} %bitcast.2, s32[8,16]{1,0:T(8,128)} %bitcast.3), custom_call_target="tpu_custom_call" | custom-call | flops 10000000000 | bytes 2441406 | tf_op jit(solution)/shard_map/pack/pallas_call | solution.py:148
  1.1 0.0 copy-start
  1.1 4.1 %collective-permute-start.7 = (bf16[16,2176]{1,0:T(8,128)(2,1)S(1)}, bf16[16,2176]{1,0:T(8,128)(2,1)S(1)}, u32[]{:S(2)}, u32[]{:S(2)}) collective-permute-start(bf16[16,2176]{1,0:T(8,128)(2,1)S(1)} %pack.1.source_ref), channel_id=1, source_target_pairs={{0,8},{1,9},{2,10},{3,11},{4,12},{5,13},{6,14},{7,15},{8,0},{9,1},... | collective-permute-start | bytes 208904 | tf_op jit(solution)/shard_map/ppermute | solution.py:118
  5.2 2.5 %collective-permute-start.1 = (bf16[16,2176]{1,0:T(8,128)(2,1)S(1)}, bf16[16,2176]{1,0:T(8,128)(2,1)S(1)}, u32[]{:S(2)}, u32[]{:S(2)}) collective-permute-start(bf16[16,2176]{1,0:T(8,128)(2,1)S(1)} %again.1.refs_7_), channel_id=1, source_target_pairs={{0,6},{1,7},{2,4},{3,5},{4,2},{5,3},{6,0},{7,1},{8,14},{9,15},{10,... | collective-permute-start | bytes 208904 | tf_op jit(solution)/shard_map/ppermute | solution.py:118
  7.7 0.4 %collective-permute-start.3 = (bf16[16,2176]{1,0:T(8,128)(2,1)S(1)}, bf16[16,2176]{1,0:T(8,128)(2,1)S(1)}, u32[]{:S(2)}, u32[]{:S(2)}) collective-permute-start(bf16[16,2176]{1,0:T(8,128)(2,1)S(1)} %again.1.refs_7_), channel_id=1, source_target_pairs={{0,4},{1,5},{2,6},{3,7},{4,0},{5,1},{6,2},{7,3},{8,12},{9,13},{10,... | collective-permute-start | bytes 208904 | tf_op jit(solution)/shard_map/ppermute | solution.py:118
  8.1 0.2 collective-permute-done.7.refs_7_
  8.4 2.7 %collective-permute-start.8 = (bf16[16,2176]{1,0:T(8,128)(2,1)S(1)}, bf16[16,2176]{1,0:T(8,128)(2,1)S(1)}, u32[]{:S(2)}, u32[]{:S(2)}) collective-permute-start(bf16[16,2176]{1,0:T(8,128)(2,1)S(1)} %collective-permute-done.7.refs_7_), channel_id=1, source_target_pairs={{0,6},{1,7},{2,4},{3,5},{4,2},{5,3},{6,0},{7,1},{8,14},{9,15},{10,... | collective-permute-start | bytes 208904 | tf_op jit(solution)/shard_map/ppermute | solution.py:118
  11.1 0.7 %collective-permute-start.9 = (bf16[16,2176]{1,0:T(8,128)(2,1)S(1)}, bf16[16,2176]{1,0:T(8,128)(2,1)S(1)}, u32[]{:S(2)}, u32[]{:S(2)}) collective-permute-start(bf16[16,2176]{1,0:T(8,128)(2,1)S(1)} %collective-permute-done.7.refs_7_), channel_id=1, source_target_pairs={{0,4},{1,5},{2,6},{3,7},{4,0},{5,1},{6,2},{7,3},{8,12},{9,13},{10,... | collective-permute-start | bytes 208904 | tf_op jit(solution)/shard_map/ppermute | solution.py:118
  11.7 0.1 collective-permute-start.10
  11.9 0.0 collective-permute-done.1.refs_8_
  11.9 1.9 %collective-permute-start.5 = (bf16[16,2176]{1,0:T(8,128)(2,1)S(1)}, bf16[16,2176]{1,0:T(8,128)(2,1)S(1)}, u32[]{:S(2)}, u32[]{:S(2)}) collective-permute-start(bf16[16,2176]{1,0:T(8,128)(2,1)S(1)} %again.1.refs_7_), channel_id=1, source_target_pairs={{0,2},{1,3},{2,0},{3,1},{4,6},{5,7},{6,4},{7,5},{8,10},{9,11},{10,... | collective-permute-start | bytes 208904 | tf_op jit(solution)/shard_map/ppermute | solution.py:118
  13.7 0.0 collective-permute-done.3.refs_9_
  13.7 0.0 collective-permute-start.15
  13.8 0.5 %collective-permute-done.8.refs_11_.refs_8_ = bf16[16,2176]{1,0:T(8,128)(2,1)S(1)} collective-permute-done((bf16[16,2176]{1,0:T(8,128)(2,1)S(1)}, bf16[16,2176]{1,0:T(8,128)(2,1)S(1)}, u32[]{:S(2)}, u32[]{:S(2)}) %collective-permute-start.8) | collective-permute-done | bytes 69664 | tf_op jit(solution)/shard_map/ppermute | solution.py:118
  14.3 0.0 collective-permute-start.16
  14.3 1.1 %collective-permute-done.9.refs_12_.refs_9_ = bf16[16,2176]{1,0:T(8,128)(2,1)S(1)} collective-permute-done((bf16[16,2176]{1,0:T(8,128)(2,1)S(1)}, bf16[16,2176]{1,0:T(8,128)(2,1)S(1)}, u32[]{:S(2)}, u32[]{:S(2)}) %collective-permute-start.9) | collective-permute-done | bytes 69664 | tf_op jit(solution)/shard_map/ppermute | solution.py:118
  15.4 0.0 collective-permute-start.17
  15.4 0.7 %collective-permute-done.10.refs_13_.refs_10_ = bf16[16,2176]{1,0:T(8,128)(2,1)S(1)} collective-permute-done((bf16[16,2176]{1,0:T(8,128)(2,1)S(1)}, bf16[16,2176]{1,0:T(8,128)(2,1)S(1)}, u32[]{:S(2)}, u32[]{:S(2)}) %collective-permute-start.10) | collective-permute-done | bytes 69664 | tf_op jit(solution)/shard_map/ppermute | solution.py:118
  16.0 0.0 collective-permute-start.18
  16.0 0.7 %collective-permute-done.5.refs_10_ = bf16[16,2176]{1,0:T(8,128)(2,1)S(1)} collective-permute-done((bf16[16,2176]{1,0:T(8,128)(2,1)S(1)}, bf16[16,2176]{1,0:T(8,128)(2,1)S(1)}, u32[]{:S(2)}, u32[]{:S(2)}) %collective-permute-start.5) | collective-permute-done | bytes 69664 | tf_op jit(solution)/shard_map/ppermute | solution.py:118
  16.8 0.0 collective-permute-start
  16.8 0.0 collective-permute-done.15.refs_3_
  16.8 0.5 %collective-permute-start.2 = (bf16[16,2176]{1,0:T(8,128)(2,1)S(1)}, bf16[16,2176]{1,0:T(8,128)(2,1)S(1)}, u32[]{:S(2)}, u32[]{:S(2)}) collective-permute-start(bf16[16,2176]{1,0:T(8,128)(2,1)S(1)} %collective-permute-done.1.refs_8_), channel_id=1, source_target_pairs={{0,1},{1,0},{2,3},{3,2},{4,5},{5,4},{6,7},{7,6},{8,9},{9,8},{10,11... | collective-permute-start | bytes 208904 | tf_op jit(solution)/shard_map/ppermute | solution.py:121
  17.3 0.0 collective-permute-done.16.refs_4_
  17.3 0.1 collective-permute-start.4
  17.4 0.0 collective-permute-done.17.refs_5_
  17.4 0.4 %collective-permute-start.6 = (bf16[16,2176]{1,0:T(8,128)(2,1)S(1)}, bf16[16,2176]{1,0:T(8,128)(2,1)S(1)}, u32[]{:S(2)}, u32[]{:S(2)}) collective-permute-start(bf16[16,2176]{1,0:T(8,128)(2,1)S(1)} %collective-permute-done.5.refs_10_), channel_id=1, source_target_pairs={{0,1},{1,0},{2,3},{3,2},{4,5},{5,4},{6,7},{7,6},{8,9},{9,8},{10,11... | collective-permute-start | bytes 208904 | tf_op jit(solution)/shard_map/ppermute | solution.py:121
  17.8 0.0 collective-permute-done.18.refs_6_
  17.8 0.0 copy-done.1
  17.8 0.0 copy-done.2
  17.8 0.0 copy-done
  17.8 1.5 %far.1 = (bf16[64,2048]{1,0:T(8,128)(2,1)S(1)}, f32[64,2048]{1,0:T(8,128)S(1)}) custom-call(bf16[1,2048,768]{2,1,0:T(8,128)(2,1)S(1)} %copy-done, bf16[1,2048,768]{2,1,0:T(8,128)(2,1)S(1)} %copy-done.1, bf16[1,768,2048]{2,1,0:T(8,128)(2,1)S(1)} %copy-done.2, bf16[16,2176]{1,0:T(8,128)(2,1)S(1)} %collective-permute-done.15.refs_3_, ...), custom_call_target="tpu_custom_call" | custom-call | flops 1000000000 | bytes 244140 | tf_op jit(solution)/shard_map/far/pallas_call | solution.py:127
  19.4 0.0 copy-start.3
  19.4 0.1 collective-permute-start.19
  19.5 0.0 collective-permute-done.refs_3_
  19.5 0.0 collective-permute-done.2.refs_4_
  19.5 0.0 collective-permute-done.4.refs_5_
  19.5 0.0 collective-permute-done.6.refs_6_
  19.5 1.5 %near.1 = (bf16[64,2048]{1,0:T(8,128)(2,1)S(1)}, f32[64,2048]{1,0:T(8,128)S(1)}) custom-call(bf16[1,2048,768]{2,1,0:T(8,128)(2,1)S(1)} %copy-done, bf16[1,2048,768]{2,1,0:T(8,128)(2,1)S(1)} %copy-done.1, bf16[1,768,2048]{2,1,0:T(8,128)(2,1)S(1)} %copy-done.2, bf16[16,2176]{1,0:T(8,128)(2,1)S(1)} %collective-permute-done.refs_3_, ...), custom_call_target="tpu_custom_call" | custom-call | flops 1000000000 | bytes 244140 | tf_op jit(solution)/shard_map/near/pallas_call | solution.py:127
  21.1 0.5 %collective-permute-start.11 = (bf16[64,2048]{1,0:T(8,128)(2,1)S(1)}, bf16[64,2048]{1,0:T(8,128)(2,1)S(1)}, u32[]{:S(2)}, u32[]{:S(2)}) collective-permute-start(bf16[64,2048]{1,0:T(8,128)(2,1)S(1)} %get-tuple-element.18), channel_id=1, source_target_pairs={{0,1},{1,0},{2,3},{3,2},{4,5},{5,4},{6,7},{7,6},{8,9},{9,8},{10,11... | collective-permute-start | bytes 786440 | tf_op jit(solution)/shard_map/ppermute | solution.py:121
  21.6 0.0 collective-permute-done.19.other_ref
  21.6 0.1 pair.3
  21.7 2.1 %collective-permute-start.20 = (bf16[16,2048]{1,0:T(8,128)(2,1)S(1)}, bf16[16,2048]{1,0:T(8,128)(2,1)S(1)}, u32[]{:S(2)}, u32[]{:S(2)}) collective-permute-start(bf16[16,2048]{1,0:T(8,128)(2,1)S(1)} %get-tuple-element.26), channel_id=1, source_target_pairs={{0,6},{1,7},{2,4},{3,5},{4,2},{5,3},{6,0},{7,1},{8,14},{9,15},{10,... | collective-permute-start | bytes 196616 | tf_op jit(solution)/shard_map/ppermute | solution.py:118
  23.8 0.7 %collective-permute-start.21 = (bf16[16,2048]{1,0:T(8,128)(2,1)S(1)}, bf16[16,2048]{1,0:T(8,128)(2,1)S(1)}, u32[]{:S(2)}, u32[]{:S(2)}) collective-permute-start(bf16[16,2048]{1,0:T(8,128)(2,1)S(1)} %get-tuple-element.27), channel_id=1, source_target_pairs={{0,4},{1,5},{2,6},{3,7},{4,0},{5,1},{6,2},{7,3},{8,12},{9,13},{10,... | collective-permute-start | bytes 196616 | tf_op jit(solution)/shard_map/ppermute | solution.py:118
  24.5 0.7 %collective-permute-start.22 = (bf16[16,2048]{1,0:T(8,128)(2,1)S(1)}, bf16[16,2048]{1,0:T(8,128)(2,1)S(1)}, u32[]{:S(2)}, u32[]{:S(2)}) collective-permute-start(bf16[16,2048]{1,0:T(8,128)(2,1)S(1)} %get-tuple-element.28), channel_id=1, source_target_pairs={{0,2},{1,3},{2,0},{3,1},{4,6},{5,7},{6,4},{7,5},{8,10},{9,11},{10,... | collective-permute-start | bytes 196616 | tf_op jit(solution)/shard_map/ppermute | solution.py:118
  25.2 0.0 collective-permute-done.11.other_ref
  25.2 0.1 pair.2
  25.3 2.1 %collective-permute-start.12 = (bf16[16,2048]{1,0:T(8,128)(2,1)S(1)}, bf16[16,2048]{1,0:T(8,128)(2,1)S(1)}, u32[]{:S(2)}, u32[]{:S(2)}) collective-permute-start(bf16[16,2048]{1,0:T(8,128)(2,1)S(1)} %get-tuple-element.20), channel_id=1, source_target_pairs={{0,6},{1,7},{2,4},{3,5},{4,2},{5,3},{6,0},{7,1},{8,14},{9,15},{10,... | collective-permute-start | bytes 196616 | tf_op jit(solution)/shard_map/ppermute | solution.py:118
  27.4 0.7 %collective-permute-start.13 = (bf16[16,2048]{1,0:T(8,128)(2,1)S(1)}, bf16[16,2048]{1,0:T(8,128)(2,1)S(1)}, u32[]{:S(2)}, u32[]{:S(2)}) collective-permute-start(bf16[16,2048]{1,0:T(8,128)(2,1)S(1)} %get-tuple-element.21), channel_id=1, source_target_pairs={{0,4},{1,5},{2,6},{3,7},{4,0},{5,1},{6,2},{7,3},{8,12},{9,13},{10,... | collective-permute-start | bytes 196616 | tf_op jit(solution)/shard_map/ppermute | solution.py:118
  28.1 0.0 collective-permute-done.20.refs_1_
  28.1 0.7 %collective-permute-start.14 = (bf16[16,2048]{1,0:T(8,128)(2,1)S(1)}, bf16[16,2048]{1,0:T(8,128)(2,1)S(1)}, u32[]{:S(2)}, u32[]{:S(2)}) collective-permute-start(bf16[16,2048]{1,0:T(8,128)(2,1)S(1)} %get-tuple-element.22), channel_id=1, source_target_pairs={{0,2},{1,3},{2,0},{3,1},{4,6},{5,7},{6,4},{7,5},{8,10},{9,11},{10,... | collective-permute-start | bytes 196616 | tf_op jit(solution)/shard_map/ppermute | solution.py:118
  28.9 0.0 collective-permute-done.21.refs_2_
  28.9 0.6 %collective-permute-done.22.refs_3_ = bf16[16,2048]{1,0:T(8,128)(2,1)S(1)} collective-permute-done((bf16[16,2048]{1,0:T(8,128)(2,1)S(1)}, bf16[16,2048]{1,0:T(8,128)(2,1)S(1)}, u32[]{:S(2)}, u32[]{:S(2)}) %collective-permute-start.22) | collective-permute-done | bytes 65568 | tf_op jit(solution)/shard_map/ppermute | solution.py:118
  29.5 2.1 %collective-permute-start.23 = (bf16[16,2048]{1,0:T(8,128)(2,1)S(1)}, bf16[16,2048]{1,0:T(8,128)(2,1)S(1)}, u32[]{:S(2)}, u32[]{:S(2)}) collective-permute-start(bf16[16,2048]{1,0:T(8,128)(2,1)S(1)} %cross.1), channel_id=1, source_target_pairs={{0,8},{1,9},{2,10},{3,11},{4,12},{5,13},{6,14},{7,15},{8,0},{9,1},... | collective-permute-start | bytes 196616 | tf_op jit(solution)/shard_map/ppermute | solution.py:118
  31.6 0.0 collective-permute-done.12.refs_2_
  31.6 0.8 %collective-permute-done.13.refs_3_ = bf16[16,2048]{1,0:T(8,128)(2,1)S(1)} collective-permute-done((bf16[16,2048]{1,0:T(8,128)(2,1)S(1)}, bf16[16,2048]{1,0:T(8,128)(2,1)S(1)}, u32[]{:S(2)}, u32[]{:S(2)}) %collective-permute-start.13) | collective-permute-done | bytes 65568 | tf_op jit(solution)/shard_map/ppermute | solution.py:118
  32.4 0.0 collective-permute-done.14.refs_4_
  32.4 2.3 %collective-permute-done.23.refs_5_ = bf16[16,2048]{1,0:T(8,128)(2,1)S(1)} collective-permute-done((bf16[16,2048]{1,0:T(8,128)(2,1)S(1)}, bf16[16,2048]{1,0:T(8,128)(2,1)S(1)}, u32[]{:S(2)}, u32[]{:S(2)}) %collective-permute-start.23) | collective-permute-done | bytes 65568 | tf_op jit(solution)/shard_map/ppermute | solution.py:118
  34.7 0.0 copy-done.3
  34.7 0.7 %mix.1 = bf16[16,2048]{1,0:T(8,128)(2,1)} custom-call(bf16[16,2048]{1,0:T(8,128)(2,1)S(1)} %copy-done.3, f32[16,2048]{1,0:T(8,128)S(1)} %get-tuple-element.19.refs_1_, bf16[16,2048]{1,0:T(8,128)(2,1)S(1)} %collective-permute-done.12.refs_2_, bf16[16,2048]{1,0:T(8,128)(2,1)S(1)} %collective-permute-done.13.refs_3_, ...), custom_call_target="tpu_custom_call" | custom-call | tf_op jit(solution)/shard_map/mix/pallas_call | solution.py:146
  (2 shorter events, 0.0 us)
Async XLA Ops:
  0.0 17.8 %copy-start.1 = (bf16[1,2048,768]{2,1,0:T(8,128)(2,1)S(1)}, bf16[1,2048,768]{2,1,0:T(8,128)(2,1)}, u32[]{:S(2)}) copy-start(bf16[1,2048,768]{2,1,0:T(8,128)(2,1)} %refs_1_.3) | copy-start | bytes 9437188
  0.0 17.8 %copy-start.2 = (bf16[1,768,2048]{2,1,0:T(8,128)(2,1)S(1)}, bf16[1,768,2048]{2,1,0:T(8,128)(2,1)}, u32[]{:S(2)}) copy-start(bf16[1,768,2048]{2,1,0:T(8,128)(2,1)} %refs_2_.3) | copy-start | bytes 9437188
  1.1 16.8 %copy-start = (bf16[1,2048,768]{2,1,0:T(8,128)(2,1)S(1)}, bf16[1,2048,768]{2,1,0:T(8,128)(2,1)}, u32[]{:S(2)}) copy-start(bf16[1,2048,768]{2,1,0:T(8,128)(2,1)} %refs_0_.4) | copy-start | bytes 9437188
  1.1 7.3 %collective-permute-start.7 = (bf16[16,2176]{1,0:T(8,128)(2,1)S(1)}, bf16[16,2176]{1,0:T(8,128)(2,1)S(1)}, u32[]{:S(2)}, u32[]{:S(2)}) collective-permute-start(bf16[16,2176]{1,0:T(8,128)(2,1)S(1)} %pack.1.source_ref), channel_id=1, source_target_pairs={{0,8},{1,9},{2,10},{3,11},{4,12},{5,13},{6,14},{7,15},{8,0},{9,1},... | collective-permute-start | bytes 208904 | tf_op jit(solution)/shard_map/ppermute | solution.py:118
  5.2 6.7 %collective-permute-start.1 = (bf16[16,2176]{1,0:T(8,128)(2,1)S(1)}, bf16[16,2176]{1,0:T(8,128)(2,1)S(1)}, u32[]{:S(2)}, u32[]{:S(2)}) collective-permute-start(bf16[16,2176]{1,0:T(8,128)(2,1)S(1)} %again.1.refs_7_), channel_id=1, source_target_pairs={{0,6},{1,7},{2,4},{3,5},{4,2},{5,3},{6,0},{7,1},{8,14},{9,15},{10,... | collective-permute-start | bytes 208904 | tf_op jit(solution)/shard_map/ppermute | solution.py:118
  7.7 6.1 %collective-permute-start.3 = (bf16[16,2176]{1,0:T(8,128)(2,1)S(1)}, bf16[16,2176]{1,0:T(8,128)(2,1)S(1)}, u32[]{:S(2)}, u32[]{:S(2)}) collective-permute-start(bf16[16,2176]{1,0:T(8,128)(2,1)S(1)} %again.1.refs_7_), channel_id=1, source_target_pairs={{0,4},{1,5},{2,6},{3,7},{4,0},{5,1},{6,2},{7,3},{8,12},{9,13},{10,... | collective-permute-start | bytes 208904 | tf_op jit(solution)/shard_map/ppermute | solution.py:118
  8.4 5.9 %collective-permute-start.8 = (bf16[16,2176]{1,0:T(8,128)(2,1)S(1)}, bf16[16,2176]{1,0:T(8,128)(2,1)S(1)}, u32[]{:S(2)}, u32[]{:S(2)}) collective-permute-start(bf16[16,2176]{1,0:T(8,128)(2,1)S(1)} %collective-permute-done.7.refs_7_), channel_id=1, source_target_pairs={{0,6},{1,7},{2,4},{3,5},{4,2},{5,3},{6,0},{7,1},{8,14},{9,15},{10,... | collective-permute-start | bytes 208904 | tf_op jit(solution)/shard_map/ppermute | solution.py:118
  11.1 4.3 %collective-permute-start.9 = (bf16[16,2176]{1,0:T(8,128)(2,1)S(1)}, bf16[16,2176]{1,0:T(8,128)(2,1)S(1)}, u32[]{:S(2)}, u32[]{:S(2)}) collective-permute-start(bf16[16,2176]{1,0:T(8,128)(2,1)S(1)} %collective-permute-done.7.refs_7_), channel_id=1, source_target_pairs={{0,4},{1,5},{2,6},{3,7},{4,0},{5,1},{6,2},{7,3},{8,12},{9,13},{10,... | collective-permute-start | bytes 208904 | tf_op jit(solution)/shard_map/ppermute | solution.py:118
  11.7 4.3 %collective-permute-start.10 = (bf16[16,2176]{1,0:T(8,128)(2,1)S(1)}, bf16[16,2176]{1,0:T(8,128)(2,1)S(1)}, u32[]{:S(2)}, u32[]{:S(2)}) collective-permute-start(bf16[16,2176]{1,0:T(8,128)(2,1)S(1)} %collective-permute-done.7.refs_7_), channel_id=1, source_target_pairs={{0,2},{1,3},{2,0},{3,1},{4,6},{5,7},{6,4},{7,5},{8,10},{9,11},{10,... | collective-permute-start | bytes 208904 | tf_op jit(solution)/shard_map/ppermute | solution.py:118
  11.9 4.9 %collective-permute-start.5 = (bf16[16,2176]{1,0:T(8,128)(2,1)S(1)}, bf16[16,2176]{1,0:T(8,128)(2,1)S(1)}, u32[]{:S(2)}, u32[]{:S(2)}) collective-permute-start(bf16[16,2176]{1,0:T(8,128)(2,1)S(1)} %again.1.refs_7_), channel_id=1, source_target_pairs={{0,2},{1,3},{2,0},{3,1},{4,6},{5,7},{6,4},{7,5},{8,10},{9,11},{10,... | collective-permute-start | bytes 208904 | tf_op jit(solution)/shard_map/ppermute | solution.py:118
  13.7 3.0 %collective-permute-start.15 = (bf16[16,2176]{1,0:T(8,128)(2,1)S(1)}, bf16[16,2176]{1,0:T(8,128)(2,1)S(1)}, u32[]{:S(2)}, u32[]{:S(2)}) collective-permute-start(bf16[16,2176]{1,0:T(8,128)(2,1)S(1)} %collective-permute-done.7.refs_7_), channel_id=1, source_target_pairs={{0,1},{1,0},{2,3},{3,2},{4,5},{5,4},{6,7},{7,6},{8,9},{9,8},{10,11... | collective-permute-start | bytes 208904 | tf_op jit(solution)/shard_map/ppermute | solution.py:121
  14.3 3.0 %collective-permute-start.16 = (bf16[16,2176]{1,0:T(8,128)(2,1)S(1)}, bf16[16,2176]{1,0:T(8,128)(2,1)S(1)}, u32[]{:S(2)}, u32[]{:S(2)}) collective-permute-start(bf16[16,2176]{1,0:T(8,128)(2,1)S(1)} %collective-permute-done.8.refs_11_.refs_8_), channel_id=1, source_target_pairs={{0,1},{1,0},{2,3},{3,2},{4,5},{5,4},{6,7},{7,6},{8,9},{9,8},{10,11... | collective-permute-start | bytes 208904 | tf_op jit(solution)/shard_map/ppermute | solution.py:121
  15.4 2.0 %collective-permute-start.17 = (bf16[16,2176]{1,0:T(8,128)(2,1)S(1)}, bf16[16,2176]{1,0:T(8,128)(2,1)S(1)}, u32[]{:S(2)}, u32[]{:S(2)}) collective-permute-start(bf16[16,2176]{1,0:T(8,128)(2,1)S(1)} %collective-permute-done.9.refs_12_.refs_9_), channel_id=1, source_target_pairs={{0,1},{1,0},{2,3},{3,2},{4,5},{5,4},{6,7},{7,6},{8,9},{9,8},{10,11... | collective-permute-start | bytes 208904 | tf_op jit(solution)/shard_map/ppermute | solution.py:121
  16.0 1.8 %collective-permute-start.18 = (bf16[16,2176]{1,0:T(8,128)(2,1)S(1)}, bf16[16,2176]{1,0:T(8,128)(2,1)S(1)}, u32[]{:S(2)}, u32[]{:S(2)}) collective-permute-start(bf16[16,2176]{1,0:T(8,128)(2,1)S(1)} %collective-permute-done.10.refs_13_.refs_10_), channel_id=1, source_target_pairs={{0,1},{1,0},{2,3},{3,2},{4,5},{5,4},{6,7},{7,6},{8,9},{9,8},{10,11... | collective-permute-start | bytes 208904 | tf_op jit(solution)/shard_map/ppermute | solution.py:121
  16.8 2.8 %collective-permute-start = (bf16[16,2176]{1,0:T(8,128)(2,1)S(1)}, bf16[16,2176]{1,0:T(8,128)(2,1)S(1)}, u32[]{:S(2)}, u32[]{:S(2)}) collective-permute-start(bf16[16,2176]{1,0:T(8,128)(2,1)S(1)} %again.1.refs_7_), channel_id=1, source_target_pairs={{0,1},{1,0},{2,3},{3,2},{4,5},{5,4},{6,7},{7,6},{8,9},{9,8},{10,11... | collective-permute-start | bytes 208904 | tf_op jit(solution)/shard_map/ppermute | solution.py:121
  16.8 2.8 %collective-permute-start.2 = (bf16[16,2176]{1,0:T(8,128)(2,1)S(1)}, bf16[16,2176]{1,0:T(8,128)(2,1)S(1)}, u32[]{:S(2)}, u32[]{:S(2)}) collective-permute-start(bf16[16,2176]{1,0:T(8,128)(2,1)S(1)} %collective-permute-done.1.refs_8_), channel_id=1, source_target_pairs={{0,1},{1,0},{2,3},{3,2},{4,5},{5,4},{6,7},{7,6},{8,9},{9,8},{10,11... | collective-permute-start | bytes 208904 | tf_op jit(solution)/shard_map/ppermute | solution.py:121
  17.3 2.2 %collective-permute-start.4 = (bf16[16,2176]{1,0:T(8,128)(2,1)S(1)}, bf16[16,2176]{1,0:T(8,128)(2,1)S(1)}, u32[]{:S(2)}, u32[]{:S(2)}) collective-permute-start(bf16[16,2176]{1,0:T(8,128)(2,1)S(1)} %collective-permute-done.3.refs_9_), channel_id=1, source_target_pairs={{0,1},{1,0},{2,3},{3,2},{4,5},{5,4},{6,7},{7,6},{8,9},{9,8},{10,11... | collective-permute-start | bytes 208904 | tf_op jit(solution)/shard_map/ppermute | solution.py:121
  17.4 2.2 %collective-permute-start.6 = (bf16[16,2176]{1,0:T(8,128)(2,1)S(1)}, bf16[16,2176]{1,0:T(8,128)(2,1)S(1)}, u32[]{:S(2)}, u32[]{:S(2)}) collective-permute-start(bf16[16,2176]{1,0:T(8,128)(2,1)S(1)} %collective-permute-done.5.refs_10_), channel_id=1, source_target_pairs={{0,1},{1,0},{2,3},{3,2},{4,5},{5,4},{6,7},{7,6},{8,9},{9,8},{10,11... | collective-permute-start | bytes 208904 | tf_op jit(solution)/shard_map/ppermute | solution.py:121
  19.4 15.4 %copy-start.3 = (bf16[16,2048]{1,0:T(8,128)(2,1)S(1)}, bf16[16,2048]{1,0:T(8,128)(2,1)}, u32[]{:S(2)}) copy-start(bf16[16,2048]{1,0:T(8,128)(2,1)} %refs_0_.5) | copy-start | bytes 196612
  19.4 2.2 %collective-permute-start.19 = (bf16[64,2048]{1,0:T(8,128)(2,1)S(1)}, bf16[64,2048]{1,0:T(8,128)(2,1)S(1)}, u32[]{:S(2)}, u32[]{:S(2)}) collective-permute-start(bf16[64,2048]{1,0:T(8,128)(2,1)S(1)} %get-tuple-element.24), channel_id=1, source_target_pairs={{0,1},{1,0},{2,3},{3,2},{4,5},{5,4},{6,7},{7,6},{8,9},{9,8},{10,11... | collective-permute-start | bytes 786440 | tf_op jit(solution)/shard_map/ppermute | solution.py:121
  21.1 4.1 %collective-permute-start.11 = (bf16[64,2048]{1,0:T(8,128)(2,1)S(1)}, bf16[64,2048]{1,0:T(8,128)(2,1)S(1)}, u32[]{:S(2)}, u32[]{:S(2)}) collective-permute-start(bf16[64,2048]{1,0:T(8,128)(2,1)S(1)} %get-tuple-element.18), channel_id=1, source_target_pairs={{0,1},{1,0},{2,3},{3,2},{4,5},{5,4},{6,7},{7,6},{8,9},{9,8},{10,11... | collective-permute-start | bytes 786440 | tf_op jit(solution)/shard_map/ppermute | solution.py:121
  21.7 6.4 %collective-permute-start.20 = (bf16[16,2048]{1,0:T(8,128)(2,1)S(1)}, bf16[16,2048]{1,0:T(8,128)(2,1)S(1)}, u32[]{:S(2)}, u32[]{:S(2)}) collective-permute-start(bf16[16,2048]{1,0:T(8,128)(2,1)S(1)} %get-tuple-element.26), channel_id=1, source_target_pairs={{0,6},{1,7},{2,4},{3,5},{4,2},{5,3},{6,0},{7,1},{8,14},{9,15},{10,... | collective-permute-start | bytes 196616 | tf_op jit(solution)/shard_map/ppermute | solution.py:118
  23.8 5.0 %collective-permute-start.21 = (bf16[16,2048]{1,0:T(8,128)(2,1)S(1)}, bf16[16,2048]{1,0:T(8,128)(2,1)S(1)}, u32[]{:S(2)}, u32[]{:S(2)}) collective-permute-start(bf16[16,2048]{1,0:T(8,128)(2,1)S(1)} %get-tuple-element.27), channel_id=1, source_target_pairs={{0,4},{1,5},{2,6},{3,7},{4,0},{5,1},{6,2},{7,3},{8,12},{9,13},{10,... | collective-permute-start | bytes 196616 | tf_op jit(solution)/shard_map/ppermute | solution.py:118
  24.5 5.0 %collective-permute-start.22 = (bf16[16,2048]{1,0:T(8,128)(2,1)S(1)}, bf16[16,2048]{1,0:T(8,128)(2,1)S(1)}, u32[]{:S(2)}, u32[]{:S(2)}) collective-permute-start(bf16[16,2048]{1,0:T(8,128)(2,1)S(1)} %get-tuple-element.28), channel_id=1, source_target_pairs={{0,2},{1,3},{2,0},{3,1},{4,6},{5,7},{6,4},{7,5},{8,10},{9,11},{10,... | collective-permute-start | bytes 196616 | tf_op jit(solution)/shard_map/ppermute | solution.py:118
  25.3 6.3 %collective-permute-start.12 = (bf16[16,2048]{1,0:T(8,128)(2,1)S(1)}, bf16[16,2048]{1,0:T(8,128)(2,1)S(1)}, u32[]{:S(2)}, u32[]{:S(2)}) collective-permute-start(bf16[16,2048]{1,0:T(8,128)(2,1)S(1)} %get-tuple-element.20), channel_id=1, source_target_pairs={{0,6},{1,7},{2,4},{3,5},{4,2},{5,3},{6,0},{7,1},{8,14},{9,15},{10,... | collective-permute-start | bytes 196616 | tf_op jit(solution)/shard_map/ppermute | solution.py:118
  27.4 5.0 %collective-permute-start.13 = (bf16[16,2048]{1,0:T(8,128)(2,1)S(1)}, bf16[16,2048]{1,0:T(8,128)(2,1)S(1)}, u32[]{:S(2)}, u32[]{:S(2)}) collective-permute-start(bf16[16,2048]{1,0:T(8,128)(2,1)S(1)} %get-tuple-element.21), channel_id=1, source_target_pairs={{0,4},{1,5},{2,6},{3,7},{4,0},{5,1},{6,2},{7,3},{8,12},{9,13},{10,... | collective-permute-start | bytes 196616 | tf_op jit(solution)/shard_map/ppermute | solution.py:118
  28.1 4.3 %collective-permute-start.14 = (bf16[16,2048]{1,0:T(8,128)(2,1)S(1)}, bf16[16,2048]{1,0:T(8,128)(2,1)S(1)}, u32[]{:S(2)}, u32[]{:S(2)}) collective-permute-start(bf16[16,2048]{1,0:T(8,128)(2,1)S(1)} %get-tuple-element.22), channel_id=1, source_target_pairs={{0,2},{1,3},{2,0},{3,1},{4,6},{5,7},{6,4},{7,5},{8,10},{9,11},{10,... | collective-permute-start | bytes 196616 | tf_op jit(solution)/shard_map/ppermute | solution.py:118
  29.5 5.2 %collective-permute-start.23 = (bf16[16,2048]{1,0:T(8,128)(2,1)S(1)}, bf16[16,2048]{1,0:T(8,128)(2,1)S(1)}, u32[]{:S(2)}, u32[]{:S(2)}) collective-permute-start(bf16[16,2048]{1,0:T(8,128)(2,1)S(1)} %cross.1), channel_id=1, source_target_pairs={{0,8},{1,9},{2,10},{3,11},{4,12},{5,13},{6,14},{7,15},{8,0},{9,1},... | collective-permute-start | bytes 196616 | tf_op jit(solution)/shard_map/ppermute | solution.py:118

commit v7 on v6

--- a/solution.py
+++ b/solution.py
@@ -78,6 +78,12 @@
     out_ref[...] = source_ref[...]
 
 
+def join_kernel(*refs):
+    row_count = refs[0].shape[0]
+    for b, ref in enumerate(refs[:-1]):
+        refs[-1][pl.ds(b * row_count, row_count), :] = ref[...]
+
+
 def pair_kernel(own_ref, other_ref, first_ref, *outs):
     row_count = first_ref.shape[0]
     for k, out in enumerate((first_ref,) + outs):
@@ -159,11 +165,15 @@
     )(*map(in_hbm, (tokens, route_weight.T, replica.T)))
     crossed = partner(packed, half)
     again = on_core(again_kernel, "again", shape(row_count, wide, width + LANES), [VMEM], flops=10**9)(packed)
-    order = range(half - 1, 0, -1)
+    order = [1, *range(half - 1, 1, -1)]
     near = [again] + [partner(again, k) for k in order]
     far = [crossed] + [partner(crossed, k) for k in order]
     crossed_other = swap(crossed)
-    near_other = [swap(block) for block in near]
+    def join(blocks):
+        rows = shape(len(blocks) * row_count, wide, width + LANES)
+        return on_core(join_kernel, "join", rows, [VMEM] * len(blocks), flops=10**8)(*blocks)
+
+    near_other = [swap(join(near[: half // 2])), swap(join(near[half // 2 :]))]
     near_away, near_own = experts("near", near_other + near, far[1:])
     far_other = [crossed_other] + [swap(block) for block in far[1:]]
     far_away, far_own = experts("far", far_other + far)
@@ -215,7 +225,7 @@
     peer_count = lax.axis_size("expert")
     if (
         lax.axis_size("tensor") == 1
-        and peer_count in (4, 8, 16, 32, 64)
+        and peer_count in (16, 32, 64)
         and 2 * top_count >= peer_count
         and row_count % 16 == 0
         and row_count <= LANES

time: 35.6 us -> 34.6 us (0.972)
  waiting for transfers between devices: 7.04 us -> 5.09 us
  starting transfers between devices: 23.3 us -> 24.4 us
    ppermute x14, waiting for transfers between devices: 7.01 us -> 4.74 us  [partner(): lax.ppermute(array, 'expert', [(i, i ^ 2 * k) for i in range(peer_count)])]
    ppermute x14, starting transfers between devices: 21.6 us -> 22.5 us  [partner(): lax.ppermute(array, 'expert', [(i, i ^ 2 * k) for i in range(peer_count)])]
    ppermute x10 -> x8, starting transfers between devices: 1.67 us -> 1.83 us  [swap(): lax.ppermute(array, 'expert', [(i, i ^ 1) for i in range(peer_count)])]
  transfers between devices with their start and end apart: 24 -> 22, of which waited for: 8 -> 9; matrix products, arithmetic and copies ran while one was open for 0% -> 0% of each run, Pallas kernels for 9% -> 9%
where the time goes in v7:
time: 34.6 us; the launch traced here: 34.5 us
  starting transfers between devices  24.4 us (71%)
  waiting for transfers between devices  5.09 us (15%)
  Pallas kernels  4.93 us (14%)
    ppermute x14, starting transfers between devices, partner(): lax.ppermute(array, 'expert', [(i, i ^ 2 * k) for i in range(peer_count)])  22.5 us
    ppermute x14, waiting for transfers between devices, partner(): lax.ppermute(array, 'expert', [(i, i ^ 2 * k) for i in range(peer_count)])  4.74 us
    pallas_call x2, Pallas kernels, experts(): on_core(functools.partial(expert_kernel, len(blocks)), name, (shape(half_...  3.02 us
    ppermute x8, starting transfers between devices, swap(): lax.ppermute(array, 'expert', [(i, i ^ 1) for i in range(peer_count)])  1.83 us
    pallas_call x1, Pallas kernels, dense_shards(): on_core(pack_kernel, 'pack', shape(row_count, wide, width + LANES), [HBM]...  1.05 us
    pallas_call x2, Pallas kernels, total(): on_core(sum_kernel, name, shape(row_count, wide), [VMEM] * len(terms))  0.71 us
  transfers between devices with their start and end apart: 22, of which 9 were waited for; matrix products, arithmetic and copies ran while one was open for 0% of the time, Pallas kernels for 9%

profile of v7, /device:TPU:0, one launch (start us, length us, event | category | flops | bytes accessed | tf_op | source)
XLA Modules:
  0.0 34.5 jit_solution(3644436304575327252)
XLA Ops:
  0.0 0.0 copy-start.1
  0.0 0.0 copy-start.2
  0.0 1.0 %pack.1.source_ref = bf16[16,2176]{1,0:T(8,128)(2,1)S(1)} custom-call(bf16[16,2048]{1,0:T(8,128)(2,1)} %refs_0_.5, f32[8,16]{1,0:T(8,128)} %bitcast.2, s32[8,16]{1,0:T(8,128)} %bitcast.3), custom_call_target="tpu_custom_call" | custom-call | flops 10000000000 | bytes 2441406 | tf_op jit(solution)/shard_map/pack/pallas_call | solution.py:154
  1.1 0.0 copy-start
  1.1 4.1 %collective-permute-start.5 = (bf16[16,2176]{1,0:T(8,128)(2,1)S(1)}, bf16[16,2176]{1,0:T(8,128)(2,1)S(1)}, u32[]{:S(2)}, u32[]{:S(2)}) collective-permute-start(bf16[16,2176]{1,0:T(8,128)(2,1)S(1)} %pack.1.source_ref), channel_id=1, source_target_pairs={{0,8},{1,9},{2,10},{3,11},{4,12},{5,13},{6,14},{7,15},{8,0},{9,1},... | collective-permute-start | bytes 208904 | tf_op jit(solution)/shard_map/ppermute | solution.py:124
  5.2 2.5 %collective-permute-start.2 = (bf16[16,2176]{1,0:T(8,128)(2,1)S(1)}, bf16[16,2176]{1,0:T(8,128)(2,1)S(1)}, u32[]{:S(2)}, u32[]{:S(2)}) collective-permute-start(bf16[16,2176]{1,0:T(8,128)(2,1)S(1)} %again.1.refs_0_.refs_5_), channel_id=1, source_target_pairs={{0,6},{1,7},{2,4},{3,5},{4,2},{5,3},{6,0},{7,1},{8,14},{9,15},{10,... | collective-permute-start | bytes 208904 | tf_op jit(solution)/shard_map/ppermute | solution.py:124
  7.7 0.4 %collective-permute-start.3 = (bf16[16,2176]{1,0:T(8,128)(2,1)S(1)}, bf16[16,2176]{1,0:T(8,128)(2,1)S(1)}, u32[]{:S(2)}, u32[]{:S(2)}) collective-permute-start(bf16[16,2176]{1,0:T(8,128)(2,1)S(1)} %again.1.refs_0_.refs_5_), channel_id=1, source_target_pairs={{0,4},{1,5},{2,6},{3,7},{4,0},{5,1},{6,2},{7,3},{8,12},{9,13},{10,... | collective-permute-start | bytes 208904 | tf_op jit(solution)/shard_map/ppermute | solution.py:124
  8.1 0.2 collective-permute-done.5.refs_7_
  8.4 1.9 %collective-permute-start.6 = (bf16[16,2176]{1,0:T(8,128)(2,1)S(1)}, bf16[16,2176]{1,0:T(8,128)(2,1)S(1)}, u32[]{:S(2)}, u32[]{:S(2)}) collective-permute-start(bf16[16,2176]{1,0:T(8,128)(2,1)S(1)} %collective-permute-done.5.refs_7_), channel_id=1, source_target_pairs={{0,2},{1,3},{2,0},{3,1},{4,6},{5,7},{6,4},{7,5},{8,10},{9,11},{10,... | collective-permute-start | bytes 208904 | tf_op jit(solution)/shard_map/ppermute | solution.py:124
  10.3 1.3 %collective-permute-start.7 = (bf16[16,2176]{1,0:T(8,128)(2,1)S(1)}, bf16[16,2176]{1,0:T(8,128)(2,1)S(1)}, u32[]{:S(2)}, u32[]{:S(2)}) collective-permute-start(bf16[16,2176]{1,0:T(8,128)(2,1)S(1)} %collective-permute-done.5.refs_7_), channel_id=1, source_target_pairs={{0,6},{1,7},{2,4},{3,5},{4,2},{5,3},{6,0},{7,1},{8,14},{9,15},{10,... | collective-permute-start | bytes 208904 | tf_op jit(solution)/shard_map/ppermute | solution.py:124
  11.6 0.3 collective-permute-start.8
  11.9 0.0 collective-permute-done.2.refs_0_.refs_7_
  11.9 1.9 %collective-permute-start = (bf16[16,2176]{1,0:T(8,128)(2,1)S(1)}, bf16[16,2176]{1,0:T(8,128)(2,1)S(1)}, u32[]{:S(2)}, u32[]{:S(2)}) collective-permute-start(bf16[16,2176]{1,0:T(8,128)(2,1)S(1)} %again.1.refs_0_.refs_5_), channel_id=1, source_target_pairs={{0,2},{1,3},{2,0},{3,1},{4,6},{5,7},{6,4},{7,5},{8,10},{9,11},{10,... | collective-permute-start | bytes 208904 | tf_op jit(solution)/shard_map/ppermute | solution.py:124
  13.7 0.0 collective-permute-done.3.refs_1_.refs_8_
  13.7 0.0 collective-permute-start.13
  13.8 0.0 collective-permute-done.6.refs_9_.refs_8_
  13.8 0.5 %collective-permute-start.14 = (bf16[16,2176]{1,0:T(8,128)(2,1)S(1)}, bf16[16,2176]{1,0:T(8,128)(2,1)S(1)}, u32[]{:S(2)}, u32[]{:S(2)}) collective-permute-start(bf16[16,2176]{1,0:T(8,128)(2,1)S(1)} %collective-permute-done.6.refs_9_.refs_8_), channel_id=1, source_target_pairs={{0,1},{1,0},{2,3},{3,2},{4,5},{5,4},{6,7},{7,6},{8,9},{9,8},{10,11... | collective-permute-start | bytes 208904 | tf_op jit(solution)/shard_map/ppermute | solution.py:127
  14.3 1.2 %collective-permute-done.7.refs_10_.refs_9_ = bf16[16,2176]{1,0:T(8,128)(2,1)S(1)} collective-permute-done((bf16[16,2176]{1,0:T(8,128)(2,1)S(1)}, bf16[16,2176]{1,0:T(8,128)(2,1)S(1)}, u32[]{:S(2)}, u32[]{:S(2)}) %collective-permute-start.7) | collective-permute-done | bytes 69664 | tf_op jit(solution)/shard_map/ppermute | solution.py:124
  15.5 0.0 collective-permute-start.15
  15.5 0.4 %collective-permute-done.8.refs_11_.refs_10_ = bf16[16,2176]{1,0:T(8,128)(2,1)S(1)} collective-permute-done((bf16[16,2176]{1,0:T(8,128)(2,1)S(1)}, bf16[16,2176]{1,0:T(8,128)(2,1)S(1)}, u32[]{:S(2)}, u32[]{:S(2)}) %collective-permute-start.8) | collective-permute-done | bytes 69664 | tf_op jit(solution)/shard_map/ppermute | solution.py:124
  15.9 0.1 collective-permute-start.16
  16.0 0.2 collective-permute-done.refs_1_.refs_6_
  16.2 0.3 collective-permute-start.4
  16.5 0.0 collective-permute-done.13.refs_3_
  16.5 0.3 collective-permute-start.1
  16.8 0.0 collective-permute-done.14.refs_4_
  16.8 0.0 collective-permute-done.15.refs_5_
  16.8 0.3 collective-permute-done.16.refs_6_
  17.1 0.0 copy-done.1
  17.1 0.0 copy-done.2
  17.1 0.0 copy-done
  17.1 1.5 %far.1 = (bf16[64,2048]{1,0:T(8,128)(2,1)S(1)}, f32[64,2048]{1,0:T(8,128)S(1)}) custom-call(bf16[1,2048,768]{2,1,0:T(8,128)(2,1)S(1)} %copy-done, bf16[1,2048,768]{2,1,0:T(8,128)(2,1)S(1)} %copy-done.1, bf16[1,768,2048]{2,1,0:T(8,128)(2,1)S(1)} %copy-done.2, bf16[16,2176]{1,0:T(8,128)(2,1)S(1)} %collective-permute-done.13.refs_3_, ...), custom_call_target="tpu_custom_call" | custom-call | flops 1000000000 | bytes 244140 | tf_op jit(solution)/shard_map/far/pallas_call | solution.py:133
  18.7 0.0 copy-start.3
  18.7 0.2 collective-permute-start.17
  18.9 0.0 collective-permute-done.4.refs_4_
  18.9 0.0 collective-permute-done.1.refs_3_
  18.9 1.5 %near.1 = (bf16[64,2048]{1,0:T(8,128)(2,1)S(1)}, f32[64,2048]{1,0:T(8,128)S(1)}) custom-call(bf16[1,2048,768]{2,1,0:T(8,128)(2,1)S(1)} %copy-done, bf16[1,2048,768]{2,1,0:T(8,128)(2,1)S(1)} %copy-done.1, bf16[1,768,2048]{2,1,0:T(8,128)(2,1)S(1)} %copy-done.2, bf16[32,2176]{1,0:T(8,128)(2,1)S(1)} %collective-permute-done.1.refs_3_, ...), custom_call_target="tpu_custom_call" | custom-call | flops 1000000000 | bytes 244140 | tf_op jit(solution)/shard_map/near/pallas_call | solution.py:133
  20.4 0.4 %collective-permute-start.9 = (bf16[64,2048]{1,0:T(8,128)(2,1)S(1)}, bf16[64,2048]{1,0:T(8,128)(2,1)S(1)}, u32[]{:S(2)}, u32[]{:S(2)}) collective-permute-start(bf16[64,2048]{1,0:T(8,128)(2,1)S(1)} %get-tuple-element.18), channel_id=1, source_target_pairs={{0,1},{1,0},{2,3},{3,2},{4,5},{5,4},{6,7},{7,6},{8,9},{9,8},{10,11... | collective-permute-start | bytes 786440 | tf_op jit(solution)/shard_map/ppermute | solution.py:127
  20.9 0.0 collective-permute-done.17.other_ref
  20.9 0.1 pair.3
  20.9 1.6 %collective-permute-start.18 = (bf16[16,2048]{1,0:T(8,128)(2,1)S(1)}, bf16[16,2048]{1,0:T(8,128)(2,1)S(1)}, u32[]{:S(2)}, u32[]{:S(2)}) collective-permute-start(bf16[16,2048]{1,0:T(8,128)(2,1)S(1)} %get-tuple-element.26), channel_id=1, source_target_pairs={{0,2},{1,3},{2,0},{3,1},{4,6},{5,7},{6,4},{7,5},{8,10},{9,11},{10,... | collective-permute-start | bytes 196616 | tf_op jit(solution)/shard_map/ppermute | solution.py:124
  22.5 1.3 %collective-permute-start.19 = (bf16[16,2048]{1,0:T(8,128)(2,1)S(1)}, bf16[16,2048]{1,0:T(8,128)(2,1)S(1)}, u32[]{:S(2)}, u32[]{:S(2)}) collective-permute-start(bf16[16,2048]{1,0:T(8,128)(2,1)S(1)} %get-tuple-element.27), channel_id=1, source_target_pairs={{0,6},{1,7},{2,4},{3,5},{4,2},{5,3},{6,0},{7,1},{8,14},{9,15},{10,... | collective-permute-start | bytes 196616 | tf_op jit(solution)/shard_map/ppermute | solution.py:124
  23.8 0.6 %collective-permute-start.20 = (bf16[16,2048]{1,0:T(8,128)(2,1)S(1)}, bf16[16,2048]{1,0:T(8,128)(2,1)S(1)}, u32[]{:S(2)}, u32[]{:S(2)}) collective-permute-start(bf16[16,2048]{1,0:T(8,128)(2,1)S(1)} %get-tuple-element.28), channel_id=1, source_target_pairs={{0,4},{1,5},{2,6},{3,7},{4,0},{5,1},{6,2},{7,3},{8,12},{9,13},{10,... | collective-permute-start | bytes 196616 | tf_op jit(solution)/shard_map/ppermute | solution.py:124
  24.5 0.0 collective-permute-done.9.other_ref
  24.5 0.1 pair.2
  24.5 1.6 %collective-permute-start.10 = (bf16[16,2048]{1,0:T(8,128)(2,1)S(1)}, bf16[16,2048]{1,0:T(8,128)(2,1)S(1)}, u32[]{:S(2)}, u32[]{:S(2)}) collective-permute-start(bf16[16,2048]{1,0:T(8,128)(2,1)S(1)} %get-tuple-element.20), channel_id=1, source_target_pairs={{0,2},{1,3},{2,0},{3,1},{4,6},{5,7},{6,4},{7,5},{8,10},{9,11},{10,... | collective-permute-start | bytes 196616 | tf_op jit(solution)/shard_map/ppermute | solution.py:124
  26.1 1.3 %collective-permute-start.11 = (bf16[16,2048]{1,0:T(8,128)(2,1)S(1)}, bf16[16,2048]{1,0:T(8,128)(2,1)S(1)}, u32[]{:S(2)}, u32[]{:S(2)}) collective-permute-start(bf16[16,2048]{1,0:T(8,128)(2,1)S(1)} %get-tuple-element.21), channel_id=1, source_target_pairs={{0,6},{1,7},{2,4},{3,5},{4,2},{5,3},{6,0},{7,1},{8,14},{9,15},{10,... | collective-permute-start | bytes 196616 | tf_op jit(solution)/shard_map/ppermute | solution.py:124
  27.5 0.0 collective-permute-done.18.refs_1_
  27.5 0.6 %collective-permute-start.12 = (bf16[16,2048]{1,0:T(8,128)(2,1)S(1)}, bf16[16,2048]{1,0:T(8,128)(2,1)S(1)}, u32[]{:S(2)}, u32[]{:S(2)}) collective-permute-start(bf16[16,2048]{1,0:T(8,128)(2,1)S(1)} %get-tuple-element.22), channel_id=1, source_target_pairs={{0,4},{1,5},{2,6},{3,7},{4,0},{5,1},{6,2},{7,3},{8,12},{9,13},{10,... | collective-permute-start | bytes 196616 | tf_op jit(solution)/shard_map/ppermute | solution.py:124
  28.1 0.2 collective-permute-done.19.refs_2_
  28.3 0.3 collective-permute-done.20.refs_3_
  28.6 3.0 %collective-permute-start.21 = (bf16[16,2048]{1,0:T(8,128)(2,1)S(1)}, bf16[16,2048]{1,0:T(8,128)(2,1)S(1)}, u32[]{:S(2)}, u32[]{:S(2)}) collective-permute-start(bf16[16,2048]{1,0:T(8,128)(2,1)S(1)} %cross.1), channel_id=1, source_target_pairs={{0,8},{1,9},{2,10},{3,11},{4,12},{5,13},{6,14},{7,15},{8,0},{9,1},... | collective-permute-start | bytes 196616 | tf_op jit(solution)/shard_map/ppermute | solution.py:124
  31.6 0.0 collective-permute-done.10.refs_2_
  31.6 0.0 collective-permute-done.11.refs_3_
  31.6 0.9 %collective-permute-done.12.refs_4_ = bf16[16,2048]{1,0:T(8,128)(2,1)S(1)} collective-permute-done((bf16[16,2048]{1,0:T(8,128)(2,1)S(1)}, bf16[16,2048]{1,0:T(8,128)(2,1)S(1)}, u32[]{:S(2)}, u32[]{:S(2)}) %collective-permute-start.12) | collective-permute-done | bytes 65568 | tf_op jit(solution)/shard_map/ppermute | solution.py:124
  32.4 1.4 %collective-permute-done.21.refs_5_ = bf16[16,2048]{1,0:T(8,128)(2,1)S(1)} collective-permute-done((bf16[16,2048]{1,0:T(8,128)(2,1)S(1)}, bf16[16,2048]{1,0:T(8,128)(2,1)S(1)}, u32[]{:S(2)}, u32[]{:S(2)}) %collective-permute-start.21) | collective-permute-done | bytes 65568 | tf_op jit(solution)/shard_map/ppermute | solution.py:124
  33.8 0.0 copy-done.3
  33.8 0.7 %mix.1 = bf16[16,2048]{1,0:T(8,128)(2,1)} custom-call(bf16[16,2048]{1,0:T(8,128)(2,1)S(1)} %copy-done.3, f32[16,2048]{1,0:T(8,128)S(1)} %get-tuple-element.19.refs_1_, bf16[16,2048]{1,0:T(8,128)(2,1)S(1)} %collective-permute-done.10.refs_2_, bf16[16,2048]{1,0:T(8,128)(2,1)S(1)} %collective-permute-done.11.refs_3_, ...), custom_call_target="tpu_custom_call" | custom-call | tf_op jit(solution)/shard_map/mix/pallas_call | solution.py:152
  (4 shorter events, 0.1 us)
Async XLA Ops:
  0.0 17.1 %copy-start.1 = (bf16[1,2048,768]{2,1,0:T(8,128)(2,1)S(1)}, bf16[1,2048,768]{2,1,0:T(8,128)(2,1)}, u32[]{:S(2)}) copy-start(bf16[1,2048,768]{2,1,0:T(8,128)(2,1)} %refs_1_.3) | copy-start | bytes 9437188
  0.0 17.1 %copy-start.2 = (bf16[1,768,2048]{2,1,0:T(8,128)(2,1)S(1)}, bf16[1,768,2048]{2,1,0:T(8,128)(2,1)}, u32[]{:S(2)}) copy-start(bf16[1,768,2048]{2,1,0:T(8,128)(2,1)} %refs_2_.3) | copy-start | bytes 9437188
  1.1 16.1 %copy-start = (bf16[1,2048,768]{2,1,0:T(8,128)(2,1)S(1)}, bf16[1,2048,768]{2,1,0:T(8,128)(2,1)}, u32[]{:S(2)}) copy-start(bf16[1,2048,768]{2,1,0:T(8,128)(2,1)} %refs_0_.4) | copy-start | bytes 9437188
  1.1 7.3 %collective-permute-start.5 = (bf16[16,2176]{1,0:T(8,128)(2,1)S(1)}, bf16[16,2176]{1,0:T(8,128)(2,1)S(1)}, u32[]{:S(2)}, u32[]{:S(2)}) collective-permute-start(bf16[16,2176]{1,0:T(8,128)(2,1)S(1)} %pack.1.source_ref), channel_id=1, source_target_pairs={{0,8},{1,9},{2,10},{3,11},{4,12},{5,13},{6,14},{7,15},{8,0},{9,1},... | collective-permute-start | bytes 208904 | tf_op jit(solution)/shard_map/ppermute | solution.py:124
  5.2 6.7 %collective-permute-start.2 = (bf16[16,2176]{1,0:T(8,128)(2,1)S(1)}, bf16[16,2176]{1,0:T(8,128)(2,1)S(1)}, u32[]{:S(2)}, u32[]{:S(2)}) collective-permute-start(bf16[16,2176]{1,0:T(8,128)(2,1)S(1)} %again.1.refs_0_.refs_5_), channel_id=1, source_target_pairs={{0,6},{1,7},{2,4},{3,5},{4,2},{5,3},{6,0},{7,1},{8,14},{9,15},{10,... | collective-permute-start | bytes 208904 | tf_op jit(solution)/shard_map/ppermute | solution.py:124
  7.7 6.1 %collective-permute-start.3 = (bf16[16,2176]{1,0:T(8,128)(2,1)S(1)}, bf16[16,2176]{1,0:T(8,128)(2,1)S(1)}, u32[]{:S(2)}, u32[]{:S(2)}) collective-permute-start(bf16[16,2176]{1,0:T(8,128)(2,1)S(1)} %again.1.refs_0_.refs_5_), channel_id=1, source_target_pairs={{0,4},{1,5},{2,6},{3,7},{4,0},{5,1},{6,2},{7,3},{8,12},{9,13},{10,... | collective-permute-start | bytes 208904 | tf_op jit(solution)/shard_map/ppermute | solution.py:124
  8.4 5.4 %collective-permute-start.6 = (bf16[16,2176]{1,0:T(8,128)(2,1)S(1)}, bf16[16,2176]{1,0:T(8,128)(2,1)S(1)}, u32[]{:S(2)}, u32[]{:S(2)}) collective-permute-start(bf16[16,2176]{1,0:T(8,128)(2,1)S(1)} %collective-permute-done.5.refs_7_), channel_id=1, source_target_pairs={{0,2},{1,3},{2,0},{3,1},{4,6},{5,7},{6,4},{7,5},{8,10},{9,11},{10,... | collective-permute-start | bytes 208904 | tf_op jit(solution)/shard_map/ppermute | solution.py:124
  10.3 5.2 %collective-permute-start.7 = (bf16[16,2176]{1,0:T(8,128)(2,1)S(1)}, bf16[16,2176]{1,0:T(8,128)(2,1)S(1)}, u32[]{:S(2)}, u32[]{:S(2)}) collective-permute-start(bf16[16,2176]{1,0:T(8,128)(2,1)S(1)} %collective-permute-done.5.refs_7_), channel_id=1, source_target_pairs={{0,6},{1,7},{2,4},{3,5},{4,2},{5,3},{6,0},{7,1},{8,14},{9,15},{10,... | collective-permute-start | bytes 208904 | tf_op jit(solution)/shard_map/ppermute | solution.py:124
  11.6 4.3 %collective-permute-start.8 = (bf16[16,2176]{1,0:T(8,128)(2,1)S(1)}, bf16[16,2176]{1,0:T(8,128)(2,1)S(1)}, u32[]{:S(2)}, u32[]{:S(2)}) collective-permute-start(bf16[16,2176]{1,0:T(8,128)(2,1)S(1)} %collective-permute-done.5.refs_7_), channel_id=1, source_target_pairs={{0,4},{1,5},{2,6},{3,7},{4,0},{5,1},{6,2},{7,3},{8,12},{9,13},{10,... | collective-permute-start | bytes 208904 | tf_op jit(solution)/shard_map/ppermute | solution.py:124
  11.9 4.3 %collective-permute-start = (bf16[16,2176]{1,0:T(8,128)(2,1)S(1)}, bf16[16,2176]{1,0:T(8,128)(2,1)S(1)}, u32[]{:S(2)}, u32[]{:S(2)}) collective-permute-start(bf16[16,2176]{1,0:T(8,128)(2,1)S(1)} %again.1.refs_0_.refs_5_), channel_id=1, source_target_pairs={{0,2},{1,3},{2,0},{3,1},{4,6},{5,7},{6,4},{7,5},{8,10},{9,11},{10,... | collective-permute-start | bytes 208904 | tf_op jit(solution)/shard_map/ppermute | solution.py:124
  13.7 2.7 %collective-permute-start.13 = (bf16[16,2176]{1,0:T(8,128)(2,1)S(1)}, bf16[16,2176]{1,0:T(8,128)(2,1)S(1)}, u32[]{:S(2)}, u32[]{:S(2)}) collective-permute-start(bf16[16,2176]{1,0:T(8,128)(2,1)S(1)} %collective-permute-done.5.refs_7_), channel_id=1, source_target_pairs={{0,1},{1,0},{2,3},{3,2},{4,5},{5,4},{6,7},{7,6},{8,9},{9,8},{10,11... | collective-permute-start | bytes 208904 | tf_op jit(solution)/shard_map/ppermute | solution.py:127
  13.8 3.1 %collective-permute-start.14 = (bf16[16,2176]{1,0:T(8,128)(2,1)S(1)}, bf16[16,2176]{1,0:T(8,128)(2,1)S(1)}, u32[]{:S(2)}, u32[]{:S(2)}) collective-permute-start(bf16[16,2176]{1,0:T(8,128)(2,1)S(1)} %collective-permute-done.6.refs_9_.refs_8_), channel_id=1, source_target_pairs={{0,1},{1,0},{2,3},{3,2},{4,5},{5,4},{6,7},{7,6},{8,9},{9,8},{10,11... | collective-permute-start | bytes 208904 | tf_op jit(solution)/shard_map/ppermute | solution.py:127
  15.5 1.4 %collective-permute-start.15 = (bf16[16,2176]{1,0:T(8,128)(2,1)S(1)}, bf16[16,2176]{1,0:T(8,128)(2,1)S(1)}, u32[]{:S(2)}, u32[]{:S(2)}) collective-permute-start(bf16[16,2176]{1,0:T(8,128)(2,1)S(1)} %collective-permute-done.7.refs_10_.refs_9_), channel_id=1, source_target_pairs={{0,1},{1,0},{2,3},{3,2},{4,5},{5,4},{6,7},{7,6},{8,9},{9,8},{10,11... | collective-permute-start | bytes 208904 | tf_op jit(solution)/shard_map/ppermute | solution.py:127
  15.9 1.3 %collective-permute-start.16 = (bf16[16,2176]{1,0:T(8,128)(2,1)S(1)}, bf16[16,2176]{1,0:T(8,128)(2,1)S(1)}, u32[]{:S(2)}, u32[]{:S(2)}) collective-permute-start(bf16[16,2176]{1,0:T(8,128)(2,1)S(1)} %collective-permute-done.8.refs_11_.refs_10_), channel_id=1, source_target_pairs={{0,1},{1,0},{2,3},{3,2},{4,5},{5,4},{6,7},{7,6},{8,9},{9,8},{10,11... | collective-permute-start | bytes 208904 | tf_op jit(solution)/shard_map/ppermute | solution.py:127
  16.2 2.7 %collective-permute-start.4 = (bf16[32,2176]{1,0:T(8,128)(2,1)S(1)}, bf16[32,2176]{1,0:T(8,128)(2,1)S(1)}, u32[]{:S(2)}, u32[]{:S(2)}) collective-permute-start(bf16[32,2176]{1,0:T(8,128)(2,1)S(1)} %join.3), channel_id=1, source_target_pairs={{0,1},{1,0},{2,3},{3,2},{4,5},{5,4},{6,7},{7,6},{8,9},{9,8},{10,11... | collective-permute-start | bytes 417800 | tf_op jit(solution)/shard_map/ppermute | solution.py:127
  16.5 2.4 %collective-permute-start.1 = (bf16[32,2176]{1,0:T(8,128)(2,1)S(1)}, bf16[32,2176]{1,0:T(8,128)(2,1)S(1)}, u32[]{:S(2)}, u32[]{:S(2)}) collective-permute-start(bf16[32,2176]{1,0:T(8,128)(2,1)S(1)} %join.2), channel_id=1, source_target_pairs={{0,1},{1,0},{2,3},{3,2},{4,5},{5,4},{6,7},{7,6},{8,9},{9,8},{10,11... | collective-permute-start | bytes 417800 | tf_op jit(solution)/shard_map/ppermute | solution.py:127
  18.7 15.2 %copy-start.3 = (bf16[16,2048]{1,0:T(8,128)(2,1)S(1)}, bf16[16,2048]{1,0:T(8,128)(2,1)}, u32[]{:S(2)}) copy-start(bf16[16,2048]{1,0:T(8,128)(2,1)} %refs_0_.5) | copy-start | bytes 196612
  18.7 2.2 %collective-permute-start.17 = (bf16[64,2048]{1,0:T(8,128)(2,1)S(1)}, bf16[64,2048]{1,0:T(8,128)(2,1)S(1)}, u32[]{:S(2)}, u32[]{:S(2)}) collective-permute-start(bf16[64,2048]{1,0:T(8,128)(2,1)S(1)} %get-tuple-element.24), channel_id=1, source_target_pairs={{0,1},{1,0},{2,3},{3,2},{4,5},{5,4},{6,7},{7,6},{8,9},{9,8},{10,11... | collective-permute-start | bytes 786440 | tf_op jit(solution)/shard_map/ppermute | solution.py:127
  20.4 4.1 %collective-permute-start.9 = (bf16[64,2048]{1,0:T(8,128)(2,1)S(1)}, bf16[64,2048]{1,0:T(8,128)(2,1)S(1)}, u32[]{:S(2)}, u32[]{:S(2)}) collective-permute-start(bf16[64,2048]{1,0:T(8,128)(2,1)S(1)} %get-tuple-element.18), channel_id=1, source_target_pairs={{0,1},{1,0},{2,3},{3,2},{4,5},{5,4},{6,7},{7,6},{8,9},{9,8},{10,11... | collective-permute-start | bytes 786440 | tf_op jit(solution)/shard_map/ppermute | solution.py:127
  20.9 6.5 %collective-permute-start.18 = (bf16[16,2048]{1,0:T(8,128)(2,1)S(1)}, bf16[16,2048]{1,0:T(8,128)(2,1)S(1)}, u32[]{:S(2)}, u32[]{:S(2)}) collective-permute-start(bf16[16,2048]{1,0:T(8,128)(2,1)S(1)} %get-tuple-element.26), channel_id=1, source_target_pairs={{0,2},{1,3},{2,0},{3,1},{4,6},{5,7},{6,4},{7,5},{8,10},{9,11},{10,... | collective-permute-start | bytes 196616 | tf_op jit(solution)/shard_map/ppermute | solution.py:124
  22.5 5.7 %collective-permute-start.19 = (bf16[16,2048]{1,0:T(8,128)(2,1)S(1)}, bf16[16,2048]{1,0:T(8,128)(2,1)S(1)}, u32[]{:S(2)}, u32[]{:S(2)}) collective-permute-start(bf16[16,2048]{1,0:T(8,128)(2,1)S(1)} %get-tuple-element.27), channel_id=1, source_target_pairs={{0,6},{1,7},{2,4},{3,5},{4,2},{5,3},{6,0},{7,1},{8,14},{9,15},{10,... | collective-permute-start | bytes 196616 | tf_op jit(solution)/shard_map/ppermute | solution.py:124
  23.8 4.7 %collective-permute-start.20 = (bf16[16,2048]{1,0:T(8,128)(2,1)S(1)}, bf16[16,2048]{1,0:T(8,128)(2,1)S(1)}, u32[]{:S(2)}, u32[]{:S(2)}) collective-permute-start(bf16[16,2048]{1,0:T(8,128)(2,1)S(1)} %get-tuple-element.28), channel_id=1, source_target_pairs={{0,4},{1,5},{2,6},{3,7},{4,0},{5,1},{6,2},{7,3},{8,12},{9,13},{10,... | collective-permute-start | bytes 196616 | tf_op jit(solution)/shard_map/ppermute | solution.py:124
  24.5 7.0 %collective-permute-start.10 = (bf16[16,2048]{1,0:T(8,128)(2,1)S(1)}, bf16[16,2048]{1,0:T(8,128)(2,1)S(1)}, u32[]{:S(2)}, u32[]{:S(2)}) collective-permute-start(bf16[16,2048]{1,0:T(8,128)(2,1)S(1)} %get-tuple-element.20), channel_id=1, source_target_pairs={{0,2},{1,3},{2,0},{3,1},{4,6},{5,7},{6,4},{7,5},{8,10},{9,11},{10,... | collective-permute-start | bytes 196616 | tf_op jit(solution)/shard_map/ppermute | solution.py:124
  26.1 5.4 %collective-permute-start.11 = (bf16[16,2048]{1,0:T(8,128)(2,1)S(1)}, bf16[16,2048]{1,0:T(8,128)(2,1)S(1)}, u32[]{:S(2)}, u32[]{:S(2)}) collective-permute-start(bf16[16,2048]{1,0:T(8,128)(2,1)S(1)} %get-tuple-element.21), channel_id=1, source_target_pairs={{0,6},{1,7},{2,4},{3,5},{4,2},{5,3},{6,0},{7,1},{8,14},{9,15},{10,... | collective-permute-start | bytes 196616 | tf_op jit(solution)/shard_map/ppermute | solution.py:124
  27.5 5.0 %collective-permute-start.12 = (bf16[16,2048]{1,0:T(8,128)(2,1)S(1)}, bf16[16,2048]{1,0:T(8,128)(2,1)S(1)}, u32[]{:S(2)}, u32[]{:S(2)}) collective-permute-start(bf16[16,2048]{1,0:T(8,128)(2,1)S(1)} %get-tuple-element.22), channel_id=1, source_target_pairs={{0,4},{1,5},{2,6},{3,7},{4,0},{5,1},{6,2},{7,3},{8,12},{9,13},{10,... | collective-permute-start | bytes 196616 | tf_op jit(solution)/shard_map/ppermute | solution.py:124
  28.6 5.3 %collective-permute-start.21 = (bf16[16,2048]{1,0:T(8,128)(2,1)S(1)}, bf16[16,2048]{1,0:T(8,128)(2,1)S(1)}, u32[]{:S(2)}, u32[]{:S(2)}) collective-permute-start(bf16[16,2048]{1,0:T(8,128)(2,1)S(1)} %cross.1), channel_id=1, source_target_pairs={{0,8},{1,9},{2,10},{3,11},{4,12},{5,13},{6,14},{7,15},{8,0},{9,1},... | collective-permute-start | bytes 196616 | tf_op jit(solution)/shard_map/ppermute | solution.py:124

commit v8 on v7

--- a/solution.py
+++ b/solution.py
@@ -15,7 +15,7 @@
     return pltpu.with_memory_space_constraint(array, pltpu.HBM)
 
 
-def pack_kernel(token_ref, weight_hbm, replica_hbm, out_ref, weight_ref, replica_ref, sems):
+def pack_kernel(slot_count, token_ref, weight_hbm, replica_hbm, out_ref, weight_ref, replica_ref, sems):
     width = token_ref.shape[1]
     copies = [
         pltpu.make_async_copy(weight_hbm, weight_ref, sems.at[0]),
@@ -29,15 +29,14 @@
     weight = weight_ref[...]
     probability = weight / jnp.sum(weight, axis=0, keepdims=True)
     top_count, row_count = weight.shape
-    slot = lax.broadcasted_iota(jnp.int32, (LANES // 2, row_count), 0)
-    dense = jnp.zeros((LANES // 2, row_count), jnp.float32)
+    slot = lax.broadcasted_iota(jnp.int32, (slot_count, row_count), 0)
+    dense = jnp.zeros((slot_count, row_count), jnp.float32)
     for k in range(top_count):
         dense += jnp.where(replica_ref[k : k + 1, :] == slot, probability[k : k + 1, :], 0.0)
     high = dense.astype(jnp.bfloat16).astype(jnp.float32)
-    low = dense - high
-    both = jnp.concatenate([high, low], axis=0)
-    both = jnp.concatenate([both, jnp.zeros((LANES, LANES - row_count), jnp.float32)], axis=1)
-    out_ref[:, width:] = both.T[:row_count].astype(jnp.bfloat16)
+    both = jnp.concatenate([high, dense - high], axis=0).T
+    rest = jnp.zeros((row_count, LANES - 2 * slot_count), jnp.float32)
+    out_ref[:, width:] = jnp.concatenate([both, rest], axis=1).astype(jnp.bfloat16)
     copies[2].wait()
 
 
@@ -56,7 +55,7 @@
         rows_ref[at, :] = block[:, :width]
         extra = block[:, width:].astype(jnp.float32)
         lane = lax.broadcasted_iota(jnp.int32, extra.shape, 1)
-        chosen = (lane == slot) | (lane == slot + LANES // 2)
+        chosen = (lane == slot) | (lane == slot + lax.axis_size("expert"))
         share = jnp.sum(jnp.where(chosen, extra, 0.0), axis=1, keepdims=True)
         share_ref[at, :] = jnp.broadcast_to(share, (row_count, LANES))
     rows = rows_ref[...]
@@ -152,7 +151,7 @@
         return on_core(sum_kernel, name, shape(row_count, wide), [VMEM] * len(terms))(*terms)
 
     packed = on_core(
-        pack_kernel,
+        functools.partial(pack_kernel, peer_count),
         "pack",
         shape(row_count, wide, width + LANES),
         [HBM] * 3,
@@ -164,7 +163,7 @@
         flops=10**10,
     )(*map(in_hbm, (tokens, route_weight.T, replica.T)))
     crossed = partner(packed, half)
-    again = on_core(again_kernel, "again", shape(row_count, wide, width + LANES), [VMEM], flops=10**9)(packed)
+    again = on_core(again_kernel, "again", shape(row_count, wide, width + LANES), [VMEM], flops=10**10)(packed)
     order = [1, *range(half - 1, 1, -1)]
     near = [again] + [partner(again, k) for k in order]
     far = [crossed] + [partner(crossed, k) for k in order]

time: 34.6 us -> 34.5 us (level)
  no operation moved by 1% of the time
where the time goes in v8:
time: 34.5 us; the launch traced here: 34.4 us
  starting transfers between devices  24.4 us (71%)
  waiting for transfers between devices  5.09 us (15%)
  Pallas kernels  4.78 us (14%)
    ppermute x14, starting transfers between devices, partner(): lax.ppermute(array, 'expert', [(i, i ^ 2 * k) for i in range(peer_count)])  22.5 us
    ppermute x14, waiting for transfers between devices, partner(): lax.ppermute(array, 'expert', [(i, i ^ 2 * k) for i in range(peer_count)])  4.75 us
    pallas_call x2, Pallas kernels, experts(): on_core(functools.partial(expert_kernel, len(blocks)), name, (shape(half_...  3.02 us
    ppermute x8, starting transfers between devices, swap(): lax.ppermute(array, 'expert', [(i, i ^ 1) for i in range(peer_count)])  1.82 us
    pallas_call x1, Pallas kernels, dense_shards(): on_core(functools.partial(pack_kernel, peer_count), 'pack', shape(row_cou...  0.9 us
    pallas_call x2, Pallas kernels, total(): on_core(sum_kernel, name, shape(row_count, wide), [VMEM] * len(terms))  0.71 us
  transfers between devices with their start and end apart: 22, of which 9 were waited for; matrix products, arithmetic and copies ran while one was open for 0% of the time, Pallas kernels for 9%

profile of v8, /device:TPU:0, one launch (start us, length us, event | category | flops | bytes accessed | tf_op | source)
XLA Modules:
  0.0 34.4 jit_solution(11664439889285400227)
XLA Ops:
  0.0 0.9 %pack.1.source_ref = bf16[16,2176]{1,0:T(8,128)(2,1)S(1)} custom-call(bf16[16,2048]{1,0:T(8,128)(2,1)} %refs_0_.5, f32[8,16]{1,0:T(8,128)} %bitcast.2, s32[8,16]{1,0:T(8,128)} %bitcast.3), custom_call_target="tpu_custom_call" | custom-call | flops 10000000000 | bytes 2441406 | tf_op jit(solution)/shard_map/pack/pallas_call | solution.py:153
  0.9 0.0 copy-start
  0.9 0.0 copy-start.1
  0.9 0.0 copy-start.2
  0.9 4.1 %collective-permute-start.5 = (bf16[16,2176]{1,0:T(8,128)(2,1)S(1)}, bf16[16,2176]{1,0:T(8,128)(2,1)S(1)}, u32[]{:S(2)}, u32[]{:S(2)}) collective-permute-start(bf16[16,2176]{1,0:T(8,128)(2,1)S(1)} %pack.1.source_ref), channel_id=1, source_target_pairs={{0,8},{1,9},{2,10},{3,11},{4,12},{5,13},{6,14},{7,15},{8,0},{9,1},... | collective-permute-start | bytes 208904 | tf_op jit(solution)/shard_map/ppermute | solution.py:123
  5.0 2.5 %collective-permute-start.2 = (bf16[16,2176]{1,0:T(8,128)(2,1)S(1)}, bf16[16,2176]{1,0:T(8,128)(2,1)S(1)}, u32[]{:S(2)}, u32[]{:S(2)}) collective-permute-start(bf16[16,2176]{1,0:T(8,128)(2,1)S(1)} %again.1.refs_0_.refs_5_), channel_id=1, source_target_pairs={{0,6},{1,7},{2,4},{3,5},{4,2},{5,3},{6,0},{7,1},{8,14},{9,15},{10,... | collective-permute-start | bytes 208904 | tf_op jit(solution)/shard_map/ppermute | solution.py:123
  7.6 0.4 %collective-permute-start.3 = (bf16[16,2176]{1,0:T(8,128)(2,1)S(1)}, bf16[16,2176]{1,0:T(8,128)(2,1)S(1)}, u32[]{:S(2)}, u32[]{:S(2)}) collective-permute-start(bf16[16,2176]{1,0:T(8,128)(2,1)S(1)} %again.1.refs_0_.refs_5_), channel_id=1, source_target_pairs={{0,4},{1,5},{2,6},{3,7},{4,0},{5,1},{6,2},{7,3},{8,12},{9,13},{10,... | collective-permute-start | bytes 208904 | tf_op jit(solution)/shard_map/ppermute | solution.py:123
  8.0 0.2 collective-permute-done.5.refs_7_
  8.2 1.9 %collective-permute-start.6 = (bf16[16,2176]{1,0:T(8,128)(2,1)S(1)}, bf16[16,2176]{1,0:T(8,128)(2,1)S(1)}, u32[]{:S(2)}, u32[]{:S(2)}) collective-permute-start(bf16[16,2176]{1,0:T(8,128)(2,1)S(1)} %collective-permute-done.5.refs_7_), channel_id=1, source_target_pairs={{0,2},{1,3},{2,0},{3,1},{4,6},{5,7},{6,4},{7,5},{8,10},{9,11},{10,... | collective-permute-start | bytes 208904 | tf_op jit(solution)/shard_map/ppermute | solution.py:123
  10.1 1.3 %collective-permute-start.7 = (bf16[16,2176]{1,0:T(8,128)(2,1)S(1)}, bf16[16,2176]{1,0:T(8,128)(2,1)S(1)}, u32[]{:S(2)}, u32[]{:S(2)}) collective-permute-start(bf16[16,2176]{1,0:T(8,128)(2,1)S(1)} %collective-permute-done.5.refs_7_), channel_id=1, source_target_pairs={{0,6},{1,7},{2,4},{3,5},{4,2},{5,3},{6,0},{7,1},{8,14},{9,15},{10,... | collective-permute-start | bytes 208904 | tf_op jit(solution)/shard_map/ppermute | solution.py:123
  11.4 0.3 collective-permute-start.8
  11.7 0.0 collective-permute-done.2.refs_0_.refs_7_
  11.7 1.9 %collective-permute-start = (bf16[16,2176]{1,0:T(8,128)(2,1)S(1)}, bf16[16,2176]{1,0:T(8,128)(2,1)S(1)}, u32[]{:S(2)}, u32[]{:S(2)}) collective-permute-start(bf16[16,2176]{1,0:T(8,128)(2,1)S(1)} %again.1.refs_0_.refs_5_), channel_id=1, source_target_pairs={{0,2},{1,3},{2,0},{3,1},{4,6},{5,7},{6,4},{7,5},{8,10},{9,11},{10,... | collective-permute-start | bytes 208904 | tf_op jit(solution)/shard_map/ppermute | solution.py:123
  13.6 0.0 collective-permute-done.3.refs_1_.refs_8_
  13.6 0.0 collective-permute-start.13
  13.6 0.0 collective-permute-done.6.refs_9_.refs_8_
  13.6 0.5 %collective-permute-start.14 = (bf16[16,2176]{1,0:T(8,128)(2,1)S(1)}, bf16[16,2176]{1,0:T(8,128)(2,1)S(1)}, u32[]{:S(2)}, u32[]{:S(2)}) collective-permute-start(bf16[16,2176]{1,0:T(8,128)(2,1)S(1)} %collective-permute-done.6.refs_9_.refs_8_), channel_id=1, source_target_pairs={{0,1},{1,0},{2,3},{3,2},{4,5},{5,4},{6,7},{7,6},{8,9},{9,8},{10,11... | collective-permute-start | bytes 208904 | tf_op jit(solution)/shard_map/ppermute | solution.py:126
  14.1 1.2 %collective-permute-done.7.refs_10_.refs_9_ = bf16[16,2176]{1,0:T(8,128)(2,1)S(1)} collective-permute-done((bf16[16,2176]{1,0:T(8,128)(2,1)S(1)}, bf16[16,2176]{1,0:T(8,128)(2,1)S(1)}, u32[]{:S(2)}, u32[]{:S(2)}) %collective-permute-start.7) | collective-permute-done | bytes 69664 | tf_op jit(solution)/shard_map/ppermute | solution.py:123
  15.3 0.0 collective-permute-start.15
  15.3 0.4 %collective-permute-done.8.refs_11_.refs_10_ = bf16[16,2176]{1,0:T(8,128)(2,1)S(1)} collective-permute-done((bf16[16,2176]{1,0:T(8,128)(2,1)S(1)}, bf16[16,2176]{1,0:T(8,128)(2,1)S(1)}, u32[]{:S(2)}, u32[]{:S(2)}) %collective-permute-start.8) | collective-permute-done | bytes 69664 | tf_op jit(solution)/shard_map/ppermute | solution.py:123
  15.7 0.1 collective-permute-start.16
  15.9 0.2 collective-permute-done.refs_1_.refs_6_
  16.1 0.3 collective-permute-start.4
  16.4 0.0 collective-permute-done.13.refs_3_
  16.4 0.3 collective-permute-start.1
  16.7 0.0 collective-permute-done.14.refs_4_
  16.7 0.0 collective-permute-done.15.refs_5_
  16.7 0.3 collective-permute-done.16.refs_6_
  17.0 0.0 copy-done
  17.0 0.0 copy-done.1
  17.0 0.0 copy-done.2
  17.0 1.5 %far.1 = (bf16[64,2048]{1,0:T(8,128)(2,1)S(1)}, f32[64,2048]{1,0:T(8,128)S(1)}) custom-call(bf16[1,2048,768]{2,1,0:T(8,128)(2,1)S(1)} %copy-done, bf16[1,2048,768]{2,1,0:T(8,128)(2,1)S(1)} %copy-done.1, bf16[1,768,2048]{2,1,0:T(8,128)(2,1)S(1)} %copy-done.2, bf16[16,2176]{1,0:T(8,128)(2,1)S(1)} %collective-permute-done.13.refs_3_, ...), custom_call_target="tpu_custom_call" | custom-call | flops 1000000000 | bytes 244140 | tf_op jit(solution)/shard_map/far/pallas_call | solution.py:132
  18.5 0.0 copy-start.3
  18.5 0.2 collective-permute-start.17
  18.8 0.0 collective-permute-done.4.refs_4_
  18.8 0.0 collective-permute-done.1.refs_3_
  18.8 1.5 %near.1 = (bf16[64,2048]{1,0:T(8,128)(2,1)S(1)}, f32[64,2048]{1,0:T(8,128)S(1)}) custom-call(bf16[1,2048,768]{2,1,0:T(8,128)(2,1)S(1)} %copy-done, bf16[1,2048,768]{2,1,0:T(8,128)(2,1)S(1)} %copy-done.1, bf16[1,768,2048]{2,1,0:T(8,128)(2,1)S(1)} %copy-done.2, bf16[32,2176]{1,0:T(8,128)(2,1)S(1)} %collective-permute-done.1.refs_3_, ...), custom_call_target="tpu_custom_call" | custom-call | flops 1000000000 | bytes 244140 | tf_op jit(solution)/shard_map/near/pallas_call | solution.py:132
  20.3 0.4 %collective-permute-start.9 = (bf16[64,2048]{1,0:T(8,128)(2,1)S(1)}, bf16[64,2048]{1,0:T(8,128)(2,1)S(1)}, u32[]{:S(2)}, u32[]{:S(2)}) collective-permute-start(bf16[64,2048]{1,0:T(8,128)(2,1)S(1)} %get-tuple-element.18), channel_id=1, source_target_pairs={{0,1},{1,0},{2,3},{3,2},{4,5},{5,4},{6,7},{7,6},{8,9},{9,8},{10,11... | collective-permute-start | bytes 786440 | tf_op jit(solution)/shard_map/ppermute | solution.py:126
  20.7 0.0 collective-permute-done.17.other_ref
  20.7 0.1 pair.3
  20.8 1.6 %collective-permute-start.18 = (bf16[16,2048]{1,0:T(8,128)(2,1)S(1)}, bf16[16,2048]{1,0:T(8,128)(2,1)S(1)}, u32[]{:S(2)}, u32[]{:S(2)}) collective-permute-start(bf16[16,2048]{1,0:T(8,128)(2,1)S(1)} %get-tuple-element.26), channel_id=1, source_target_pairs={{0,2},{1,3},{2,0},{3,1},{4,6},{5,7},{6,4},{7,5},{8,10},{9,11},{10,... | collective-permute-start | bytes 196616 | tf_op jit(solution)/shard_map/ppermute | solution.py:123
  22.4 1.3 %collective-permute-start.19 = (bf16[16,2048]{1,0:T(8,128)(2,1)S(1)}, bf16[16,2048]{1,0:T(8,128)(2,1)S(1)}, u32[]{:S(2)}, u32[]{:S(2)}) collective-permute-start(bf16[16,2048]{1,0:T(8,128)(2,1)S(1)} %get-tuple-element.27), channel_id=1, source_target_pairs={{0,6},{1,7},{2,4},{3,5},{4,2},{5,3},{6,0},{7,1},{8,14},{9,15},{10,... | collective-permute-start | bytes 196616 | tf_op jit(solution)/shard_map/ppermute | solution.py:123
  23.7 0.6 %collective-permute-start.20 = (bf16[16,2048]{1,0:T(8,128)(2,1)S(1)}, bf16[16,2048]{1,0:T(8,128)(2,1)S(1)}, u32[]{:S(2)}, u32[]{:S(2)}) collective-permute-start(bf16[16,2048]{1,0:T(8,128)(2,1)S(1)} %get-tuple-element.28), channel_id=1, source_target_pairs={{0,4},{1,5},{2,6},{3,7},{4,0},{5,1},{6,2},{7,3},{8,12},{9,13},{10,... | collective-permute-start | bytes 196616 | tf_op jit(solution)/shard_map/ppermute | solution.py:123
  24.3 0.0 collective-permute-done.9.other_ref
  24.3 0.1 pair.2
  24.4 1.6 %collective-permute-start.10 = (bf16[16,2048]{1,0:T(8,128)(2,1)S(1)}, bf16[16,2048]{1,0:T(8,128)(2,1)S(1)}, u32[]{:S(2)}, u32[]{:S(2)}) collective-permute-start(bf16[16,2048]{1,0:T(8,128)(2,1)S(1)} %get-tuple-element.20), channel_id=1, source_target_pairs={{0,2},{1,3},{2,0},{3,1},{4,6},{5,7},{6,4},{7,5},{8,10},{9,11},{10,... | collective-permute-start | bytes 196616 | tf_op jit(solution)/shard_map/ppermute | solution.py:123
  26.0 1.3 %collective-permute-start.11 = (bf16[16,2048]{1,0:T(8,128)(2,1)S(1)}, bf16[16,2048]{1,0:T(8,128)(2,1)S(1)}, u32[]{:S(2)}, u32[]{:S(2)}) collective-permute-start(bf16[16,2048]{1,0:T(8,128)(2,1)S(1)} %get-tuple-element.21), channel_id=1, source_target_pairs={{0,6},{1,7},{2,4},{3,5},{4,2},{5,3},{6,0},{7,1},{8,14},{9,15},{10,... | collective-permute-start | bytes 196616 | tf_op jit(solution)/shard_map/ppermute | solution.py:123
  27.3 0.0 collective-permute-done.18.refs_1_
  27.3 0.6 %collective-permute-start.12 = (bf16[16,2048]{1,0:T(8,128)(2,1)S(1)}, bf16[16,2048]{1,0:T(8,128)(2,1)S(1)}, u32[]{:S(2)}, u32[]{:S(2)}) collective-permute-start(bf16[16,2048]{1,0:T(8,128)(2,1)S(1)} %get-tuple-element.22), channel_id=1, source_target_pairs={{0,4},{1,5},{2,6},{3,7},{4,0},{5,1},{6,2},{7,3},{8,12},{9,13},{10,... | collective-permute-start | bytes 196616 | tf_op jit(solution)/shard_map/ppermute | solution.py:123
  28.0 0.2 collective-permute-done.19.refs_2_
  28.1 0.2 collective-permute-done.20.refs_3_
  28.4 3.0 %collective-permute-start.21 = (bf16[16,2048]{1,0:T(8,128)(2,1)S(1)}, bf16[16,2048]{1,0:T(8,128)(2,1)S(1)}, u32[]{:S(2)}, u32[]{:S(2)}) collective-permute-start(bf16[16,2048]{1,0:T(8,128)(2,1)S(1)} %cross.1), channel_id=1, source_target_pairs={{0,8},{1,9},{2,10},{3,11},{4,12},{5,13},{6,14},{7,15},{8,0},{9,1},... | collective-permute-start | bytes 196616 | tf_op jit(solution)/shard_map/ppermute | solution.py:123
  31.4 0.0 collective-permute-done.10.refs_2_
  31.4 0.0 collective-permute-done.11.refs_3_
  31.4 0.9 %collective-permute-done.12.refs_4_ = bf16[16,2048]{1,0:T(8,128)(2,1)S(1)} collective-permute-done((bf16[16,2048]{1,0:T(8,128)(2,1)S(1)}, bf16[16,2048]{1,0:T(8,128)(2,1)S(1)}, u32[]{:S(2)}, u32[]{:S(2)}) %collective-permute-start.12) | collective-permute-done | bytes 65568 | tf_op jit(solution)/shard_map/ppermute | solution.py:123
  32.3 1.4 %collective-permute-done.21.refs_5_ = bf16[16,2048]{1,0:T(8,128)(2,1)S(1)} collective-permute-done((bf16[16,2048]{1,0:T(8,128)(2,1)S(1)}, bf16[16,2048]{1,0:T(8,128)(2,1)S(1)}, u32[]{:S(2)}, u32[]{:S(2)}) %collective-permute-start.21) | collective-permute-done | bytes 65568 | tf_op jit(solution)/shard_map/ppermute | solution.py:123
  33.7 0.0 copy-done.3
  33.7 0.7 %mix.1 = bf16[16,2048]{1,0:T(8,128)(2,1)} custom-call(bf16[16,2048]{1,0:T(8,128)(2,1)S(1)} %copy-done.3, f32[16,2048]{1,0:T(8,128)S(1)} %get-tuple-element.19.refs_1_, bf16[16,2048]{1,0:T(8,128)(2,1)S(1)} %collective-permute-done.10.refs_2_, bf16[16,2048]{1,0:T(8,128)(2,1)S(1)} %collective-permute-done.11.refs_3_, ...), custom_call_target="tpu_custom_call" | custom-call | tf_op jit(solution)/shard_map/mix/pallas_call | solution.py:151
  (4 shorter events, 0.1 us)
Async XLA Ops:
  0.9 16.1 %copy-start = (bf16[1,2048,768]{2,1,0:T(8,128)(2,1)S(1)}, bf16[1,2048,768]{2,1,0:T(8,128)(2,1)}, u32[]{:S(2)}) copy-start(bf16[1,2048,768]{2,1,0:T(8,128)(2,1)} %refs_0_.4) | copy-start | bytes 9437188
  0.9 16.1 %copy-start.1 = (bf16[1,2048,768]{2,1,0:T(8,128)(2,1)S(1)}, bf16[1,2048,768]{2,1,0:T(8,128)(2,1)}, u32[]{:S(2)}) copy-start(bf16[1,2048,768]{2,1,0:T(8,128)(2,1)} %refs_1_.3) | copy-start | bytes 9437188
  0.9 16.1 %copy-start.2 = (bf16[1,768,2048]{2,1,0:T(8,128)(2,1)S(1)}, bf16[1,768,2048]{2,1,0:T(8,128)(2,1)}, u32[]{:S(2)}) copy-start(bf16[1,768,2048]{2,1,0:T(8,128)(2,1)} %refs_2_.3) | copy-start | bytes 9437188
  0.9 7.3 %collective-permute-start.5 = (bf16[16,2176]{1,0:T(8,128)(2,1)S(1)}, bf16[16,2176]{1,0:T(8,128)(2,1)S(1)}, u32[]{:S(2)}, u32[]{:S(2)}) collective-permute-start(bf16[16,2176]{1,0:T(8,128)(2,1)S(1)} %pack.1.source_ref), channel_id=1, source_target_pairs={{0,8},{1,9},{2,10},{3,11},{4,12},{5,13},{6,14},{7,15},{8,0},{9,1},... | collective-permute-start | bytes 208904 | tf_op jit(solution)/shard_map/ppermute | solution.py:123
  5.0 6.7 %collective-permute-start.2 = (bf16[16,2176]{1,0:T(8,128)(2,1)S(1)}, bf16[16,2176]{1,0:T(8,128)(2,1)S(1)}, u32[]{:S(2)}, u32[]{:S(2)}) collective-permute-start(bf16[16,2176]{1,0:T(8,128)(2,1)S(1)} %again.1.refs_0_.refs_5_), channel_id=1, source_target_pairs={{0,6},{1,7},{2,4},{3,5},{4,2},{5,3},{6,0},{7,1},{8,14},{9,15},{10,... | collective-permute-start | bytes 208904 | tf_op jit(solution)/shard_map/ppermute | solution.py:123
  7.6 6.1 %collective-permute-start.3 = (bf16[16,2176]{1,0:T(8,128)(2,1)S(1)}, bf16[16,2176]{1,0:T(8,128)(2,1)S(1)}, u32[]{:S(2)}, u32[]{:S(2)}) collective-permute-start(bf16[16,2176]{1,0:T(8,128)(2,1)S(1)} %again.1.refs_0_.refs_5_), channel_id=1, source_target_pairs={{0,4},{1,5},{2,6},{3,7},{4,0},{5,1},{6,2},{7,3},{8,12},{9,13},{10,... | collective-permute-start | bytes 208904 | tf_op jit(solution)/shard_map/ppermute | solution.py:123
  8.2 5.4 %collective-permute-start.6 = (bf16[16,2176]{1,0:T(8,128)(2,1)S(1)}, bf16[16,2176]{1,0:T(8,128)(2,1)S(1)}, u32[]{:S(2)}, u32[]{:S(2)}) collective-permute-start(bf16[16,2176]{1,0:T(8,128)(2,1)S(1)} %collective-permute-done.5.refs_7_), channel_id=1, source_target_pairs={{0,2},{1,3},{2,0},{3,1},{4,6},{5,7},{6,4},{7,5},{8,10},{9,11},{10,... | collective-permute-start | bytes 208904 | tf_op jit(solution)/shard_map/ppermute | solution.py:123
  10.1 5.2 %collective-permute-start.7 = (bf16[16,2176]{1,0:T(8,128)(2,1)S(1)}, bf16[16,2176]{1,0:T(8,128)(2,1)S(1)}, u32[]{:S(2)}, u32[]{:S(2)}) collective-permute-start(bf16[16,2176]{1,0:T(8,128)(2,1)S(1)} %collective-permute-done.5.refs_7_), channel_id=1, source_target_pairs={{0,6},{1,7},{2,4},{3,5},{4,2},{5,3},{6,0},{7,1},{8,14},{9,15},{10,... | collective-permute-start | bytes 208904 | tf_op jit(solution)/shard_map/ppermute | solution.py:123
  11.4 4.3 %collective-permute-start.8 = (bf16[16,2176]{1,0:T(8,128)(2,1)S(1)}, bf16[16,2176]{1,0:T(8,128)(2,1)S(1)}, u32[]{:S(2)}, u32[]{:S(2)}) collective-permute-start(bf16[16,2176]{1,0:T(8,128)(2,1)S(1)} %collective-permute-done.5.refs_7_), channel_id=1, source_target_pairs={{0,4},{1,5},{2,6},{3,7},{4,0},{5,1},{6,2},{7,3},{8,12},{9,13},{10,... | collective-permute-start | bytes 208904 | tf_op jit(solution)/shard_map/ppermute | solution.py:123
  11.7 4.3 %collective-permute-start = (bf16[16,2176]{1,0:T(8,128)(2,1)S(1)}, bf16[16,2176]{1,0:T(8,128)(2,1)S(1)}, u32[]{:S(2)}, u32[]{:S(2)}) collective-permute-start(bf16[16,2176]{1,0:T(8,128)(2,1)S(1)} %again.1.refs_0_.refs_5_), channel_id=1, source_target_pairs={{0,2},{1,3},{2,0},{3,1},{4,6},{5,7},{6,4},{7,5},{8,10},{9,11},{10,... | collective-permute-start | bytes 208904 | tf_op jit(solution)/shard_map/ppermute | solution.py:123
  13.6 2.7 %collective-permute-start.13 = (bf16[16,2176]{1,0:T(8,128)(2,1)S(1)}, bf16[16,2176]{1,0:T(8,128)(2,1)S(1)}, u32[]{:S(2)}, u32[]{:S(2)}) collective-permute-start(bf16[16,2176]{1,0:T(8,128)(2,1)S(1)} %collective-permute-done.5.refs_7_), channel_id=1, source_target_pairs={{0,1},{1,0},{2,3},{3,2},{4,5},{5,4},{6,7},{7,6},{8,9},{9,8},{10,11... | collective-permute-start | bytes 208904 | tf_op jit(solution)/shard_map/ppermute | solution.py:126
  13.6 3.1 %collective-permute-start.14 = (bf16[16,2176]{1,0:T(8,128)(2,1)S(1)}, bf16[16,2176]{1,0:T(8,128)(2,1)S(1)}, u32[]{:S(2)}, u32[]{:S(2)}) collective-permute-start(bf16[16,2176]{1,0:T(8,128)(2,1)S(1)} %collective-permute-done.6.refs_9_.refs_8_), channel_id=1, source_target_pairs={{0,1},{1,0},{2,3},{3,2},{4,5},{5,4},{6,7},{7,6},{8,9},{9,8},{10,11... | collective-permute-start | bytes 208904 | tf_op jit(solution)/shard_map/ppermute | solution.py:126
  15.3 1.4 %collective-permute-start.15 = (bf16[16,2176]{1,0:T(8,128)(2,1)S(1)}, bf16[16,2176]{1,0:T(8,128)(2,1)S(1)}, u32[]{:S(2)}, u32[]{:S(2)}) collective-permute-start(bf16[16,2176]{1,0:T(8,128)(2,1)S(1)} %collective-permute-done.7.refs_10_.refs_9_), channel_id=1, source_target_pairs={{0,1},{1,0},{2,3},{3,2},{4,5},{5,4},{6,7},{7,6},{8,9},{9,8},{10,11... | collective-permute-start | bytes 208904 | tf_op jit(solution)/shard_map/ppermute | solution.py:126
  15.7 1.3 %collective-permute-start.16 = (bf16[16,2176]{1,0:T(8,128)(2,1)S(1)}, bf16[16,2176]{1,0:T(8,128)(2,1)S(1)}, u32[]{:S(2)}, u32[]{:S(2)}) collective-permute-start(bf16[16,2176]{1,0:T(8,128)(2,1)S(1)} %collective-permute-done.8.refs_11_.refs_10_), channel_id=1, source_target_pairs={{0,1},{1,0},{2,3},{3,2},{4,5},{5,4},{6,7},{7,6},{8,9},{9,8},{10,11... | collective-permute-start | bytes 208904 | tf_op jit(solution)/shard_map/ppermute | solution.py:126
  16.1 2.7 %collective-permute-start.4 = (bf16[32,2176]{1,0:T(8,128)(2,1)S(1)}, bf16[32,2176]{1,0:T(8,128)(2,1)S(1)}, u32[]{:S(2)}, u32[]{:S(2)}) collective-permute-start(bf16[32,2176]{1,0:T(8,128)(2,1)S(1)} %join.3), channel_id=1, source_target_pairs={{0,1},{1,0},{2,3},{3,2},{4,5},{5,4},{6,7},{7,6},{8,9},{9,8},{10,11... | collective-permute-start | bytes 417800 | tf_op jit(solution)/shard_map/ppermute | solution.py:126
  16.4 2.4 %collective-permute-start.1 = (bf16[32,2176]{1,0:T(8,128)(2,1)S(1)}, bf16[32,2176]{1,0:T(8,128)(2,1)S(1)}, u32[]{:S(2)}, u32[]{:S(2)}) collective-permute-start(bf16[32,2176]{1,0:T(8,128)(2,1)S(1)} %join.2), channel_id=1, source_target_pairs={{0,1},{1,0},{2,3},{3,2},{4,5},{5,4},{6,7},{7,6},{8,9},{9,8},{10,11... | collective-permute-start | bytes 417800 | tf_op jit(solution)/shard_map/ppermute | solution.py:126
  18.5 15.2 %copy-start.3 = (bf16[16,2048]{1,0:T(8,128)(2,1)S(1)}, bf16[16,2048]{1,0:T(8,128)(2,1)}, u32[]{:S(2)}) copy-start(bf16[16,2048]{1,0:T(8,128)(2,1)} %refs_0_.5) | copy-start | bytes 196612
  18.5 2.2 %collective-permute-start.17 = (bf16[64,2048]{1,0:T(8,128)(2,1)S(1)}, bf16[64,2048]{1,0:T(8,128)(2,1)S(1)}, u32[]{:S(2)}, u32[]{:S(2)}) collective-permute-start(bf16[64,2048]{1,0:T(8,128)(2,1)S(1)} %get-tuple-element.24), channel_id=1, source_target_pairs={{0,1},{1,0},{2,3},{3,2},{4,5},{5,4},{6,7},{7,6},{8,9},{9,8},{10,11... | collective-permute-start | bytes 786440 | tf_op jit(solution)/shard_map/ppermute | solution.py:126
  20.3 4.0 %collective-permute-start.9 = (bf16[64,2048]{1,0:T(8,128)(2,1)S(1)}, bf16[64,2048]{1,0:T(8,128)(2,1)S(1)}, u32[]{:S(2)}, u32[]{:S(2)}) collective-permute-start(bf16[64,2048]{1,0:T(8,128)(2,1)S(1)} %get-tuple-element.18), channel_id=1, source_target_pairs={{0,1},{1,0},{2,3},{3,2},{4,5},{5,4},{6,7},{7,6},{8,9},{9,8},{10,11... | collective-permute-start | bytes 786440 | tf_op jit(solution)/shard_map/ppermute | solution.py:126
  20.8 6.6 %collective-permute-start.18 = (bf16[16,2048]{1,0:T(8,128)(2,1)S(1)}, bf16[16,2048]{1,0:T(8,128)(2,1)S(1)}, u32[]{:S(2)}, u32[]{:S(2)}) collective-permute-start(bf16[16,2048]{1,0:T(8,128)(2,1)S(1)} %get-tuple-element.26), channel_id=1, source_target_pairs={{0,2},{1,3},{2,0},{3,1},{4,6},{5,7},{6,4},{7,5},{8,10},{9,11},{10,... | collective-permute-start | bytes 196616 | tf_op jit(solution)/shard_map/ppermute | solution.py:123
  22.4 5.8 %collective-permute-start.19 = (bf16[16,2048]{1,0:T(8,128)(2,1)S(1)}, bf16[16,2048]{1,0:T(8,128)(2,1)S(1)}, u32[]{:S(2)}, u32[]{:S(2)}) collective-permute-start(bf16[16,2048]{1,0:T(8,128)(2,1)S(1)} %get-tuple-element.27), channel_id=1, source_target_pairs={{0,6},{1,7},{2,4},{3,5},{4,2},{5,3},{6,0},{7,1},{8,14},{9,15},{10,... | collective-permute-start | bytes 196616 | tf_op jit(solution)/shard_map/ppermute | solution.py:123
  23.7 4.7 %collective-permute-start.20 = (bf16[16,2048]{1,0:T(8,128)(2,1)S(1)}, bf16[16,2048]{1,0:T(8,128)(2,1)S(1)}, u32[]{:S(2)}, u32[]{:S(2)}) collective-permute-start(bf16[16,2048]{1,0:T(8,128)(2,1)S(1)} %get-tuple-element.28), channel_id=1, source_target_pairs={{0,4},{1,5},{2,6},{3,7},{4,0},{5,1},{6,2},{7,3},{8,12},{9,13},{10,... | collective-permute-start | bytes 196616 | tf_op jit(solution)/shard_map/ppermute | solution.py:123
  24.4 7.0 %collective-permute-start.10 = (bf16[16,2048]{1,0:T(8,128)(2,1)S(1)}, bf16[16,2048]{1,0:T(8,128)(2,1)S(1)}, u32[]{:S(2)}, u32[]{:S(2)}) collective-permute-start(bf16[16,2048]{1,0:T(8,128)(2,1)S(1)} %get-tuple-element.20), channel_id=1, source_target_pairs={{0,2},{1,3},{2,0},{3,1},{4,6},{5,7},{6,4},{7,5},{8,10},{9,11},{10,... | collective-permute-start | bytes 196616 | tf_op jit(solution)/shard_map/ppermute | solution.py:123
  26.0 5.4 %collective-permute-start.11 = (bf16[16,2048]{1,0:T(8,128)(2,1)S(1)}, bf16[16,2048]{1,0:T(8,128)(2,1)S(1)}, u32[]{:S(2)}, u32[]{:S(2)}) collective-permute-start(bf16[16,2048]{1,0:T(8,128)(2,1)S(1)} %get-tuple-element.21), channel_id=1, source_target_pairs={{0,6},{1,7},{2,4},{3,5},{4,2},{5,3},{6,0},{7,1},{8,14},{9,15},{10,... | collective-permute-start | bytes 196616 | tf_op jit(solution)/shard_map/ppermute | solution.py:123
  27.3 5.0 %collective-permute-start.12 = (bf16[16,2048]{1,0:T(8,128)(2,1)S(1)}, bf16[16,2048]{1,0:T(8,128)(2,1)S(1)}, u32[]{:S(2)}, u32[]{:S(2)}) collective-permute-start(bf16[16,2048]{1,0:T(8,128)(2,1)S(1)} %get-tuple-element.22), channel_id=1, source_target_pairs={{0,4},{1,5},{2,6},{3,7},{4,0},{5,1},{6,2},{7,3},{8,12},{9,13},{10,... | collective-permute-start | bytes 196616 | tf_op jit(solution)/shard_map/ppermute | solution.py:123
  28.4 5.3 %collective-permute-start.21 = (bf16[16,2048]{1,0:T(8,128)(2,1)S(1)}, bf16[16,2048]{1,0:T(8,128)(2,1)S(1)}, u32[]{:S(2)}, u32[]{:S(2)}) collective-permute-start(bf16[16,2048]{1,0:T(8,128)(2,1)S(1)} %cross.1), channel_id=1, source_target_pairs={{0,8},{1,9},{2,10},{3,11},{4,12},{5,13},{6,14},{7,15},{8,0},{9,1},... | collective-permute-start | bytes 196616 | tf_op jit(solution)/shard_map/ppermute | solution.py:123

commit v9 on v8

--- a/solution.py
+++ b/solution.py
@@ -20,8 +20,11 @@
     copies = [
         pltpu.make_async_copy(weight_hbm, weight_ref, sems.at[0]),
         pltpu.make_async_copy(replica_hbm, replica_ref, sems.at[1]),
-        pltpu.make_async_copy(token_ref, out_ref.at[:, :width], sems.at[2]),
     ]
+    piece = width // 2
+    for p in range(2):
+        at = pl.ds(p * piece, piece)
+        copies.append(pltpu.make_async_copy(token_ref.at[:, at], out_ref.at[:, at], sems.at[2 + p]))
     for copy in copies:
         copy.start()
     copies[0].wait()
@@ -37,7 +40,8 @@
     both = jnp.concatenate([high, dense - high], axis=0).T
     rest = jnp.zeros((row_count, LANES - 2 * slot_count), jnp.float32)
     out_ref[:, width:] = jnp.concatenate([both, rest], axis=1).astype(jnp.bfloat16)
-    copies[2].wait()
+    for copy in copies[2:]:
+        copy.wait()
 
 
 def expert_kernel(block_count, *refs):
@@ -158,7 +162,7 @@
         (
             pltpu.VMEM(replica.shape[::-1], full),
             pltpu.VMEM(replica.shape[::-1], jnp.int32),
-            pltpu.SemaphoreType.DMA((3,)),
+            pltpu.SemaphoreType.DMA((4,)),
         ),
         flops=10**10,
     )(*map(in_hbm, (tokens, route_weight.T, replica.T)))

time: 34.5 us -> 34.5 us (level)
  no operation moved by 1% of the time
where the time goes in v9:
time: 34.5 us; the launch traced here: 34.3 us
  starting transfers between devices  24.4 us (71%)
  waiting for transfers between devices  5.1 us (15%)
  Pallas kernels  4.72 us (14%)
    ppermute x14, starting transfers between devices, partner(): lax.ppermute(array, 'expert', [(i, i ^ 2 * k) for i in range(peer_count)])  22.5 us
    ppermute x14, waiting for transfers between devices, partner(): lax.ppermute(array, 'expert', [(i, i ^ 2 * k) for i in range(peer_count)])  4.75 us
    pallas_call x2, Pallas kernels, experts(): on_core(functools.partial(expert_kernel, len(blocks)), name, (shape(half_...  3.02 us
    ppermute x8, starting transfers between devices, swap(): lax.ppermute(array, 'expert', [(i, i ^ 1) for i in range(peer_count)])  1.82 us
    pallas_call x1, Pallas kernels, dense_shards(): on_core(functools.partial(pack_kernel, peer_count), 'pack', shape(row_cou...  0.84 us
    pallas_call x2, Pallas kernels, total(): on_core(sum_kernel, name, shape(row_count, wide), [VMEM] * len(terms))  0.71 us
  transfers between devices with their start and end apart: 22, of which 9 were waited for; matrix products, arithmetic and copies ran while one was open for 0% of the time, Pallas kernels for 9%

profile of v9, /device:TPU:0, one launch (start us, length us, event | category | flops | bytes accessed | tf_op | source)
XLA Modules:
  0.0 34.3 jit_solution(1194333591244993763)
XLA Ops:
  0.0 0.8 %pack.1.source_ref = bf16[16,2176]{1,0:T(8,128)(2,1)S(1)} custom-call(bf16[16,2048]{1,0:T(8,128)(2,1)} %refs_0_.5, f32[8,16]{1,0:T(8,128)} %bitcast.2, s32[8,16]{1,0:T(8,128)} %bitcast.3), custom_call_target="tpu_custom_call" | custom-call | flops 10000000000 | bytes 2441406 | tf_op jit(solution)/shard_map/pack/pallas_call | solution.py:157
  0.8 0.0 copy-start
  0.9 0.0 copy-start.1
  0.9 0.0 copy-start.2
  0.9 4.1 %collective-permute-start.5 = (bf16[16,2176]{1,0:T(8,128)(2,1)S(1)}, bf16[16,2176]{1,0:T(8,128)(2,1)S(1)}, u32[]{:S(2)}, u32[]{:S(2)}) collective-permute-start(bf16[16,2176]{1,0:T(8,128)(2,1)S(1)} %pack.1.source_ref), channel_id=1, source_target_pairs={{0,8},{1,9},{2,10},{3,11},{4,12},{5,13},{6,14},{7,15},{8,0},{9,1},... | collective-permute-start | bytes 208904 | tf_op jit(solution)/shard_map/ppermute | solution.py:127
  5.0 2.5 %collective-permute-start.2 = (bf16[16,2176]{1,0:T(8,128)(2,1)S(1)}, bf16[16,2176]{1,0:T(8,128)(2,1)S(1)}, u32[]{:S(2)}, u32[]{:S(2)}) collective-permute-start(bf16[16,2176]{1,0:T(8,128)(2,1)S(1)} %again.1.refs_0_.refs_5_), channel_id=1, source_target_pairs={{0,6},{1,7},{2,4},{3,5},{4,2},{5,3},{6,0},{7,1},{8,14},{9,15},{10,... | collective-permute-start | bytes 208904 | tf_op jit(solution)/shard_map/ppermute | solution.py:127
  7.5 0.4 %collective-permute-start.3 = (bf16[16,2176]{1,0:T(8,128)(2,1)S(1)}, bf16[16,2176]{1,0:T(8,128)(2,1)S(1)}, u32[]{:S(2)}, u32[]{:S(2)}) collective-permute-start(bf16[16,2176]{1,0:T(8,128)(2,1)S(1)} %again.1.refs_0_.refs_5_), channel_id=1, source_target_pairs={{0,4},{1,5},{2,6},{3,7},{4,0},{5,1},{6,2},{7,3},{8,12},{9,13},{10,... | collective-permute-start | bytes 208904 | tf_op jit(solution)/shard_map/ppermute | solution.py:127
  7.9 0.2 collective-permute-done.5.refs_7_
  8.2 1.9 %collective-permute-start.6 = (bf16[16,2176]{1,0:T(8,128)(2,1)S(1)}, bf16[16,2176]{1,0:T(8,128)(2,1)S(1)}, u32[]{:S(2)}, u32[]{:S(2)}) collective-permute-start(bf16[16,2176]{1,0:T(8,128)(2,1)S(1)} %collective-permute-done.5.refs_7_), channel_id=1, source_target_pairs={{0,2},{1,3},{2,0},{3,1},{4,6},{5,7},{6,4},{7,5},{8,10},{9,11},{10,... | collective-permute-start | bytes 208904 | tf_op jit(solution)/shard_map/ppermute | solution.py:127
  10.1 1.3 %collective-permute-start.7 = (bf16[16,2176]{1,0:T(8,128)(2,1)S(1)}, bf16[16,2176]{1,0:T(8,128)(2,1)S(1)}, u32[]{:S(2)}, u32[]{:S(2)}) collective-permute-start(bf16[16,2176]{1,0:T(8,128)(2,1)S(1)} %collective-permute-done.5.refs_7_), channel_id=1, source_target_pairs={{0,6},{1,7},{2,4},{3,5},{4,2},{5,3},{6,0},{7,1},{8,14},{9,15},{10,... | collective-permute-start | bytes 208904 | tf_op jit(solution)/shard_map/ppermute | solution.py:127
  11.4 0.3 collective-permute-start.8
  11.7 0.0 collective-permute-done.2.refs_0_.refs_7_
  11.7 1.9 %collective-permute-start = (bf16[16,2176]{1,0:T(8,128)(2,1)S(1)}, bf16[16,2176]{1,0:T(8,128)(2,1)S(1)}, u32[]{:S(2)}, u32[]{:S(2)}) collective-permute-start(bf16[16,2176]{1,0:T(8,128)(2,1)S(1)} %again.1.refs_0_.refs_5_), channel_id=1, source_target_pairs={{0,2},{1,3},{2,0},{3,1},{4,6},{5,7},{6,4},{7,5},{8,10},{9,11},{10,... | collective-permute-start | bytes 208904 | tf_op jit(solution)/shard_map/ppermute | solution.py:127
  13.6 0.0 collective-permute-done.3.refs_1_.refs_8_
  13.6 0.0 collective-permute-start.13
  13.6 0.0 collective-permute-done.6.refs_9_.refs_8_
  13.6 0.5 %collective-permute-start.14 = (bf16[16,2176]{1,0:T(8,128)(2,1)S(1)}, bf16[16,2176]{1,0:T(8,128)(2,1)S(1)}, u32[]{:S(2)}, u32[]{:S(2)}) collective-permute-start(bf16[16,2176]{1,0:T(8,128)(2,1)S(1)} %collective-permute-done.6.refs_9_.refs_8_), channel_id=1, source_target_pairs={{0,1},{1,0},{2,3},{3,2},{4,5},{5,4},{6,7},{7,6},{8,9},{9,8},{10,11... | collective-permute-start | bytes 208904 | tf_op jit(solution)/shard_map/ppermute | solution.py:130
  14.1 1.2 %collective-permute-done.7.refs_10_.refs_9_ = bf16[16,2176]{1,0:T(8,128)(2,1)S(1)} collective-permute-done((bf16[16,2176]{1,0:T(8,128)(2,1)S(1)}, bf16[16,2176]{1,0:T(8,128)(2,1)S(1)}, u32[]{:S(2)}, u32[]{:S(2)}) %collective-permute-start.7) | collective-permute-done | bytes 69664 | tf_op jit(solution)/shard_map/ppermute | solution.py:127
  15.3 0.0 collective-permute-start.15
  15.3 0.4 %collective-permute-done.8.refs_11_.refs_10_ = bf16[16,2176]{1,0:T(8,128)(2,1)S(1)} collective-permute-done((bf16[16,2176]{1,0:T(8,128)(2,1)S(1)}, bf16[16,2176]{1,0:T(8,128)(2,1)S(1)}, u32[]{:S(2)}, u32[]{:S(2)}) %collective-permute-start.8) | collective-permute-done | bytes 69664 | tf_op jit(solution)/shard_map/ppermute | solution.py:127
  15.7 0.1 collective-permute-start.16
  15.8 0.2 collective-permute-done.refs_1_.refs_6_
  16.0 0.3 collective-permute-start.4
  16.3 0.0 collective-permute-done.13.refs_3_
  16.3 0.3 collective-permute-start.1
  16.6 0.0 collective-permute-done.14.refs_4_
  16.6 0.0 collective-permute-done.15.refs_5_
  16.6 0.3 collective-permute-done.16.refs_6_
  17.0 0.0 copy-done
  17.0 0.0 copy-done.1
  17.0 0.0 copy-done.2
  17.0 1.5 %far.1 = (bf16[64,2048]{1,0:T(8,128)(2,1)S(1)}, f32[64,2048]{1,0:T(8,128)S(1)}) custom-call(bf16[1,2048,768]{2,1,0:T(8,128)(2,1)S(1)} %copy-done, bf16[1,2048,768]{2,1,0:T(8,128)(2,1)S(1)} %copy-done.1, bf16[1,768,2048]{2,1,0:T(8,128)(2,1)S(1)} %copy-done.2, bf16[16,2176]{1,0:T(8,128)(2,1)S(1)} %collective-permute-done.13.refs_3_, ...), custom_call_target="tpu_custom_call" | custom-call | flops 1000000000 | bytes 244140 | tf_op jit(solution)/shard_map/far/pallas_call | solution.py:136
  18.5 0.0 copy-start.3
  18.5 0.2 collective-permute-start.17
  18.7 0.0 collective-permute-done.4.refs_4_
  18.7 0.0 collective-permute-done.1.refs_3_
  18.7 1.5 %near.1 = (bf16[64,2048]{1,0:T(8,128)(2,1)S(1)}, f32[64,2048]{1,0:T(8,128)S(1)}) custom-call(bf16[1,2048,768]{2,1,0:T(8,128)(2,1)S(1)} %copy-done, bf16[1,2048,768]{2,1,0:T(8,128)(2,1)S(1)} %copy-done.1, bf16[1,768,2048]{2,1,0:T(8,128)(2,1)S(1)} %copy-done.2, bf16[32,2176]{1,0:T(8,128)(2,1)S(1)} %collective-permute-done.1.refs_3_, ...), custom_call_target="tpu_custom_call" | custom-call | flops 1000000000 | bytes 244140 | tf_op jit(solution)/shard_map/near/pallas_call | solution.py:136
  20.2 0.4 %collective-permute-start.9 = (bf16[64,2048]{1,0:T(8,128)(2,1)S(1)}, bf16[64,2048]{1,0:T(8,128)(2,1)S(1)}, u32[]{:S(2)}, u32[]{:S(2)}) collective-permute-start(bf16[64,2048]{1,0:T(8,128)(2,1)S(1)} %get-tuple-element.18), channel_id=1, source_target_pairs={{0,1},{1,0},{2,3},{3,2},{4,5},{5,4},{6,7},{7,6},{8,9},{9,8},{10,11... | collective-permute-start | bytes 786440 | tf_op jit(solution)/shard_map/ppermute | solution.py:130
  20.7 0.0 collective-permute-done.17.other_ref
  20.7 0.1 pair.3
  20.7 1.6 %collective-permute-start.18 = (bf16[16,2048]{1,0:T(8,128)(2,1)S(1)}, bf16[16,2048]{1,0:T(8,128)(2,1)S(1)}, u32[]{:S(2)}, u32[]{:S(2)}) collective-permute-start(bf16[16,2048]{1,0:T(8,128)(2,1)S(1)} %get-tuple-element.26), channel_id=1, source_target_pairs={{0,2},{1,3},{2,0},{3,1},{4,6},{5,7},{6,4},{7,5},{8,10},{9,11},{10,... | collective-permute-start | bytes 196616 | tf_op jit(solution)/shard_map/ppermute | solution.py:127
  22.3 1.3 %collective-permute-start.19 = (bf16[16,2048]{1,0:T(8,128)(2,1)S(1)}, bf16[16,2048]{1,0:T(8,128)(2,1)S(1)}, u32[]{:S(2)}, u32[]{:S(2)}) collective-permute-start(bf16[16,2048]{1,0:T(8,128)(2,1)S(1)} %get-tuple-element.27), channel_id=1, source_target_pairs={{0,6},{1,7},{2,4},{3,5},{4,2},{5,3},{6,0},{7,1},{8,14},{9,15},{10,... | collective-permute-start | bytes 196616 | tf_op jit(solution)/shard_map/ppermute | solution.py:127
  23.7 0.6 %collective-permute-start.20 = (bf16[16,2048]{1,0:T(8,128)(2,1)S(1)}, bf16[16,2048]{1,0:T(8,128)(2,1)S(1)}, u32[]{:S(2)}, u32[]{:S(2)}) collective-permute-start(bf16[16,2048]{1,0:T(8,128)(2,1)S(1)} %get-tuple-element.28), channel_id=1, source_target_pairs={{0,4},{1,5},{2,6},{3,7},{4,0},{5,1},{6,2},{7,3},{8,12},{9,13},{10,... | collective-permute-start | bytes 196616 | tf_op jit(solution)/shard_map/ppermute | solution.py:127
  24.3 0.0 collective-permute-done.9.other_ref
  24.3 0.1 pair.2
  24.3 1.6 %collective-permute-start.10 = (bf16[16,2048]{1,0:T(8,128)(2,1)S(1)}, bf16[16,2048]{1,0:T(8,128)(2,1)S(1)}, u32[]{:S(2)}, u32[]{:S(2)}) collective-permute-start(bf16[16,2048]{1,0:T(8,128)(2,1)S(1)} %get-tuple-element.20), channel_id=1, source_target_pairs={{0,2},{1,3},{2,0},{3,1},{4,6},{5,7},{6,4},{7,5},{8,10},{9,11},{10,... | collective-permute-start | bytes 196616 | tf_op jit(solution)/shard_map/ppermute | solution.py:127
  26.0 1.3 %collective-permute-start.11 = (bf16[16,2048]{1,0:T(8,128)(2,1)S(1)}, bf16[16,2048]{1,0:T(8,128)(2,1)S(1)}, u32[]{:S(2)}, u32[]{:S(2)}) collective-permute-start(bf16[16,2048]{1,0:T(8,128)(2,1)S(1)} %get-tuple-element.21), channel_id=1, source_target_pairs={{0,6},{1,7},{2,4},{3,5},{4,2},{5,3},{6,0},{7,1},{8,14},{9,15},{10,... | collective-permute-start | bytes 196616 | tf_op jit(solution)/shard_map/ppermute | solution.py:127
  27.3 0.0 collective-permute-done.18.refs_1_
  27.3 0.6 %collective-permute-start.12 = (bf16[16,2048]{1,0:T(8,128)(2,1)S(1)}, bf16[16,2048]{1,0:T(8,128)(2,1)S(1)}, u32[]{:S(2)}, u32[]{:S(2)}) collective-permute-start(bf16[16,2048]{1,0:T(8,128)(2,1)S(1)} %get-tuple-element.22), channel_id=1, source_target_pairs={{0,4},{1,5},{2,6},{3,7},{4,0},{5,1},{6,2},{7,3},{8,12},{9,13},{10,... | collective-permute-start | bytes 196616 | tf_op jit(solution)/shard_map/ppermute | solution.py:127
  27.9 0.2 collective-permute-done.19.refs_2_
  28.1 0.3 collective-permute-done.20.refs_3_
  28.4 3.0 %collective-permute-start.21 = (bf16[16,2048]{1,0:T(8,128)(2,1)S(1)}, bf16[16,2048]{1,0:T(8,128)(2,1)S(1)}, u32[]{:S(2)}, u32[]{:S(2)}) collective-permute-start(bf16[16,2048]{1,0:T(8,128)(2,1)S(1)} %cross.1), channel_id=1, source_target_pairs={{0,8},{1,9},{2,10},{3,11},{4,12},{5,13},{6,14},{7,15},{8,0},{9,1},... | collective-permute-start | bytes 196616 | tf_op jit(solution)/shard_map/ppermute | solution.py:127
  31.4 0.0 collective-permute-done.10.refs_2_
  31.4 0.0 collective-permute-done.11.refs_3_
  31.4 0.9 %collective-permute-done.12.refs_4_ = bf16[16,2048]{1,0:T(8,128)(2,1)S(1)} collective-permute-done((bf16[16,2048]{1,0:T(8,128)(2,1)S(1)}, bf16[16,2048]{1,0:T(8,128)(2,1)S(1)}, u32[]{:S(2)}, u32[]{:S(2)}) %collective-permute-start.12) | collective-permute-done | bytes 65568 | tf_op jit(solution)/shard_map/ppermute | solution.py:127
  32.3 1.4 %collective-permute-done.21.refs_5_ = bf16[16,2048]{1,0:T(8,128)(2,1)S(1)} collective-permute-done((bf16[16,2048]{1,0:T(8,128)(2,1)S(1)}, bf16[16,2048]{1,0:T(8,128)(2,1)S(1)}, u32[]{:S(2)}, u32[]{:S(2)}) %collective-permute-start.21) | collective-permute-done | bytes 65568 | tf_op jit(solution)/shard_map/ppermute | solution.py:127
  33.6 0.0 copy-done.3
  33.6 0.7 %mix.1 = bf16[16,2048]{1,0:T(8,128)(2,1)} custom-call(bf16[16,2048]{1,0:T(8,128)(2,1)S(1)} %copy-done.3, f32[16,2048]{1,0:T(8,128)S(1)} %get-tuple-element.19.refs_1_, bf16[16,2048]{1,0:T(8,128)(2,1)S(1)} %collective-permute-done.10.refs_2_, bf16[16,2048]{1,0:T(8,128)(2,1)S(1)} %collective-permute-done.11.refs_3_, ...), custom_call_target="tpu_custom_call" | custom-call | tf_op jit(solution)/shard_map/mix/pallas_call | solution.py:155
  (4 shorter events, 0.1 us)
Async XLA Ops:
  0.8 16.1 %copy-start = (bf16[1,2048,768]{2,1,0:T(8,128)(2,1)S(1)}, bf16[1,2048,768]{2,1,0:T(8,128)(2,1)}, u32[]{:S(2)}) copy-start(bf16[1,2048,768]{2,1,0:T(8,128)(2,1)} %refs_0_.4) | copy-start | bytes 9437188
  0.9 16.1 %copy-start.1 = (bf16[1,2048,768]{2,1,0:T(8,128)(2,1)S(1)}, bf16[1,2048,768]{2,1,0:T(8,128)(2,1)}, u32[]{:S(2)}) copy-start(bf16[1,2048,768]{2,1,0:T(8,128)(2,1)} %refs_1_.3) | copy-start | bytes 9437188
  0.9 16.1 %copy-start.2 = (bf16[1,768,2048]{2,1,0:T(8,128)(2,1)S(1)}, bf16[1,768,2048]{2,1,0:T(8,128)(2,1)}, u32[]{:S(2)}) copy-start(bf16[1,768,2048]{2,1,0:T(8,128)(2,1)} %refs_2_.3) | copy-start | bytes 9437188
  0.9 7.3 %collective-permute-start.5 = (bf16[16,2176]{1,0:T(8,128)(2,1)S(1)}, bf16[16,2176]{1,0:T(8,128)(2,1)S(1)}, u32[]{:S(2)}, u32[]{:S(2)}) collective-permute-start(bf16[16,2176]{1,0:T(8,128)(2,1)S(1)} %pack.1.source_ref), channel_id=1, source_target_pairs={{0,8},{1,9},{2,10},{3,11},{4,12},{5,13},{6,14},{7,15},{8,0},{9,1},... | collective-permute-start | bytes 208904 | tf_op jit(solution)/shard_map/ppermute | solution.py:127
  5.0 6.7 %collective-permute-start.2 = (bf16[16,2176]{1,0:T(8,128)(2,1)S(1)}, bf16[16,2176]{1,0:T(8,128)(2,1)S(1)}, u32[]{:S(2)}, u32[]{:S(2)}) collective-permute-start(bf16[16,2176]{1,0:T(8,128)(2,1)S(1)} %again.1.refs_0_.refs_5_), channel_id=1, source_target_pairs={{0,6},{1,7},{2,4},{3,5},{4,2},{5,3},{6,0},{7,1},{8,14},{9,15},{10,... | collective-permute-start | bytes 208904 | tf_op jit(solution)/shard_map/ppermute | solution.py:127
  7.5 6.1 %collective-permute-start.3 = (bf16[16,2176]{1,0:T(8,128)(2,1)S(1)}, bf16[16,2176]{1,0:T(8,128)(2,1)S(1)}, u32[]{:S(2)}, u32[]{:S(2)}) collective-permute-start(bf16[16,2176]{1,0:T(8,128)(2,1)S(1)} %again.1.refs_0_.refs_5_), channel_id=1, source_target_pairs={{0,4},{1,5},{2,6},{3,7},{4,0},{5,1},{6,2},{7,3},{8,12},{9,13},{10,... | collective-permute-start | bytes 208904 | tf_op jit(solution)/shard_map/ppermute | solution.py:127
  8.2 5.4 %collective-permute-start.6 = (bf16[16,2176]{1,0:T(8,128)(2,1)S(1)}, bf16[16,2176]{1,0:T(8,128)(2,1)S(1)}, u32[]{:S(2)}, u32[]{:S(2)}) collective-permute-start(bf16[16,2176]{1,0:T(8,128)(2,1)S(1)} %collective-permute-done.5.refs_7_), channel_id=1, source_target_pairs={{0,2},{1,3},{2,0},{3,1},{4,6},{5,7},{6,4},{7,5},{8,10},{9,11},{10,... | collective-permute-start | bytes 208904 | tf_op jit(solution)/shard_map/ppermute | solution.py:127
  10.1 5.2 %collective-permute-start.7 = (bf16[16,2176]{1,0:T(8,128)(2,1)S(1)}, bf16[16,2176]{1,0:T(8,128)(2,1)S(1)}, u32[]{:S(2)}, u32[]{:S(2)}) collective-permute-start(bf16[16,2176]{1,0:T(8,128)(2,1)S(1)} %collective-permute-done.5.refs_7_), channel_id=1, source_target_pairs={{0,6},{1,7},{2,4},{3,5},{4,2},{5,3},{6,0},{7,1},{8,14},{9,15},{10,... | collective-permute-start | bytes 208904 | tf_op jit(solution)/shard_map/ppermute | solution.py:127
  11.4 4.3 %collective-permute-start.8 = (bf16[16,2176]{1,0:T(8,128)(2,1)S(1)}, bf16[16,2176]{1,0:T(8,128)(2,1)S(1)}, u32[]{:S(2)}, u32[]{:S(2)}) collective-permute-start(bf16[16,2176]{1,0:T(8,128)(2,1)S(1)} %collective-permute-done.5.refs_7_), channel_id=1, source_target_pairs={{0,4},{1,5},{2,6},{3,7},{4,0},{5,1},{6,2},{7,3},{8,12},{9,13},{10,... | collective-permute-start | bytes 208904 | tf_op jit(solution)/shard_map/ppermute | solution.py:127
  11.7 4.3 %collective-permute-start = (bf16[16,2176]{1,0:T(8,128)(2,1)S(1)}, bf16[16,2176]{1,0:T(8,128)(2,1)S(1)}, u32[]{:S(2)}, u32[]{:S(2)}) collective-permute-start(bf16[16,2176]{1,0:T(8,128)(2,1)S(1)} %again.1.refs_0_.refs_5_), channel_id=1, source_target_pairs={{0,2},{1,3},{2,0},{3,1},{4,6},{5,7},{6,4},{7,5},{8,10},{9,11},{10,... | collective-permute-start | bytes 208904 | tf_op jit(solution)/shard_map/ppermute | solution.py:127
  13.6 2.7 %collective-permute-start.13 = (bf16[16,2176]{1,0:T(8,128)(2,1)S(1)}, bf16[16,2176]{1,0:T(8,128)(2,1)S(1)}, u32[]{:S(2)}, u32[]{:S(2)}) collective-permute-start(bf16[16,2176]{1,0:T(8,128)(2,1)S(1)} %collective-permute-done.5.refs_7_), channel_id=1, source_target_pairs={{0,1},{1,0},{2,3},{3,2},{4,5},{5,4},{6,7},{7,6},{8,9},{9,8},{10,11... | collective-permute-start | bytes 208904 | tf_op jit(solution)/shard_map/ppermute | solution.py:130
  13.6 3.1 %collective-permute-start.14 = (bf16[16,2176]{1,0:T(8,128)(2,1)S(1)}, bf16[16,2176]{1,0:T(8,128)(2,1)S(1)}, u32[]{:S(2)}, u32[]{:S(2)}) collective-permute-start(bf16[16,2176]{1,0:T(8,128)(2,1)S(1)} %collective-permute-done.6.refs_9_.refs_8_), channel_id=1, source_target_pairs={{0,1},{1,0},{2,3},{3,2},{4,5},{5,4},{6,7},{7,6},{8,9},{9,8},{10,11... | collective-permute-start | bytes 208904 | tf_op jit(solution)/shard_map/ppermute | solution.py:130
  15.3 1.4 %collective-permute-start.15 = (bf16[16,2176]{1,0:T(8,128)(2,1)S(1)}, bf16[16,2176]{1,0:T(8,128)(2,1)S(1)}, u32[]{:S(2)}, u32[]{:S(2)}) collective-permute-start(bf16[16,2176]{1,0:T(8,128)(2,1)S(1)} %collective-permute-done.7.refs_10_.refs_9_), channel_id=1, source_target_pairs={{0,1},{1,0},{2,3},{3,2},{4,5},{5,4},{6,7},{7,6},{8,9},{9,8},{10,11... | collective-permute-start | bytes 208904 | tf_op jit(solution)/shard_map/ppermute | solution.py:130
  15.7 1.3 %collective-permute-start.16 = (bf16[16,2176]{1,0:T(8,128)(2,1)S(1)}, bf16[16,2176]{1,0:T(8,128)(2,1)S(1)}, u32[]{:S(2)}, u32[]{:S(2)}) collective-permute-start(bf16[16,2176]{1,0:T(8,128)(2,1)S(1)} %collective-permute-done.8.refs_11_.refs_10_), channel_id=1, source_target_pairs={{0,1},{1,0},{2,3},{3,2},{4,5},{5,4},{6,7},{7,6},{8,9},{9,8},{10,11... | collective-permute-start | bytes 208904 | tf_op jit(solution)/shard_map/ppermute | solution.py:130
  16.0 2.7 %collective-permute-start.4 = (bf16[32,2176]{1,0:T(8,128)(2,1)S(1)}, bf16[32,2176]{1,0:T(8,128)(2,1)S(1)}, u32[]{:S(2)}, u32[]{:S(2)}) collective-permute-start(bf16[32,2176]{1,0:T(8,128)(2,1)S(1)} %join.3), channel_id=1, source_target_pairs={{0,1},{1,0},{2,3},{3,2},{4,5},{5,4},{6,7},{7,6},{8,9},{9,8},{10,11... | collective-permute-start | bytes 417800 | tf_op jit(solution)/shard_map/ppermute | solution.py:130
  16.3 2.4 %collective-permute-start.1 = (bf16[32,2176]{1,0:T(8,128)(2,1)S(1)}, bf16[32,2176]{1,0:T(8,128)(2,1)S(1)}, u32[]{:S(2)}, u32[]{:S(2)}) collective-permute-start(bf16[32,2176]{1,0:T(8,128)(2,1)S(1)} %join.2), channel_id=1, source_target_pairs={{0,1},{1,0},{2,3},{3,2},{4,5},{5,4},{6,7},{7,6},{8,9},{9,8},{10,11... | collective-permute-start | bytes 417800 | tf_op jit(solution)/shard_map/ppermute | solution.py:130
  18.5 15.2 %copy-start.3 = (bf16[16,2048]{1,0:T(8,128)(2,1)S(1)}, bf16[16,2048]{1,0:T(8,128)(2,1)}, u32[]{:S(2)}) copy-start(bf16[16,2048]{1,0:T(8,128)(2,1)} %refs_0_.5) | copy-start | bytes 196612
  18.5 2.2 %collective-permute-start.17 = (bf16[64,2048]{1,0:T(8,128)(2,1)S(1)}, bf16[64,2048]{1,0:T(8,128)(2,1)S(1)}, u32[]{:S(2)}, u32[]{:S(2)}) collective-permute-start(bf16[64,2048]{1,0:T(8,128)(2,1)S(1)} %get-tuple-element.24), channel_id=1, source_target_pairs={{0,1},{1,0},{2,3},{3,2},{4,5},{5,4},{6,7},{7,6},{8,9},{9,8},{10,11... | collective-permute-start | bytes 786440 | tf_op jit(solution)/shard_map/ppermute | solution.py:130
  20.2 4.0 %collective-permute-start.9 = (bf16[64,2048]{1,0:T(8,128)(2,1)S(1)}, bf16[64,2048]{1,0:T(8,128)(2,1)S(1)}, u32[]{:S(2)}, u32[]{:S(2)}) collective-permute-start(bf16[64,2048]{1,0:T(8,128)(2,1)S(1)} %get-tuple-element.18), channel_id=1, source_target_pairs={{0,1},{1,0},{2,3},{3,2},{4,5},{5,4},{6,7},{7,6},{8,9},{9,8},{10,11... | collective-permute-start | bytes 786440 | tf_op jit(solution)/shard_map/ppermute | solution.py:130
  20.7 6.6 %collective-permute-start.18 = (bf16[16,2048]{1,0:T(8,128)(2,1)S(1)}, bf16[16,2048]{1,0:T(8,128)(2,1)S(1)}, u32[]{:S(2)}, u32[]{:S(2)}) collective-permute-start(bf16[16,2048]{1,0:T(8,128)(2,1)S(1)} %get-tuple-element.26), channel_id=1, source_target_pairs={{0,2},{1,3},{2,0},{3,1},{4,6},{5,7},{6,4},{7,5},{8,10},{9,11},{10,... | collective-permute-start | bytes 196616 | tf_op jit(solution)/shard_map/ppermute | solution.py:127
  22.3 5.7 %collective-permute-start.19 = (bf16[16,2048]{1,0:T(8,128)(2,1)S(1)}, bf16[16,2048]{1,0:T(8,128)(2,1)S(1)}, u32[]{:S(2)}, u32[]{:S(2)}) collective-permute-start(bf16[16,2048]{1,0:T(8,128)(2,1)S(1)} %get-tuple-element.27), channel_id=1, source_target_pairs={{0,6},{1,7},{2,4},{3,5},{4,2},{5,3},{6,0},{7,1},{8,14},{9,15},{10,... | collective-permute-start | bytes 196616 | tf_op jit(solution)/shard_map/ppermute | solution.py:127
  23.7 4.7 %collective-permute-start.20 = (bf16[16,2048]{1,0:T(8,128)(2,1)S(1)}, bf16[16,2048]{1,0:T(8,128)(2,1)S(1)}, u32[]{:S(2)}, u32[]{:S(2)}) collective-permute-start(bf16[16,2048]{1,0:T(8,128)(2,1)S(1)} %get-tuple-element.28), channel_id=1, source_target_pairs={{0,4},{1,5},{2,6},{3,7},{4,0},{5,1},{6,2},{7,3},{8,12},{9,13},{10,... | collective-permute-start | bytes 196616 | tf_op jit(solution)/shard_map/ppermute | solution.py:127
  24.3 7.0 %collective-permute-start.10 = (bf16[16,2048]{1,0:T(8,128)(2,1)S(1)}, bf16[16,2048]{1,0:T(8,128)(2,1)S(1)}, u32[]{:S(2)}, u32[]{:S(2)}) collective-permute-start(bf16[16,2048]{1,0:T(8,128)(2,1)S(1)} %get-tuple-element.20), channel_id=1, source_target_pairs={{0,2},{1,3},{2,0},{3,1},{4,6},{5,7},{6,4},{7,5},{8,10},{9,11},{10,... | collective-permute-start | bytes 196616 | tf_op jit(solution)/shard_map/ppermute | solution.py:127
  26.0 5.4 %collective-permute-start.11 = (bf16[16,2048]{1,0:T(8,128)(2,1)S(1)}, bf16[16,2048]{1,0:T(8,128)(2,1)S(1)}, u32[]{:S(2)}, u32[]{:S(2)}) collective-permute-start(bf16[16,2048]{1,0:T(8,128)(2,1)S(1)} %get-tuple-element.21), channel_id=1, source_target_pairs={{0,6},{1,7},{2,4},{3,5},{4,2},{5,3},{6,0},{7,1},{8,14},{9,15},{10,... | collective-permute-start | bytes 196616 | tf_op jit(solution)/shard_map/ppermute | solution.py:127
  27.3 5.0 %collective-permute-start.12 = (bf16[16,2048]{1,0:T(8,128)(2,1)S(1)}, bf16[16,2048]{1,0:T(8,128)(2,1)S(1)}, u32[]{:S(2)}, u32[]{:S(2)}) collective-permute-start(bf16[16,2048]{1,0:T(8,128)(2,1)S(1)} %get-tuple-element.22), channel_id=1, source_target_pairs={{0,4},{1,5},{2,6},{3,7},{4,0},{5,1},{6,2},{7,3},{8,12},{9,13},{10,... | collective-permute-start | bytes 196616 | tf_op jit(solution)/shard_map/ppermute | solution.py:127
  28.4 5.3 %collective-permute-start.21 = (bf16[16,2048]{1,0:T(8,128)(2,1)S(1)}, bf16[16,2048]{1,0:T(8,128)(2,1)S(1)}, u32[]{:S(2)}, u32[]{:S(2)}) collective-permute-start(bf16[16,2048]{1,0:T(8,128)(2,1)S(1)} %cross.1), channel_id=1, source_target_pairs={{0,8},{1,9},{2,10},{3,11},{4,12},{5,13},{6,14},{7,15},{8,0},{9,1},... | collective-permute-start | bytes 196616 | tf_op jit(solution)/shard_map/ppermute | solution.py:127

commit v10 on v9

--- a/solution.py
+++ b/solution.py
@@ -102,6 +102,22 @@
     refs[-1][...] = total.astype(jnp.bfloat16)
 
 
+def mix_kernel(*refs):
+    out_hbm, total_ref, sems = refs[-3:]
+    piece = total_ref.shape[1] // 2
+    copies = []
+    for p in range(2):
+        at = pl.ds(p * piece, piece)
+        total = refs[0][:, at].astype(jnp.float32)
+        for ref in refs[1:-3]:
+            total += ref[:, at].astype(jnp.float32)
+        total_ref[:, at] = total.astype(jnp.bfloat16)
+        copies.append(pltpu.make_async_copy(total_ref.at[:, at], out_hbm.at[:, at], sems.at[p]))
+        copies[-1].start()
+    for copy in copies:
+        copy.wait()
+
+
 def on_core(kernel, name, outs, ins, scratch=(), limit=8, flops=0):
     return pl.pallas_call(
         kernel,
@@ -185,7 +201,16 @@
     far_back = [partner(block, k) for block, k in zip(far_sums, order)]
     near_back = [partner(block, k) for block, k in zip(near_sums, order)]
     crossing = partner(total("cross", far_first, *far_back), half)
-    return total("mix", tokens, near_first, *near_back, crossing)
+    terms = (tokens, near_first, *near_back, crossing)
+    return pl.pallas_call(
+        mix_kernel,
+        out_shape=shape(row_count, wide),
+        in_specs=[VMEM] * len(terms),
+        out_specs=HBM,
+        scratch_shapes=[pltpu.VMEM((row_count, width), wide), pltpu.SemaphoreType.DMA((2,))],
+        compiler_params=pltpu.CompilerParams(vmem_limit_bytes=8 * 2**20),
+        name="mix",
+    )(*terms)
 
 
 def routed_shards(tokens, route_weight, replica, w_gate, w_up, w_down):

time: 34.5 us -> 34.5 us (level)
    pallas_call x0 -> x1, Pallas kernels: none -> 0.68 us  [dense_shards(): pl.pallas_call(mix_kernel, out_shape=shape(row_count, wide), in_specs=[VM...]
    pallas_call x2 -> x1, Pallas kernels: 0.71 us -> 0.03 us  [total(): on_core(sum_kernel, name, shape(row_count, wide), [VMEM] * len(terms))]
where the time goes in v10:
time: 34.5 us; the launch traced here: 34.3 us
  starting transfers between devices  24.4 us (71%)
  waiting for transfers between devices  5.1 us (15%)
  Pallas kernels  4.72 us (14%)
    ppermute x14, starting transfers between devices, partner(): lax.ppermute(array, 'expert', [(i, i ^ 2 * k) for i in range(peer_count)])  22.5 us
    ppermute x14, waiting for transfers between devices, partner(): lax.ppermute(array, 'expert', [(i, i ^ 2 * k) for i in range(peer_count)])  4.75 us
    pallas_call x2, Pallas kernels, experts(): on_core(functools.partial(expert_kernel, len(blocks)), name, (shape(half_...  3.02 us
    ppermute x8, starting transfers between devices, swap(): lax.ppermute(array, 'expert', [(i, i ^ 1) for i in range(peer_count)])  1.82 us
    pallas_call x1, Pallas kernels, dense_shards(): on_core(functools.partial(pack_kernel, peer_count), 'pack', shape(row_cou...  0.84 us
  transfers between devices with their start and end apart: 22, of which 9 were waited for; matrix products, arithmetic and copies ran while one was open for 0% of the time, Pallas kernels for 9%

profile of v10, /device:TPU:0, one launch (start us, length us, event | category | flops | bytes accessed | tf_op | source)
XLA Modules:
  0.0 34.3 jit_solution(3341495744710153098)
XLA Ops:
  0.0 0.8 %pack.1.source_ref = bf16[16,2176]{1,0:T(8,128)(2,1)S(1)} custom-call(bf16[16,2048]{1,0:T(8,128)(2,1)} %refs_0_.5, f32[8,16]{1,0:T(8,128)} %bitcast.2, s32[8,16]{1,0:T(8,128)} %bitcast.3), custom_call_target="tpu_custom_call" | custom-call | flops 10000000000 | bytes 2441406 | tf_op jit(solution)/shard_map/pack/pallas_call | solution.py:173
  0.8 0.0 copy-start
  0.9 0.0 copy-start.1
  0.9 0.0 copy-start.2
  0.9 4.1 %collective-permute-start.5 = (bf16[16,2176]{1,0:T(8,128)(2,1)S(1)}, bf16[16,2176]{1,0:T(8,128)(2,1)S(1)}, u32[]{:S(2)}, u32[]{:S(2)}) collective-permute-start(bf16[16,2176]{1,0:T(8,128)(2,1)S(1)} %pack.1.source_ref), channel_id=1, source_target_pairs={{0,8},{1,9},{2,10},{3,11},{4,12},{5,13},{6,14},{7,15},{8,0},{9,1},... | collective-permute-start | bytes 208904 | tf_op jit(solution)/shard_map/ppermute | solution.py:143
  5.0 2.5 %collective-permute-start.2 = (bf16[16,2176]{1,0:T(8,128)(2,1)S(1)}, bf16[16,2176]{1,0:T(8,128)(2,1)S(1)}, u32[]{:S(2)}, u32[]{:S(2)}) collective-permute-start(bf16[16,2176]{1,0:T(8,128)(2,1)S(1)} %again.1.refs_0_.refs_5_), channel_id=1, source_target_pairs={{0,6},{1,7},{2,4},{3,5},{4,2},{5,3},{6,0},{7,1},{8,14},{9,15},{10,... | collective-permute-start | bytes 208904 | tf_op jit(solution)/shard_map/ppermute | solution.py:143
  7.5 0.4 %collective-permute-start.3 = (bf16[16,2176]{1,0:T(8,128)(2,1)S(1)}, bf16[16,2176]{1,0:T(8,128)(2,1)S(1)}, u32[]{:S(2)}, u32[]{:S(2)}) collective-permute-start(bf16[16,2176]{1,0:T(8,128)(2,1)S(1)} %again.1.refs_0_.refs_5_), channel_id=1, source_target_pairs={{0,4},{1,5},{2,6},{3,7},{4,0},{5,1},{6,2},{7,3},{8,12},{9,13},{10,... | collective-permute-start | bytes 208904 | tf_op jit(solution)/shard_map/ppermute | solution.py:143
  7.9 0.2 collective-permute-done.5.refs_7_
  8.2 1.9 %collective-permute-start.6 = (bf16[16,2176]{1,0:T(8,128)(2,1)S(1)}, bf16[16,2176]{1,0:T(8,128)(2,1)S(1)}, u32[]{:S(2)}, u32[]{:S(2)}) collective-permute-start(bf16[16,2176]{1,0:T(8,128)(2,1)S(1)} %collective-permute-done.5.refs_7_), channel_id=1, source_target_pairs={{0,2},{1,3},{2,0},{3,1},{4,6},{5,7},{6,4},{7,5},{8,10},{9,11},{10,... | collective-permute-start | bytes 208904 | tf_op jit(solution)/shard_map/ppermute | solution.py:143
  10.1 1.3 %collective-permute-start.7 = (bf16[16,2176]{1,0:T(8,128)(2,1)S(1)}, bf16[16,2176]{1,0:T(8,128)(2,1)S(1)}, u32[]{:S(2)}, u32[]{:S(2)}) collective-permute-start(bf16[16,2176]{1,0:T(8,128)(2,1)S(1)} %collective-permute-done.5.refs_7_), channel_id=1, source_target_pairs={{0,6},{1,7},{2,4},{3,5},{4,2},{5,3},{6,0},{7,1},{8,14},{9,15},{10,... | collective-permute-start | bytes 208904 | tf_op jit(solution)/shard_map/ppermute | solution.py:143
  11.4 0.3 collective-permute-start.8
  11.7 0.0 collective-permute-done.2.refs_0_.refs_7_
  11.7 1.9 %collective-permute-start = (bf16[16,2176]{1,0:T(8,128)(2,1)S(1)}, bf16[16,2176]{1,0:T(8,128)(2,1)S(1)}, u32[]{:S(2)}, u32[]{:S(2)}) collective-permute-start(bf16[16,2176]{1,0:T(8,128)(2,1)S(1)} %again.1.refs_0_.refs_5_), channel_id=1, source_target_pairs={{0,2},{1,3},{2,0},{3,1},{4,6},{5,7},{6,4},{7,5},{8,10},{9,11},{10,... | collective-permute-start | bytes 208904 | tf_op jit(solution)/shard_map/ppermute | solution.py:143
  13.6 0.0 collective-permute-done.3.refs_1_.refs_8_
  13.6 0.0 collective-permute-start.13
  13.6 0.0 collective-permute-done.6.refs_9_.refs_8_
  13.6 0.5 %collective-permute-start.14 = (bf16[16,2176]{1,0:T(8,128)(2,1)S(1)}, bf16[16,2176]{1,0:T(8,128)(2,1)S(1)}, u32[]{:S(2)}, u32[]{:S(2)}) collective-permute-start(bf16[16,2176]{1,0:T(8,128)(2,1)S(1)} %collective-permute-done.6.refs_9_.refs_8_), channel_id=1, source_target_pairs={{0,1},{1,0},{2,3},{3,2},{4,5},{5,4},{6,7},{7,6},{8,9},{9,8},{10,11... | collective-permute-start | bytes 208904 | tf_op jit(solution)/shard_map/ppermute | solution.py:146
  14.1 1.2 %collective-permute-done.7.refs_10_.refs_9_ = bf16[16,2176]{1,0:T(8,128)(2,1)S(1)} collective-permute-done((bf16[16,2176]{1,0:T(8,128)(2,1)S(1)}, bf16[16,2176]{1,0:T(8,128)(2,1)S(1)}, u32[]{:S(2)}, u32[]{:S(2)}) %collective-permute-start.7) | collective-permute-done | bytes 69664 | tf_op jit(solution)/shard_map/ppermute | solution.py:143
  15.3 0.0 collective-permute-start.15
  15.3 0.4 %collective-permute-done.8.refs_11_.refs_10_ = bf16[16,2176]{1,0:T(8,128)(2,1)S(1)} collective-permute-done((bf16[16,2176]{1,0:T(8,128)(2,1)S(1)}, bf16[16,2176]{1,0:T(8,128)(2,1)S(1)}, u32[]{:S(2)}, u32[]{:S(2)}) %collective-permute-start.8) | collective-permute-done | bytes 69664 | tf_op jit(solution)/shard_map/ppermute | solution.py:143
  15.7 0.1 collective-permute-start.16
  15.8 0.2 collective-permute-done.refs_1_.refs_6_
  16.0 0.3 collective-permute-start.4
  16.3 0.0 collective-permute-done.13.refs_3_
  16.3 0.3 collective-permute-start.1
  16.6 0.0 collective-permute-done.14.refs_4_
  16.6 0.0 collective-permute-done.15.refs_5_
  16.6 0.3 collective-permute-done.16.refs_6_
  17.0 0.0 copy-done
  17.0 0.0 copy-done.1
  17.0 0.0 copy-done.2
  17.0 1.5 %far.1 = (bf16[64,2048]{1,0:T(8,128)(2,1)S(1)}, f32[64,2048]{1,0:T(8,128)S(1)}) custom-call(bf16[1,2048,768]{2,1,0:T(8,128)(2,1)S(1)} %copy-done, bf16[1,2048,768]{2,1,0:T(8,128)(2,1)S(1)} %copy-done.1, bf16[1,768,2048]{2,1,0:T(8,128)(2,1)S(1)} %copy-done.2, bf16[16,2176]{1,0:T(8,128)(2,1)S(1)} %collective-permute-done.13.refs_3_, ...), custom_call_target="tpu_custom_call" | custom-call | flops 1000000000 | bytes 244140 | tf_op jit(solution)/shard_map/far/pallas_call | solution.py:152
  18.5 0.0 copy-start.3
  18.5 0.2 collective-permute-start.17
  18.7 0.0 collective-permute-done.4.refs_4_
  18.7 0.0 collective-permute-done.1.refs_3_
  18.7 1.5 %near.1 = (bf16[64,2048]{1,0:T(8,128)(2,1)S(1)}, f32[64,2048]{1,0:T(8,128)S(1)}) custom-call(bf16[1,2048,768]{2,1,0:T(8,128)(2,1)S(1)} %copy-done, bf16[1,2048,768]{2,1,0:T(8,128)(2,1)S(1)} %copy-done.1, bf16[1,768,2048]{2,1,0:T(8,128)(2,1)S(1)} %copy-done.2, bf16[32,2176]{1,0:T(8,128)(2,1)S(1)} %collective-permute-done.1.refs_3_, ...), custom_call_target="tpu_custom_call" | custom-call | flops 1000000000 | bytes 244140 | tf_op jit(solution)/shard_map/near/pallas_call | solution.py:152
  20.2 0.4 %collective-permute-start.9 = (bf16[64,2048]{1,0:T(8,128)(2,1)S(1)}, bf16[64,2048]{1,0:T(8,128)(2,1)S(1)}, u32[]{:S(2)}, u32[]{:S(2)}) collective-permute-start(bf16[64,2048]{1,0:T(8,128)(2,1)S(1)} %get-tuple-element.18), channel_id=1, source_target_pairs={{0,1},{1,0},{2,3},{3,2},{4,5},{5,4},{6,7},{7,6},{8,9},{9,8},{10,11... | collective-permute-start | bytes 786440 | tf_op jit(solution)/shard_map/ppermute | solution.py:146
  20.7 0.0 collective-permute-done.17.other_ref
  20.7 0.1 pair.3
  20.7 1.6 %collective-permute-start.18 = (bf16[16,2048]{1,0:T(8,128)(2,1)S(1)}, bf16[16,2048]{1,0:T(8,128)(2,1)S(1)}, u32[]{:S(2)}, u32[]{:S(2)}) collective-permute-start(bf16[16,2048]{1,0:T(8,128)(2,1)S(1)} %get-tuple-element.26), channel_id=1, source_target_pairs={{0,2},{1,3},{2,0},{3,1},{4,6},{5,7},{6,4},{7,5},{8,10},{9,11},{10,... | collective-permute-start | bytes 196616 | tf_op jit(solution)/shard_map/ppermute | solution.py:143
  22.3 1.3 %collective-permute-start.19 = (bf16[16,2048]{1,0:T(8,128)(2,1)S(1)}, bf16[16,2048]{1,0:T(8,128)(2,1)S(1)}, u32[]{:S(2)}, u32[]{:S(2)}) collective-permute-start(bf16[16,2048]{1,0:T(8,128)(2,1)S(1)} %get-tuple-element.27), channel_id=1, source_target_pairs={{0,6},{1,7},{2,4},{3,5},{4,2},{5,3},{6,0},{7,1},{8,14},{9,15},{10,... | collective-permute-start | bytes 196616 | tf_op jit(solution)/shard_map/ppermute | solution.py:143
  23.7 0.6 %collective-permute-start.20 = (bf16[16,2048]{1,0:T(8,128)(2,1)S(1)}, bf16[16,2048]{1,0:T(8,128)(2,1)S(1)}, u32[]{:S(2)}, u32[]{:S(2)}) collective-permute-start(bf16[16,2048]{1,0:T(8,128)(2,1)S(1)} %get-tuple-element.28), channel_id=1, source_target_pairs={{0,4},{1,5},{2,6},{3,7},{4,0},{5,1},{6,2},{7,3},{8,12},{9,13},{10,... | collective-permute-start | bytes 196616 | tf_op jit(solution)/shard_map/ppermute | solution.py:143
  24.3 0.0 collective-permute-done.9.other_ref
  24.3 0.1 pair.2
  24.3 1.6 %collective-permute-start.10 = (bf16[16,2048]{1,0:T(8,128)(2,1)S(1)}, bf16[16,2048]{1,0:T(8,128)(2,1)S(1)}, u32[]{:S(2)}, u32[]{:S(2)}) collective-permute-start(bf16[16,2048]{1,0:T(8,128)(2,1)S(1)} %get-tuple-element.20), channel_id=1, source_target_pairs={{0,2},{1,3},{2,0},{3,1},{4,6},{5,7},{6,4},{7,5},{8,10},{9,11},{10,... | collective-permute-start | bytes 196616 | tf_op jit(solution)/shard_map/ppermute | solution.py:143
  26.0 1.3 %collective-permute-start.11 = (bf16[16,2048]{1,0:T(8,128)(2,1)S(1)}, bf16[16,2048]{1,0:T(8,128)(2,1)S(1)}, u32[]{:S(2)}, u32[]{:S(2)}) collective-permute-start(bf16[16,2048]{1,0:T(8,128)(2,1)S(1)} %get-tuple-element.21), channel_id=1, source_target_pairs={{0,6},{1,7},{2,4},{3,5},{4,2},{5,3},{6,0},{7,1},{8,14},{9,15},{10,... | collective-permute-start | bytes 196616 | tf_op jit(solution)/shard_map/ppermute | solution.py:143
  27.3 0.0 collective-permute-done.18.refs_1_
  27.3 0.6 %collective-permute-start.12 = (bf16[16,2048]{1,0:T(8,128)(2,1)S(1)}, bf16[16,2048]{1,0:T(8,128)(2,1)S(1)}, u32[]{:S(2)}, u32[]{:S(2)}) collective-permute-start(bf16[16,2048]{1,0:T(8,128)(2,1)S(1)} %get-tuple-element.22), channel_id=1, source_target_pairs={{0,4},{1,5},{2,6},{3,7},{4,0},{5,1},{6,2},{7,3},{8,12},{9,13},{10,... | collective-permute-start | bytes 196616 | tf_op jit(solution)/shard_map/ppermute | solution.py:143
  27.9 0.2 collective-permute-done.19.refs_2_
  28.1 0.3 collective-permute-done.20.refs_3_
  28.4 3.0 %collective-permute-start.21 = (bf16[16,2048]{1,0:T(8,128)(2,1)S(1)}, bf16[16,2048]{1,0:T(8,128)(2,1)S(1)}, u32[]{:S(2)}, u32[]{:S(2)}) collective-permute-start(bf16[16,2048]{1,0:T(8,128)(2,1)S(1)} %cross.1), channel_id=1, source_target_pairs={{0,8},{1,9},{2,10},{3,11},{4,12},{5,13},{6,14},{7,15},{8,0},{9,1},... | collective-permute-start | bytes 196616 | tf_op jit(solution)/shard_map/ppermute | solution.py:143
  31.4 0.0 collective-permute-done.10.refs_2_
  31.4 0.0 collective-permute-done.11.refs_3_
  31.4 0.9 %collective-permute-done.12.refs_4_ = bf16[16,2048]{1,0:T(8,128)(2,1)S(1)} collective-permute-done((bf16[16,2048]{1,0:T(8,128)(2,1)S(1)}, bf16[16,2048]{1,0:T(8,128)(2,1)S(1)}, u32[]{:S(2)}, u32[]{:S(2)}) %collective-permute-start.12) | collective-permute-done | bytes 65568 | tf_op jit(solution)/shard_map/ppermute | solution.py:143
  32.3 1.4 %collective-permute-done.21.refs_5_ = bf16[16,2048]{1,0:T(8,128)(2,1)S(1)} collective-permute-done((bf16[16,2048]{1,0:T(8,128)(2,1)S(1)}, bf16[16,2048]{1,0:T(8,128)(2,1)S(1)}, u32[]{:S(2)}, u32[]{:S(2)}) %collective-permute-start.21) | collective-permute-done | bytes 65568 | tf_op jit(solution)/shard_map/ppermute | solution.py:143
  33.6 0.0 copy-done.3
  33.6 0.7 %mix.1 = bf16[16,2048]{1,0:T(8,128)(2,1)} custom-call(bf16[16,2048]{1,0:T(8,128)(2,1)S(1)} %copy-done.3, f32[16,2048]{1,0:T(8,128)S(1)} %get-tuple-element.19.refs_1_, bf16[16,2048]{1,0:T(8,128)(2,1)S(1)} %collective-permute-done.10.refs_2_, bf16[16,2048]{1,0:T(8,128)(2,1)S(1)} %collective-permute-done.11.refs_3_, ...), custom_call_target="tpu_custom_call" | custom-call | tf_op jit(solution)/shard_map/mix/pallas_call | solution.py:205
  (4 shorter events, 0.1 us)
Async XLA Ops:
  0.8 16.1 %copy-start = (bf16[1,2048,768]{2,1,0:T(8,128)(2,1)S(1)}, bf16[1,2048,768]{2,1,0:T(8,128)(2,1)}, u32[]{:S(2)}) copy-start(bf16[1,2048,768]{2,1,0:T(8,128)(2,1)} %refs_0_.4) | copy-start | bytes 9437188
  0.9 16.1 %copy-start.1 = (bf16[1,2048,768]{2,1,0:T(8,128)(2,1)S(1)}, bf16[1,2048,768]{2,1,0:T(8,128)(2,1)}, u32[]{:S(2)}) copy-start(bf16[1,2048,768]{2,1,0:T(8,128)(2,1)} %refs_1_.3) | copy-start | bytes 9437188
  0.9 16.1 %copy-start.2 = (bf16[1,768,2048]{2,1,0:T(8,128)(2,1)S(1)}, bf16[1,768,2048]{2,1,0:T(8,128)(2,1)}, u32[]{:S(2)}) copy-start(bf16[1,768,2048]{2,1,0:T(8,128)(2,1)} %refs_2_.3) | copy-start | bytes 9437188
  0.9 7.3 %collective-permute-start.5 = (bf16[16,2176]{1,0:T(8,128)(2,1)S(1)}, bf16[16,2176]{1,0:T(8,128)(2,1)S(1)}, u32[]{:S(2)}, u32[]{:S(2)}) collective-permute-start(bf16[16,2176]{1,0:T(8,128)(2,1)S(1)} %pack.1.source_ref), channel_id=1, source_target_pairs={{0,8},{1,9},{2,10},{3,11},{4,12},{5,13},{6,14},{7,15},{8,0},{9,1},... | collective-permute-start | bytes 208904 | tf_op jit(solution)/shard_map/ppermute | solution.py:143
  5.0 6.7 %collective-permute-start.2 = (bf16[16,2176]{1,0:T(8,128)(2,1)S(1)}, bf16[16,2176]{1,0:T(8,128)(2,1)S(1)}, u32[]{:S(2)}, u32[]{:S(2)}) collective-permute-start(bf16[16,2176]{1,0:T(8,128)(2,1)S(1)} %again.1.refs_0_.refs_5_), channel_id=1, source_target_pairs={{0,6},{1,7},{2,4},{3,5},{4,2},{5,3},{6,0},{7,1},{8,14},{9,15},{10,... | collective-permute-start | bytes 208904 | tf_op jit(solution)/shard_map/ppermute | solution.py:143
  7.5 6.1 %collective-permute-start.3 = (bf16[16,2176]{1,0:T(8,128)(2,1)S(1)}, bf16[16,2176]{1,0:T(8,128)(2,1)S(1)}, u32[]{:S(2)}, u32[]{:S(2)}) collective-permute-start(bf16[16,2176]{1,0:T(8,128)(2,1)S(1)} %again.1.refs_0_.refs_5_), channel_id=1, source_target_pairs={{0,4},{1,5},{2,6},{3,7},{4,0},{5,1},{6,2},{7,3},{8,12},{9,13},{10,... | collective-permute-start | bytes 208904 | tf_op jit(solution)/shard_map/ppermute | solution.py:143
  8.2 5.4 %collective-permute-start.6 = (bf16[16,2176]{1,0:T(8,128)(2,1)S(1)}, bf16[16,2176]{1,0:T(8,128)(2,1)S(1)}, u32[]{:S(2)}, u32[]{:S(2)}) collective-permute-start(bf16[16,2176]{1,0:T(8,128)(2,1)S(1)} %collective-permute-done.5.refs_7_), channel_id=1, source_target_pairs={{0,2},{1,3},{2,0},{3,1},{4,6},{5,7},{6,4},{7,5},{8,10},{9,11},{10,... | collective-permute-start | bytes 208904 | tf_op jit(solution)/shard_map/ppermute | solution.py:143
  10.1 5.2 %collective-permute-start.7 = (bf16[16,2176]{1,0:T(8,128)(2,1)S(1)}, bf16[16,2176]{1,0:T(8,128)(2,1)S(1)}, u32[]{:S(2)}, u32[]{:S(2)}) collective-permute-start(bf16[16,2176]{1,0:T(8,128)(2,1)S(1)} %collective-permute-done.5.refs_7_), channel_id=1, source_target_pairs={{0,6},{1,7},{2,4},{3,5},{4,2},{5,3},{6,0},{7,1},{8,14},{9,15},{10,... | collective-permute-start | bytes 208904 | tf_op jit(solution)/shard_map/ppermute | solution.py:143
  11.4 4.3 %collective-permute-start.8 = (bf16[16,2176]{1,0:T(8,128)(2,1)S(1)}, bf16[16,2176]{1,0:T(8,128)(2,1)S(1)}, u32[]{:S(2)}, u32[]{:S(2)}) collective-permute-start(bf16[16,2176]{1,0:T(8,128)(2,1)S(1)} %collective-permute-done.5.refs_7_), channel_id=1, source_target_pairs={{0,4},{1,5},{2,6},{3,7},{4,0},{5,1},{6,2},{7,3},{8,12},{9,13},{10,... | collective-permute-start | bytes 208904 | tf_op jit(solution)/shard_map/ppermute | solution.py:143
  11.7 4.3 %collective-permute-start = (bf16[16,2176]{1,0:T(8,128)(2,1)S(1)}, bf16[16,2176]{1,0:T(8,128)(2,1)S(1)}, u32[]{:S(2)}, u32[]{:S(2)}) collective-permute-start(bf16[16,2176]{1,0:T(8,128)(2,1)S(1)} %again.1.refs_0_.refs_5_), channel_id=1, source_target_pairs={{0,2},{1,3},{2,0},{3,1},{4,6},{5,7},{6,4},{7,5},{8,10},{9,11},{10,... | collective-permute-start | bytes 208904 | tf_op jit(solution)/shard_map/ppermute | solution.py:143
  13.6 2.7 %collective-permute-start.13 = (bf16[16,2176]{1,0:T(8,128)(2,1)S(1)}, bf16[16,2176]{1,0:T(8,128)(2,1)S(1)}, u32[]{:S(2)}, u32[]{:S(2)}) collective-permute-start(bf16[16,2176]{1,0:T(8,128)(2,1)S(1)} %collective-permute-done.5.refs_7_), channel_id=1, source_target_pairs={{0,1},{1,0},{2,3},{3,2},{4,5},{5,4},{6,7},{7,6},{8,9},{9,8},{10,11... | collective-permute-start | bytes 208904 | tf_op jit(solution)/shard_map/ppermute | solution.py:146
  13.6 3.1 %collective-permute-start.14 = (bf16[16,2176]{1,0:T(8,128)(2,1)S(1)}, bf16[16,2176]{1,0:T(8,128)(2,1)S(1)}, u32[]{:S(2)}, u32[]{:S(2)}) collective-permute-start(bf16[16,2176]{1,0:T(8,128)(2,1)S(1)} %collective-permute-done.6.refs_9_.refs_8_), channel_id=1, source_target_pairs={{0,1},{1,0},{2,3},{3,2},{4,5},{5,4},{6,7},{7,6},{8,9},{9,8},{10,11... | collective-permute-start | bytes 208904 | tf_op jit(solution)/shard_map/ppermute | solution.py:146
  15.3 1.4 %collective-permute-start.15 = (bf16[16,2176]{1,0:T(8,128)(2,1)S(1)}, bf16[16,2176]{1,0:T(8,128)(2,1)S(1)}, u32[]{:S(2)}, u32[]{:S(2)}) collective-permute-start(bf16[16,2176]{1,0:T(8,128)(2,1)S(1)} %collective-permute-done.7.refs_10_.refs_9_), channel_id=1, source_target_pairs={{0,1},{1,0},{2,3},{3,2},{4,5},{5,4},{6,7},{7,6},{8,9},{9,8},{10,11... | collective-permute-start | bytes 208904 | tf_op jit(solution)/shard_map/ppermute | solution.py:146
  15.7 1.3 %collective-permute-start.16 = (bf16[16,2176]{1,0:T(8,128)(2,1)S(1)}, bf16[16,2176]{1,0:T(8,128)(2,1)S(1)}, u32[]{:S(2)}, u32[]{:S(2)}) collective-permute-start(bf16[16,2176]{1,0:T(8,128)(2,1)S(1)} %collective-permute-done.8.refs_11_.refs_10_), channel_id=1, source_target_pairs={{0,1},{1,0},{2,3},{3,2},{4,5},{5,4},{6,7},{7,6},{8,9},{9,8},{10,11... | collective-permute-start | bytes 208904 | tf_op jit(solution)/shard_map/ppermute | solution.py:146
  16.0 2.7 %collective-permute-start.4 = (bf16[32,2176]{1,0:T(8,128)(2,1)S(1)}, bf16[32,2176]{1,0:T(8,128)(2,1)S(1)}, u32[]{:S(2)}, u32[]{:S(2)}) collective-permute-start(bf16[32,2176]{1,0:T(8,128)(2,1)S(1)} %join.3), channel_id=1, source_target_pairs={{0,1},{1,0},{2,3},{3,2},{4,5},{5,4},{6,7},{7,6},{8,9},{9,8},{10,11... | collective-permute-start | bytes 417800 | tf_op jit(solution)/shard_map/ppermute | solution.py:146
  16.3 2.4 %collective-permute-start.1 = (bf16[32,2176]{1,0:T(8,128)(2,1)S(1)}, bf16[32,2176]{1,0:T(8,128)(2,1)S(1)}, u32[]{:S(2)}, u32[]{:S(2)}) collective-permute-start(bf16[32,2176]{1,0:T(8,128)(2,1)S(1)} %join.2), channel_id=1, source_target_pairs={{0,1},{1,0},{2,3},{3,2},{4,5},{5,4},{6,7},{7,6},{8,9},{9,8},{10,11... | collective-permute-start | bytes 417800 | tf_op jit(solution)/shard_map/ppermute | solution.py:146
  18.5 15.2 %copy-start.3 = (bf16[16,2048]{1,0:T(8,128)(2,1)S(1)}, bf16[16,2048]{1,0:T(8,128)(2,1)}, u32[]{:S(2)}) copy-start(bf16[16,2048]{1,0:T(8,128)(2,1)} %refs_0_.5) | copy-start | bytes 196612
  18.5 2.2 %collective-permute-start.17 = (bf16[64,2048]{1,0:T(8,128)(2,1)S(1)}, bf16[64,2048]{1,0:T(8,128)(2,1)S(1)}, u32[]{:S(2)}, u32[]{:S(2)}) collective-permute-start(bf16[64,2048]{1,0:T(8,128)(2,1)S(1)} %get-tuple-element.24), channel_id=1, source_target_pairs={{0,1},{1,0},{2,3},{3,2},{4,5},{5,4},{6,7},{7,6},{8,9},{9,8},{10,11... | collective-permute-start | bytes 786440 | tf_op jit(solution)/shard_map/ppermute | solution.py:146
  20.2 4.0 %collective-permute-start.9 = (bf16[64,2048]{1,0:T(8,128)(2,1)S(1)}, bf16[64,2048]{1,0:T(8,128)(2,1)S(1)}, u32[]{:S(2)}, u32[]{:S(2)}) collective-permute-start(bf16[64,2048]{1,0:T(8,128)(2,1)S(1)} %get-tuple-element.18), channel_id=1, source_target_pairs={{0,1},{1,0},{2,3},{3,2},{4,5},{5,4},{6,7},{7,6},{8,9},{9,8},{10,11... | collective-permute-start | bytes 786440 | tf_op jit(solution)/shard_map/ppermute | solution.py:146
  20.7 6.6 %collective-permute-start.18 = (bf16[16,2048]{1,0:T(8,128)(2,1)S(1)}, bf16[16,2048]{1,0:T(8,128)(2,1)S(1)}, u32[]{:S(2)}, u32[]{:S(2)}) collective-permute-start(bf16[16,2048]{1,0:T(8,128)(2,1)S(1)} %get-tuple-element.26), channel_id=1, source_target_pairs={{0,2},{1,3},{2,0},{3,1},{4,6},{5,7},{6,4},{7,5},{8,10},{9,11},{10,... | collective-permute-start | bytes 196616 | tf_op jit(solution)/shard_map/ppermute | solution.py:143
  22.3 5.7 %collective-permute-start.19 = (bf16[16,2048]{1,0:T(8,128)(2,1)S(1)}, bf16[16,2048]{1,0:T(8,128)(2,1)S(1)}, u32[]{:S(2)}, u32[]{:S(2)}) collective-permute-start(bf16[16,2048]{1,0:T(8,128)(2,1)S(1)} %get-tuple-element.27), channel_id=1, source_target_pairs={{0,6},{1,7},{2,4},{3,5},{4,2},{5,3},{6,0},{7,1},{8,14},{9,15},{10,... | collective-permute-start | bytes 196616 | tf_op jit(solution)/shard_map/ppermute | solution.py:143
  23.7 4.7 %collective-permute-start.20 = (bf16[16,2048]{1,0:T(8,128)(2,1)S(1)}, bf16[16,2048]{1,0:T(8,128)(2,1)S(1)}, u32[]{:S(2)}, u32[]{:S(2)}) collective-permute-start(bf16[16,2048]{1,0:T(8,128)(2,1)S(1)} %get-tuple-element.28), channel_id=1, source_target_pairs={{0,4},{1,5},{2,6},{3,7},{4,0},{5,1},{6,2},{7,3},{8,12},{9,13},{10,... | collective-permute-start | bytes 196616 | tf_op jit(solution)/shard_map/ppermute | solution.py:143
  24.3 7.0 %collective-permute-start.10 = (bf16[16,2048]{1,0:T(8,128)(2,1)S(1)}, bf16[16,2048]{1,0:T(8,128)(2,1)S(1)}, u32[]{:S(2)}, u32[]{:S(2)}) collective-permute-start(bf16[16,2048]{1,0:T(8,128)(2,1)S(1)} %get-tuple-element.20), channel_id=1, source_target_pairs={{0,2},{1,3},{2,0},{3,1},{4,6},{5,7},{6,4},{7,5},{8,10},{9,11},{10,... | collective-permute-start | bytes 196616 | tf_op jit(solution)/shard_map/ppermute | solution.py:143
  26.0 5.4 %collective-permute-start.11 = (bf16[16,2048]{1,0:T(8,128)(2,1)S(1)}, bf16[16,2048]{1,0:T(8,128)(2,1)S(1)}, u32[]{:S(2)}, u32[]{:S(2)}) collective-permute-start(bf16[16,2048]{1,0:T(8,128)(2,1)S(1)} %get-tuple-element.21), channel_id=1, source_target_pairs={{0,6},{1,7},{2,4},{3,5},{4,2},{5,3},{6,0},{7,1},{8,14},{9,15},{10,... | collective-permute-start | bytes 196616 | tf_op jit(solution)/shard_map/ppermute | solution.py:143
  27.3 5.0 %collective-permute-start.12 = (bf16[16,2048]{1,0:T(8,128)(2,1)S(1)}, bf16[16,2048]{1,0:T(8,128)(2,1)S(1)}, u32[]{:S(2)}, u32[]{:S(2)}) collective-permute-start(bf16[16,2048]{1,0:T(8,128)(2,1)S(1)} %get-tuple-element.22), channel_id=1, source_target_pairs={{0,4},{1,5},{2,6},{3,7},{4,0},{5,1},{6,2},{7,3},{8,12},{9,13},{10,... | collective-permute-start | bytes 196616 | tf_op jit(solution)/shard_map/ppermute | solution.py:143
  28.4 5.3 %collective-permute-start.21 = (bf16[16,2048]{1,0:T(8,128)(2,1)S(1)}, bf16[16,2048]{1,0:T(8,128)(2,1)S(1)}, u32[]{:S(2)}, u32[]{:S(2)}) collective-permute-start(bf16[16,2048]{1,0:T(8,128)(2,1)S(1)} %cross.1), channel_id=1, source_target_pairs={{0,8},{1,9},{2,10},{3,11},{4,12},{5,13},{6,14},{7,15},{8,0},{9,1},... | collective-permute-start | bytes 196616 | tf_op jit(solution)/shard_map/ppermute | solution.py:143
